TPU v7x, 256 devices: a whole 4x4x8 slice. The times are simulated.
256 devices in a mesh: dp: 4 (over z_hi), expert: 8 (over z_lo, y), tensor: 8 (over x, core).
Axes of the slice: x: 4, y: 4, z: 8 (z_hi: 4, z_lo: 2; z = z_hi * 2 + z_lo), core: 2. Of those that a mesh axis runs over, the one named last changes fastest.
Arguments:
- tokens: bfloat16 [2048, 6144], P(('dp', 'expert', 'tensor'))
- norm_gain: float32 [6144], replicated, may hold values from 0.1 to 1.9
- routes: int32 [2048, 2], P(('dp', 'expert', 'tensor')), may hold values from 0 to 7, all different within a row; in each aligned block of 8 rows (0 to 7, 8 to 15, ...) at most 4 rows name the same one
- route_weights: float32 [2048, 2], P(('dp', 'expert', 'tensor')), may hold values from 0.2 to 1
- w_gate: bfloat16 [8, 6144, 8192], P('expert', None, ('dp', 'tensor')), may hold values from -0.078125 to 0.078125
- w_up: bfloat16 [8, 6144, 8192], P('expert', None, ('dp', 'tensor')), may hold values from -0.078125 to 0.078125
- w_down: bfloat16 [8, 8192, 6144], P('expert', ('dp', 'tensor')), may hold values from -0.0625 to 0.0625
Outputs:
- mixed: bfloat16 [2048, 6144], P(('dp', 'expert', 'tensor'))
Inputs may be any that keep to these rules, and one draw needn't show every extreme that they name: `routes`: A token's two experts differ. In each aligned block of 8 tokens (the tokens of one device) no expert is named more than 4 times, a bound that some block reaches.
All inputs are finite; a program needn't handle non-finite values.
Results may differ from a plain program's by a relative error of at most 0.013.
Values may be sent and summed in bfloat16 or wider, within the bound.
No kernel may reach another device: no remote copies, remote signals or barrier semaphores. Data moves between devices by JAX's collectives and lax.ppermute only.
A program may use at most 128 MiB of HBM per device.

v0:
```python
import functools

import jax
import jax.numpy as jnp
from jax import lax
from jax.experimental import pallas as pl
from jax.experimental.pallas import tpu as pltpu
from jax.sharding import Mesh
from jax.sharding import PartitionSpec as P

AXES = ("dp", "zl", "y", "x", "c")
STEPS = 6


def shift(value, axis, by):
    n = lax.axis_size(axis)
    return lax.ppermute(value, axis, [(i, (i + by) % n) for i in range(n)])


DIMS = {"xa": ("x", 1), "xb": ("x", 3), "za": ("dp", 1), "zb": ("dp", 3)}
CHAINS = (
    (0, 2048, ("za", "zb", "xb", "xa")),
    (2048, 2048, ("zb", "za", "xa", "xb")),
    (4096, 1024, ("xa", "xb", "zb", "za")),
    (5120, 1024, ("xb", "xa", "za", "zb")),
)
CANON = ("xa", "xb", "za", "zb")
UNIT = 32
HALF = 8 * UNIT


def canon_block(order, index):
    return sum(((index >> k) & 1) << CANON.index(d) for k, d in enumerate(order))


def trade(value, dim):
    axis, mask = DIMS[dim]
    return lax.ppermute(value, axis, [(i, i ^ mask) for i in range(4)])


def add(a, b):
    return (a.astype(jnp.float32) + b.astype(jnp.float32)).astype(a.dtype)


def expert_kernel(*refs):
    n = len(CHAINS)
    ins = refs[: 2 * n]
    wg0, wu0, wg1, wu1, wd0, wd1 = refs[2 * n : 2 * n + 6]
    outs = refs[2 * n + 6 : 4 * n + 6]
    part, acc, hidden = refs[4 * n + 6 :]
    step = pl.program_id(0)
    f32 = jnp.float32
    at = 0
    for c, (_, width, order) in enumerate(CHAINS):
        steps = width // PART

        @pl.when((step >= at) & (step < at + steps))
        def _(c=c, order=order):
            for index in range(16):
                to = canon_block(order, index) * UNIT
                row = (index % 8) * UNIT
                part[to : to + UNIT, :] = ins[2 * c + index // 8][row : row + UNIT, :]

        at += steps

    @pl.when(step == 0)
    def _():
        acc[...] = jnp.zeros_like(acc)

    @pl.when(step < STEPS)
    def _():
        for i, w in enumerate((wg0, wu0, wg1, wu1)):
            acc[i] += jnp.dot(part[...], w[...], preferred_element_type=f32)

    @pl.when(step == STEPS - 1)
    def _():
        for i in range(2):
            gate = acc[2 * i]
            hidden[i] = (gate / (1.0 + jnp.exp(-gate)) * acc[2 * i + 1]).astype(hidden.dtype)

    at = STEPS
    for c, (_, width, order) in enumerate(CHAINS):
        steps = width // PART

        @pl.when((step >= at) & (step < at + steps))
        def _(c=c, order=order):
            total = jnp.dot(hidden[0], wd0[...], preferred_element_type=f32) + jnp.dot(
                hidden[1], wd1[...], preferred_element_type=f32
            )
            total = total.astype(jnp.bfloat16)
            for index in range(16):
                row = canon_block(order, index) * UNIT
                to = (index % 8) * UNIT
                outs[2 * c + index // 8][to : to + UNIT, :] = total[row : row + UNIT]

        at += steps


PART = 1024


def expert(pieces, weights):
    width, units = weights[0].shape
    count = 2 * HALF
    first = lambda i: (jnp.minimum(i, STEPS - 1), 0)
    second = lambda i: (0, jnp.maximum(i - STEPS, 0))
    in_specs, out_specs, out_shape = [], [], []
    for start, size, _ in CHAINS:
        low, steps = start // PART, size // PART
        to = lambda i, low=low, steps=steps: (0, jnp.clip(i - low, 0, steps - 1))
        back = lambda i, low=low, steps=steps: (0, jnp.clip(i - STEPS - low, 0, steps - 1))
        in_specs += [pl.BlockSpec((HALF, PART), to)] * 2
        out_specs += [pl.BlockSpec((HALF, PART), back)] * 2
        out_shape += [jax.ShapeDtypeStruct((HALF, size), jnp.bfloat16)] * 2
    return pl.pallas_call(
        expert_kernel,
        grid=(2 * STEPS,),
        out_shape=out_shape,
        in_specs=in_specs
        + [pl.BlockSpec((PART, units), first)] * 4
        + [pl.BlockSpec((units, PART), second)] * 2,
        out_specs=out_specs,
        scratch_shapes=[
            pltpu.VMEM((count, PART), jnp.bfloat16),
            pltpu.VMEM((4, count, units), jnp.float32),
            pltpu.VMEM((2, count, units), jnp.bfloat16),
        ],
        compiler_params=pltpu.CompilerParams(vmem_limit_bytes=40 << 20),
        cost_estimate=pl.CostEstimate(
            flops=12 * count * width * units,
            bytes_accessed=12 * width * units + 4 * count * width,
            transcendentals=2 * count * units,
        ),
        name="expert",
    )(*pieces, *weights)


def relative_slots(routes, cap):
    flat = routes.reshape(-1)
    y_count = lax.axis_size("y")
    z = flat // y_count
    y = flat % y_count
    z = (z + lax.axis_index("zl")) % 2
    y = (y - lax.axis_index("y") + y_count) % y_count
    experts = 2 * y_count
    rel = z * y_count + y
    onehot = (rel[:, None] == jnp.arange(experts, dtype=jnp.int32)[None, :]).astype(jnp.int32)
    before = jnp.cumsum(onehot, axis=0) - onehot
    rank = jnp.sum(before * onehot, axis=1)
    return (rel * cap + rank).reshape(routes.shape)


def per_device(tokens, norm_gain, routes, route_weights, w_gate, w_up, w_down):
    f32 = jnp.float32
    wg0, wu0, wd0 = w_gate[0], w_up[0], w_down[0]
    wg1, wu1, wd1 = (shift(w, "c", 1) for w in (wg0, wu0, wd0))
    weights = (wg0, wu0, wg1, wu1, wd0, wd1)

    cap = 4
    slot_count = 32
    wide = tokens.astype(f32)
    scale = lax.rsqrt(jnp.mean(wide * wide, axis=1, keepdims=True) + 1e-05)
    normed = (wide * scale * norm_gain[None, :]).astype(jnp.bfloat16)
    slots = relative_slots(routes, cap)
    hits = (slots[:, :, None] == jnp.arange(slot_count, dtype=jnp.int32)[None, None, :]).astype(f32)
    picked = jnp.transpose(jnp.sum(hits, axis=1)).astype(jnp.bfloat16)
    buffer = jnp.dot(picked, normed, preferred_element_type=f32).astype(jnp.bfloat16)
    combine = jnp.sum(route_weights[:, :, None] * hits, axis=1)

    keep = buffer[:16]
    got = shift(buffer[16:], "zl", 1)
    blocks = []
    for by in range(4):
        at = slice(by * cap, (by + 1) * cap)
        block = jnp.concatenate([keep[at], got[at]], axis=0)
        blocks.append(shift(block, "y", by) if by else block)
    rows = jnp.concatenate(blocks, axis=0)

    pieces = []
    held = [rows[:, start : start + size] for start, size, _ in CHAINS]
    for step in range(4):
        came = [trade(h, order[step]) for h, (_, _, order) in zip(held, CHAINS)]
        if step < 3:
            held = [jnp.concatenate([h, r], axis=0) for h, r in zip(held, came)]
    for h, r in zip(held, came):
        pieces += [h, r]

    done = expert(pieces, weights)

    held, away = done[0::2], done[1::2]
    for step in (3, 2, 1, 0):
        came = [trade(a, order[step]) for a, (_, _, order) in zip(away, CHAINS)]
        held = [add(h, r) for h, r in zip(held, came)]
        half = held[0].shape[0] // 2
        if step:
            held, away = [h[:half] for h in held], [h[half:] for h in held]
    mine = jnp.concatenate(held, axis=1)

    results = []
    for by in range(4):
        block = mine[8 * by : 8 * by + 8]
        results.append(shift(block, "y", -by) if by else block)
    kept = jnp.concatenate([r[:cap] for r in results], axis=0)
    away = jnp.concatenate([r[cap:] for r in results], axis=0)
    back = jnp.concatenate([kept, shift(away, "zl", 1)], axis=0)
    moe = jnp.dot(combine, back.astype(f32), precision=lax.Precision.HIGHEST)
    return (wide + moe).astype(jnp.bfloat16)


def solution(mesh):
    fine = Mesh(mesh.devices.reshape(4, 2, 4, 4, 2), AXES)
    rows = P(AXES, None)
    return jax.shard_map(
        per_device,
        mesh=fine,
        in_specs=(
            rows,
            P(),
            rows,
            rows,
            P(("zl", "y"), None, ("dp", "x", "c")),
            P(("zl", "y"), None, ("dp", "x", "c")),
            P(("zl", "y"), ("dp", "x", "c"), None),
        ),
        out_specs=rows,
        check_vma=False,
    )
```

profile of v0, /device:TPU:2, one launch (start us, length us, event | category | flops | bytes accessed | tf_op | source)
XLA Modules:
  0.0 251.0 jit_solution(4190827333797762711)
XLA Ops:
  6.5 4.8 %collective-permute-done = bf16[16,6144]{1,0:T(8,128)(2,1)S(1)} collective-permute-done((bf16[16,6144]{1,0:T(8,128)(2,1)S(1)}, bf16[16,6144]{1,0:T(8,128)(2,1)S(1)}, u32[]{:S(2)}, u32[]{:S(2)}) %collective-permute-start) | collective-permute-done | bytes 196640 | tf_op jit(solution)/shard_map/ppermute | solution.py:17
  28.7 4.4 %collective-permute-start.8 = (bf16[32,2048]{1,0:T(8,128)(2,1)S(1)}, bf16[32,2048]{1,0:T(8,128)(2,1)S(1)}, u32[]{:S(2)}, u32[]{:S(2)}) collective-permute-start(bf16[32,2048]{1,0:T(8,128)(2,1)S(1)} %get-tuple-element.28), channel_id=1, source_target_pairs={{0,192},{64,128},{128,64},{192,0},{1,193},{65,129},{129,65},{193,1... | collective-permute-start | bytes 393224 | tf_op jit(solution)/shard_map/ppermute | solution.py:38
  42.1 4.4 %collective-permute-start.5 = (bf16[64,2048]{1,0:T(8,128)(2,1)S(1)}, bf16[64,2048]{1,0:T(8,128)(2,1)S(1)}, u32[]{:S(2)}, u32[]{:S(2)}) collective-permute-start(bf16[64,2048]{1,0:T(8,128)(2,1)S(1)} %pad_maximum_fusion.7), channel_id=1, source_target_pairs={{0,192},{64,128},{128,64},{192,0},{1,193},{65,129},{129,65},{193,1... | collective-permute-start | bytes 786440 | tf_op jit(solution)/shard_map/ppermute | solution.py:38
  50.8 4.3 %collective-permute-done.5 = bf16[64,2048]{1,0:T(8,128)(2,1)S(1)} collective-permute-done((bf16[64,2048]{1,0:T(8,128)(2,1)S(1)}, bf16[64,2048]{1,0:T(8,128)(2,1)S(1)}, u32[]{:S(2)}, u32[]{:S(2)}) %collective-permute-start.5) | collective-permute-done | bytes 262176 | tf_op jit(solution)/shard_map/ppermute | solution.py:38
  55.1 4.7 %collective-permute-start.14 = (bf16[128,1024]{1,0:T(8,128)(2,1)S(1)}, bf16[128,1024]{1,0:T(8,128)(2,1)S(1)}, u32[]{:S(2)}, u32[]{:S(2)}) collective-permute-start(bf16[128,1024]{1,0:T(8,128)(2,1)S(1)} %pad_maximum_fusion.9), channel_id=1, source_target_pairs={{0,192},{64,128},{128,64},{192,0},{1,193},{65,129},{129,65},{193,1... | collective-permute-start | bytes 786440 | tf_op jit(solution)/shard_map/ppermute | solution.py:38
  60.0 3.9 %collective-permute-start.10 = (bf16[128,2048]{1,0:T(8,128)(2,1)S(1)}, bf16[128,2048]{1,0:T(8,128)(2,1)S(1)}, u32[]{:S(2)}, u32[]{:S(2)}) collective-permute-start(bf16[128,2048]{1,0:T(8,128)(2,1)S(1)} %pad_maximum_fusion.3), channel_id=1, source_target_pairs={{0,2},{2,0},{4,6},{6,4},{1,3},{3,1},{5,7},{7,5},{8,10},{10,8},{12,... | collective-permute-start | bytes 1572872 | tf_op jit(solution)/shard_map/ppermute | solution.py:38
  71.3 4.5 %collective-permute-done.6 = bf16[128,2048]{1,0:T(8,128)(2,1)S(1)} collective-permute-done((bf16[128,2048]{1,0:T(8,128)(2,1)S(1)}, bf16[128,2048]{1,0:T(8,128)(2,1)S(1)}, u32[]{:S(2)}, u32[]{:S(2)}) %collective-permute-start.6) | collective-permute-done | bytes 524320 | tf_op jit(solution)/shard_map/ppermute | solution.py:38
  79.5 10.9 %collective-permute-done.15.refs_5_ = bf16[256,1024]{1,0:T(8,128)(2,1)S(1)} collective-permute-done((bf16[256,1024]{1,0:T(8,128)(2,1)S(1)}, bf16[256,1024]{1,0:T(8,128)(2,1)S(1)}, u32[]{:S(2)}, u32[]{:S(2)}) %collective-permute-start.15) | collective-permute-done | bytes 524320 | tf_op jit(solution)/shard_map/ppermute | solution.py:38
  91.1 4.3 %collective-permute-done.19.refs_7_ = bf16[256,1024]{1,0:T(8,128)(2,1)S(1)} collective-permute-done((bf16[256,1024]{1,0:T(8,128)(2,1)S(1)}, bf16[256,1024]{1,0:T(8,128)(2,1)S(1)}, u32[]{:S(2)}, u32[]{:S(2)}) %collective-permute-start.19) | collective-permute-done | bytes 524320 | tf_op jit(solution)/shard_map/ppermute | solution.py:38
  97.5 15.7 %collective-permute-done.7.refs_1_ = bf16[256,2048]{1,0:T(8,128)(2,1)S(1)} collective-permute-done((bf16[256,2048]{1,0:T(8,128)(2,1)S(1)}, bf16[256,2048]{1,0:T(8,128)(2,1)S(1)}, u32[]{:S(2)}, u32[]{:S(2)}) %collective-permute-start.7) | collective-permute-done | bytes 1048608 | tf_op jit(solution)/shard_map/ppermute | solution.py:38
  113.2 5.3 %collective-permute-done.11.refs_3_ = bf16[256,2048]{1,0:T(8,128)(2,1)S(1)} collective-permute-done((bf16[256,2048]{1,0:T(8,128)(2,1)S(1)}, bf16[256,2048]{1,0:T(8,128)(2,1)S(1)}, u32[]{:S(2)}, u32[]{:S(2)}) %collective-permute-start.11) | collective-permute-done | bytes 1048608 | tf_op jit(solution)/shard_map/ppermute | solution.py:38
  118.5 17.6 %expert.1 = (bf16[256,2048]{1,0:T(8,128)(2,1)S(1)}, bf16[256,2048]{1,0:T(8,128)(2,1)S(1)}, bf16[256,2048]{1,0:T(8,128)(2,1)S(1)}, bf16[256,2048]{1,0:T(8,128)(2,...) custom-call(bf16[256,2048]{1,0:T(8,128)(2,1)S(1)} %pad_maximum_fusio, ...), custom_call_target="tpu_custom_call" | custom-call | flops 9663676416 | bytes 31457280 | tf_op jit(solution)/shard_map/expert/pallas_call | solution.py:115
  136.1 5.3 %collective-permute-start.31 = (bf16[256,1024]{1,0:T(8,128)(2,1)S(1)}, bf16[256,1024]{1,0:T(8,128)(2,1)S(1)}, u32[]{:S(2)}, u32[]{:S(2)}) collective-permute-start(bf16[256,1024]{1,0:T(8,128)(2,1)S(1)} %get-tuple-element.18), channel_id=1, source_target_pairs={{0,64},{64,0},{128,192},{192,128},{1,65},{65,1},{129,193},{193,129... | collective-permute-start | bytes 1572872 | tf_op jit(solution)/shard_map/ppermute | solution.py:38
  141.4 4.6 %collective-permute-start.35 = (bf16[256,1024]{1,0:T(8,128)(2,1)S(1)}, bf16[256,1024]{1,0:T(8,128)(2,1)S(1)}, u32[]{:S(2)}, u32[]{:S(2)}) collective-permute-start(bf16[256,1024]{1,0:T(8,128)(2,1)S(1)} %get-tuple-element.20), channel_id=1, source_target_pairs={{0,192},{64,128},{128,64},{192,0},{1,193},{65,129},{129,65},{193,1... | collective-permute-start | bytes 1572872 | tf_op jit(solution)/shard_map/ppermute | solution.py:38
  146.0 13.0 %collective-permute-done.31 = bf16[256,1024]{1,0:T(8,128)(2,1)S(1)} collective-permute-done((bf16[256,1024]{1,0:T(8,128)(2,1)S(1)}, bf16[256,1024]{1,0:T(8,128)(2,1)S(1)}, u32[]{:S(2)}, u32[]{:S(2)}) %collective-permute-start.31) | collective-permute-done | bytes 524320 | tf_op jit(solution)/shard_map/ppermute | solution.py:38
  159.1 5.0 %collective-permute-start.32 = (bf16[128,1024]{1,0:T(8,128)(2,1)S(1)}, bf16[128,1024]{1,0:T(8,128)(2,1)S(1)}, u32[]{:S(2)}, u32[]{:S(2)}) collective-permute-start(bf16[128,1024]{1,0:T(8,128)(2,1)S(1)} %slice.226), channel_id=1, source_target_pairs={{0,192},{64,128},{128,64},{192,0},{1,193},{65,129},{129,65},{193,1... | collective-permute-start | bytes 786440 | tf_op jit(solution)/shard_map/ppermute | solution.py:38
  164.5 9.6 %collective-permute-start.23 = (bf16[256,2048]{1,0:T(8,128)(2,1)S(1)}, bf16[256,2048]{1,0:T(8,128)(2,1)S(1)}, u32[]{:S(2)}, u32[]{:S(2)}) collective-permute-start(bf16[256,2048]{1,0:T(8,128)(2,1)S(1)} %get-tuple-element.14), channel_id=1, source_target_pairs={{0,2},{2,0},{4,6},{6,4},{1,3},{3,1},{5,7},{7,5},{8,10},{10,8},{12,... | collective-permute-start | bytes 3145736 | tf_op jit(solution)/shard_map/ppermute | solution.py:38
  180.2 18.1 %collective-permute-done.33 = bf16[64,1024]{1,0:T(8,128)(2,1)S(1)} collective-permute-done((bf16[64,1024]{1,0:T(8,128)(2,1)S(1)}, bf16[64,1024]{1,0:T(8,128)(2,1)S(1)}, u32[]{:S(2)}, u32[]{:S(2)}) %collective-permute-start.33) | collective-permute-done | bytes 131104 | tf_op jit(solution)/shard_map/ppermute | solution.py:38
  205.9 7.2 %collective-permute-done.24 = bf16[128,2048]{1,0:T(8,128)(2,1)S(1)} collective-permute-done((bf16[128,2048]{1,0:T(8,128)(2,1)S(1)}, bf16[128,2048]{1,0:T(8,128)(2,1)S(1)}, u32[]{:S(2)}, u32[]{:S(2)}) %collective-permute-start.24) | collective-permute-done | bytes 524320 | tf_op jit(solution)/shard_map/ppermute | solution.py:38
  213.2 5.4 %collective-permute-start.25 = (bf16[64,2048]{1,0:T(8,128)(2,1)S(1)}, bf16[64,2048]{1,0:T(8,128)(2,1)S(1)}, u32[]{:S(2)}, u32[]{:S(2)}) collective-permute-start(bf16[64,2048]{1,0:T(8,128)(2,1)S(1)} %slice.216), channel_id=1, source_target_pairs={{0,192},{64,128},{128,64},{192,0},{1,193},{65,129},{129,65},{193,1... | collective-permute-start | bytes 786440 | tf_op jit(solution)/shard_map/ppermute | solution.py:38
  219.7 4.6 %collective-permute-done.25 = bf16[64,2048]{1,0:T(8,128)(2,1)S(1)} collective-permute-done((bf16[64,2048]{1,0:T(8,128)(2,1)S(1)}, bf16[64,2048]{1,0:T(8,128)(2,1)S(1)}, u32[]{:S(2)}, u32[]{:S(2)}) %collective-permute-start.25) | collective-permute-done | bytes 262176 | tf_op jit(solution)/shard_map/ppermute | solution.py:38
  224.7 4.1 %collective-permute-done.29 = bf16[64,2048]{1,0:T(8,128)(2,1)S(1)} collective-permute-done((bf16[64,2048]{1,0:T(8,128)(2,1)S(1)}, bf16[64,2048]{1,0:T(8,128)(2,1)S(1)}, u32[]{:S(2)}, u32[]{:S(2)}) %collective-permute-start.29) | collective-permute-done | bytes 262176 | tf_op jit(solution)/shard_map/ppermute | solution.py:38
  230.4 5.6 %collective-permute-done.30 = bf16[32,2048]{1,0:T(8,128)(2,1)S(1)} collective-permute-done((bf16[32,2048]{1,0:T(8,128)(2,1)S(1)}, bf16[32,2048]{1,0:T(8,128)(2,1)S(1)}, u32[]{:S(2)}, u32[]{:S(2)}) %collective-permute-start.30) | collective-permute-done | bytes 131104 | tf_op jit(solution)/shard_map/ppermute | solution.py:38
  244.3 5.6 %collective-permute-done.42 = bf16[16,6144]{1,0:T(8,128)(2,1)S(1)} collective-permute-done((bf16[16,6144]{1,0:T(8,128)(2,1)S(1)}, bf16[16,6144]{1,0:T(8,128)(2,1)S(1)}, u32[]{:S(2)}, u32[]{:S(2)}) %collective-permute-start.42) | collective-permute-done | bytes 196640 | tf_op jit(solution)/shard_map/ppermute | solution.py:17
  (136 shorter events, 77.5 us)
Async XLA Ops:
  17.6 100.8 %collective-permute-start.20 = (bf16[6144,256]{1,0:T(8,128)(2,1)}, bf16[6144,256]{1,0:T(8,128)(2,1)}, u32[]{:S(2)}, u32[]{:S(2)}) collective-permute-start(bf16[6144,256]{1,0:T(8,128)(2,1)} %bitcast.6), channel_id=1, source_target_pairs={{0,1},{1,0},{2,3},{3,2},{4,5},{5,4},{6,7},{7,6},{8,9},{9,8},{10,11... | collective-permute-start | bytes 9437192 | tf_op jit(solution)/shard_map/ppermute | solution.py:17
  17.7 100.8 %collective-permute-start.21 = (bf16[6144,256]{1,0:T(8,128)(2,1)}, bf16[6144,256]{1,0:T(8,128)(2,1)}, u32[]{:S(2)}, u32[]{:S(2)}) collective-permute-start(bf16[6144,256]{1,0:T(8,128)(2,1)} %bitcast.8), channel_id=1, source_target_pairs={{0,1},{1,0},{2,3},{3,2},{4,5},{5,4},{6,7},{7,6},{8,9},{9,8},{10,11... | collective-permute-start | bytes 9437192 | tf_op jit(solution)/shard_map/ppermute | solution.py:17
  18.4 100.0 %collective-permute-start.22 = (bf16[256,6144]{1,0:T(8,128)(2,1)}, bf16[256,6144]{1,0:T(8,128)(2,1)}, u32[]{:S(2)}, u32[]{:S(2)}) collective-permute-start(bf16[256,6144]{1,0:T(8,128)(2,1)} %bitcast.10), channel_id=1, source_target_pairs={{0,1},{1,0},{2,3},{3,2},{4,5},{5,4},{6,7},{7,6},{8,9},{9,8},{10,11... | collective-permute-start | bytes 9437192 | tf_op jit(solution)/shard_map/ppermute | solution.py:17
  38.6 10.9 %collective-permute-start.9 = (bf16[64,2048]{1,0:T(8,128)(2,1)S(1)}, bf16[64,2048]{1,0:T(8,128)(2,1)S(1)}, u32[]{:S(2)}, u32[]{:S(2)}) collective-permute-start(bf16[64,2048]{1,0:T(8,128)(2,1)S(1)} %pad_maximum_fusion.8), channel_id=1, source_target_pairs={{0,64},{64,0},{128,192},{192,128},{1,65},{65,1},{129,193},{193,129... | collective-permute-start | bytes 786440 | tf_op jit(solution)/shard_map/ppermute | solution.py:38
  42.1 13.1 %collective-permute-start.5 = (bf16[64,2048]{1,0:T(8,128)(2,1)S(1)}, bf16[64,2048]{1,0:T(8,128)(2,1)S(1)}, u32[]{:S(2)}, u32[]{:S(2)}) collective-permute-start(bf16[64,2048]{1,0:T(8,128)(2,1)S(1)} %pad_maximum_fusion.7), channel_id=1, source_target_pairs={{0,192},{64,128},{128,64},{192,0},{1,193},{65,129},{129,65},{193,1... | collective-permute-start | bytes 786440 | tf_op jit(solution)/shard_map/ppermute | solution.py:38
  49.5 10.5 %collective-permute-start.18 = (bf16[128,1024]{1,0:T(8,128)(2,1)S(1)}, bf16[128,1024]{1,0:T(8,128)(2,1)S(1)}, u32[]{:S(2)}, u32[]{:S(2)}) collective-permute-start(bf16[128,1024]{1,0:T(8,128)(2,1)S(1)} %pad_maximum_fusion.10), channel_id=1, source_target_pairs={{0,64},{64,0},{128,192},{192,128},{1,65},{65,1},{129,193},{193,129... | collective-permute-start | bytes 786440 | tf_op jit(solution)/shard_map/ppermute | solution.py:38
  55.1 10.3 %collective-permute-start.14 = (bf16[128,1024]{1,0:T(8,128)(2,1)S(1)}, bf16[128,1024]{1,0:T(8,128)(2,1)S(1)}, u32[]{:S(2)}, u32[]{:S(2)}) collective-permute-start(bf16[128,1024]{1,0:T(8,128)(2,1)S(1)} %pad_maximum_fusion.9), channel_id=1, source_target_pairs={{0,192},{64,128},{128,64},{192,0},{1,193},{65,129},{129,65},{193,1... | collective-permute-start | bytes 786440 | tf_op jit(solution)/shard_map/ppermute | solution.py:38
  60.0 11.1 %collective-permute-start.10 = (bf16[128,2048]{1,0:T(8,128)(2,1)S(1)}, bf16[128,2048]{1,0:T(8,128)(2,1)S(1)}, u32[]{:S(2)}, u32[]{:S(2)}) collective-permute-start(bf16[128,2048]{1,0:T(8,128)(2,1)S(1)} %pad_maximum_fusion.3), channel_id=1, source_target_pairs={{0,2},{2,0},{4,6},{6,4},{1,3},{3,1},{5,7},{7,5},{8,10},{10,8},{12,... | collective-permute-start | bytes 1572872 | tf_op jit(solution)/shard_map/ppermute | solution.py:38
  65.5 10.3 %collective-permute-start.6 = (bf16[128,2048]{1,0:T(8,128)(2,1)S(1)}, bf16[128,2048]{1,0:T(8,128)(2,1)S(1)}, u32[]{:S(2)}, u32[]{:S(2)}) collective-permute-start(bf16[128,2048]{1,0:T(8,128)(2,1)S(1)} %pad_maximum_fusion.2), channel_id=1, source_target_pairs={{0,6},{2,4},{4,2},{6,0},{1,7},{3,5},{5,3},{7,1},{8,14},{10,12},{12... | collective-permute-start | bytes 1572872 | tf_op jit(solution)/shard_map/ppermute | solution.py:38
  71.1 19.3 %collective-permute-start.15 = (bf16[256,1024]{1,0:T(8,128)(2,1)S(1)}, bf16[256,1024]{1,0:T(8,128)(2,1)S(1)}, u32[]{:S(2)}, u32[]{:S(2)}) collective-permute-start(bf16[256,1024]{1,0:T(8,128)(2,1)S(1)} %pad_maximum_fusion.4.refs_4_), channel_id=1, source_target_pairs={{0,64},{64,0},{128,192},{192,128},{1,65},{65,1},{129,193},{193,129... | collective-permute-start | bytes 1572872 | tf_op jit(solution)/shard_map/ppermute | solution.py:38
  75.8 19.7 %collective-permute-start.19 = (bf16[256,1024]{1,0:T(8,128)(2,1)S(1)}, bf16[256,1024]{1,0:T(8,128)(2,1)S(1)}, u32[]{:S(2)}, u32[]{:S(2)}) collective-permute-start(bf16[256,1024]{1,0:T(8,128)(2,1)S(1)} %pad_maximum_fusion.5.refs_6_), channel_id=1, source_target_pairs={{0,192},{64,128},{128,64},{192,0},{1,193},{65,129},{129,65},{193,1... | collective-permute-start | bytes 1572872 | tf_op jit(solution)/shard_map/ppermute | solution.py:38
  90.3 22.9 %collective-permute-start.7 = (bf16[256,2048]{1,0:T(8,128)(2,1)S(1)}, bf16[256,2048]{1,0:T(8,128)(2,1)S(1)}, u32[]{:S(2)}, u32[]{:S(2)}) collective-permute-start(bf16[256,2048]{1,0:T(8,128)(2,1)S(1)} %pad_maximum_fusion.refs_0_), channel_id=1, source_target_pairs={{0,2},{2,0},{4,6},{6,4},{1,3},{3,1},{5,7},{7,5},{8,10},{10,8},{12,... | collective-permute-start | bytes 3145736 | tf_op jit(solution)/shard_map/ppermute | solution.py:38
  95.5 23.0 %collective-permute-start.11 = (bf16[256,2048]{1,0:T(8,128)(2,1)S(1)}, bf16[256,2048]{1,0:T(8,128)(2,1)S(1)}, u32[]{:S(2)}, u32[]{:S(2)}) collective-permute-start(bf16[256,2048]{1,0:T(8,128)(2,1)S(1)} %pad_maximum_fusion.1.refs_2_), channel_id=1, source_target_pairs={{0,6},{2,4},{4,2},{6,0},{1,7},{3,5},{5,3},{7,1},{8,14},{10,12},{12... | collective-permute-start | bytes 3145736 | tf_op jit(solution)/shard_map/ppermute | solution.py:38
  136.1 22.8 %collective-permute-start.31 = (bf16[256,1024]{1,0:T(8,128)(2,1)S(1)}, bf16[256,1024]{1,0:T(8,128)(2,1)S(1)}, u32[]{:S(2)}, u32[]{:S(2)}) collective-permute-start(bf16[256,1024]{1,0:T(8,128)(2,1)S(1)} %get-tuple-element.18), channel_id=1, source_target_pairs={{0,64},{64,0},{128,192},{192,128},{1,65},{65,1},{129,193},{193,129... | collective-permute-start | bytes 1572872 | tf_op jit(solution)/shard_map/ppermute | solution.py:38
  141.4 22.8 %collective-permute-start.35 = (bf16[256,1024]{1,0:T(8,128)(2,1)S(1)}, bf16[256,1024]{1,0:T(8,128)(2,1)S(1)}, u32[]{:S(2)}, u32[]{:S(2)}) collective-permute-start(bf16[256,1024]{1,0:T(8,128)(2,1)S(1)} %get-tuple-element.20), channel_id=1, source_target_pairs={{0,192},{64,128},{128,64},{192,0},{1,193},{65,129},{129,65},{193,1... | collective-permute-start | bytes 1572872 | tf_op jit(solution)/shard_map/ppermute | solution.py:38
  159.1 15.2 %collective-permute-start.32 = (bf16[128,1024]{1,0:T(8,128)(2,1)S(1)}, bf16[128,1024]{1,0:T(8,128)(2,1)S(1)}, u32[]{:S(2)}, u32[]{:S(2)}) collective-permute-start(bf16[128,1024]{1,0:T(8,128)(2,1)S(1)} %slice.226), channel_id=1, source_target_pairs={{0,192},{64,128},{128,64},{192,0},{1,193},{65,129},{129,65},{193,1... | collective-permute-start | bytes 786440 | tf_op jit(solution)/shard_map/ppermute | solution.py:38
  164.4 12.0 %collective-permute-start.36 = (bf16[128,1024]{1,0:T(8,128)(2,1)S(1)}, bf16[128,1024]{1,0:T(8,128)(2,1)S(1)}, u32[]{:S(2)}, u32[]{:S(2)}) collective-permute-start(bf16[128,1024]{1,0:T(8,128)(2,1)S(1)} %slice.232), channel_id=1, source_target_pairs={{0,64},{64,0},{128,192},{192,128},{1,65},{65,1},{129,193},{193,129... | collective-permute-start | bytes 786440 | tf_op jit(solution)/shard_map/ppermute | solution.py:38
  164.5 38.9 %collective-permute-start.23 = (bf16[256,2048]{1,0:T(8,128)(2,1)S(1)}, bf16[256,2048]{1,0:T(8,128)(2,1)S(1)}, u32[]{:S(2)}, u32[]{:S(2)}) collective-permute-start(bf16[256,2048]{1,0:T(8,128)(2,1)S(1)} %get-tuple-element.14), channel_id=1, source_target_pairs={{0,2},{2,0},{4,6},{6,4},{1,3},{3,1},{5,7},{7,5},{8,10},{10,8},{12,... | collective-permute-start | bytes 3145736 | tf_op jit(solution)/shard_map/ppermute | solution.py:38
  174.1 29.8 %collective-permute-start.27 = (bf16[256,2048]{1,0:T(8,128)(2,1)S(1)}, bf16[256,2048]{1,0:T(8,128)(2,1)S(1)}, u32[]{:S(2)}, u32[]{:S(2)}) collective-permute-start(bf16[256,2048]{1,0:T(8,128)(2,1)S(1)} %get-tuple-element.16), channel_id=1, source_target_pairs={{0,6},{2,4},{4,2},{6,0},{1,7},{3,5},{5,3},{7,1},{8,14},{10,12},{12... | collective-permute-start | bytes 3145736 | tf_op jit(solution)/shard_map/ppermute | solution.py:38
  174.4 23.8 %collective-permute-start.33 = (bf16[64,1024]{1,0:T(8,128)(2,1)S(1)}, bf16[64,1024]{1,0:T(8,128)(2,1)S(1)}, u32[]{:S(2)}, u32[]{:S(2)}) collective-permute-start(bf16[64,1024]{1,0:T(8,128)(2,1)S(1)} %slice.228), channel_id=1, source_target_pairs={{0,6},{2,4},{4,2},{6,0},{1,7},{3,5},{5,3},{7,1},{8,14},{10,12},{12... | collective-permute-start | bytes 393224 | tf_op jit(solution)/shard_map/ppermute | solution.py:38
  176.4 23.4 %collective-permute-start.37 = (bf16[64,1024]{1,0:T(8,128)(2,1)S(1)}, bf16[64,1024]{1,0:T(8,128)(2,1)S(1)}, u32[]{:S(2)}, u32[]{:S(2)}) collective-permute-start(bf16[64,1024]{1,0:T(8,128)(2,1)S(1)} %slice.234), channel_id=1, source_target_pairs={{0,2},{2,0},{4,6},{6,4},{1,3},{3,1},{5,7},{7,5},{8,10},{10,8},{12,... | collective-permute-start | bytes 393224 | tf_op jit(solution)/shard_map/ppermute | solution.py:38
  204.3 14.3 %collective-permute-start.28 = (bf16[128,2048]{1,0:T(8,128)(2,1)S(1)}, bf16[128,2048]{1,0:T(8,128)(2,1)S(1)}, u32[]{:S(2)}, u32[]{:S(2)}) collective-permute-start(bf16[128,2048]{1,0:T(8,128)(2,1)S(1)} %slice.220), channel_id=1, source_target_pairs={{0,2},{2,0},{4,6},{6,4},{1,3},{3,1},{5,7},{7,5},{8,10},{10,8},{12,... | collective-permute-start | bytes 1572872 | tf_op jit(solution)/shard_map/ppermute | solution.py:38
  213.2 11.1 %collective-permute-start.25 = (bf16[64,2048]{1,0:T(8,128)(2,1)S(1)}, bf16[64,2048]{1,0:T(8,128)(2,1)S(1)}, u32[]{:S(2)}, u32[]{:S(2)}) collective-permute-start(bf16[64,2048]{1,0:T(8,128)(2,1)S(1)} %slice.216), channel_id=1, source_target_pairs={{0,192},{64,128},{128,64},{192,0},{1,193},{65,129},{129,65},{193,1... | collective-permute-start | bytes 786440 | tf_op jit(solution)/shard_map/ppermute | solution.py:38
  218.8 9.9 %collective-permute-start.29 = (bf16[64,2048]{1,0:T(8,128)(2,1)S(1)}, bf16[64,2048]{1,0:T(8,128)(2,1)S(1)}, u32[]{:S(2)}, u32[]{:S(2)}) collective-permute-start(bf16[64,2048]{1,0:T(8,128)(2,1)S(1)} %slice.222), channel_id=1, source_target_pairs={{0,64},{64,0},{128,192},{192,128},{1,65},{65,1},{129,193},{193,129... | collective-permute-start | bytes 786440 | tf_op jit(solution)/shard_map/ppermute | solution.py:38
  (20 other events, 143.1 us)
where the time goes:
time: 253 us; the launch traced here: 251 us
  waiting for transfers between devices  131 us (52%)
  starting transfers between devices  92.9 us (37%)
  Pallas kernels  17.6 us (7%)
  other arithmetic  4.81 us (2%)
    ppermute x32, waiting for transfers between devices, trade(): return lax.ppermute(value, axis, [(i, i ^ mask) for i in range(4)])  114 us
    ppermute x32, starting transfers between devices, trade(): return lax.ppermute(value, axis, [(i, i ^ mask) for i in range(4)])  80.9 us
    ppermute x11, waiting for transfers between devices, shift(): return lax.ppermute(value, axis, [(i, (i + by) % n) for i in range(n)])  17.7 us
    pallas_call x1, Pallas kernels, expert(): pl.pallas_call(expert_kernel, grid=(2 * STEPS,), out_shape=out_shape, in_...  17.6 us
    ppermute x11, starting transfers between devices, shift(): return lax.ppermute(value, axis, [(i, (i + by) % n) for i in range(n)])  12 us
  transfers between devices with their start and end apart: 43, of which 27 were waited for; matrix products, arithmetic and copies ran while one was open for 1% of the time, Pallas kernels for 0%

commit v1 on v0

--- a/solution.py
+++ b/solution.py
@@ -153,9 +153,6 @@
 def per_device(tokens, norm_gain, routes, route_weights, w_gate, w_up, w_down):
     f32 = jnp.float32
     wg0, wu0, wd0 = w_gate[0], w_up[0], w_down[0]
-    wg1, wu1, wd1 = (shift(w, "c", 1) for w in (wg0, wu0, wd0))
-    weights = (wg0, wu0, wg1, wu1, wd0, wd1)
-
     cap = 4
     slot_count = 32
     wide = tokens.astype(f32)
@@ -168,28 +165,38 @@
     combine = jnp.sum(route_weights[:, :, None] * hits, axis=1)
 
     keep = buffer[:16]
-    got = shift(buffer[16:], "zl", 1)
+    got, wg1 = lax.optimization_barrier((shift(buffer[16:], "zl", 1), shift(wg0, "c", 1)))
     blocks = []
     for by in range(4):
         at = slice(by * cap, (by + 1) * cap)
         block = jnp.concatenate([keep[at], got[at]], axis=0)
         blocks.append(shift(block, "y", by) if by else block)
+    blocks, wu0, wg1 = lax.optimization_barrier((blocks, wu0, wg1))
+    wu1 = shift(wu0, "c", 1)
     rows = jnp.concatenate(blocks, axis=0)
 
     pieces = []
     held = [rows[:, start : start + size] for start, size, _ in CHAINS]
     for step in range(4):
         came = [trade(h, order[step]) for h, (_, _, order) in zip(held, CHAINS)]
+        if step == 0:
+            came, wu1, wd0 = lax.optimization_barrier((came, wu1, wd0))
+        elif step == 1:
+            wd1 = shift(wd0, "c", 1)
+            came, wd1 = lax.optimization_barrier((came, wd1))
+        else:
+            came = lax.optimization_barrier(came)
         if step < 3:
             held = [jnp.concatenate([h, r], axis=0) for h, r in zip(held, came)]
     for h, r in zip(held, came):
         pieces += [h, r]
 
-    done = expert(pieces, weights)
+    done = expert(pieces, (wg0, wu0, wg1, wu1, wd0, wd1))
 
     held, away = done[0::2], done[1::2]
     for step in (3, 2, 1, 0):
         came = [trade(a, order[step]) for a, (_, _, order) in zip(away, CHAINS)]
+        came = lax.optimization_barrier(came)
         held = [add(h, r) for h, r in zip(held, came)]
         half = held[0].shape[0] // 2
         if step:

time: 253 us -> 213 us (0.84)
  starting transfers between devices: 92.9 us -> 68.4 us
  waiting for transfers between devices: 131 us -> 117 us
    ppermute x32, starting transfers between devices: 80.9 us -> 55 us  [trade(): return lax.ppermute(value, axis, [(i, i ^ mask) for i in range(4)])]
    ppermute x32, waiting for transfers between devices: 114 us -> 98.7 us  [trade(): return lax.ppermute(value, axis, [(i, i ^ mask) for i in range(4)])]
  transfers between devices with their start and end apart: 43 -> 43, of which waited for: 27 -> 27; matrix products, arithmetic and copies ran while one was open for 1% -> 3% of each run, Pallas kernels for 0% -> 0%
where the time goes in v1:
time: 213 us; the launch traced here: 212 us
  waiting for transfers between devices  117 us (55%)
  starting transfers between devices  68.4 us (32%)
  Pallas kernels  17.6 us (8%)
  other arithmetic  5.07 us (2%)
  matrix products  2.14 us (1%)
    ppermute x32, waiting for transfers between devices, trade(): return lax.ppermute(value, axis, [(i, i ^ mask) for i in range(4)])  98.7 us
    ppermute x32, starting transfers between devices, trade(): return lax.ppermute(value, axis, [(i, i ^ mask) for i in range(4)])  55 us
    ppermute x11, waiting for transfers between devices, shift(): return lax.ppermute(value, axis, [(i, (i + by) % n) for i in range(n)])  17.9 us
    pallas_call x1, Pallas kernels, expert(): pl.pallas_call(expert_kernel, grid=(2 * STEPS,), out_shape=out_shape, in_...  17.6 us
    ppermute x11, starting transfers between devices, shift(): return lax.ppermute(value, axis, [(i, (i + by) % n) for i in range(n)])  13.4 us
  transfers between devices with their start and end apart: 43, of which 27 were waited for; matrix products, arithmetic and copies ran while one was open for 3% of the time, Pallas kernels for 0%

profile of v1, /device:TPU:2, one launch (start us, length us, event | category | flops | bytes accessed | tf_op | source)
XLA Modules:
  0.0 212.1 jit_solution(11810430548025321288)
XLA Ops:
  6.7 5.5 %collective-permute-done = bf16[16,6144]{1,0:T(8,128)(2,1)S(1)} collective-permute-done((bf16[16,6144]{1,0:T(8,128)(2,1)S(1)}, bf16[16,6144]{1,0:T(8,128)(2,1)S(1)}, u32[]{:S(2)}, u32[]{:S(2)}) %collective-permute-start) | collective-permute-done | bytes 196640 | tf_op jit(solution)/shard_map/ppermute | solution.py:17
  14.0 3.0 %collective-permute-start.3 = (bf16[8,6144]{1,0:T(8,128)(2,1)S(1)}, bf16[8,6144]{1,0:T(8,128)(2,1)S(1)}, u32[]{:S(2)}, u32[]{:S(2)}) collective-permute-start(bf16[8,6144]{1,0:T(8,128)(2,1)S(1)} %pad_maximum_fusion.15), channel_id=1, source_target_pairs={{0,16},{8,24},{16,0},{24,8},{1,17},{9,25},{17,1},{25,9},{2,18},{10... | collective-permute-start | bytes 294920 | tf_op jit(solution)/shard_map/ppermute | solution.py:17
  18.6 2.9 %collective-permute-done.3 = bf16[8,6144]{1,0:T(8,128)(2,1)S(1)} collective-permute-done((bf16[8,6144]{1,0:T(8,128)(2,1)S(1)}, bf16[8,6144]{1,0:T(8,128)(2,1)S(1)}, u32[]{:S(2)}, u32[]{:S(2)}) %collective-permute-start.3) | collective-permute-done | bytes 98336 | tf_op jit(solution)/shard_map/ppermute | solution.py:17
  21.9 6.2 %collective-permute-start.6 = (bf16[32,2048]{1,0:T(8,128)(2,1)S(1)}, bf16[32,2048]{1,0:T(8,128)(2,1)S(1)}, u32[]{:S(2)}, u32[]{:S(2)}) collective-permute-start(bf16[32,2048]{1,0:T(8,128)(2,1)S(1)} %get-tuple-element.114), channel_id=1, source_target_pairs={{0,192},{64,128},{128,64},{192,0},{1,193},{65,129},{129,65},{193,1... | collective-permute-start | bytes 393224 | tf_op jit(solution)/shard_map/ppermute | solution.py:38
  42.4 2.6 %collective-permute-done.13 = bf16[64,1024]{1,0:T(8,128)(2,1)S(1)} collective-permute-done((bf16[64,1024]{1,0:T(8,128)(2,1)S(1)}, bf16[64,1024]{1,0:T(8,128)(2,1)S(1)}, u32[]{:S(2)}, u32[]{:S(2)}) %collective-permute-start.13) | collective-permute-done | bytes 131104 | tf_op jit(solution)/shard_map/ppermute | solution.py:38
  45.7 7.0 %collective-permute-done.11 = bf16[64,2048]{1,0:T(8,128)(2,1)S(1)} collective-permute-done((bf16[64,2048]{1,0:T(8,128)(2,1)S(1)}, bf16[64,2048]{1,0:T(8,128)(2,1)S(1)}, u32[]{:S(2)}, u32[]{:S(2)}) %collective-permute-start.11) | collective-permute-done | bytes 262176 | tf_op jit(solution)/shard_map/ppermute | solution.py:38
  56.3 3.4 %collective-permute-start.18 = (bf16[128,1024]{1,0:T(8,128)(2,1)S(1)}, bf16[128,1024]{1,0:T(8,128)(2,1)S(1)}, u32[]{:S(2)}, u32[]{:S(2)}) collective-permute-start(bf16[128,1024]{1,0:T(8,128)(2,1)S(1)} %pad_maximum_fusion.10), channel_id=1, source_target_pairs={{0,64},{64,0},{128,192},{192,128},{1,65},{65,1},{129,193},{193,129... | collective-permute-start | bytes 786440 | tf_op jit(solution)/shard_map/ppermute | solution.py:38
  60.2 11.0 %collective-permute-done.18 = bf16[128,1024]{1,0:T(8,128)(2,1)S(1)} collective-permute-done((bf16[128,1024]{1,0:T(8,128)(2,1)S(1)}, bf16[128,1024]{1,0:T(8,128)(2,1)S(1)}, u32[]{:S(2)}, u32[]{:S(2)}) %collective-permute-start.18) | collective-permute-done | bytes 262176 | tf_op jit(solution)/shard_map/ppermute | solution.py:38
  71.3 3.5 %collective-permute-done.17 = bf16[128,1024]{1,0:T(8,128)(2,1)S(1)} collective-permute-done((bf16[128,1024]{1,0:T(8,128)(2,1)S(1)}, bf16[128,1024]{1,0:T(8,128)(2,1)S(1)}, u32[]{:S(2)}, u32[]{:S(2)}) %collective-permute-start.17) | collective-permute-done | bytes 262176 | tf_op jit(solution)/shard_map/ppermute | solution.py:38
  79.3 24.1 %collective-permute-done.22.refs_7_ = bf16[256,1024]{1,0:T(8,128)(2,1)S(1)} collective-permute-done((bf16[256,1024]{1,0:T(8,128)(2,1)S(1)}, bf16[256,1024]{1,0:T(8,128)(2,1)S(1)}, u32[]{:S(2)}, u32[]{:S(2)}) %collective-permute-start.22) | collective-permute-done | bytes 524320 | tf_op jit(solution)/shard_map/ppermute | solution.py:38
  103.4 17.6 %expert.1 = (bf16[256,2048]{1,0:T(8,128)(2,1)S(1)}, bf16[256,2048]{1,0:T(8,128)(2,1)S(1)}, bf16[256,2048]{1,0:T(8,128)(2,1)S(1)}, bf16[256,2048]{1,0:T(8,128)(2,...) custom-call(bf16[256,2048]{1,0:T(8,128)(2,1)S(1)} %pad_maximum_fusio, ...), custom_call_target="tpu_custom_call" | custom-call | flops 9663676416 | bytes 31457280 | tf_op jit(solution)/shard_map/expert/pallas_call | solution.py:115
  122.9 2.5 %collective-permute-start.26 = (bf16[256,1024]{1,0:T(8,128)(2,1)S(1)}, bf16[256,1024]{1,0:T(8,128)(2,1)S(1)}, u32[]{:S(2)}, u32[]{:S(2)}) collective-permute-start(bf16[256,1024]{1,0:T(8,128)(2,1)S(1)} %get-tuple-element.87), channel_id=1, source_target_pairs={{0,192},{64,128},{128,64},{192,0},{1,193},{65,129},{129,65},{193,1... | collective-permute-start | bytes 1572872 | tf_op jit(solution)/shard_map/ppermute | solution.py:38
  125.4 22.1 %collective-permute-done.25 = bf16[256,1024]{1,0:T(8,128)(2,1)S(1)} collective-permute-done((bf16[256,1024]{1,0:T(8,128)(2,1)S(1)}, bf16[256,1024]{1,0:T(8,128)(2,1)S(1)}, u32[]{:S(2)}, u32[]{:S(2)}) %collective-permute-start.25) | collective-permute-done | bytes 524320 | tf_op jit(solution)/shard_map/ppermute | solution.py:38
  149.7 3.5 %collective-permute-start.28 = (bf16[128,2048]{1,0:T(8,128)(2,1)S(1)}, bf16[128,2048]{1,0:T(8,128)(2,1)S(1)}, u32[]{:S(2)}, u32[]{:S(2)}) collective-permute-start(bf16[128,2048]{1,0:T(8,128)(2,1)S(1)} %slice.211), channel_id=1, source_target_pairs={{0,2},{2,0},{4,6},{6,4},{1,3},{3,1},{5,7},{7,5},{8,10},{10,8},{12,... | collective-permute-start | bytes 1572872 | tf_op jit(solution)/shard_map/ppermute | solution.py:38
  153.5 2.6 %collective-permute-start.30 = (bf16[128,1024]{1,0:T(8,128)(2,1)S(1)}, bf16[128,1024]{1,0:T(8,128)(2,1)S(1)}, u32[]{:S(2)}, u32[]{:S(2)}) collective-permute-start(bf16[128,1024]{1,0:T(8,128)(2,1)S(1)} %slice.213), channel_id=1, source_target_pairs={{0,64},{64,0},{128,192},{192,128},{1,65},{65,1},{129,193},{193,129... | collective-permute-start | bytes 786440 | tf_op jit(solution)/shard_map/ppermute | solution.py:38
  156.1 2.8 %collective-permute-start.29 = (bf16[128,1024]{1,0:T(8,128)(2,1)S(1)}, bf16[128,1024]{1,0:T(8,128)(2,1)S(1)}, u32[]{:S(2)}, u32[]{:S(2)}) collective-permute-start(bf16[128,1024]{1,0:T(8,128)(2,1)S(1)} %slice.212), channel_id=1, source_target_pairs={{0,192},{64,128},{128,64},{192,0},{1,193},{65,129},{129,65},{193,1... | collective-permute-start | bytes 786440 | tf_op jit(solution)/shard_map/ppermute | solution.py:38
  158.9 6.7 %collective-permute-done.30 = bf16[128,1024]{1,0:T(8,128)(2,1)S(1)} collective-permute-done((bf16[128,1024]{1,0:T(8,128)(2,1)S(1)}, bf16[128,1024]{1,0:T(8,128)(2,1)S(1)}, u32[]{:S(2)}, u32[]{:S(2)}) %collective-permute-start.30) | collective-permute-done | bytes 262176 | tf_op jit(solution)/shard_map/ppermute | solution.py:38
  165.6 5.4 %collective-permute-done.29 = bf16[128,1024]{1,0:T(8,128)(2,1)S(1)} collective-permute-done((bf16[128,1024]{1,0:T(8,128)(2,1)S(1)}, bf16[128,1024]{1,0:T(8,128)(2,1)S(1)}, u32[]{:S(2)}, u32[]{:S(2)}) %collective-permute-start.29) | collective-permute-done | bytes 262176 | tf_op jit(solution)/shard_map/ppermute | solution.py:38
  171.4 4.3 %collective-permute-start.31 = (bf16[64,2048]{1,0:T(8,128)(2,1)S(1)}, bf16[64,2048]{1,0:T(8,128)(2,1)S(1)}, u32[]{:S(2)}, u32[]{:S(2)}) collective-permute-start(bf16[64,2048]{1,0:T(8,128)(2,1)S(1)} %slice.215), channel_id=1, source_target_pairs={{0,192},{64,128},{128,64},{192,0},{1,193},{65,129},{129,65},{193,1... | collective-permute-start | bytes 786440 | tf_op jit(solution)/shard_map/ppermute | solution.py:38
  178.3 2.6 %collective-permute-done.34 = bf16[64,1024]{1,0:T(8,128)(2,1)S(1)} collective-permute-done((bf16[64,1024]{1,0:T(8,128)(2,1)S(1)}, bf16[64,1024]{1,0:T(8,128)(2,1)S(1)}, u32[]{:S(2)}, u32[]{:S(2)}) %collective-permute-start.34) | collective-permute-done | bytes 131104 | tf_op jit(solution)/shard_map/ppermute | solution.py:38
  181.2 2.8 %collective-permute-done.31 = bf16[64,2048]{1,0:T(8,128)(2,1)S(1)} collective-permute-done((bf16[64,2048]{1,0:T(8,128)(2,1)S(1)}, bf16[64,2048]{1,0:T(8,128)(2,1)S(1)}, u32[]{:S(2)}, u32[]{:S(2)}) %collective-permute-start.31) | collective-permute-done | bytes 262176 | tf_op jit(solution)/shard_map/ppermute | solution.py:38
  186.0 3.5 %collective-permute-start.36 = (bf16[32,2048]{1,0:T(8,128)(2,1)S(1)}, bf16[32,2048]{1,0:T(8,128)(2,1)S(1)}, u32[]{:S(2)}, u32[]{:S(2)}) collective-permute-start(bf16[32,2048]{1,0:T(8,128)(2,1)S(1)} %slice.225), channel_id=1, source_target_pairs={{0,192},{64,128},{128,64},{192,0},{1,193},{65,129},{129,65},{193,1... | collective-permute-start | bytes 393224 | tf_op jit(solution)/shard_map/ppermute | solution.py:38
  196.7 3.7 %collective-permute-start.40 = (bf16[8,6144]{1,0:T(8,128)(2,1)S(1)}, bf16[8,6144]{1,0:T(8,128)(2,1)S(1)}, u32[]{:S(2)}, u32[]{:S(2)}) collective-permute-start(bf16[8,6144]{1,0:T(8,128)(2,1)S(1)} %get-tuple-element.110), channel_id=1, source_target_pairs={{0,16},{8,24},{16,0},{24,8},{1,17},{9,25},{17,1},{25,9},{2,18},{10... | collective-permute-start | bytes 294920 | tf_op jit(solution)/shard_map/ppermute | solution.py:17
  206.1 4.8 %collective-permute-done.42 = bf16[16,6144]{1,0:T(8,128)(2,1)S(1)} collective-permute-done((bf16[16,6144]{1,0:T(8,128)(2,1)S(1)}, bf16[16,6144]{1,0:T(8,128)(2,1)S(1)}, u32[]{:S(2)}, u32[]{:S(2)}) %collective-permute-start.42) | collective-permute-done | bytes 196640 | tf_op jit(solution)/shard_map/ppermute | solution.py:17
  (144 shorter events, 57.3 us)
Async XLA Ops:
  0.0 12.2 %collective-permute-start.1 = (bf16[6144,256]{1,0:T(8,128)(2,1)}, bf16[6144,256]{1,0:T(8,128)(2,1)}, u32[]{:S(2)}, u32[]{:S(2)}) collective-permute-start(bf16[6144,256]{1,0:T(8,128)(2,1)} %bitcast.6), channel_id=1, source_target_pairs={{0,1},{1,0},{2,3},{3,2},{4,5},{5,4},{6,7},{7,6},{8,9},{9,8},{10,11... | collective-permute-start | bytes 9437192 | tf_op jit(solution)/shard_map/ppermute | solution.py:17
  21.8 15.6 %collective-permute-start.9 = (bf16[6144,256]{1,0:T(8,128)(2,1)}, bf16[6144,256]{1,0:T(8,128)(2,1)S(1)}, u32[]{:S(2)}, u32[]{:S(2)}) collective-permute-start(bf16[6144,256]{1,0:T(8,128)(2,1)} %bitcast.8), channel_id=1, source_target_pairs={{0,1},{1,0},{2,3},{3,2},{4,5},{5,4},{6,7},{7,6},{8,9},{9,8},{10,11... | collective-permute-start | bytes 9437192 | tf_op jit(solution)/shard_map/ppermute | solution.py:17
  21.9 13.5 %collective-permute-start.6 = (bf16[32,2048]{1,0:T(8,128)(2,1)S(1)}, bf16[32,2048]{1,0:T(8,128)(2,1)S(1)}, u32[]{:S(2)}, u32[]{:S(2)}) collective-permute-start(bf16[32,2048]{1,0:T(8,128)(2,1)S(1)} %get-tuple-element.114), channel_id=1, source_target_pairs={{0,192},{64,128},{128,64},{192,0},{1,193},{65,129},{129,65},{193,1... | collective-permute-start | bytes 393224 | tf_op jit(solution)/shard_map/ppermute | solution.py:38
  37.4 15.8 %collective-permute-start.14 = (bf16[256,6144]{1,0:T(8,128)(2,1)S(1)}, bf16[256,6144]{1,0:T(8,128)(2,1)S(1)}, u32[]{:S(2)}, u32[]{:S(2)}) collective-permute-start(bf16[256,6144]{1,0:T(8,128)(2,1)S(1)} %bitcast.11), channel_id=1, source_target_pairs={{0,1},{1,0},{2,3},{3,2},{4,5},{5,4},{6,7},{7,6},{8,9},{9,8},{10,11... | collective-permute-start | bytes 9437192 | tf_op jit(solution)/shard_map/ppermute | solution.py:17
  37.6 15.2 %collective-permute-start.11 = (bf16[64,2048]{1,0:T(8,128)(2,1)S(1)}, bf16[64,2048]{1,0:T(8,128)(2,1)S(1)}, u32[]{:S(2)}, u32[]{:S(2)}) collective-permute-start(bf16[64,2048]{1,0:T(8,128)(2,1)S(1)} %pad_maximum_fusion.8), channel_id=1, source_target_pairs={{0,64},{64,0},{128,192},{192,128},{1,65},{65,1},{129,193},{193,129... | collective-permute-start | bytes 786440 | tf_op jit(solution)/shard_map/ppermute | solution.py:38
  38.7 14.6 %collective-permute-start.10 = (bf16[64,2048]{1,0:T(8,128)(2,1)S(1)}, bf16[64,2048]{1,0:T(8,128)(2,1)S(1)}, u32[]{:S(2)}, u32[]{:S(2)}) collective-permute-start(bf16[64,2048]{1,0:T(8,128)(2,1)S(1)} %pad_maximum_fusion.7), channel_id=1, source_target_pairs={{0,192},{64,128},{128,64},{192,0},{1,193},{65,129},{129,65},{193,1... | collective-permute-start | bytes 786440 | tf_op jit(solution)/shard_map/ppermute | solution.py:38
  53.4 21.4 %collective-permute-start.16 = (bf16[128,2048]{1,0:T(8,128)(2,1)S(1)}, bf16[128,2048]{1,0:T(8,128)(2,1)S(1)}, u32[]{:S(2)}, u32[]{:S(2)}) collective-permute-start(bf16[128,2048]{1,0:T(8,128)(2,1)S(1)} %pad_maximum_fusion.3), channel_id=1, source_target_pairs={{0,2},{2,0},{4,6},{6,4},{1,3},{3,1},{5,7},{7,5},{8,10},{10,8},{12,... | collective-permute-start | bytes 1572872 | tf_op jit(solution)/shard_map/ppermute | solution.py:38
  54.1 20.6 %collective-permute-start.15 = (bf16[128,2048]{1,0:T(8,128)(2,1)S(1)}, bf16[128,2048]{1,0:T(8,128)(2,1)S(1)}, u32[]{:S(2)}, u32[]{:S(2)}) collective-permute-start(bf16[128,2048]{1,0:T(8,128)(2,1)S(1)} %pad_maximum_fusion.2), channel_id=1, source_target_pairs={{0,6},{2,4},{4,2},{6,0},{1,7},{3,5},{5,3},{7,1},{8,14},{10,12},{12... | collective-permute-start | bytes 1572872 | tf_op jit(solution)/shard_map/ppermute | solution.py:38
  56.3 15.0 %collective-permute-start.18 = (bf16[128,1024]{1,0:T(8,128)(2,1)S(1)}, bf16[128,1024]{1,0:T(8,128)(2,1)S(1)}, u32[]{:S(2)}, u32[]{:S(2)}) collective-permute-start(bf16[128,1024]{1,0:T(8,128)(2,1)S(1)} %pad_maximum_fusion.10), channel_id=1, source_target_pairs={{0,64},{64,0},{128,192},{192,128},{1,65},{65,1},{129,193},{193,129... | collective-permute-start | bytes 786440 | tf_op jit(solution)/shard_map/ppermute | solution.py:38
  59.7 15.1 %collective-permute-start.17 = (bf16[128,1024]{1,0:T(8,128)(2,1)S(1)}, bf16[128,1024]{1,0:T(8,128)(2,1)S(1)}, u32[]{:S(2)}, u32[]{:S(2)}) collective-permute-start(bf16[128,1024]{1,0:T(8,128)(2,1)S(1)} %pad_maximum_fusion.9), channel_id=1, source_target_pairs={{0,192},{64,128},{128,64},{192,0},{1,193},{65,129},{129,65},{193,1... | collective-permute-start | bytes 786440 | tf_op jit(solution)/shard_map/ppermute | solution.py:38
  75.0 28.4 %collective-permute-start.20 = (bf16[256,2048]{1,0:T(8,128)(2,1)S(1)}, bf16[256,2048]{1,0:T(8,128)(2,1)S(1)}, u32[]{:S(2)}, u32[]{:S(2)}) collective-permute-start(bf16[256,2048]{1,0:T(8,128)(2,1)S(1)} %pad_maximum_fusion.1.refs_2_), channel_id=1, source_target_pairs={{0,6},{2,4},{4,2},{6,0},{1,7},{3,5},{5,3},{7,1},{8,14},{10,12},{12... | collective-permute-start | bytes 3145736 | tf_op jit(solution)/shard_map/ppermute | solution.py:38
  75.9 27.5 %collective-permute-start.19 = (bf16[256,2048]{1,0:T(8,128)(2,1)S(1)}, bf16[256,2048]{1,0:T(8,128)(2,1)S(1)}, u32[]{:S(2)}, u32[]{:S(2)}) collective-permute-start(bf16[256,2048]{1,0:T(8,128)(2,1)S(1)} %pad_maximum_fusion.refs_0_), channel_id=1, source_target_pairs={{0,2},{2,0},{4,6},{6,4},{1,3},{3,1},{5,7},{7,5},{8,10},{10,8},{12,... | collective-permute-start | bytes 3145736 | tf_op jit(solution)/shard_map/ppermute | solution.py:38
  77.8 25.6 %collective-permute-start.22 = (bf16[256,1024]{1,0:T(8,128)(2,1)S(1)}, bf16[256,1024]{1,0:T(8,128)(2,1)S(1)}, u32[]{:S(2)}, u32[]{:S(2)}) collective-permute-start(bf16[256,1024]{1,0:T(8,128)(2,1)S(1)} %pad_maximum_fusion.5.refs_6_), channel_id=1, source_target_pairs={{0,192},{64,128},{128,64},{192,0},{1,193},{65,129},{129,65},{193,1... | collective-permute-start | bytes 1572872 | tf_op jit(solution)/shard_map/ppermute | solution.py:38
  78.9 24.5 %collective-permute-start.21 = (bf16[256,1024]{1,0:T(8,128)(2,1)S(1)}, bf16[256,1024]{1,0:T(8,128)(2,1)S(1)}, u32[]{:S(2)}, u32[]{:S(2)}) collective-permute-start(bf16[256,1024]{1,0:T(8,128)(2,1)S(1)} %pad_maximum_fusion.4.refs_4_), channel_id=1, source_target_pairs={{0,64},{64,0},{128,192},{192,128},{1,65},{65,1},{129,193},{193,129... | collective-permute-start | bytes 1572872 | tf_op jit(solution)/shard_map/ppermute | solution.py:38
  121.0 27.5 %collective-permute-start.23 = (bf16[256,2048]{1,0:T(8,128)(2,1)S(1)}, bf16[256,2048]{1,0:T(8,128)(2,1)S(1)}, u32[]{:S(2)}, u32[]{:S(2)}) collective-permute-start(bf16[256,2048]{1,0:T(8,128)(2,1)S(1)} %get-tuple-element.84), channel_id=1, source_target_pairs={{0,2},{2,0},{4,6},{6,4},{1,3},{3,1},{5,7},{7,5},{8,10},{10,8},{12,... | collective-permute-start | bytes 3145736 | tf_op jit(solution)/shard_map/ppermute | solution.py:38
  121.4 27.1 %collective-permute-start.24 = (bf16[256,2048]{1,0:T(8,128)(2,1)S(1)}, bf16[256,2048]{1,0:T(8,128)(2,1)S(1)}, u32[]{:S(2)}, u32[]{:S(2)}) collective-permute-start(bf16[256,2048]{1,0:T(8,128)(2,1)S(1)} %get-tuple-element.85), channel_id=1, source_target_pairs={{0,6},{2,4},{4,2},{6,0},{1,7},{3,5},{5,3},{7,1},{8,14},{10,12},{12... | collective-permute-start | bytes 3145736 | tf_op jit(solution)/shard_map/ppermute | solution.py:38
  122.9 24.6 %collective-permute-start.25 = (bf16[256,1024]{1,0:T(8,128)(2,1)S(1)}, bf16[256,1024]{1,0:T(8,128)(2,1)S(1)}, u32[]{:S(2)}, u32[]{:S(2)}) collective-permute-start(bf16[256,1024]{1,0:T(8,128)(2,1)S(1)} %get-tuple-element.86), channel_id=1, source_target_pairs={{0,64},{64,0},{128,192},{192,128},{1,65},{65,1},{129,193},{193,129... | collective-permute-start | bytes 1572872 | tf_op jit(solution)/shard_map/ppermute | solution.py:38
  122.9 25.6 %collective-permute-start.26 = (bf16[256,1024]{1,0:T(8,128)(2,1)S(1)}, bf16[256,1024]{1,0:T(8,128)(2,1)S(1)}, u32[]{:S(2)}, u32[]{:S(2)}) collective-permute-start(bf16[256,1024]{1,0:T(8,128)(2,1)S(1)} %get-tuple-element.87), channel_id=1, source_target_pairs={{0,192},{64,128},{128,64},{192,0},{1,193},{65,129},{129,65},{193,1... | collective-permute-start | bytes 1572872 | tf_op jit(solution)/shard_map/ppermute | solution.py:38
  149.6 21.4 %collective-permute-start.27 = (bf16[128,2048]{1,0:T(8,128)(2,1)S(1)}, bf16[128,2048]{1,0:T(8,128)(2,1)S(1)}, u32[]{:S(2)}, u32[]{:S(2)}) collective-permute-start(bf16[128,2048]{1,0:T(8,128)(2,1)S(1)} %slice.210), channel_id=1, source_target_pairs={{0,6},{2,4},{4,2},{6,0},{1,7},{3,5},{5,3},{7,1},{8,14},{10,12},{12... | collective-permute-start | bytes 1572872 | tf_op jit(solution)/shard_map/ppermute | solution.py:38
  149.7 21.3 %collective-permute-start.28 = (bf16[128,2048]{1,0:T(8,128)(2,1)S(1)}, bf16[128,2048]{1,0:T(8,128)(2,1)S(1)}, u32[]{:S(2)}, u32[]{:S(2)}) collective-permute-start(bf16[128,2048]{1,0:T(8,128)(2,1)S(1)} %slice.211), channel_id=1, source_target_pairs={{0,2},{2,0},{4,6},{6,4},{1,3},{3,1},{5,7},{7,5},{8,10},{10,8},{12,... | collective-permute-start | bytes 1572872 | tf_op jit(solution)/shard_map/ppermute | solution.py:38
  153.5 12.1 %collective-permute-start.30 = (bf16[128,1024]{1,0:T(8,128)(2,1)S(1)}, bf16[128,1024]{1,0:T(8,128)(2,1)S(1)}, u32[]{:S(2)}, u32[]{:S(2)}) collective-permute-start(bf16[128,1024]{1,0:T(8,128)(2,1)S(1)} %slice.213), channel_id=1, source_target_pairs={{0,64},{64,0},{128,192},{192,128},{1,65},{65,1},{129,193},{193,129... | collective-permute-start | bytes 786440 | tf_op jit(solution)/shard_map/ppermute | solution.py:38
  156.1 15.0 %collective-permute-start.29 = (bf16[128,1024]{1,0:T(8,128)(2,1)S(1)}, bf16[128,1024]{1,0:T(8,128)(2,1)S(1)}, u32[]{:S(2)}, u32[]{:S(2)}) collective-permute-start(bf16[128,1024]{1,0:T(8,128)(2,1)S(1)} %slice.212), channel_id=1, source_target_pairs={{0,192},{64,128},{128,64},{192,0},{1,193},{65,129},{129,65},{193,1... | collective-permute-start | bytes 786440 | tf_op jit(solution)/shard_map/ppermute | solution.py:38
  171.4 12.6 %collective-permute-start.31 = (bf16[64,2048]{1,0:T(8,128)(2,1)S(1)}, bf16[64,2048]{1,0:T(8,128)(2,1)S(1)}, u32[]{:S(2)}, u32[]{:S(2)}) collective-permute-start(bf16[64,2048]{1,0:T(8,128)(2,1)S(1)} %slice.215), channel_id=1, source_target_pairs={{0,192},{64,128},{128,64},{192,0},{1,193},{65,129},{129,65},{193,1... | collective-permute-start | bytes 786440 | tf_op jit(solution)/shard_map/ppermute | solution.py:38
  185.0 11.0 %collective-permute-start.35 = (bf16[32,2048]{1,0:T(8,128)(2,1)S(1)}, bf16[32,2048]{1,0:T(8,128)(2,1)S(1)}, u32[]{:S(2)}, u32[]{:S(2)}) collective-permute-start(bf16[32,2048]{1,0:T(8,128)(2,1)S(1)} %slice.223), channel_id=1, source_target_pairs={{0,64},{64,0},{128,192},{192,128},{1,65},{65,1},{129,193},{193,129... | collective-permute-start | bytes 393224 | tf_op jit(solution)/shard_map/ppermute | solution.py:38
  (23 other events, 189.4 us)

commit v2 on v0

--- a/solution.py
+++ b/solution.py
@@ -42,13 +42,17 @@
     return (a.astype(jnp.float32) + b.astype(jnp.float32)).astype(a.dtype)
 
 
-def expert_kernel(*refs):
+def after(value, *others):
+    return lax.optimization_barrier((value, *others))[0]
+
+
+def hidden_kernel(*refs):
     n = len(CHAINS)
     ins = refs[: 2 * n]
-    wg0, wu0, wg1, wu1, wd0, wd1 = refs[2 * n : 2 * n + 6]
-    outs = refs[2 * n + 6 : 4 * n + 6]
-    part, acc, hidden = refs[4 * n + 6 :]
+    wg0, wu0, wg1, wu1 = refs[2 * n : 2 * n + 4]
+    hidden, part, acc = refs[2 * n + 4 :]
     step = pl.program_id(0)
+    units = wg0.shape[1]
     f32 = jnp.float32
     at = 0
     for c, (_, width, order) in enumerate(CHAINS):
@@ -67,72 +71,81 @@
     def _():
         acc[...] = jnp.zeros_like(acc)
 
-    @pl.when(step < STEPS)
-    def _():
-        for i, w in enumerate((wg0, wu0, wg1, wu1)):
-            acc[i] += jnp.dot(part[...], w[...], preferred_element_type=f32)
+    for i, w in enumerate((wg0, wu0, wg1, wu1)):
+        acc[i] += jnp.dot(part[...], w[...], preferred_element_type=f32)
 
     @pl.when(step == STEPS - 1)
     def _():
         for i in range(2):
             gate = acc[2 * i]
-            hidden[i] = (gate / (1.0 + jnp.exp(-gate)) * acc[2 * i + 1]).astype(hidden.dtype)
-
-    at = STEPS
-    for c, (_, width, order) in enumerate(CHAINS):
-        steps = width // PART
-
-        @pl.when((step >= at) & (step < at + steps))
-        def _(c=c, order=order):
-            total = jnp.dot(hidden[0], wd0[...], preferred_element_type=f32) + jnp.dot(
-                hidden[1], wd1[...], preferred_element_type=f32
-            )
-            total = total.astype(jnp.bfloat16)
-            for index in range(16):
-                row = canon_block(order, index) * UNIT
-                to = (index % 8) * UNIT
-                outs[2 * c + index // 8][to : to + UNIT, :] = total[row : row + UNIT]
-
-        at += steps
+            value = gate / (1.0 + jnp.exp(-gate)) * acc[2 * i + 1]
+            hidden[:, i * units : (i + 1) * units] = value.astype(hidden.dtype)
+
+
+def out_kernel(order, hidden, wd0, wd1, keep, away):
+    units = wd0.shape[0]
+    f32 = jnp.float32
+    total = jnp.dot(hidden[:, :units], wd0[...], preferred_element_type=f32) + jnp.dot(
+        hidden[:, units:], wd1[...], preferred_element_type=f32
+    )
+    total = total.astype(jnp.bfloat16)
+    for index in range(16):
+        row = canon_block(order, index) * UNIT
+        to = (index % 8) * UNIT
+        (keep, away)[index // 8][to : to + UNIT, :] = total[row : row + UNIT]
 
 
 PART = 1024
 
 
-def expert(pieces, weights):
+def hidden_units(pieces, weights):
     width, units = weights[0].shape
     count = 2 * HALF
-    first = lambda i: (jnp.minimum(i, STEPS - 1), 0)
-    second = lambda i: (0, jnp.maximum(i - STEPS, 0))
-    in_specs, out_specs, out_shape = [], [], []
+    in_specs = []
     for start, size, _ in CHAINS:
         low, steps = start // PART, size // PART
         to = lambda i, low=low, steps=steps: (0, jnp.clip(i - low, 0, steps - 1))
-        back = lambda i, low=low, steps=steps: (0, jnp.clip(i - STEPS - low, 0, steps - 1))
         in_specs += [pl.BlockSpec((HALF, PART), to)] * 2
-        out_specs += [pl.BlockSpec((HALF, PART), back)] * 2
-        out_shape += [jax.ShapeDtypeStruct((HALF, size), jnp.bfloat16)] * 2
     return pl.pallas_call(
-        expert_kernel,
-        grid=(2 * STEPS,),
-        out_shape=out_shape,
-        in_specs=in_specs
-        + [pl.BlockSpec((PART, units), first)] * 4
-        + [pl.BlockSpec((units, PART), second)] * 2,
-        out_specs=out_specs,
+        hidden_kernel,
+        grid=(STEPS,),
+        out_shape=jax.ShapeDtypeStruct((count, 2 * units), jnp.bfloat16),
+        in_specs=in_specs + [pl.BlockSpec((PART, units), lambda i: (i, 0))] * 4,
+        out_specs=pl.BlockSpec((count, 2 * units), lambda i: (0, 0)),
         scratch_shapes=[
             pltpu.VMEM((count, PART), jnp.bfloat16),
             pltpu.VMEM((4, count, units), jnp.float32),
-            pltpu.VMEM((2, count, units), jnp.bfloat16),
         ],
-        compiler_params=pltpu.CompilerParams(vmem_limit_bytes=40 << 20),
+        compiler_params=pltpu.CompilerParams(vmem_limit_bytes=32 << 20),
         cost_estimate=pl.CostEstimate(
-            flops=12 * count * width * units,
-            bytes_accessed=12 * width * units + 4 * count * width,
+            flops=8 * count * width * units,
+            bytes_accessed=8 * width * units + 2 * count * width,
             transcendentals=2 * count * units,
         ),
-        name="expert",
+        name="hidden",
     )(*pieces, *weights)
+
+
+def expert_out(hidden, wd0, wd1, chain):
+    start, size, order = CHAINS[chain]
+    units = wd0.shape[0]
+    low, count = start // PART, 2 * HALF
+    shape = jax.ShapeDtypeStruct((HALF, size), jnp.bfloat16)
+    return pl.pallas_call(
+        functools.partial(out_kernel, order),
+        grid=(size // PART,),
+        out_shape=[shape] * 2,
+        in_specs=[pl.BlockSpec((count, 2 * units), lambda i: (0, 0))]
+        + [pl.BlockSpec((units, PART), lambda i: (0, low + i))] * 2,
+        out_specs=[pl.BlockSpec((HALF, PART), lambda i: (0, i))] * 2,
+        compiler_params=pltpu.CompilerParams(vmem_limit_bytes=24 << 20),
+        cost_estimate=pl.CostEstimate(
+            flops=4 * count * size * units,
+            bytes_accessed=4 * size * units + 2 * count * size,
+            transcendentals=0,
+        ),
+        name="out",
+    )(hidden, wd0, wd1)
 
 
 def relative_slots(routes, cap):
@@ -153,9 +166,6 @@
 def per_device(tokens, norm_gain, routes, route_weights, w_gate, w_up, w_down):
     f32 = jnp.float32
     wg0, wu0, wd0 = w_gate[0], w_up[0], w_down[0]
-    wg1, wu1, wd1 = (shift(w, "c", 1) for w in (wg0, wu0, wd0))
-    weights = (wg0, wu0, wg1, wu1, wd0, wd1)
-
     cap = 4
     slot_count = 32
     wide = tokens.astype(f32)
@@ -168,32 +178,45 @@
     combine = jnp.sum(route_weights[:, :, None] * hits, axis=1)
 
     keep = buffer[:16]
-    got = shift(buffer[16:], "zl", 1)
+    wg1, wu1, wd1 = (shift(w, "c", 1) for w in (wg0, wu0, wd0))
+    got, wg1 = lax.optimization_barrier((shift(buffer[16:], "zl", 1), wg1))
     blocks = []
     for by in range(4):
         at = slice(by * cap, (by + 1) * cap)
         block = jnp.concatenate([keep[at], got[at]], axis=0)
         blocks.append(shift(block, "y", by) if by else block)
+    blocks, wu1, wd1 = lax.optimization_barrier((blocks, wu1, wd1))
     rows = jnp.concatenate(blocks, axis=0)
 
     pieces = []
     held = [rows[:, start : start + size] for start, size, _ in CHAINS]
+    last = None
     for step in range(4):
         came = [trade(h, order[step]) for h, (_, _, order) in zip(held, CHAINS)]
-        if step < 3:
-            held = [jnp.concatenate([h, r], axis=0) for h, r in zip(held, came)]
-    for h, r in zip(held, came):
-        pieces += [h, r]
-
-    done = expert(pieces, weights)
-
-    held, away = done[0::2], done[1::2]
+        for j in range(4):
+            got = came[j] if last is None else after(came[j], last)
+            if step < 3:
+                held[j] = last = jnp.concatenate([held[j], got], axis=0)
+            else:
+                pieces += [held[j], got]
+                last = got
+
+    hidden = hidden_units(pieces, (wg0, wu0, wg1, wu1))
+
+    held, away = [None] * 4, [None] * 4
+    for j in range(4):
+        held[j], away[j] = expert_out(hidden if j == 0 else after(hidden, away[j - 1]), wd0, wd1, j)
+    last = None
     for step in (3, 2, 1, 0):
         came = [trade(a, order[step]) for a, (_, _, order) in zip(away, CHAINS)]
-        held = [add(h, r) for h, r in zip(held, came)]
         half = held[0].shape[0] // 2
-        if step:
-            held, away = [h[:half] for h in held], [h[half:] for h in held]
+        for j in range(4):
+            got = came[j] if last is None else after(came[j], last)
+            if step:
+                away[j] = last = add(held[j][half:], got[half:])
+                held[j] = add(held[j][:half], got[:half])
+            else:
+                held[j] = last = add(held[j], got)
     mine = jnp.concatenate(held, axis=1)
 
     results = []

time: 253 us -> 204 us (0.81)
  waiting for transfers between devices: 131 us -> 106 us
  starting transfers between devices: 92.9 us -> 72.3 us
  Pallas kernels: 17.6 us -> 13.9 us
    ppermute x32, starting transfers between devices: 80.9 us -> 52.6 us  [trade(): return lax.ppermute(value, axis, [(i, i ^ mask) for i in range(4)])]
    ppermute x32, waiting for transfers between devices: 114 us -> 90.2 us  [trade(): return lax.ppermute(value, axis, [(i, i ^ mask) for i in range(4)])]
    ppermute x11, starting transfers between devices: 12 us -> 19.8 us  [shift(): return lax.ppermute(value, axis, [(i, (i + by) % n) for i in range(n)])]
    pallas_call x1 -> x5, Pallas kernels: 17.6 us -> 13.9 us  [the longest x1 8.99 us: hidden_units(): pl.pallas_call(hidden_kernel, grid=(STEPS,), out_shape=jax.ShapeDtypeStru...]
  transfers between devices with their start and end apart: 43 -> 43, of which waited for: 27 -> 25; matrix products, arithmetic and copies ran while one was open for 1% -> 3% of each run, Pallas kernels for 0% -> 2%
where the time goes in v2:
time: 204 us; the launch traced here: 201 us
  waiting for transfers between devices  106 us (52%)
  starting transfers between devices  72.3 us (35%)
  Pallas kernels  13.9 us (7%)
  other arithmetic  4.78 us (2%)
  matrix products  2.13 us (1%)
    ppermute x32, waiting for transfers between devices, trade(): return lax.ppermute(value, axis, [(i, i ^ mask) for i in range(4)])  90.2 us
    ppermute x32, starting transfers between devices, trade(): return lax.ppermute(value, axis, [(i, i ^ mask) for i in range(4)])  52.6 us
    ppermute x11, starting transfers between devices, shift(): return lax.ppermute(value, axis, [(i, (i + by) % n) for i in range(n)])  19.8 us
    ppermute x11, waiting for transfers between devices, shift(): return lax.ppermute(value, axis, [(i, (i + by) % n) for i in range(n)])  15.9 us
    pallas_call x1, Pallas kernels, hidden_units(): pl.pallas_call(hidden_kernel, grid=(STEPS,), out_shape=jax.ShapeDtypeStru...  8.99 us
    pallas_call x4, Pallas kernels, expert_out(): pl.pallas_call(functools.partial(out_kernel, order), grid=(size // PART,)...  4.88 us
  transfers between devices with their start and end apart: 43, of which 25 were waited for; matrix products, arithmetic and copies ran while one was open for 3% of the time, Pallas kernels for 2%

profile of v2, /device:TPU:2, one launch (start us, length us, event | category | flops | bytes accessed | tf_op | source)
XLA Modules:
  0.0 201.3 jit_solution(17600575742085838205)
XLA Ops:
  7.0 5.0 %collective-permute-done = bf16[16,6144]{1,0:T(8,128)(2,1)S(1)} collective-permute-done((bf16[16,6144]{1,0:T(8,128)(2,1)S(1)}, bf16[16,6144]{1,0:T(8,128)(2,1)S(1)}, u32[]{:S(2)}, u32[]{:S(2)}) %collective-permute-start) | collective-permute-done | bytes 196640 | tf_op jit(solution)/shard_map/ppermute | solution.py:17
  13.9 3.0 %collective-permute-start.3 = (bf16[8,6144]{1,0:T(8,128)(2,1)S(1)}, bf16[8,6144]{1,0:T(8,128)(2,1)S(1)}, u32[]{:S(2)}, u32[]{:S(2)}) collective-permute-start(bf16[8,6144]{1,0:T(8,128)(2,1)S(1)} %pad_maximum_fusion.15), channel_id=1, source_target_pairs={{0,16},{8,24},{16,0},{24,8},{1,17},{9,25},{17,1},{25,9},{2,18},{10... | collective-permute-start | bytes 294920 | tf_op jit(solution)/shard_map/ppermute | solution.py:17
  18.4 2.9 %collective-permute-done.3 = bf16[8,6144]{1,0:T(8,128)(2,1)S(1)} collective-permute-done((bf16[8,6144]{1,0:T(8,128)(2,1)S(1)}, bf16[8,6144]{1,0:T(8,128)(2,1)S(1)}, u32[]{:S(2)}, u32[]{:S(2)}) %collective-permute-start.3) | collective-permute-done | bytes 98336 | tf_op jit(solution)/shard_map/ppermute | solution.py:17
  21.7 3.4 %collective-permute-start.7 = (bf16[32,2048]{1,0:T(8,128)(2,1)S(1)}, bf16[32,2048]{1,0:T(8,128)(2,1)S(1)}, u32[]{:S(2)}, u32[]{:S(2)}) collective-permute-start(bf16[32,2048]{1,0:T(8,128)(2,1)S(1)} %get-tuple-element.125), channel_id=1, source_target_pairs={{0,64},{64,0},{128,192},{192,128},{1,65},{65,1},{129,193},{193,129... | collective-permute-start | bytes 393224 | tf_op jit(solution)/shard_map/ppermute | solution.py:38
  27.8 4.3 %collective-permute-start.11 = (bf16[32,2048]{1,0:T(8,128)(2,1)S(1)}, bf16[32,2048]{1,0:T(8,128)(2,1)S(1)}, u32[]{:S(2)}, u32[]{:S(2)}) collective-permute-start(bf16[32,2048]{1,0:T(8,128)(2,1)S(1)} %get-tuple-element.124), channel_id=1, source_target_pairs={{0,192},{64,128},{128,64},{192,0},{1,193},{65,129},{129,65},{193,1... | collective-permute-start | bytes 393224 | tf_op jit(solution)/shard_map/ppermute | solution.py:38
  34.0 7.1 %collective-permute-done.11 = bf16[32,2048]{1,0:T(8,128)(2,1)S(1)} collective-permute-done((bf16[32,2048]{1,0:T(8,128)(2,1)S(1)}, bf16[32,2048]{1,0:T(8,128)(2,1)S(1)}, u32[]{:S(2)}, u32[]{:S(2)}) %collective-permute-start.11) | collective-permute-done | bytes 131104 | tf_op jit(solution)/shard_map/ppermute | solution.py:38
  42.0 4.6 %collective-permute-done.8 = bf16[64,2048]{1,0:T(8,128)(2,1)S(1)} collective-permute-done((bf16[64,2048]{1,0:T(8,128)(2,1)S(1)}, bf16[64,2048]{1,0:T(8,128)(2,1)S(1)}, u32[]{:S(2)}, u32[]{:S(2)}) %collective-permute-start.8) | collective-permute-done | bytes 262176 | tf_op jit(solution)/shard_map/ppermute | solution.py:38
  51.7 9.5 %collective-permute-done.14 = bf16[64,1024]{1,0:T(8,128)(2,1)S(1)} collective-permute-done((bf16[64,1024]{1,0:T(8,128)(2,1)S(1)}, bf16[64,1024]{1,0:T(8,128)(2,1)S(1)}, u32[]{:S(2)}, u32[]{:S(2)}) %collective-permute-start.14) | collective-permute-done | bytes 131104 | tf_op jit(solution)/shard_map/ppermute | solution.py:38
  61.2 3.3 %collective-permute-done.13 = bf16[64,1024]{1,0:T(8,128)(2,1)S(1)} collective-permute-done((bf16[64,1024]{1,0:T(8,128)(2,1)S(1)}, bf16[64,1024]{1,0:T(8,128)(2,1)S(1)}, u32[]{:S(2)}, u32[]{:S(2)}) %collective-permute-start.13) | collective-permute-done | bytes 131104 | tf_op jit(solution)/shard_map/ppermute | solution.py:38
  67.3 4.7 %collective-permute-start.18 = (bf16[128,1024]{1,0:T(8,128)(2,1)S(1)}, bf16[128,1024]{1,0:T(8,128)(2,1)S(1)}, u32[]{:S(2)}, u32[]{:S(2)}) collective-permute-start(bf16[128,1024]{1,0:T(8,128)(2,1)S(1)} %pad_maximum_fusion.9), channel_id=1, source_target_pairs={{0,192},{64,128},{128,64},{192,0},{1,193},{65,129},{129,65},{193,1... | collective-permute-start | bytes 786440 | tf_op jit(solution)/shard_map/ppermute | solution.py:38
  72.0 9.8 %collective-permute-done.18 = bf16[128,1024]{1,0:T(8,128)(2,1)S(1)} collective-permute-done((bf16[128,1024]{1,0:T(8,128)(2,1)S(1)}, bf16[128,1024]{1,0:T(8,128)(2,1)S(1)}, u32[]{:S(2)}, u32[]{:S(2)}) %collective-permute-start.18) | collective-permute-done | bytes 262176 | tf_op jit(solution)/shard_map/ppermute | solution.py:38
  82.0 3.0 %collective-permute-done.17 = bf16[128,1024]{1,0:T(8,128)(2,1)S(1)} collective-permute-done((bf16[128,1024]{1,0:T(8,128)(2,1)S(1)}, bf16[128,1024]{1,0:T(8,128)(2,1)S(1)}, u32[]{:S(2)}, u32[]{:S(2)}) %collective-permute-start.17) | collective-permute-done | bytes 262176 | tf_op jit(solution)/shard_map/ppermute | solution.py:38
  88.9 11.5 %collective-permute-done.21.refs_5_ = bf16[256,1024]{1,0:T(8,128)(2,1)S(1)} collective-permute-done((bf16[256,1024]{1,0:T(8,128)(2,1)S(1)}, bf16[256,1024]{1,0:T(8,128)(2,1)S(1)}, u32[]{:S(2)}, u32[]{:S(2)}) %collective-permute-start.21) | collective-permute-done | bytes 524320 | tf_op jit(solution)/shard_map/ppermute | solution.py:38
  100.4 6.0 %collective-permute-done.22.refs_7_ = bf16[256,1024]{1,0:T(8,128)(2,1)S(1)} collective-permute-done((bf16[256,1024]{1,0:T(8,128)(2,1)S(1)}, bf16[256,1024]{1,0:T(8,128)(2,1)S(1)}, u32[]{:S(2)}, u32[]{:S(2)}) %collective-permute-start.22) | collective-permute-done | bytes 524320 | tf_op jit(solution)/shard_map/ppermute | solution.py:38
  106.4 9.0 %hidden.1 = bf16[512,512]{1,0:T(8,128)(2,1)S(1)} custom-call(bf16[256,2048]{1,0:T(8,128)(2,1)S(1)} %pad_maximum_fusion.refs_0_, bf16[256,2048]{1,0:T(8,128)(2,1)S(1)} %collective-permute-done.16.refs_1_, bf16[256,2048]{1,0:T(8,128)(2,1)S(1)} %pad_maximum_fusion.1.refs_2_, bf16[256,2048]{1,0:T(8,128)(2,1)S(1)} %collective-permute-done.20.refs_3_, ...), custom_call_target="tpu_custom_call" | custom-call | flops 6442450944 | bytes 18874368 | tf_op jit(solution)/shard_map/hidden/pallas_call | solution.py:109
  122.6 4.1 %collective-permute-start.25 = (bf16[256,1024]{1,0:T(8,128)(2,1)S(1)}, bf16[256,1024]{1,0:T(8,128)(2,1)S(1)}, u32[]{:S(2)}, u32[]{:S(2)}) collective-permute-start(bf16[256,1024]{1,0:T(8,128)(2,1)S(1)} %get-tuple-element.85), channel_id=1, source_target_pairs={{0,192},{64,128},{128,64},{192,0},{1,193},{65,129},{129,65},{193,1... | collective-permute-start | bytes 1572872 | tf_op jit(solution)/shard_map/ppermute | solution.py:38
  126.7 9.8 %collective-permute-done.23 = bf16[256,2048]{1,0:T(8,128)(2,1)S(1)} collective-permute-done((bf16[256,2048]{1,0:T(8,128)(2,1)S(1)}, bf16[256,2048]{1,0:T(8,128)(2,1)S(1)}, u32[]{:S(2)}, u32[]{:S(2)}) %collective-permute-start.23) | collective-permute-done | bytes 1048608 | tf_op jit(solution)/shard_map/ppermute | solution.py:38
  136.8 4.0 %collective-permute-start.24 = (bf16[128,2048]{1,0:T(8,128)(2,1)S(1)}, bf16[128,2048]{1,0:T(8,128)(2,1)S(1)}, u32[]{:S(2)}, u32[]{:S(2)}) collective-permute-start(bf16[128,2048]{1,0:T(8,128)(2,1)S(1)} %get-tuple-element.106), channel_id=1, source_target_pairs={{0,6},{2,4},{4,2},{6,0},{1,7},{3,5},{5,3},{7,1},{8,14},{10,12},{12... | collective-permute-start | bytes 1572872 | tf_op jit(solution)/shard_map/ppermute | solution.py:38
  143.8 4.0 %collective-permute-start.31 = (bf16[128,2048]{1,0:T(8,128)(2,1)S(1)}, bf16[128,2048]{1,0:T(8,128)(2,1)S(1)}, u32[]{:S(2)}, u32[]{:S(2)}) collective-permute-start(bf16[128,2048]{1,0:T(8,128)(2,1)S(1)} %get-tuple-element.108), channel_id=1, source_target_pairs={{0,2},{2,0},{4,6},{6,4},{1,3},{3,1},{5,7},{7,5},{8,10},{10,8},{12,... | collective-permute-start | bytes 1572872 | tf_op jit(solution)/shard_map/ppermute | solution.py:38
  151.9 3.4 %collective-permute-start.28 = (bf16[64,2048]{1,0:T(8,128)(2,1)S(1)}, bf16[64,2048]{1,0:T(8,128)(2,1)S(1)}, u32[]{:S(2)}, u32[]{:S(2)}) collective-permute-start(bf16[64,2048]{1,0:T(8,128)(2,1)S(1)} %get-tuple-element.110), channel_id=1, source_target_pairs={{0,192},{64,128},{128,64},{192,0},{1,193},{65,129},{129,65},{193,1... | collective-permute-start | bytes 786440 | tf_op jit(solution)/shard_map/ppermute | solution.py:38
  157.7 9.1 %collective-permute-done.30 = bf16[128,1024]{1,0:T(8,128)(2,1)S(1)} collective-permute-done((bf16[128,1024]{1,0:T(8,128)(2,1)S(1)}, bf16[128,1024]{1,0:T(8,128)(2,1)S(1)}, u32[]{:S(2)}, u32[]{:S(2)}) %collective-permute-start.30) | collective-permute-done | bytes 262176 | tf_op jit(solution)/shard_map/ppermute | solution.py:38
  167.7 3.9 %collective-permute-done.28 = bf16[64,2048]{1,0:T(8,128)(2,1)S(1)} collective-permute-done((bf16[64,2048]{1,0:T(8,128)(2,1)S(1)}, bf16[64,2048]{1,0:T(8,128)(2,1)S(1)}, u32[]{:S(2)}, u32[]{:S(2)}) %collective-permute-start.28) | collective-permute-done | bytes 262176 | tf_op jit(solution)/shard_map/ppermute | solution.py:38
  183.2 6.3 %collective-permute-start.40 = (bf16[8,6144]{1,0:T(8,128)(2,1)S(1)}, bf16[8,6144]{1,0:T(8,128)(2,1)S(1)}, u32[]{:S(2)}, u32[]{:S(2)}) collective-permute-start(bf16[8,6144]{1,0:T(8,128)(2,1)S(1)} %get-tuple-element.122), channel_id=1, source_target_pairs={{0,16},{8,24},{16,0},{24,8},{1,17},{9,25},{17,1},{25,9},{2,18},{10... | collective-permute-start | bytes 294920 | tf_op jit(solution)/shard_map/ppermute | solution.py:17
  194.5 5.6 %collective-permute-done.42 = bf16[16,6144]{1,0:T(8,128)(2,1)S(1)} collective-permute-done((bf16[16,6144]{1,0:T(8,128)(2,1)S(1)}, bf16[16,6144]{1,0:T(8,128)(2,1)S(1)}, u32[]{:S(2)}, u32[]{:S(2)}) %collective-permute-start.42) | collective-permute-done | bytes 196640 | tf_op jit(solution)/shard_map/ppermute | solution.py:17
  (138 shorter events, 63.4 us)
Async XLA Ops:
  0.0 12.0 %collective-permute-start.1 = (bf16[6144,256]{1,0:T(8,128)(2,1)}, bf16[6144,256]{1,0:T(8,128)(2,1)S(1)}, u32[]{:S(2)}, u32[]{:S(2)}) collective-permute-start(bf16[6144,256]{1,0:T(8,128)(2,1)} %bitcast.11), channel_id=1, source_target_pairs={{0,1},{1,0},{2,3},{3,2},{4,5},{5,4},{6,7},{7,6},{8,9},{9,8},{10,11... | collective-permute-start | bytes 9437192 | tf_op jit(solution)/shard_map/ppermute | solution.py:17
  25.1 16.9 %collective-permute-start.10 = (bf16[32,1024]{1,0:T(8,128)(2,1)S(1)}, bf16[32,1024]{1,0:T(8,128)(2,1)S(1)}, u32[]{:S(2)}, u32[]{:S(2)}) collective-permute-start(bf16[32,1024]{1,0:T(8,128)(2,1)S(1)} %get-tuple-element.126), channel_id=1, source_target_pairs={{0,2},{2,0},{4,6},{6,4},{1,3},{3,1},{5,7},{7,5},{8,10},{10,8},{12,... | collective-permute-start | bytes 196616 | tf_op jit(solution)/shard_map/ppermute | solution.py:38
  25.7 16.3 %collective-permute-start.9 = (bf16[32,1024]{1,0:T(8,128)(2,1)S(1)}, bf16[32,1024]{1,0:T(8,128)(2,1)S(1)}, u32[]{:S(2)}, u32[]{:S(2)}) collective-permute-start(bf16[32,1024]{1,0:T(8,128)(2,1)S(1)} %get-tuple-element.127), channel_id=1, source_target_pairs={{0,6},{2,4},{4,2},{6,0},{1,7},{3,5},{5,3},{7,1},{8,14},{10,12},{12... | collective-permute-start | bytes 196616 | tf_op jit(solution)/shard_map/ppermute | solution.py:38
  27.8 13.3 %collective-permute-start.11 = (bf16[32,2048]{1,0:T(8,128)(2,1)S(1)}, bf16[32,2048]{1,0:T(8,128)(2,1)S(1)}, u32[]{:S(2)}, u32[]{:S(2)}) collective-permute-start(bf16[32,2048]{1,0:T(8,128)(2,1)S(1)} %get-tuple-element.124), channel_id=1, source_target_pairs={{0,192},{64,128},{128,64},{192,0},{1,193},{65,129},{129,65},{193,1... | collective-permute-start | bytes 393224 | tf_op jit(solution)/shard_map/ppermute | solution.py:38
  32.2 14.4 %collective-permute-start.8 = (bf16[64,2048]{1,0:T(8,128)(2,1)S(1)}, bf16[64,2048]{1,0:T(8,128)(2,1)S(1)}, u32[]{:S(2)}, u32[]{:S(2)}) collective-permute-start(bf16[64,2048]{1,0:T(8,128)(2,1)S(1)} %pad_maximum_fusion.7), channel_id=1, source_target_pairs={{0,192},{64,128},{128,64},{192,0},{1,193},{65,129},{129,65},{193,1... | collective-permute-start | bytes 786440 | tf_op jit(solution)/shard_map/ppermute | solution.py:38
  46.6 17.9 %collective-permute-start.12 = (bf16[128,2048]{1,0:T(8,128)(2,1)S(1)}, bf16[128,2048]{1,0:T(8,128)(2,1)S(1)}, u32[]{:S(2)}, u32[]{:S(2)}) collective-permute-start(bf16[128,2048]{1,0:T(8,128)(2,1)S(1)} %pad_maximum_fusion.2), channel_id=1, source_target_pairs={{0,6},{2,4},{4,2},{6,0},{1,7},{3,5},{5,3},{7,1},{8,14},{10,12},{12... | collective-permute-start | bytes 1572872 | tf_op jit(solution)/shard_map/ppermute | solution.py:38
  47.0 14.2 %collective-permute-start.14 = (bf16[64,1024]{1,0:T(8,128)(2,1)S(1)}, bf16[64,1024]{1,0:T(8,128)(2,1)S(1)}, u32[]{:S(2)}, u32[]{:S(2)}) collective-permute-start(bf16[64,1024]{1,0:T(8,128)(2,1)S(1)} %pad_maximum_fusion.11), channel_id=1, source_target_pairs={{0,6},{2,4},{4,2},{6,0},{1,7},{3,5},{5,3},{7,1},{8,14},{10,12},{12... | collective-permute-start | bytes 393224 | tf_op jit(solution)/shard_map/ppermute | solution.py:38
  49.6 17.0 %collective-permute-start.19 = (bf16[128,2048]{1,0:T(8,128)(2,1)S(1)}, bf16[128,2048]{1,0:T(8,128)(2,1)S(1)}, u32[]{:S(2)}, u32[]{:S(2)}) collective-permute-start(bf16[128,2048]{1,0:T(8,128)(2,1)S(1)} %pad_maximum_fusion.3), channel_id=1, source_target_pairs={{0,2},{2,0},{4,6},{6,4},{1,3},{3,1},{5,7},{7,5},{8,10},{10,8},{12,... | collective-permute-start | bytes 1572872 | tf_op jit(solution)/shard_map/ppermute | solution.py:38
  51.6 13.0 %collective-permute-start.13 = (bf16[64,1024]{1,0:T(8,128)(2,1)S(1)}, bf16[64,1024]{1,0:T(8,128)(2,1)S(1)}, u32[]{:S(2)}, u32[]{:S(2)}) collective-permute-start(bf16[64,1024]{1,0:T(8,128)(2,1)S(1)} %pad_maximum_fusion.12), channel_id=1, source_target_pairs={{0,2},{2,0},{4,6},{6,4},{1,3},{3,1},{5,7},{7,5},{8,10},{10,8},{12,... | collective-permute-start | bytes 393224 | tf_op jit(solution)/shard_map/ppermute | solution.py:38
  64.7 22.5 %collective-permute-start.16 = (bf16[256,2048]{1,0:T(8,128)(2,1)S(1)}, bf16[256,2048]{1,0:T(8,128)(2,1)S(1)}, u32[]{:S(2)}, u32[]{:S(2)}) collective-permute-start(bf16[256,2048]{1,0:T(8,128)(2,1)S(1)} %pad_maximum_fusion.refs_0_), channel_id=1, source_target_pairs={{0,2},{2,0},{4,6},{6,4},{1,3},{3,1},{5,7},{7,5},{8,10},{10,8},{12,... | collective-permute-start | bytes 3145736 | tf_op jit(solution)/shard_map/ppermute | solution.py:38
  66.7 22.2 %collective-permute-start.20 = (bf16[256,2048]{1,0:T(8,128)(2,1)S(1)}, bf16[256,2048]{1,0:T(8,128)(2,1)S(1)}, u32[]{:S(2)}, u32[]{:S(2)}) collective-permute-start(bf16[256,2048]{1,0:T(8,128)(2,1)S(1)} %pad_maximum_fusion.1.refs_2_), channel_id=1, source_target_pairs={{0,6},{2,4},{4,2},{6,0},{1,7},{3,5},{5,3},{7,1},{8,14},{10,12},{12... | collective-permute-start | bytes 3145736 | tf_op jit(solution)/shard_map/ppermute | solution.py:38
  67.3 14.5 %collective-permute-start.18 = (bf16[128,1024]{1,0:T(8,128)(2,1)S(1)}, bf16[128,1024]{1,0:T(8,128)(2,1)S(1)}, u32[]{:S(2)}, u32[]{:S(2)}) collective-permute-start(bf16[128,1024]{1,0:T(8,128)(2,1)S(1)} %pad_maximum_fusion.9), channel_id=1, source_target_pairs={{0,192},{64,128},{128,64},{192,0},{1,193},{65,129},{129,65},{193,1... | collective-permute-start | bytes 786440 | tf_op jit(solution)/shard_map/ppermute | solution.py:38
  72.0 13.0 %collective-permute-start.17 = (bf16[128,1024]{1,0:T(8,128)(2,1)S(1)}, bf16[128,1024]{1,0:T(8,128)(2,1)S(1)}, u32[]{:S(2)}, u32[]{:S(2)}) collective-permute-start(bf16[128,1024]{1,0:T(8,128)(2,1)S(1)} %pad_maximum_fusion.10), channel_id=1, source_target_pairs={{0,64},{64,0},{128,192},{192,128},{1,65},{65,1},{129,193},{193,129... | collective-permute-start | bytes 786440 | tf_op jit(solution)/shard_map/ppermute | solution.py:38
  81.9 18.5 %collective-permute-start.21 = (bf16[256,1024]{1,0:T(8,128)(2,1)S(1)}, bf16[256,1024]{1,0:T(8,128)(2,1)S(1)}, u32[]{:S(2)}, u32[]{:S(2)}) collective-permute-start(bf16[256,1024]{1,0:T(8,128)(2,1)S(1)} %pad_maximum_fusion.4.refs_4_), channel_id=1, source_target_pairs={{0,64},{64,0},{128,192},{192,128},{1,65},{65,1},{129,193},{193,129... | collective-permute-start | bytes 1572872 | tf_op jit(solution)/shard_map/ppermute | solution.py:38
  85.0 21.3 %collective-permute-start.22 = (bf16[256,1024]{1,0:T(8,128)(2,1)S(1)}, bf16[256,1024]{1,0:T(8,128)(2,1)S(1)}, u32[]{:S(2)}, u32[]{:S(2)}) collective-permute-start(bf16[256,1024]{1,0:T(8,128)(2,1)S(1)} %pad_maximum_fusion.5.refs_6_), channel_id=1, source_target_pairs={{0,192},{64,128},{128,64},{192,0},{1,193},{65,129},{129,65},{193,1... | collective-permute-start | bytes 1572872 | tf_op jit(solution)/shard_map/ppermute | solution.py:38
  117.1 19.4 %collective-permute-start.23 = (bf16[256,2048]{1,0:T(8,128)(2,1)S(1)}, bf16[256,2048]{1,0:T(8,128)(2,1)S(1)}, u32[]{:S(2)}, u32[]{:S(2)}) collective-permute-start(bf16[256,2048]{1,0:T(8,128)(2,1)S(1)} %get-tuple-element.78), channel_id=1, source_target_pairs={{0,2},{2,0},{4,6},{6,4},{1,3},{3,1},{5,7},{7,5},{8,10},{10,8},{12,... | collective-permute-start | bytes 3145736 | tf_op jit(solution)/shard_map/ppermute | solution.py:38
  119.0 24.4 %collective-permute-start.27 = (bf16[256,2048]{1,0:T(8,128)(2,1)S(1)}, bf16[256,2048]{1,0:T(8,128)(2,1)S(1)}, u32[]{:S(2)}, u32[]{:S(2)}) collective-permute-start(bf16[256,2048]{1,0:T(8,128)(2,1)S(1)} %get-tuple-element.80), channel_id=1, source_target_pairs={{0,6},{2,4},{4,2},{6,0},{1,7},{3,5},{5,3},{7,1},{8,14},{10,12},{12... | collective-permute-start | bytes 3145736 | tf_op jit(solution)/shard_map/ppermute | solution.py:38
  121.6 26.3 %collective-permute-start.26 = (bf16[256,1024]{1,0:T(8,128)(2,1)S(1)}, bf16[256,1024]{1,0:T(8,128)(2,1)S(1)}, u32[]{:S(2)}, u32[]{:S(2)}) collective-permute-start(bf16[256,1024]{1,0:T(8,128)(2,1)S(1)} %get-tuple-element.82), channel_id=1, source_target_pairs={{0,64},{64,0},{128,192},{192,128},{1,65},{65,1},{129,193},{193,129... | collective-permute-start | bytes 1572872 | tf_op jit(solution)/shard_map/ppermute | solution.py:38
  122.6 25.5 %collective-permute-start.25 = (bf16[256,1024]{1,0:T(8,128)(2,1)S(1)}, bf16[256,1024]{1,0:T(8,128)(2,1)S(1)}, u32[]{:S(2)}, u32[]{:S(2)}) collective-permute-start(bf16[256,1024]{1,0:T(8,128)(2,1)S(1)} %get-tuple-element.85), channel_id=1, source_target_pairs={{0,192},{64,128},{128,64},{192,0},{1,193},{65,129},{129,65},{193,1... | collective-permute-start | bytes 1572872 | tf_op jit(solution)/shard_map/ppermute | solution.py:38
  136.8 14.9 %collective-permute-start.24 = (bf16[128,2048]{1,0:T(8,128)(2,1)S(1)}, bf16[128,2048]{1,0:T(8,128)(2,1)S(1)}, u32[]{:S(2)}, u32[]{:S(2)}) collective-permute-start(bf16[128,2048]{1,0:T(8,128)(2,1)S(1)} %get-tuple-element.106), channel_id=1, source_target_pairs={{0,6},{2,4},{4,2},{6,0},{1,7},{3,5},{5,3},{7,1},{8,14},{10,12},{12... | collective-permute-start | bytes 1572872 | tf_op jit(solution)/shard_map/ppermute | solution.py:38
  148.0 18.8 %collective-permute-start.30 = (bf16[128,1024]{1,0:T(8,128)(2,1)S(1)}, bf16[128,1024]{1,0:T(8,128)(2,1)S(1)}, u32[]{:S(2)}, u32[]{:S(2)}) collective-permute-start(bf16[128,1024]{1,0:T(8,128)(2,1)S(1)} %get-tuple-element.114), channel_id=1, source_target_pairs={{0,192},{64,128},{128,64},{192,0},{1,193},{65,129},{129,65},{193,1... | collective-permute-start | bytes 786440 | tf_op jit(solution)/shard_map/ppermute | solution.py:38
  148.3 19.0 %collective-permute-start.29 = (bf16[128,1024]{1,0:T(8,128)(2,1)S(1)}, bf16[128,1024]{1,0:T(8,128)(2,1)S(1)}, u32[]{:S(2)}, u32[]{:S(2)}) collective-permute-start(bf16[128,1024]{1,0:T(8,128)(2,1)S(1)} %get-tuple-element.115), channel_id=1, source_target_pairs={{0,64},{64,0},{128,192},{192,128},{1,65},{65,1},{129,193},{193,129... | collective-permute-start | bytes 786440 | tf_op jit(solution)/shard_map/ppermute | solution.py:38
  151.9 19.7 %collective-permute-start.28 = (bf16[64,2048]{1,0:T(8,128)(2,1)S(1)}, bf16[64,2048]{1,0:T(8,128)(2,1)S(1)}, u32[]{:S(2)}, u32[]{:S(2)}) collective-permute-start(bf16[64,2048]{1,0:T(8,128)(2,1)S(1)} %get-tuple-element.110), channel_id=1, source_target_pairs={{0,192},{64,128},{128,64},{192,0},{1,193},{65,129},{129,65},{193,1... | collective-permute-start | bytes 786440 | tf_op jit(solution)/shard_map/ppermute | solution.py:38
  155.4 18.1 %collective-permute-start.35 = (bf16[64,2048]{1,0:T(8,128)(2,1)S(1)}, bf16[64,2048]{1,0:T(8,128)(2,1)S(1)}, u32[]{:S(2)}, u32[]{:S(2)}) collective-permute-start(bf16[64,2048]{1,0:T(8,128)(2,1)S(1)} %get-tuple-element.112), channel_id=1, source_target_pairs={{0,64},{64,0},{128,192},{192,128},{1,65},{65,1},{129,193},{193,129... | collective-permute-start | bytes 786440 | tf_op jit(solution)/shard_map/ppermute | solution.py:38
  (23 other events, 264.2 us)

commit v3 on v2

--- a/solution.py
+++ b/solution.py
@@ -193,13 +193,15 @@
     last = None
     for step in range(4):
         came = [trade(h, order[step]) for h, (_, _, order) in zip(held, CHAINS)]
-        for j in range(4):
-            got = came[j] if last is None else after(came[j], last)
+        for j in (2, 3, 0, 1):
+            if last is not None:
+                came[j] = after(came[j], last)
             if step < 3:
-                held[j] = last = jnp.concatenate([held[j], got], axis=0)
+                held[j] = last = jnp.concatenate([held[j], came[j]], axis=0)
             else:
-                pieces += [held[j], got]
-                last = got
+                last = came[j]
+    for h, c in zip(held, came):
+        pieces += [h, c]
 
     hidden = hidden_units(pieces, (wg0, wu0, wg1, wu1))
 

time: 204 us -> 191 us (0.936)
  waiting for transfers between devices: 106 us -> 99.8 us
  starting transfers between devices: 72.3 us -> 66.4 us
    ppermute x32, waiting for transfers between devices: 90.2 us -> 85.8 us  [trade(): return lax.ppermute(value, axis, [(i, i ^ mask) for i in range(4)])]
    ppermute x32, starting transfers between devices: 52.6 us -> 49.4 us  [trade(): return lax.ppermute(value, axis, [(i, i ^ mask) for i in range(4)])]
    ppermute x11, starting transfers between devices: 19.8 us -> 16.9 us  [shift(): return lax.ppermute(value, axis, [(i, (i + by) % n) for i in range(n)])]
  transfers between devices with their start and end apart: 43 -> 43, of which waited for: 25 -> 21; matrix products, arithmetic and copies ran while one was open for 3% -> 4% of each run, Pallas kernels for 2% -> 2%
where the time goes in v3:
time: 191 us; the launch traced here: 189 us
  waiting for transfers between devices  99.8 us (52%)
  starting transfers between devices  66.4 us (35%)
  Pallas kernels  13.9 us (7%)
  other arithmetic  4.78 us (3%)
  matrix products  2.13 us (1%)
    ppermute x32, waiting for transfers between devices, trade(): return lax.ppermute(value, axis, [(i, i ^ mask) for i in range(4)])  85.8 us
    ppermute x32, starting transfers between devices, trade(): return lax.ppermute(value, axis, [(i, i ^ mask) for i in range(4)])  49.4 us
    ppermute x11, starting transfers between devices, shift(): return lax.ppermute(value, axis, [(i, (i + by) % n) for i in range(n)])  16.9 us
    ppermute x11, waiting for transfers between devices, shift(): return lax.ppermute(value, axis, [(i, (i + by) % n) for i in range(n)])  13.9 us
    pallas_call x1, Pallas kernels, hidden_units(): pl.pallas_call(hidden_kernel, grid=(STEPS,), out_shape=jax.ShapeDtypeStru...  9 us
    pallas_call x4, Pallas kernels, expert_out(): pl.pallas_call(functools.partial(out_kernel, order), grid=(size // PART,)...  4.87 us
  transfers between devices with their start and end apart: 43, of which 21 were waited for; matrix products, arithmetic and copies ran while one was open for 4% of the time, Pallas kernels for 2%

profile of v3, /device:TPU:2, one launch (start us, length us, event | category | flops | bytes accessed | tf_op | source)
XLA Modules:
  0.0 189.1 jit_solution(5728239761552236572)
XLA Ops:
  7.0 5.0 %collective-permute-done = bf16[16,6144]{1,0:T(8,128)(2,1)S(1)} collective-permute-done((bf16[16,6144]{1,0:T(8,128)(2,1)S(1)}, bf16[16,6144]{1,0:T(8,128)(2,1)S(1)}, u32[]{:S(2)}, u32[]{:S(2)}) %collective-permute-start) | collective-permute-done | bytes 196640 | tf_op jit(solution)/shard_map/ppermute | solution.py:17
  13.9 3.0 %collective-permute-start.3 = (bf16[8,6144]{1,0:T(8,128)(2,1)S(1)}, bf16[8,6144]{1,0:T(8,128)(2,1)S(1)}, u32[]{:S(2)}, u32[]{:S(2)}) collective-permute-start(bf16[8,6144]{1,0:T(8,128)(2,1)S(1)} %pad_maximum_fusion.15), channel_id=1, source_target_pairs={{0,16},{8,24},{16,0},{24,8},{1,17},{9,25},{17,1},{25,9},{2,18},{10... | collective-permute-start | bytes 294920 | tf_op jit(solution)/shard_map/ppermute | solution.py:17
  18.4 2.9 %collective-permute-done.3 = bf16[8,6144]{1,0:T(8,128)(2,1)S(1)} collective-permute-done((bf16[8,6144]{1,0:T(8,128)(2,1)S(1)}, bf16[8,6144]{1,0:T(8,128)(2,1)S(1)}, u32[]{:S(2)}, u32[]{:S(2)}) %collective-permute-start.3) | collective-permute-done | bytes 98336 | tf_op jit(solution)/shard_map/ppermute | solution.py:17
  24.6 6.1 %collective-permute-start.13 = (bf16[32,2048]{1,0:T(8,128)(2,1)S(1)}, bf16[32,2048]{1,0:T(8,128)(2,1)S(1)}, u32[]{:S(2)}, u32[]{:S(2)}) collective-permute-start(bf16[32,2048]{1,0:T(8,128)(2,1)S(1)} %get-tuple-element.124), channel_id=1, source_target_pairs={{0,192},{64,128},{128,64},{192,0},{1,193},{65,129},{129,65},{193,1... | collective-permute-start | bytes 393224 | tf_op jit(solution)/shard_map/ppermute | solution.py:38
  32.4 2.6 %collective-permute-start.11 = (bf16[64,1024]{1,0:T(8,128)(2,1)S(1)}, bf16[64,1024]{1,0:T(8,128)(2,1)S(1)}, u32[]{:S(2)}, u32[]{:S(2)}) collective-permute-start(bf16[64,1024]{1,0:T(8,128)(2,1)S(1)} %pad_maximum_fusion.12), channel_id=1, source_target_pairs={{0,2},{2,0},{4,6},{6,4},{1,3},{3,1},{5,7},{7,5},{8,10},{10,8},{12,... | collective-permute-start | bytes 393224 | tf_op jit(solution)/shard_map/ppermute | solution.py:38
  34.9 3.7 %collective-permute-done.7 = bf16[32,2048]{1,0:T(8,128)(2,1)S(1)} collective-permute-done((bf16[32,2048]{1,0:T(8,128)(2,1)S(1)}, bf16[32,2048]{1,0:T(8,128)(2,1)S(1)}, u32[]{:S(2)}, u32[]{:S(2)}) %collective-permute-start.7) | collective-permute-done | bytes 131104 | tf_op jit(solution)/shard_map/ppermute | solution.py:38
  38.9 15.7 %collective-permute-done.10 = bf16[64,2048]{1,0:T(8,128)(2,1)S(1)} collective-permute-done((bf16[64,2048]{1,0:T(8,128)(2,1)S(1)}, bf16[64,2048]{1,0:T(8,128)(2,1)S(1)}, u32[]{:S(2)}, u32[]{:S(2)}) %collective-permute-start.10) | collective-permute-done | bytes 262176 | tf_op jit(solution)/shard_map/ppermute | solution.py:38
  55.0 2.4 %collective-permute-start.21 = (bf16[128,2048]{1,0:T(8,128)(2,1)S(1)}, bf16[128,2048]{1,0:T(8,128)(2,1)S(1)}, u32[]{:S(2)}, u32[]{:S(2)}) collective-permute-start(bf16[128,2048]{1,0:T(8,128)(2,1)S(1)} %pad_maximum_fusion.3), channel_id=1, source_target_pairs={{0,2},{2,0},{4,6},{6,4},{1,3},{3,1},{5,7},{7,5},{8,10},{10,8},{12,... | collective-permute-start | bytes 1572872 | tf_op jit(solution)/shard_map/ppermute | solution.py:38
  57.4 6.5 %collective-permute-done.16 = bf16[128,1024]{1,0:T(8,128)(2,1)S(1)} collective-permute-done((bf16[128,1024]{1,0:T(8,128)(2,1)S(1)}, bf16[128,1024]{1,0:T(8,128)(2,1)S(1)}, u32[]{:S(2)}, u32[]{:S(2)}) %collective-permute-start.16) | collective-permute-done | bytes 262176 | tf_op jit(solution)/shard_map/ppermute | solution.py:38
  69.0 3.2 %collective-permute-start.22 = (bf16[256,2048]{1,0:T(8,128)(2,1)S(1)}, bf16[256,2048]{1,0:T(8,128)(2,1)S(1)}, u32[]{:S(2)}, u32[]{:S(2)}) collective-permute-start(bf16[256,2048]{1,0:T(8,128)(2,1)S(1)} %pad_maximum_fusion.1.refs_2_), channel_id=1, source_target_pairs={{0,6},{2,4},{4,2},{6,0},{1,7},{3,5},{5,3},{7,1},{8,14},{10,12},{12... | collective-permute-start | bytes 3145736 | tf_op jit(solution)/shard_map/ppermute | solution.py:38
  72.2 4.2 %collective-permute-start.19 = (bf16[256,1024]{1,0:T(8,128)(2,1)S(1)}, bf16[256,1024]{1,0:T(8,128)(2,1)S(1)}, u32[]{:S(2)}, u32[]{:S(2)}) collective-permute-start(bf16[256,1024]{1,0:T(8,128)(2,1)S(1)} %pad_maximum_fusion.5.refs_6_), channel_id=1, source_target_pairs={{0,192},{64,128},{128,64},{192,0},{1,193},{65,129},{129,65},{193,1... | collective-permute-start | bytes 1572872 | tf_op jit(solution)/shard_map/ppermute | solution.py:38
  76.4 16.8 %collective-permute-done.20.refs_5_ = bf16[256,1024]{1,0:T(8,128)(2,1)S(1)} collective-permute-done((bf16[256,1024]{1,0:T(8,128)(2,1)S(1)}, bf16[256,1024]{1,0:T(8,128)(2,1)S(1)}, u32[]{:S(2)}, u32[]{:S(2)}) %collective-permute-start.20) | collective-permute-done | bytes 524320 | tf_op jit(solution)/shard_map/ppermute | solution.py:38
  93.2 4.2 %collective-permute-done.19.refs_7_ = bf16[256,1024]{1,0:T(8,128)(2,1)S(1)} collective-permute-done((bf16[256,1024]{1,0:T(8,128)(2,1)S(1)}, bf16[256,1024]{1,0:T(8,128)(2,1)S(1)}, u32[]{:S(2)}, u32[]{:S(2)}) %collective-permute-start.19) | collective-permute-done | bytes 524320 | tf_op jit(solution)/shard_map/ppermute | solution.py:38
  97.4 9.0 %hidden.1 = bf16[512,512]{1,0:T(8,128)(2,1)S(1)} custom-call(bf16[256,2048]{1,0:T(8,128)(2,1)S(1)} %pad_maximum_fusion.refs_0_, bf16[256,2048]{1,0:T(8,128)(2,1)S(1)} %collective-permute-done.18.refs_1_, bf16[256,2048]{1,0:T(8,128)(2,1)S(1)} %pad_maximum_fusion.1.refs_2_, bf16[256,2048]{1,0:T(8,128)(2,1)S(1)} %collective-permute-done.22.refs_3_, ...), custom_call_target="tpu_custom_call" | custom-call | flops 6442450944 | bytes 18874368 | tf_op jit(solution)/shard_map/hidden/pallas_call | solution.py:109
  114.4 16.9 %collective-permute-done.23 = bf16[256,2048]{1,0:T(8,128)(2,1)S(1)} collective-permute-done((bf16[256,2048]{1,0:T(8,128)(2,1)S(1)}, bf16[256,2048]{1,0:T(8,128)(2,1)S(1)}, u32[]{:S(2)}, u32[]{:S(2)}) %collective-permute-start.23) | collective-permute-done | bytes 1048608 | tf_op jit(solution)/shard_map/ppermute | solution.py:38
  131.7 3.6 %collective-permute-start.24 = (bf16[128,2048]{1,0:T(8,128)(2,1)S(1)}, bf16[128,2048]{1,0:T(8,128)(2,1)S(1)}, u32[]{:S(2)}, u32[]{:S(2)}) collective-permute-start(bf16[128,2048]{1,0:T(8,128)(2,1)S(1)} %get-tuple-element.106), channel_id=1, source_target_pairs={{0,6},{2,4},{4,2},{6,0},{1,7},{3,5},{5,3},{7,1},{8,14},{10,12},{12... | collective-permute-start | bytes 1572872 | tf_op jit(solution)/shard_map/ppermute | solution.py:38
  135.7 3.9 %collective-permute-start.31 = (bf16[128,2048]{1,0:T(8,128)(2,1)S(1)}, bf16[128,2048]{1,0:T(8,128)(2,1)S(1)}, u32[]{:S(2)}, u32[]{:S(2)}) collective-permute-start(bf16[128,2048]{1,0:T(8,128)(2,1)S(1)} %get-tuple-element.108), channel_id=1, source_target_pairs={{0,2},{2,0},{4,6},{6,4},{1,3},{3,1},{5,7},{7,5},{8,10},{10,8},{12,... | collective-permute-start | bytes 1572872 | tf_op jit(solution)/shard_map/ppermute | solution.py:38
  141.9 4.6 %collective-permute-done.24 = bf16[128,2048]{1,0:T(8,128)(2,1)S(1)} collective-permute-done((bf16[128,2048]{1,0:T(8,128)(2,1)S(1)}, bf16[128,2048]{1,0:T(8,128)(2,1)S(1)}, u32[]{:S(2)}, u32[]{:S(2)}) %collective-permute-start.24) | collective-permute-done | bytes 524320 | tf_op jit(solution)/shard_map/ppermute | solution.py:38
  148.6 9.2 %collective-permute-done.30 = bf16[128,1024]{1,0:T(8,128)(2,1)S(1)} collective-permute-done((bf16[128,1024]{1,0:T(8,128)(2,1)S(1)}, bf16[128,1024]{1,0:T(8,128)(2,1)S(1)}, u32[]{:S(2)}, u32[]{:S(2)}) %collective-permute-start.30) | collective-permute-done | bytes 262176 | tf_op jit(solution)/shard_map/ppermute | solution.py:38
  157.9 3.5 %collective-permute-start.34 = (bf16[64,1024]{1,0:T(8,128)(2,1)S(1)}, bf16[64,1024]{1,0:T(8,128)(2,1)S(1)}, u32[]{:S(2)}, u32[]{:S(2)}) collective-permute-start(bf16[64,1024]{1,0:T(8,128)(2,1)S(1)} %get-tuple-element.118), channel_id=1, source_target_pairs={{0,6},{2,4},{4,2},{6,0},{1,7},{3,5},{5,3},{7,1},{8,14},{10,12},{12... | collective-permute-start | bytes 393224 | tf_op jit(solution)/shard_map/ppermute | solution.py:38
  164.5 3.8 %collective-permute-start.36 = (bf16[32,2048]{1,0:T(8,128)(2,1)S(1)}, bf16[32,2048]{1,0:T(8,128)(2,1)S(1)}, u32[]{:S(2)}, u32[]{:S(2)}) collective-permute-start(bf16[32,2048]{1,0:T(8,128)(2,1)S(1)} %add_convert_fusion.15), channel_id=1, source_target_pairs={{0,192},{64,128},{128,64},{192,0},{1,193},{65,129},{129,65},{193,1... | collective-permute-start | bytes 393224 | tf_op jit(solution)/shard_map/ppermute | solution.py:38
  174.7 2.4 %collective-permute-start.40 = (bf16[8,6144]{1,0:T(8,128)(2,1)S(1)}, bf16[8,6144]{1,0:T(8,128)(2,1)S(1)}, u32[]{:S(2)}, u32[]{:S(2)}) collective-permute-start(bf16[8,6144]{1,0:T(8,128)(2,1)S(1)} %get-tuple-element.122), channel_id=1, source_target_pairs={{0,16},{8,24},{16,0},{24,8},{1,17},{9,25},{17,1},{25,9},{2,18},{10... | collective-permute-start | bytes 294920 | tf_op jit(solution)/shard_map/ppermute | solution.py:17
  177.2 2.5 %collective-permute-start.39 = (bf16[8,6144]{1,0:T(8,128)(2,1)S(1)}, bf16[8,6144]{1,0:T(8,128)(2,1)S(1)}, u32[]{:S(2)}, u32[]{:S(2)}) collective-permute-start(bf16[8,6144]{1,0:T(8,128)(2,1)S(1)} %get-tuple-element.123), channel_id=1, source_target_pairs={{0,24},{8,0},{16,8},{24,16},{1,25},{9,1},{17,9},{25,17},{2,26},{10... | collective-permute-start | bytes 294920 | tf_op jit(solution)/shard_map/ppermute | solution.py:17
  184.3 3.6 %collective-permute-done.42 = bf16[16,6144]{1,0:T(8,128)(2,1)S(1)} collective-permute-done((bf16[16,6144]{1,0:T(8,128)(2,1)S(1)}, bf16[16,6144]{1,0:T(8,128)(2,1)S(1)}, u32[]{:S(2)}, u32[]{:S(2)}) %collective-permute-start.42) | collective-permute-done | bytes 196640 | tf_op jit(solution)/shard_map/ppermute | solution.py:17
  (138 shorter events, 49.3 us)
Async XLA Ops:
  0.0 12.0 %collective-permute-start.1 = (bf16[6144,256]{1,0:T(8,128)(2,1)}, bf16[6144,256]{1,0:T(8,128)(2,1)S(1)}, u32[]{:S(2)}, u32[]{:S(2)}) collective-permute-start(bf16[6144,256]{1,0:T(8,128)(2,1)} %bitcast.11), channel_id=1, source_target_pairs={{0,1},{1,0},{2,3},{3,2},{4,5},{5,4},{6,7},{7,6},{8,9},{9,8},{10,11... | collective-permute-start | bytes 9437192 | tf_op jit(solution)/shard_map/ppermute | solution.py:17
  6.4 11.9 %collective-permute-start.5 = (bf16[6144,256]{1,0:T(8,128)(2,1)}, bf16[6144,256]{1,0:T(8,128)(2,1)S(1)}, u32[]{:S(2)}, u32[]{:S(2)}) collective-permute-start(bf16[6144,256]{1,0:T(8,128)(2,1)} %bitcast.13), channel_id=1, source_target_pairs={{0,1},{1,0},{2,3},{3,2},{4,5},{5,4},{6,7},{7,6},{8,9},{9,8},{10,11... | collective-permute-start | bytes 9437192 | tf_op jit(solution)/shard_map/ppermute | solution.py:17
  6.7 11.7 %collective-permute-start.6 = (bf16[256,6144]{1,0:T(8,128)(2,1)}, bf16[256,6144]{1,0:T(8,128)(2,1)S(1)}, u32[]{:S(2)}, u32[]{:S(2)}) collective-permute-start(bf16[256,6144]{1,0:T(8,128)(2,1)} %bitcast.6), channel_id=1, source_target_pairs={{0,1},{1,0},{2,3},{3,2},{4,5},{5,4},{6,7},{7,6},{8,9},{9,8},{10,11... | collective-permute-start | bytes 9437192 | tf_op jit(solution)/shard_map/ppermute | solution.py:17
  21.7 10.5 %collective-permute-start.9 = (bf16[32,1024]{1,0:T(8,128)(2,1)S(1)}, bf16[32,1024]{1,0:T(8,128)(2,1)S(1)}, u32[]{:S(2)}, u32[]{:S(2)}) collective-permute-start(bf16[32,1024]{1,0:T(8,128)(2,1)S(1)} %get-tuple-element.126), channel_id=1, source_target_pairs={{0,2},{2,0},{4,6},{6,4},{1,3},{3,1},{5,7},{7,5},{8,10},{10,8},{12,... | collective-permute-start | bytes 196616 | tf_op jit(solution)/shard_map/ppermute | solution.py:38
  24.6 14.1 %collective-permute-start.13 = (bf16[32,2048]{1,0:T(8,128)(2,1)S(1)}, bf16[32,2048]{1,0:T(8,128)(2,1)S(1)}, u32[]{:S(2)}, u32[]{:S(2)}) collective-permute-start(bf16[32,2048]{1,0:T(8,128)(2,1)S(1)} %get-tuple-element.124), channel_id=1, source_target_pairs={{0,192},{64,128},{128,64},{192,0},{1,193},{65,129},{129,65},{193,1... | collective-permute-start | bytes 393224 | tf_op jit(solution)/shard_map/ppermute | solution.py:38
  38.6 16.0 %collective-permute-start.10 = (bf16[64,2048]{1,0:T(8,128)(2,1)S(1)}, bf16[64,2048]{1,0:T(8,128)(2,1)S(1)}, u32[]{:S(2)}, u32[]{:S(2)}) collective-permute-start(bf16[64,2048]{1,0:T(8,128)(2,1)S(1)} %pad_maximum_fusion.7), channel_id=1, source_target_pairs={{0,192},{64,128},{128,64},{192,0},{1,193},{65,129},{129,65},{193,1... | collective-permute-start | bytes 786440 | tf_op jit(solution)/shard_map/ppermute | solution.py:38
  38.7 16.2 %collective-permute-start.17 = (bf16[64,2048]{1,0:T(8,128)(2,1)S(1)}, bf16[64,2048]{1,0:T(8,128)(2,1)S(1)}, u32[]{:S(2)}, u32[]{:S(2)}) collective-permute-start(bf16[64,2048]{1,0:T(8,128)(2,1)S(1)} %pad_maximum_fusion.8), channel_id=1, source_target_pairs={{0,64},{64,0},{128,192},{192,128},{1,65},{65,1},{129,193},{193,129... | collective-permute-start | bytes 786440 | tf_op jit(solution)/shard_map/ppermute | solution.py:38
  54.6 10.6 %collective-permute-start.14 = (bf16[128,2048]{1,0:T(8,128)(2,1)S(1)}, bf16[128,2048]{1,0:T(8,128)(2,1)S(1)}, u32[]{:S(2)}, u32[]{:S(2)}) collective-permute-start(bf16[128,2048]{1,0:T(8,128)(2,1)S(1)} %pad_maximum_fusion.2), channel_id=1, source_target_pairs={{0,6},{2,4},{4,2},{6,0},{1,7},{3,5},{5,3},{7,1},{8,14},{10,12},{12... | collective-permute-start | bytes 1572872 | tf_op jit(solution)/shard_map/ppermute | solution.py:38
  55.0 13.8 %collective-permute-start.21 = (bf16[128,2048]{1,0:T(8,128)(2,1)S(1)}, bf16[128,2048]{1,0:T(8,128)(2,1)S(1)}, u32[]{:S(2)}, u32[]{:S(2)}) collective-permute-start(bf16[128,2048]{1,0:T(8,128)(2,1)S(1)} %pad_maximum_fusion.3), channel_id=1, source_target_pairs={{0,2},{2,0},{4,6},{6,4},{1,3},{3,1},{5,7},{7,5},{8,10},{10,8},{12,... | collective-permute-start | bytes 1572872 | tf_op jit(solution)/shard_map/ppermute | solution.py:38
  65.4 32.0 %collective-permute-start.18 = (bf16[256,2048]{1,0:T(8,128)(2,1)S(1)}, bf16[256,2048]{1,0:T(8,128)(2,1)S(1)}, u32[]{:S(2)}, u32[]{:S(2)}) collective-permute-start(bf16[256,2048]{1,0:T(8,128)(2,1)S(1)} %pad_maximum_fusion.refs_0_), channel_id=1, source_target_pairs={{0,2},{2,0},{4,6},{6,4},{1,3},{3,1},{5,7},{7,5},{8,10},{10,8},{12,... | collective-permute-start | bytes 3145736 | tf_op jit(solution)/shard_map/ppermute | solution.py:38
  69.0 28.4 %collective-permute-start.22 = (bf16[256,2048]{1,0:T(8,128)(2,1)S(1)}, bf16[256,2048]{1,0:T(8,128)(2,1)S(1)}, u32[]{:S(2)}, u32[]{:S(2)}) collective-permute-start(bf16[256,2048]{1,0:T(8,128)(2,1)S(1)} %pad_maximum_fusion.1.refs_2_), channel_id=1, source_target_pairs={{0,6},{2,4},{4,2},{6,0},{1,7},{3,5},{5,3},{7,1},{8,14},{10,12},{12... | collective-permute-start | bytes 3145736 | tf_op jit(solution)/shard_map/ppermute | solution.py:38
  72.2 21.0 %collective-permute-start.20 = (bf16[256,1024]{1,0:T(8,128)(2,1)S(1)}, bf16[256,1024]{1,0:T(8,128)(2,1)S(1)}, u32[]{:S(2)}, u32[]{:S(2)}) collective-permute-start(bf16[256,1024]{1,0:T(8,128)(2,1)S(1)} %pad_maximum_fusion.4.refs_4_), channel_id=1, source_target_pairs={{0,64},{64,0},{128,192},{192,128},{1,65},{65,1},{129,193},{193,129... | collective-permute-start | bytes 1572872 | tf_op jit(solution)/shard_map/ppermute | solution.py:38
  72.2 25.2 %collective-permute-start.19 = (bf16[256,1024]{1,0:T(8,128)(2,1)S(1)}, bf16[256,1024]{1,0:T(8,128)(2,1)S(1)}, u32[]{:S(2)}, u32[]{:S(2)}) collective-permute-start(bf16[256,1024]{1,0:T(8,128)(2,1)S(1)} %pad_maximum_fusion.5.refs_6_), channel_id=1, source_target_pairs={{0,192},{64,128},{128,64},{192,0},{1,193},{65,129},{129,65},{193,1... | collective-permute-start | bytes 1572872 | tf_op jit(solution)/shard_map/ppermute | solution.py:38
  108.2 23.2 %collective-permute-start.23 = (bf16[256,2048]{1,0:T(8,128)(2,1)S(1)}, bf16[256,2048]{1,0:T(8,128)(2,1)S(1)}, u32[]{:S(2)}, u32[]{:S(2)}) collective-permute-start(bf16[256,2048]{1,0:T(8,128)(2,1)S(1)} %get-tuple-element.78), channel_id=1, source_target_pairs={{0,2},{2,0},{4,6},{6,4},{1,3},{3,1},{5,7},{7,5},{8,10},{10,8},{12,... | collective-permute-start | bytes 3145736 | tf_op jit(solution)/shard_map/ppermute | solution.py:38
  110.9 24.4 %collective-permute-start.27 = (bf16[256,2048]{1,0:T(8,128)(2,1)S(1)}, bf16[256,2048]{1,0:T(8,128)(2,1)S(1)}, u32[]{:S(2)}, u32[]{:S(2)}) collective-permute-start(bf16[256,2048]{1,0:T(8,128)(2,1)S(1)} %get-tuple-element.80), channel_id=1, source_target_pairs={{0,6},{2,4},{4,2},{6,0},{1,7},{3,5},{5,3},{7,1},{8,14},{10,12},{12... | collective-permute-start | bytes 3145736 | tf_op jit(solution)/shard_map/ppermute | solution.py:38
  113.3 26.3 %collective-permute-start.26 = (bf16[256,1024]{1,0:T(8,128)(2,1)S(1)}, bf16[256,1024]{1,0:T(8,128)(2,1)S(1)}, u32[]{:S(2)}, u32[]{:S(2)}) collective-permute-start(bf16[256,1024]{1,0:T(8,128)(2,1)S(1)} %get-tuple-element.82), channel_id=1, source_target_pairs={{0,64},{64,0},{128,192},{192,128},{1,65},{65,1},{129,193},{193,129... | collective-permute-start | bytes 1572872 | tf_op jit(solution)/shard_map/ppermute | solution.py:38
  114.1 25.7 %collective-permute-start.25 = (bf16[256,1024]{1,0:T(8,128)(2,1)S(1)}, bf16[256,1024]{1,0:T(8,128)(2,1)S(1)}, u32[]{:S(2)}, u32[]{:S(2)}) collective-permute-start(bf16[256,1024]{1,0:T(8,128)(2,1)S(1)} %get-tuple-element.85), channel_id=1, source_target_pairs={{0,192},{64,128},{128,64},{192,0},{1,193},{65,129},{129,65},{193,1... | collective-permute-start | bytes 1572872 | tf_op jit(solution)/shard_map/ppermute | solution.py:38
  131.7 14.8 %collective-permute-start.24 = (bf16[128,2048]{1,0:T(8,128)(2,1)S(1)}, bf16[128,2048]{1,0:T(8,128)(2,1)S(1)}, u32[]{:S(2)}, u32[]{:S(2)}) collective-permute-start(bf16[128,2048]{1,0:T(8,128)(2,1)S(1)} %get-tuple-element.106), channel_id=1, source_target_pairs={{0,6},{2,4},{4,2},{6,0},{1,7},{3,5},{5,3},{7,1},{8,14},{10,12},{12... | collective-permute-start | bytes 1572872 | tf_op jit(solution)/shard_map/ppermute | solution.py:38
  135.7 12.7 %collective-permute-start.31 = (bf16[128,2048]{1,0:T(8,128)(2,1)S(1)}, bf16[128,2048]{1,0:T(8,128)(2,1)S(1)}, u32[]{:S(2)}, u32[]{:S(2)}) collective-permute-start(bf16[128,2048]{1,0:T(8,128)(2,1)S(1)} %get-tuple-element.108), channel_id=1, source_target_pairs={{0,2},{2,0},{4,6},{6,4},{1,3},{3,1},{5,7},{7,5},{8,10},{10,8},{12,... | collective-permute-start | bytes 1572872 | tf_op jit(solution)/shard_map/ppermute | solution.py:38
  139.7 18.1 %collective-permute-start.30 = (bf16[128,1024]{1,0:T(8,128)(2,1)S(1)}, bf16[128,1024]{1,0:T(8,128)(2,1)S(1)}, u32[]{:S(2)}, u32[]{:S(2)}) collective-permute-start(bf16[128,1024]{1,0:T(8,128)(2,1)S(1)} %get-tuple-element.114), channel_id=1, source_target_pairs={{0,192},{64,128},{128,64},{192,0},{1,193},{65,129},{129,65},{193,1... | collective-permute-start | bytes 786440 | tf_op jit(solution)/shard_map/ppermute | solution.py:38
  140.1 21.3 %collective-permute-start.29 = (bf16[128,1024]{1,0:T(8,128)(2,1)S(1)}, bf16[128,1024]{1,0:T(8,128)(2,1)S(1)}, u32[]{:S(2)}, u32[]{:S(2)}) collective-permute-start(bf16[128,1024]{1,0:T(8,128)(2,1)S(1)} %get-tuple-element.115), channel_id=1, source_target_pairs={{0,64},{64,0},{128,192},{192,128},{1,65},{65,1},{129,193},{193,129... | collective-permute-start | bytes 786440 | tf_op jit(solution)/shard_map/ppermute | solution.py:38
  146.6 17.4 %collective-permute-start.28 = (bf16[64,2048]{1,0:T(8,128)(2,1)S(1)}, bf16[64,2048]{1,0:T(8,128)(2,1)S(1)}, u32[]{:S(2)}, u32[]{:S(2)}) collective-permute-start(bf16[64,2048]{1,0:T(8,128)(2,1)S(1)} %get-tuple-element.110), channel_id=1, source_target_pairs={{0,192},{64,128},{128,64},{192,0},{1,193},{65,129},{129,65},{193,1... | collective-permute-start | bytes 786440 | tf_op jit(solution)/shard_map/ppermute | solution.py:38
  148.5 15.9 %collective-permute-start.35 = (bf16[64,2048]{1,0:T(8,128)(2,1)S(1)}, bf16[64,2048]{1,0:T(8,128)(2,1)S(1)}, u32[]{:S(2)}, u32[]{:S(2)}) collective-permute-start(bf16[64,2048]{1,0:T(8,128)(2,1)S(1)} %get-tuple-element.112), channel_id=1, source_target_pairs={{0,64},{64,0},{128,192},{192,128},{1,65},{65,1},{129,193},{193,129... | collective-permute-start | bytes 786440 | tf_op jit(solution)/shard_map/ppermute | solution.py:38
  157.9 10.4 %collective-permute-start.34 = (bf16[64,1024]{1,0:T(8,128)(2,1)S(1)}, bf16[64,1024]{1,0:T(8,128)(2,1)S(1)}, u32[]{:S(2)}, u32[]{:S(2)}) collective-permute-start(bf16[64,1024]{1,0:T(8,128)(2,1)S(1)} %get-tuple-element.118), channel_id=1, source_target_pairs={{0,6},{2,4},{4,2},{6,0},{1,7},{3,5},{5,3},{7,1},{8,14},{10,12},{12... | collective-permute-start | bytes 393224 | tf_op jit(solution)/shard_map/ppermute | solution.py:38
  (23 other events, 230.8 us)

commit v4 on v3

v4 whole, which is shorter than its diff:
```python
import functools

import jax
import jax.numpy as jnp
from jax import lax
from jax.experimental import pallas as pl
from jax.experimental.pallas import tpu as pltpu
from jax.sharding import Mesh
from jax.sharding import PartitionSpec as P

AXES = ("dp", "zl", "y", "x", "c")
STEPS = 6


DIMS = {"xa": ("x", 1), "xb": ("x", 3), "za": ("dp", 1), "zb": ("dp", 3), "c": ("c", 1)}
CHAINS = (
    (0, 2048, ("za", "zb", "xb", "xa")),
    (3072, 2048, ("zb", "za", "xa", "xb")),
    (2048, 1024, ("xa", "xb", "zb", "za")),
    (5120, 1024, ("xb", "xa", "za", "zb")),
)
CANON = ("xa", "xb", "za", "zb")
UNIT = 32
HALF = 8 * UNIT


def canon_block(order, index):
    return sum(((index >> k) & 1) << CANON.index(d) for k, d in enumerate(order))


def trade(value, dim):
    axis, mask = DIMS[dim]
    n = lax.axis_size(axis)
    return lax.ppermute(value, axis, [(i, i ^ mask) for i in range(n)])


def add(a, b):
    return (a.astype(jnp.float32) + b.astype(jnp.float32)).astype(a.dtype)


def after(value, *others):
    return lax.optimization_barrier((value, *others))[0]


def hidden_kernel(chains, first, last, *refs):
    n = len(chains)
    ins = refs[: 2 * n]
    wg0, wu0, wg1, wu1 = refs[2 * n : 2 * n + 4]
    refs = refs[2 * n + 4 :]
    before = None if first else refs[0]
    refs = refs if first else refs[1:]
    total, part = refs[0], refs[1]
    acc = refs[2] if last else total
    step = pl.program_id(0)
    units = wg0.shape[1]
    f32 = jnp.float32
    at = 0
    for k, c in enumerate(chains):
        _, width, order = CHAINS[c]
        steps = width // PART

        @pl.when((step >= at) & (step < at + steps))
        def _(k=k, order=order):
            for index in range(16):
                to = canon_block(order, index) * UNIT
                row = (index % 8) * UNIT
                part[to : to + UNIT, :] = ins[2 * k + index // 8][row : row + UNIT, :]

        at += steps

    @pl.when(step == 0)
    def _():
        acc[...] = jnp.zeros_like(acc) if first else before[...]

    for i, w in enumerate((wg0, wu0, wg1, wu1)):
        acc[i] += jnp.dot(part[...], w[...], preferred_element_type=f32)

    if last:

        @pl.when(step == at - 1)
        def _():
            for i in range(2):
                gate = acc[2 * i]
                value = gate / (1.0 + jnp.exp(-gate)) * acc[2 * i + 1]
                total[:, i * units : (i + 1) * units] = value.astype(total.dtype)


def out_kernel(order, hidden, wd0, wd1, keep, away):
    units = wd0.shape[0]
    f32 = jnp.float32
    total = jnp.dot(hidden[:, :units], wd0[...], preferred_element_type=f32) + jnp.dot(
        hidden[:, units:], wd1[...], preferred_element_type=f32
    )
    total = total.astype(jnp.bfloat16)
    for index in range(16):
        row = canon_block(order, index) * UNIT
        to = (index % 8) * UNIT
        (keep, away)[index // 8][to : to + UNIT, :] = total[row : row + UNIT]


PART = 1024


def pick(table, i):
    value = table[0]
    for k, entry in enumerate(table[1:], 1):
        value = jnp.where(i >= k, entry, value)
    return value


def hidden_units(pieces, weights, chains, before, last):
    width, units = weights[0].shape
    count = 2 * HALF
    first = before is None
    in_specs, parts = [], []
    for c in chains:
        start, size, _ = CHAINS[c]
        low, steps = len(parts), size // PART
        to = lambda i, low=low, steps=steps: (0, jnp.clip(i - low, 0, steps - 1))
        in_specs += [pl.BlockSpec((HALF, PART), to)] * 2
        parts += [start // PART + k for k in range(steps)]
    whole = lambda *shape: pl.BlockSpec(shape, lambda i: (0,) * len(shape))
    in_specs += [pl.BlockSpec((PART, units), lambda i: (pick(parts, i), 0))] * 4
    sums = (4, count, units)
    if not first:
        in_specs.append(whole(*sums))
    scratch = [pltpu.VMEM((count, PART), jnp.bfloat16)]
    if last:
        out, out_spec = jax.ShapeDtypeStruct((count, 2 * units), jnp.bfloat16), whole(count, 2 * units)
        scratch.append(pltpu.VMEM(sums, jnp.float32))
    else:
        out, out_spec = jax.ShapeDtypeStruct(sums, jnp.float32), whole(*sums)
    depth = len(parts) * PART
    return pl.pallas_call(
        functools.partial(hidden_kernel, chains, first, last),
        grid=(len(parts),),
        out_shape=out,
        in_specs=in_specs,
        out_specs=out_spec,
        scratch_shapes=scratch,
        compiler_params=pltpu.CompilerParams(vmem_limit_bytes=32 << 20),
        cost_estimate=pl.CostEstimate(
            flops=8 * count * depth * units,
            bytes_accessed=8 * depth * units + 2 * count * depth,
            transcendentals=2 * count * units if last else 0,
        ),
        name="hidden",
    )(*pieces, *weights, *(() if first else (before,)))


def expert_out(hidden, wd0, wd1, chain):
    start, size, order = CHAINS[chain]
    units = wd0.shape[0]
    low, count = start // PART, 2 * HALF
    shape = jax.ShapeDtypeStruct((HALF, size), jnp.bfloat16)
    return pl.pallas_call(
        functools.partial(out_kernel, order),
        grid=(size // PART,),
        out_shape=[shape] * 2,
        in_specs=[pl.BlockSpec((count, 2 * units), lambda i: (0, 0))]
        + [pl.BlockSpec((units, PART), lambda i: (0, low + i))] * 2,
        out_specs=[pl.BlockSpec((HALF, PART), lambda i: (0, i))] * 2,
        compiler_params=pltpu.CompilerParams(vmem_limit_bytes=24 << 20),
        cost_estimate=pl.CostEstimate(
            flops=4 * count * size * units,
            bytes_accessed=4 * size * units + 2 * count * size,
            transcendentals=0,
        ),
        name="out",
    )(hidden, wd0, wd1)


def onehot(rows, columns, hit):
    row = lax.broadcasted_iota(jnp.int32, (rows, columns), 0)
    column = lax.broadcasted_iota(jnp.int32, (rows, columns), 1)
    return hit(row, column).astype(jnp.bfloat16)


def place_kernel(routes, weights, tokens, gain, folded, combine):
    f32 = jnp.float32
    count, width = tokens.shape
    half = width // 2
    wide = tokens[...].astype(f32)
    scale = lax.rsqrt(jnp.mean(wide * wide, axis=1, keepdims=True) + 1e-05)
    normed = (wide * scale * gain[...]).astype(jnp.bfloat16)
    rows = folded.shape[0]
    row = lax.broadcasted_iota(jnp.int32, (rows, 2 * count), 0)
    column = lax.broadcasted_iota(jnp.int32, (rows, 2 * count), 1)
    slot = lax.broadcasted_iota(jnp.int32, (2 * count, rows), 1)
    token = lax.broadcasted_iota(jnp.int32, (2 * count, rows), 0)
    picked = jnp.zeros((rows, 2 * count), f32)
    mixing = jnp.zeros((2 * count, rows), f32)
    flat = [routes[t, k] for t in range(count) for k in range(2)]
    for i, expert in enumerate(flat):
        rank = jnp.int32(0)
        for other in flat[:i]:
            rank += (other == expert).astype(jnp.int32)
        at = expert * 8 + rank
        weight = weights[i // 2, i % 2]
        for side in range(2):
            where = at + 4 * side
            of = i // 2 + count * side
            picked = jnp.where((row == where) & (column == of), 1.0, picked)
            mixing = jnp.where((slot == where) & (token == of), weight, mixing)
    picked = picked.astype(jnp.bfloat16)
    combine[...] = mixing
    both = jnp.concatenate([normed[:, :half], normed[:, half:]], axis=0)
    folded[...] = jnp.dot(picked, both, preferred_element_type=f32).astype(folded.dtype)


def unfold_kernel(folded, *outs):
    half = folded.shape[1]
    for side in range(2):
        take = onehot(UNIT, 2 * UNIT, lambda r, c: c == (r // 4) * 8 + r % 4 + 4 * side)
        rows = jnp.dot(take, folded[...], preferred_element_type=jnp.float32)
        for out, (start, size, _) in zip(outs, CHAINS):
            if start // half == side:
                out[...] = rows[:, start - side * half : start - side * half + size].astype(out.dtype)


def fold_kernel(*refs):
    n = len(CHAINS)
    held, came, folded = refs[:n], refs[n : 2 * n], refs[2 * n]
    half = folded.shape[1]
    f32 = jnp.float32
    for c, (start, size, _) in enumerate(CHAINS):
        total = (held[c][...].astype(f32) + came[c][...].astype(f32)).astype(folded.dtype)
        side = start // half
        give = onehot(2 * UNIT, UNIT, lambda r, c: r == (c // 4) * 8 + c % 4 + 4 * side)
        rows = jnp.dot(give, total, preferred_element_type=f32).astype(folded.dtype)
        columns = slice(start - side * half, start - side * half + size)
        if side == 0:
            folded[:, columns] = rows
        else:
            folded[:, columns] = folded[:, columns] + rows


def mix_kernel(tokens, combine, back, out):
    half = back.shape[1]
    count = tokens.shape[0]
    f32 = jnp.float32
    moe = jnp.dot(
        combine[...],
        back[...].astype(f32),
        precision=lax.Precision.HIGHEST,
        preferred_element_type=f32,
    )
    for side in range(2):
        columns = slice(side * half, side * half + half)
        total = tokens[:, columns].astype(f32) + moe[side * count : side * count + count]
        out[:, columns] = total.astype(out.dtype)


def small(kernel, out_shape, *args, scalars=0, name):
    vmem, smem = pl.BlockSpec(memory_space=pltpu.VMEM), pl.BlockSpec(memory_space=pltpu.SMEM)
    return pl.pallas_call(
        kernel,
        out_shape=out_shape,
        in_specs=[smem] * scalars + [vmem] * (len(args) - scalars),
        out_specs=jax.tree.map(lambda _: vmem, out_shape),
        compiler_params=pltpu.CompilerParams(vmem_limit_bytes=16 << 20),
        name=name,
    )(*args)


def swap_experts(folded):
    blocks = folded.reshape(8, 8, folded.shape[1])
    blocks = lax.all_to_all(blocks, ("zl", "y"), split_axis=0, concat_axis=0, tiled=True)
    return blocks.reshape(folded.shape)


def per_device(tokens, norm_gain, routes, route_weights, w_gate, w_up, w_down):
    bf16 = jnp.bfloat16
    count, width = tokens.shape
    wg0, wu0, wd0 = w_gate[0], w_up[0], w_down[0]
    wg1, wu1, wd1 = (trade(w, "c") for w in (wg0, wu0, wd0))

    folded_shape = jax.ShapeDtypeStruct((64, width // 2), bf16)
    folded, combine = small(
        place_kernel,
        [folded_shape, jax.ShapeDtypeStruct((2 * count, 64), jnp.float32)],
        routes,
        route_weights,
        tokens,
        norm_gain.reshape(1, width),
        scalars=2,
        name="place",
    )
    folded = swap_experts(folded)
    folded, wg1, wu1, wd1 = lax.optimization_barrier((folded, wg1, wu1, wd1))
    heads = [jax.ShapeDtypeStruct((UNIT, size), bf16) for _, size, _ in CHAINS]
    held = list(small(unfold_kernel, heads, folded, name="unfold"))

    last = None
    for step in range(4):
        came = [trade(h, order[step]) for h, (_, _, order) in zip(held, CHAINS)]
        if step == 3:
            break
        for j in (2, 3, 0, 1):
            if last is not None:
                came[j] = after(came[j], last)
            held[j] = last = jnp.concatenate([held[j], came[j]], axis=0)
    for j in (2, 3, 0, 1):
        came[j] = last = after(came[j], last)
    pieces = [piece for pair in zip(held, came) for piece in pair]
    hidden = hidden_units(pieces, (wg0, wu0, wg1, wu1), (0, 1, 2, 3), None, True)

    held, away = [None] * 4, [None] * 4
    for j in range(4):
        held[j], away[j] = expert_out(hidden if j == 0 else after(hidden, away[j - 1]), wd0, wd1, j)
    last = None
    for step in (3, 2, 1, 0):
        came = [trade(a, order[step]) for a, (_, _, order) in zip(away, CHAINS)]
        if not step:
            break
        half = held[0].shape[0] // 2
        for j in range(4):
            got = came[j] if last is None else after(came[j], last)
            away[j] = last = add(held[j][half:], got[half:])
            held[j] = add(held[j][:half], got[:half])

    folded = small(fold_kernel, folded_shape, *held, *came, name="fold")
    back = swap_experts(folded)
    out = jax.ShapeDtypeStruct(tokens.shape, bf16)
    return small(mix_kernel, out, tokens, combine, back, name="mix")


def solution(mesh):
    fine = Mesh(mesh.devices.reshape(4, 2, 4, 4, 2), AXES)
    rows = P(AXES, None)
    return jax.shard_map(
        per_device,
        mesh=fine,
        in_specs=(
            rows,
            P(),
            rows,
            rows,
            P(("zl", "y"), None, ("dp", "x", "c")),
            P(("zl", "y"), None, ("dp", "x", "c")),
            P(("zl", "y"), ("dp", "x", "c"), None),
        ),
        out_specs=rows,
        check_vma=False,
    )
```

time: 191 us -> 182 us (0.953)
  waiting for transfers between devices: 99.8 us -> 61.3 us
  blocking collectives: 0 us -> 32 us
  Pallas kernels: 13.9 us -> 17.9 us
  other arithmetic: 4.78 us -> 1.7 us
  matrix products: 2.13 us -> 0 us
  local copies, waits for them, and re-layouts: 1.58 us -> 3.55 us
    ppermute x43 -> x35, waiting for transfers between devices: 99.8 us -> 61.3 us  [trade(): return lax.ppermute(value, axis, [(i, i ^ mask) for i in range(n)])]
    all_to_all x0 -> x2, blocking collectives: none -> 32 us  [swap_experts(): lax.all_to_all(blocks, ('zl', 'y'), split_axis=0, concat_axis=0, tiled=True)]
    pallas_call x1 -> x5, Pallas kernels: 9 us -> 13 us  [the longest x1 10.2 us: hidden_units(): pl.pallas_call(functools.partial(hidden_kernel, chains, first, last), gri...]
    unnamed x12 -> x23, local copies, waits for them, and re-layouts: 0.8 us -> 3.4 us
    dot_general x2 -> x0, matrix products: 2.13 us -> none  [the longest x1 1.21 us: per_device(): jnp.dot(picked, normed, preferred_element_type=f32).astype(jnp.bfloat16)]
    reduce_sum x3 -> x0, other arithmetic: 2 us -> none  [the longest x1 1.06 us: per_device(): scale = lax.rsqrt(jnp.mean(wide * wide, axis=1, keepdims=True) + 1e-05)]
    ppermute x43 -> x35, starting transfers between devices: 66.4 us -> 64.8 us  [trade(): return lax.ppermute(value, axis, [(i, i ^ mask) for i in range(n)])]
  transfers between devices with their start and end apart: 43 -> 35, of which waited for: 21 -> 16; matrix products, arithmetic and copies ran while one was open for 4% -> 2% of each run, Pallas kernels for 2% -> 2%
where the time goes in v4:
time: 182 us
  starting transfers between devices  64.8 us (36%)
  waiting for transfers between devices  61.3 us (34%)
  blocking collectives  32 us (18%)
  Pallas kernels  17.9 us (10%)
  local copies, waits for them, and re-layouts  3.55 us (2%)
    ppermute x35, starting transfers between devices, trade(): return lax.ppermute(value, axis, [(i, i ^ mask) for i in range(n)])  64.8 us
    ppermute x35, waiting for transfers between devices, trade(): return lax.ppermute(value, axis, [(i, i ^ mask) for i in range(n)])  61.3 us
    all_to_all x2, blocking collectives, swap_experts(): lax.all_to_all(blocks, ('zl', 'y'), split_axis=0, concat_axis=0, tiled=True)  32 us
    pallas_call x1, Pallas kernels, hidden_units(): pl.pallas_call(functools.partial(hidden_kernel, chains, first, last), gri...  10.2 us
    pallas_call x4, Pallas kernels, expert_out(): pl.pallas_call(functools.partial(out_kernel, order), grid=(size // PART,)...  4.88 us
  transfers between devices with their start and end apart: 35, of which 16 were waited for; matrix products, arithmetic and copies ran while one was open for 2% of the time, Pallas kernels for 2%

profile of v4, /device:TPU:2, one launch (start us, length us, event | category | flops | bytes accessed | tf_op | source)
XLA Modules:
  0.0 181.6 jit_solution(5406668394865058796)
XLA Ops:
  4.8 15.0 %all_to_all.10 = bf16[8,8,3072]{2,1,0:T(8,128)(2,1)S(1)} all-to-all(bf16[8,8,3072]{2,1,0:T(8,128)(2,1)S(1)} %bitcast.16), channel_id=1, replica_groups=mesh['dp'=4,'zl'=2,'y'=4,'x'=4,'c'=2] {'zl','y'}, dimensions={0} | all-to-all | bytes 786432 | tf_op jit(solution)/shard_map/all_to_all | solution.py:268
  20.0 3.4 %collective-permute-start.3 = (bf16[32,2048]{1,0:T(8,128)(2,1)S(1)}, bf16[32,2048]{1,0:T(8,128)(2,1)S(1)}, u32[]{:S(2)}, u32[]{:S(2)}) collective-permute-start(bf16[32,2048]{1,0:T(8,128)(2,1)S(1)} %get-tuple-element.55), channel_id=1, source_target_pairs={{0,64},{64,0},{128,192},{192,128},{1,65},{65,1},{129,193},{193,129... | collective-permute-start | bytes 393224 | tf_op jit(solution)/shard_map/ppermute | solution.py:34
  23.4 3.6 %collective-permute-start.9 = (bf16[32,2048]{1,0:T(8,128)(2,1)S(1)}, bf16[32,2048]{1,0:T(8,128)(2,1)S(1)}, u32[]{:S(2)}, u32[]{:S(2)}) collective-permute-start(bf16[32,2048]{1,0:T(8,128)(2,1)S(1)} %get-tuple-element.60), channel_id=1, source_target_pairs={{0,192},{64,128},{128,64},{192,0},{1,193},{65,129},{129,65},{193,1... | collective-permute-start | bytes 393224 | tf_op jit(solution)/shard_map/ppermute | solution.py:34
  30.4 2.5 %collective-permute-done.5 = bf16[32,1024]{1,0:T(8,128)(2,1)S(1)} collective-permute-done((bf16[32,1024]{1,0:T(8,128)(2,1)S(1)}, bf16[32,1024]{1,0:T(8,128)(2,1)S(1)}, u32[]{:S(2)}, u32[]{:S(2)}) %collective-permute-start.5) | collective-permute-done | bytes 65568 | tf_op jit(solution)/shard_map/ppermute | solution.py:34
  38.0 3.3 %collective-permute-start.12 = (bf16[128,1024]{1,0:T(8,128)(2,1)S(1)}, bf16[128,1024]{1,0:T(8,128)(2,1)S(1)}, u32[]{:S(2)}, u32[]{:S(2)}) collective-permute-start(bf16[128,1024]{1,0:T(8,128)(2,1)S(1)} %get-tuple-element.134), channel_id=1, source_target_pairs={{0,192},{64,128},{128,64},{192,0},{1,193},{65,129},{129,65},{193,1... | collective-permute-start | bytes 786440 | tf_op jit(solution)/shard_map/ppermute | solution.py:34
  42.9 7.6 %collective-permute-done.6 = bf16[64,2048]{1,0:T(8,128)(2,1)S(1)} collective-permute-done((bf16[64,2048]{1,0:T(8,128)(2,1)S(1)}, bf16[64,2048]{1,0:T(8,128)(2,1)S(1)}, u32[]{:S(2)}, u32[]{:S(2)}) %collective-permute-start.6) | collective-permute-done | bytes 262176 | tf_op jit(solution)/shard_map/ppermute | solution.py:34
  50.6 3.9 %collective-permute-start.10 = (bf16[128,2048]{1,0:T(8,128)(2,1)S(1)}, bf16[128,2048]{1,0:T(8,128)(2,1)S(1)}, u32[]{:S(2)}, u32[]{:S(2)}) collective-permute-start(bf16[128,2048]{1,0:T(8,128)(2,1)S(1)} %get-tuple-element.125), channel_id=1, source_target_pairs={{0,6},{2,4},{4,2},{6,0},{1,7},{3,5},{5,3},{7,1},{8,14},{10,12},{12... | collective-permute-start | bytes 1572872 | tf_op jit(solution)/shard_map/ppermute | solution.py:34
  55.5 2.7 %collective-permute-done.11 = bf16[128,1024]{1,0:T(8,128)(2,1)S(1)} collective-permute-done((bf16[128,1024]{1,0:T(8,128)(2,1)S(1)}, bf16[128,1024]{1,0:T(8,128)(2,1)S(1)}, u32[]{:S(2)}, u32[]{:S(2)}) %collective-permute-start.11) | collective-permute-done | bytes 262176 | tf_op jit(solution)/shard_map/ppermute | solution.py:34
  58.2 4.9 %collective-permute-done.10 = bf16[128,2048]{1,0:T(8,128)(2,1)S(1)} collective-permute-done((bf16[128,2048]{1,0:T(8,128)(2,1)S(1)}, bf16[128,2048]{1,0:T(8,128)(2,1)S(1)}, u32[]{:S(2)}, u32[]{:S(2)}) %collective-permute-start.10) | collective-permute-done | bytes 524320 | tf_op jit(solution)/shard_map/ppermute | solution.py:34
  63.1 5.8 %collective-permute-start.14 = (bf16[256,2048]{1,0:T(8,128)(2,1)S(1)}, bf16[256,2048]{1,0:T(8,128)(2,1)S(1)}, u32[]{:S(2)}, u32[]{:S(2)}) collective-permute-start(bf16[256,2048]{1,0:T(8,128)(2,1)S(1)} %constant_dynamic-update-slice_fusion.28.refs_0_), channel_id=1, source_target_pairs={{0,2},{2,0},{4,6},{6,4},{1,3},{3,1},{5,7},{7,5},{8,10},{10,8},{12,... | collective-permute-start | bytes 3145736 | tf_op jit(solution)/shard_map/ppermute | solution.py:34
  73.5 11.3 %collective-permute-done.16.refs_5_ = bf16[256,1024]{1,0:T(8,128)(2,1)S(1)} collective-permute-done((bf16[256,1024]{1,0:T(8,128)(2,1)S(1)}, bf16[256,1024]{1,0:T(8,128)(2,1)S(1)}, u32[]{:S(2)}, u32[]{:S(2)}) %collective-permute-start.16) | collective-permute-done | bytes 524320 | tf_op jit(solution)/shard_map/ppermute | solution.py:34
  84.9 3.8 %collective-permute-done.15.refs_7_ = bf16[256,1024]{1,0:T(8,128)(2,1)S(1)} collective-permute-done((bf16[256,1024]{1,0:T(8,128)(2,1)S(1)}, bf16[256,1024]{1,0:T(8,128)(2,1)S(1)}, u32[]{:S(2)}, u32[]{:S(2)}) %collective-permute-start.15) | collective-permute-done | bytes 524320 | tf_op jit(solution)/shard_map/ppermute | solution.py:34
  88.7 10.2 %hidden.1 = bf16[512,512]{1,0:T(8,128)(2,1)S(1)} custom-call(bf16[256,2048]{1,0:T(8,128)(2,1)S(1)} %constant_dynamic-update-slice_fusion.28.refs_0_, bf16[256,2048]{1,0:T(8,128)(2,1)S(1)} %collective-permute-done.14.refs_1_, bf16[256,2048]{1,0:T(8,128)(2,1)S(1)} %constant_dynamic-update-slice_fusion.32.refs_2_, ...), custom_call_target="tpu_custom_call" | custom-call | flops 6442450944 | bytes 18874368 | tf_op jit(solution)/shard_map/hidden/pallas_call | solution.py:134
  102.5 2.6 %collective-permute-start.23 = (bf16[256,2048]{1,0:T(8,128)(2,1)S(1)}, bf16[256,2048]{1,0:T(8,128)(2,1)S(1)}, u32[]{:S(2)}, u32[]{:S(2)}) collective-permute-start(bf16[256,2048]{1,0:T(8,128)(2,1)S(1)} %get-tuple-element.80), channel_id=1, source_target_pairs={{0,6},{2,4},{4,2},{6,0},{1,7},{3,5},{5,3},{7,1},{8,14},{10,12},{12... | collective-permute-start | bytes 3145736 | tf_op jit(solution)/shard_map/ppermute | solution.py:34
  108.3 4.7 %collective-permute-start.21 = (bf16[256,1024]{1,0:T(8,128)(2,1)S(1)}, bf16[256,1024]{1,0:T(8,128)(2,1)S(1)}, u32[]{:S(2)}, u32[]{:S(2)}) collective-permute-start(bf16[256,1024]{1,0:T(8,128)(2,1)S(1)} %get-tuple-element.85), channel_id=1, source_target_pairs={{0,192},{64,128},{128,64},{192,0},{1,193},{65,129},{129,65},{193,1... | collective-permute-start | bytes 1572872 | tf_op jit(solution)/shard_map/ppermute | solution.py:34
  113.0 9.6 %collective-permute-done.19 = bf16[256,2048]{1,0:T(8,128)(2,1)S(1)} collective-permute-done((bf16[256,2048]{1,0:T(8,128)(2,1)S(1)}, bf16[256,2048]{1,0:T(8,128)(2,1)S(1)}, u32[]{:S(2)}, u32[]{:S(2)}) %collective-permute-start.19) | collective-permute-done | bytes 1048608 | tf_op jit(solution)/shard_map/ppermute | solution.py:34
  123.5 4.6 %collective-permute-done.23 = bf16[256,2048]{1,0:T(8,128)(2,1)S(1)} collective-permute-done((bf16[256,2048]{1,0:T(8,128)(2,1)S(1)}, bf16[256,2048]{1,0:T(8,128)(2,1)S(1)}, u32[]{:S(2)}, u32[]{:S(2)}) %collective-permute-start.23) | collective-permute-done | bytes 1048608 | tf_op jit(solution)/shard_map/ppermute | solution.py:34
  128.5 3.4 %collective-permute-start.27 = (bf16[128,2048]{1,0:T(8,128)(2,1)S(1)}, bf16[128,2048]{1,0:T(8,128)(2,1)S(1)}, u32[]{:S(2)}, u32[]{:S(2)}) collective-permute-start(bf16[128,2048]{1,0:T(8,128)(2,1)S(1)} %get-tuple-element.100), channel_id=1, source_target_pairs={{0,2},{2,0},{4,6},{6,4},{1,3},{3,1},{5,7},{7,5},{8,10},{10,8},{12,... | collective-permute-start | bytes 1572872 | tf_op jit(solution)/shard_map/ppermute | solution.py:34
  135.9 5.2 %collective-permute-start.24 = (bf16[64,2048]{1,0:T(8,128)(2,1)S(1)}, bf16[64,2048]{1,0:T(8,128)(2,1)S(1)}, u32[]{:S(2)}, u32[]{:S(2)}) collective-permute-start(bf16[64,2048]{1,0:T(8,128)(2,1)S(1)} %get-tuple-element.109), channel_id=1, source_target_pairs={{0,192},{64,128},{128,64},{192,0},{1,193},{65,129},{129,65},{193,1... | collective-permute-start | bytes 786440 | tf_op jit(solution)/shard_map/ppermute | solution.py:34
  141.2 3.0 %collective-permute-start.28 = (bf16[64,2048]{1,0:T(8,128)(2,1)S(1)}, bf16[64,2048]{1,0:T(8,128)(2,1)S(1)}, u32[]{:S(2)}, u32[]{:S(2)}) collective-permute-start(bf16[64,2048]{1,0:T(8,128)(2,1)S(1)} %get-tuple-element.104), channel_id=1, source_target_pairs={{0,64},{64,0},{128,192},{192,128},{1,65},{65,1},{129,193},{193,129... | collective-permute-start | bytes 786440 | tf_op jit(solution)/shard_map/ppermute | solution.py:34
  144.2 5.7 %collective-permute-done.26 = bf16[128,1024]{1,0:T(8,128)(2,1)S(1)} collective-permute-done((bf16[128,1024]{1,0:T(8,128)(2,1)S(1)}, bf16[128,1024]{1,0:T(8,128)(2,1)S(1)}, u32[]{:S(2)}, u32[]{:S(2)}) %collective-permute-start.26) | collective-permute-done | bytes 262176 | tf_op jit(solution)/shard_map/ppermute | solution.py:34
  154.4 4.2 %collective-permute-start.32 = (bf16[32,2048]{1,0:T(8,128)(2,1)S(1)}, bf16[32,2048]{1,0:T(8,128)(2,1)S(1)}, u32[]{:S(2)}, u32[]{:S(2)}) collective-permute-start(bf16[32,2048]{1,0:T(8,128)(2,1)S(1)} %get-tuple-element.113), channel_id=1, source_target_pairs={{0,192},{64,128},{128,64},{192,0},{1,193},{65,129},{129,65},{193,1... | collective-permute-start | bytes 393224 | tf_op jit(solution)/shard_map/ppermute | solution.py:34
  159.2 3.8 %collective-permute-done.34.refs_7_ = bf16[32,1024]{1,0:T(8,128)(2,1)S(1)} collective-permute-done((bf16[32,1024]{1,0:T(8,128)(2,1)S(1)}, bf16[32,1024]{1,0:T(8,128)(2,1)S(1)}, u32[]{:S(2)}, u32[]{:S(2)}) %collective-permute-start.34) | collective-permute-done | bytes 65568 | tf_op jit(solution)/shard_map/ppermute | solution.py:34
  163.5 17.0 %all_to_all.11 = bf16[8,8,3072]{2,1,0:T(8,128)(2,1)S(1)} all-to-all(bf16[8,8,3072]{2,1,0:T(8,128)(2,1)S(1)} %bitcast.15), channel_id=1, replica_groups=mesh['dp'=4,'zl'=2,'y'=4,'x'=4,'c'=2] {'zl','y'}, dimensions={0} | all-to-all | bytes 786432 | tf_op jit(solution)/shard_map/all_to_all | solution.py:268
  (97 shorter events, 39.7 us)
Async XLA Ops:
  0.0 19.7 %collective-permute-start = (bf16[6144,256]{1,0:T(8,128)(2,1)}, bf16[6144,256]{1,0:T(8,128)(2,1)}, u32[]{:S(2)}, u32[]{:S(2)}) collective-permute-start(bf16[6144,256]{1,0:T(8,128)(2,1)} %bitcast.18), channel_id=1, source_target_pairs={{0,1},{1,0},{2,3},{3,2},{4,5},{5,4},{6,7},{7,6},{8,9},{9,8},{10,11... | collective-permute-start | bytes 9437192 | tf_op jit(solution)/shard_map/ppermute | solution.py:34
  0.0 19.7 %collective-permute-start.1 = (bf16[6144,256]{1,0:T(8,128)(2,1)}, bf16[6144,256]{1,0:T(8,128)(2,1)}, u32[]{:S(2)}, u32[]{:S(2)}) collective-permute-start(bf16[6144,256]{1,0:T(8,128)(2,1)} %bitcast.20), channel_id=1, source_target_pairs={{0,1},{1,0},{2,3},{3,2},{4,5},{5,4},{6,7},{7,6},{8,9},{9,8},{10,11... | collective-permute-start | bytes 9437192 | tf_op jit(solution)/shard_map/ppermute | solution.py:34
  0.5 19.2 %collective-permute-start.2 = (bf16[256,6144]{1,0:T(8,128)(2,1)}, bf16[256,6144]{1,0:T(8,128)(2,1)S(1)}, u32[]{:S(2)}, u32[]{:S(2)}) collective-permute-start(bf16[256,6144]{1,0:T(8,128)(2,1)} %bitcast.8), channel_id=1, source_target_pairs={{0,1},{1,0},{2,3},{3,2},{4,5},{5,4},{6,7},{7,6},{8,9},{9,8},{10,11... | collective-permute-start | bytes 9437192 | tf_op jit(solution)/shard_map/ppermute | solution.py:34
  20.0 15.3 %collective-permute-start.3 = (bf16[32,2048]{1,0:T(8,128)(2,1)S(1)}, bf16[32,2048]{1,0:T(8,128)(2,1)S(1)}, u32[]{:S(2)}, u32[]{:S(2)}) collective-permute-start(bf16[32,2048]{1,0:T(8,128)(2,1)S(1)} %get-tuple-element.55), channel_id=1, source_target_pairs={{0,64},{64,0},{128,192},{192,128},{1,65},{65,1},{129,193},{193,129... | collective-permute-start | bytes 393224 | tf_op jit(solution)/shard_map/ppermute | solution.py:34
  23.4 12.7 %collective-permute-start.9 = (bf16[32,2048]{1,0:T(8,128)(2,1)S(1)}, bf16[32,2048]{1,0:T(8,128)(2,1)S(1)}, u32[]{:S(2)}, u32[]{:S(2)}) collective-permute-start(bf16[32,2048]{1,0:T(8,128)(2,1)S(1)} %get-tuple-element.60), channel_id=1, source_target_pairs={{0,192},{64,128},{128,64},{192,0},{1,193},{65,129},{129,65},{193,1... | collective-permute-start | bytes 393224 | tf_op jit(solution)/shard_map/ppermute | solution.py:34
  35.4 15.1 %collective-permute-start.6 = (bf16[64,2048]{1,0:T(8,128)(2,1)S(1)}, bf16[64,2048]{1,0:T(8,128)(2,1)S(1)}, u32[]{:S(2)}, u32[]{:S(2)}) collective-permute-start(bf16[64,2048]{1,0:T(8,128)(2,1)S(1)} %get-tuple-element.139), channel_id=1, source_target_pairs={{0,192},{64,128},{128,64},{192,0},{1,193},{65,129},{129,65},{193,1... | collective-permute-start | bytes 786440 | tf_op jit(solution)/shard_map/ppermute | solution.py:34
  36.1 18.4 %collective-permute-start.13 = (bf16[64,2048]{1,0:T(8,128)(2,1)S(1)}, bf16[64,2048]{1,0:T(8,128)(2,1)S(1)}, u32[]{:S(2)}, u32[]{:S(2)}) collective-permute-start(bf16[64,2048]{1,0:T(8,128)(2,1)S(1)} %get-tuple-element.129), channel_id=1, source_target_pairs={{0,64},{64,0},{128,192},{192,128},{1,65},{65,1},{129,193},{193,129... | collective-permute-start | bytes 786440 | tf_op jit(solution)/shard_map/ppermute | solution.py:34
  38.0 17.5 %collective-permute-start.12 = (bf16[128,1024]{1,0:T(8,128)(2,1)S(1)}, bf16[128,1024]{1,0:T(8,128)(2,1)S(1)}, u32[]{:S(2)}, u32[]{:S(2)}) collective-permute-start(bf16[128,1024]{1,0:T(8,128)(2,1)S(1)} %get-tuple-element.134), channel_id=1, source_target_pairs={{0,192},{64,128},{128,64},{192,0},{1,193},{65,129},{129,65},{193,1... | collective-permute-start | bytes 786440 | tf_op jit(solution)/shard_map/ppermute | solution.py:34
  41.4 16.9 %collective-permute-start.11 = (bf16[128,1024]{1,0:T(8,128)(2,1)S(1)}, bf16[128,1024]{1,0:T(8,128)(2,1)S(1)}, u32[]{:S(2)}, u32[]{:S(2)}) collective-permute-start(bf16[128,1024]{1,0:T(8,128)(2,1)S(1)} %get-tuple-element.136), channel_id=1, source_target_pairs={{0,64},{64,0},{128,192},{192,128},{1,65},{65,1},{129,193},{193,129... | collective-permute-start | bytes 786440 | tf_op jit(solution)/shard_map/ppermute | solution.py:34
  54.5 14.9 %collective-permute-start.17 = (bf16[128,2048]{1,0:T(8,128)(2,1)S(1)}, bf16[128,2048]{1,0:T(8,128)(2,1)S(1)}, u32[]{:S(2)}, u32[]{:S(2)}) collective-permute-start(bf16[128,2048]{1,0:T(8,128)(2,1)S(1)} %get-tuple-element.124), channel_id=1, source_target_pairs={{0,2},{2,0},{4,6},{6,4},{1,3},{3,1},{5,7},{7,5},{8,10},{10,8},{12,... | collective-permute-start | bytes 1572872 | tf_op jit(solution)/shard_map/ppermute | solution.py:34
  63.1 25.6 %collective-permute-start.14 = (bf16[256,2048]{1,0:T(8,128)(2,1)S(1)}, bf16[256,2048]{1,0:T(8,128)(2,1)S(1)}, u32[]{:S(2)}, u32[]{:S(2)}) collective-permute-start(bf16[256,2048]{1,0:T(8,128)(2,1)S(1)} %constant_dynamic-update-slice_fusion.28.refs_0_), channel_id=1, source_target_pairs={{0,2},{2,0},{4,6},{6,4},{1,3},{3,1},{5,7},{7,5},{8,10},{10,8},{12,... | collective-permute-start | bytes 3145736 | tf_op jit(solution)/shard_map/ppermute | solution.py:34
  69.4 19.3 %collective-permute-start.18 = (bf16[256,2048]{1,0:T(8,128)(2,1)S(1)}, bf16[256,2048]{1,0:T(8,128)(2,1)S(1)}, u32[]{:S(2)}, u32[]{:S(2)}) collective-permute-start(bf16[256,2048]{1,0:T(8,128)(2,1)S(1)} %constant_dynamic-update-slice_fusion.32.refs_2_), channel_id=1, source_target_pairs={{0,6},{2,4},{4,2},{6,0},{1,7},{3,5},{5,3},{7,1},{8,14},{10,12},{12... | collective-permute-start | bytes 3145736 | tf_op jit(solution)/shard_map/ppermute | solution.py:34
  69.5 15.3 %collective-permute-start.16 = (bf16[256,1024]{1,0:T(8,128)(2,1)S(1)}, bf16[256,1024]{1,0:T(8,128)(2,1)S(1)}, u32[]{:S(2)}, u32[]{:S(2)}) collective-permute-start(bf16[256,1024]{1,0:T(8,128)(2,1)S(1)} %constant_dynamic-update-slice_fusion.20.refs_4_), channel_id=1, source_target_pairs={{0,64},{64,0},{128,192},{192,128},{1,65},{65,1},{129,193},{193,129... | collective-permute-start | bytes 1572872 | tf_op jit(solution)/shard_map/ppermute | solution.py:34
  71.7 17.0 %collective-permute-start.15 = (bf16[256,1024]{1,0:T(8,128)(2,1)S(1)}, bf16[256,1024]{1,0:T(8,128)(2,1)S(1)}, u32[]{:S(2)}, u32[]{:S(2)}) collective-permute-start(bf16[256,1024]{1,0:T(8,128)(2,1)S(1)} %constant_dynamic-update-slice_fusion.24.refs_6_), channel_id=1, source_target_pairs={{0,192},{64,128},{128,64},{192,0},{1,193},{65,129},{129,65},{193,1... | collective-permute-start | bytes 1572872 | tf_op jit(solution)/shard_map/ppermute | solution.py:34
  100.7 21.8 %collective-permute-start.19 = (bf16[256,2048]{1,0:T(8,128)(2,1)S(1)}, bf16[256,2048]{1,0:T(8,128)(2,1)S(1)}, u32[]{:S(2)}, u32[]{:S(2)}) collective-permute-start(bf16[256,2048]{1,0:T(8,128)(2,1)S(1)} %get-tuple-element.78), channel_id=1, source_target_pairs={{0,2},{2,0},{4,6},{6,4},{1,3},{3,1},{5,7},{7,5},{8,10},{10,8},{12,... | collective-permute-start | bytes 3145736 | tf_op jit(solution)/shard_map/ppermute | solution.py:34
  102.5 25.5 %collective-permute-start.23 = (bf16[256,2048]{1,0:T(8,128)(2,1)S(1)}, bf16[256,2048]{1,0:T(8,128)(2,1)S(1)}, u32[]{:S(2)}, u32[]{:S(2)}) collective-permute-start(bf16[256,2048]{1,0:T(8,128)(2,1)S(1)} %get-tuple-element.80), channel_id=1, source_target_pairs={{0,6},{2,4},{4,2},{6,0},{1,7},{3,5},{5,3},{7,1},{8,14},{10,12},{12... | collective-permute-start | bytes 3145736 | tf_op jit(solution)/shard_map/ppermute | solution.py:34
  105.8 26.1 %collective-permute-start.22 = (bf16[256,1024]{1,0:T(8,128)(2,1)S(1)}, bf16[256,1024]{1,0:T(8,128)(2,1)S(1)}, u32[]{:S(2)}, u32[]{:S(2)}) collective-permute-start(bf16[256,1024]{1,0:T(8,128)(2,1)S(1)} %get-tuple-element.82), channel_id=1, source_target_pairs={{0,64},{64,0},{128,192},{192,128},{1,65},{65,1},{129,193},{193,129... | collective-permute-start | bytes 1572872 | tf_op jit(solution)/shard_map/ppermute | solution.py:34
  108.3 25.0 %collective-permute-start.21 = (bf16[256,1024]{1,0:T(8,128)(2,1)S(1)}, bf16[256,1024]{1,0:T(8,128)(2,1)S(1)}, u32[]{:S(2)}, u32[]{:S(2)}) collective-permute-start(bf16[256,1024]{1,0:T(8,128)(2,1)S(1)} %get-tuple-element.85), channel_id=1, source_target_pairs={{0,192},{64,128},{128,64},{192,0},{1,193},{65,129},{129,65},{193,1... | collective-permute-start | bytes 1572872 | tf_op jit(solution)/shard_map/ppermute | solution.py:34
  122.9 12.8 %collective-permute-start.20 = (bf16[128,2048]{1,0:T(8,128)(2,1)S(1)}, bf16[128,2048]{1,0:T(8,128)(2,1)S(1)}, u32[]{:S(2)}, u32[]{:S(2)}) collective-permute-start(bf16[128,2048]{1,0:T(8,128)(2,1)S(1)} %get-tuple-element.101), channel_id=1, source_target_pairs={{0,6},{2,4},{4,2},{6,0},{1,7},{3,5},{5,3},{7,1},{8,14},{10,12},{12... | collective-permute-start | bytes 1572872 | tf_op jit(solution)/shard_map/ppermute | solution.py:34
  128.5 12.6 %collective-permute-start.27 = (bf16[128,2048]{1,0:T(8,128)(2,1)S(1)}, bf16[128,2048]{1,0:T(8,128)(2,1)S(1)}, u32[]{:S(2)}, u32[]{:S(2)}) collective-permute-start(bf16[128,2048]{1,0:T(8,128)(2,1)S(1)} %get-tuple-element.100), channel_id=1, source_target_pairs={{0,2},{2,0},{4,6},{6,4},{1,3},{3,1},{5,7},{7,5},{8,10},{10,8},{12,... | collective-permute-start | bytes 1572872 | tf_op jit(solution)/shard_map/ppermute | solution.py:34
  132.1 17.7 %collective-permute-start.26 = (bf16[128,1024]{1,0:T(8,128)(2,1)S(1)}, bf16[128,1024]{1,0:T(8,128)(2,1)S(1)}, u32[]{:S(2)}, u32[]{:S(2)}) collective-permute-start(bf16[128,1024]{1,0:T(8,128)(2,1)S(1)} %get-tuple-element.106), channel_id=1, source_target_pairs={{0,192},{64,128},{128,64},{192,0},{1,193},{65,129},{129,65},{193,1... | collective-permute-start | bytes 786440 | tf_op jit(solution)/shard_map/ppermute | solution.py:34
  133.4 18.2 %collective-permute-start.25 = (bf16[128,1024]{1,0:T(8,128)(2,1)S(1)}, bf16[128,1024]{1,0:T(8,128)(2,1)S(1)}, u32[]{:S(2)}, u32[]{:S(2)}) collective-permute-start(bf16[128,1024]{1,0:T(8,128)(2,1)S(1)} %get-tuple-element.108), channel_id=1, source_target_pairs={{0,64},{64,0},{128,192},{192,128},{1,65},{65,1},{129,193},{193,129... | collective-permute-start | bytes 786440 | tf_op jit(solution)/shard_map/ppermute | solution.py:34
  135.9 18.1 %collective-permute-start.24 = (bf16[64,2048]{1,0:T(8,128)(2,1)S(1)}, bf16[64,2048]{1,0:T(8,128)(2,1)S(1)}, u32[]{:S(2)}, u32[]{:S(2)}) collective-permute-start(bf16[64,2048]{1,0:T(8,128)(2,1)S(1)} %get-tuple-element.109), channel_id=1, source_target_pairs={{0,192},{64,128},{128,64},{192,0},{1,193},{65,129},{129,65},{193,1... | collective-permute-start | bytes 786440 | tf_op jit(solution)/shard_map/ppermute | solution.py:34
  141.2 13.1 %collective-permute-start.28 = (bf16[64,2048]{1,0:T(8,128)(2,1)S(1)}, bf16[64,2048]{1,0:T(8,128)(2,1)S(1)}, u32[]{:S(2)}, u32[]{:S(2)}) collective-permute-start(bf16[64,2048]{1,0:T(8,128)(2,1)S(1)} %get-tuple-element.104), channel_id=1, source_target_pairs={{0,64},{64,0},{128,192},{192,128},{1,65},{65,1},{129,193},{193,129... | collective-permute-start | bytes 786440 | tf_op jit(solution)/shard_map/ppermute | solution.py:34
  (17 other events, 255.5 us)

commit v5 on v4

--- a/solution.py
+++ b/solution.py
@@ -190,13 +190,13 @@
     token = lax.broadcasted_iota(jnp.int32, (2 * count, rows), 0)
     picked = jnp.zeros((rows, 2 * count), f32)
     mixing = jnp.zeros((2 * count, rows), f32)
-    flat = [routes[t, k] for t in range(count) for k in range(2)]
+    flat = [routes[k, t] for t in range(count) for k in range(2)]
     for i, expert in enumerate(flat):
         rank = jnp.int32(0)
         for other in flat[:i]:
             rank += (other == expert).astype(jnp.int32)
         at = expert * 8 + rank
-        weight = weights[i // 2, i % 2]
+        weight = weights[i % 2, i // 2]
         for side in range(2):
             where = at + 4 * side
             of = i // 2 + count * side
@@ -279,8 +279,8 @@
     folded, combine = small(
         place_kernel,
         [folded_shape, jax.ShapeDtypeStruct((2 * count, 64), jnp.float32)],
-        routes,
-        route_weights,
+        routes.T,
+        route_weights.T,
         tokens,
         norm_gain.reshape(1, width),
         scalars=2,
@@ -296,7 +296,7 @@
         came = [trade(h, order[step]) for h, (_, _, order) in zip(held, CHAINS)]
         if step == 3:
             break
-        for j in (2, 3, 0, 1):
+        for j in (0, 1, 2, 3) if step == 1 else (2, 3, 0, 1):
             if last is not None:
                 came[j] = after(came[j], last)
             held[j] = last = jnp.concatenate([held[j], came[j]], axis=0)
@@ -306,15 +306,17 @@
     hidden = hidden_units(pieces, (wg0, wu0, wg1, wu1), (0, 1, 2, 3), None, True)
 
     held, away = [None] * 4, [None] * 4
-    for j in range(4):
-        held[j], away[j] = expert_out(hidden if j == 0 else after(hidden, away[j - 1]), wd0, wd1, j)
+    last = None
+    for j in (2, 3, 0, 1):
+        held[j], away[j] = expert_out(hidden if last is None else after(hidden, last), wd0, wd1, j)
+        last = away[j]
     last = None
     for step in (3, 2, 1, 0):
         came = [trade(a, order[step]) for a, (_, _, order) in zip(away, CHAINS)]
         if not step:
             break
         half = held[0].shape[0] // 2
-        for j in range(4):
+        for j in (2, 3, 0, 1):
             got = came[j] if last is None else after(came[j], last)
             away[j] = last = add(held[j][half:], got[half:])
             held[j] = add(held[j][:half], got[:half])

time: 182 us -> 185 us (1.016)
  waiting for transfers between devices: 61.3 us -> 73.1 us
  blocking collectives: 32 us -> 28.2 us
  starting transfers between devices: 64.8 us -> 61 us
    ppermute x35, waiting for transfers between devices: 61.3 us -> 73.1 us  [trade(): return lax.ppermute(value, axis, [(i, i ^ mask) for i in range(n)])]
    ppermute x35, starting transfers between devices: 64.8 us -> 61 us  [trade(): return lax.ppermute(value, axis, [(i, i ^ mask) for i in range(n)])]
    all_to_all x2, blocking collectives: 32 us -> 28.2 us  [swap_experts(): lax.all_to_all(blocks, ('zl', 'y'), split_axis=0, concat_axis=0, tiled=True)]
  transfers between devices with their start and end apart: 35 -> 35, of which waited for: 16 -> 16; matrix products, arithmetic and copies ran while one was open for 2% -> 1% of each run, Pallas kernels for 2% -> 1%
where the time goes in v5:
time: 185 us; the launch traced here: 184 us
  waiting for transfers between devices  73.1 us (40%)
  starting transfers between devices  61 us (33%)
  blocking collectives  28.2 us (15%)
  Pallas kernels  16.6 us (9%)
  local copies, waits for them, and re-layouts  3.41 us (2%)
    ppermute x35, waiting for transfers between devices, trade(): return lax.ppermute(value, axis, [(i, i ^ mask) for i in range(n)])  73.1 us
    ppermute x35, starting transfers between devices, trade(): return lax.ppermute(value, axis, [(i, i ^ mask) for i in range(n)])  61 us
    all_to_all x2, blocking collectives, swap_experts(): lax.all_to_all(blocks, ('zl', 'y'), split_axis=0, concat_axis=0, tiled=True)  28.2 us
    pallas_call x1, Pallas kernels, hidden_units(): pl.pallas_call(functools.partial(hidden_kernel, chains, first, last), gri...  9 us
    pallas_call x4, Pallas kernels, expert_out(): pl.pallas_call(functools.partial(out_kernel, order), grid=(size // PART,)...  4.87 us
  transfers between devices with their start and end apart: 35, of which 16 were waited for; matrix products, arithmetic and copies ran while one was open for 1% of the time, Pallas kernels for 1%

profile of v5, /device:TPU:2, one launch (start us, length us, event | category | flops | bytes accessed | tf_op | source)
XLA Modules:
  0.0 184.4 jit_solution(6648033296162362668)
XLA Ops:
  4.5 15.0 %all_to_all.10 = bf16[8,8,3072]{2,1,0:T(8,128)(2,1)S(1)} all-to-all(bf16[8,8,3072]{2,1,0:T(8,128)(2,1)S(1)} %bitcast.18), channel_id=1, replica_groups=mesh['dp'=4,'zl'=2,'y'=4,'x'=4,'c'=2] {'zl','y'}, dimensions={0} | all-to-all | bytes 786432 | tf_op jit(solution)/shard_map/all_to_all | solution.py:268
  19.8 3.4 %collective-permute-start.3 = (bf16[32,2048]{1,0:T(8,128)(2,1)S(1)}, bf16[32,2048]{1,0:T(8,128)(2,1)S(1)}, u32[]{:S(2)}, u32[]{:S(2)}) collective-permute-start(bf16[32,2048]{1,0:T(8,128)(2,1)S(1)} %get-tuple-element.55), channel_id=1, source_target_pairs={{0,64},{64,0},{128,192},{192,128},{1,65},{65,1},{129,193},{193,129... | collective-permute-start | bytes 393224 | tf_op jit(solution)/shard_map/ppermute | solution.py:34
  23.1 3.6 %collective-permute-start.7 = (bf16[32,2048]{1,0:T(8,128)(2,1)S(1)}, bf16[32,2048]{1,0:T(8,128)(2,1)S(1)}, u32[]{:S(2)}, u32[]{:S(2)}) collective-permute-start(bf16[32,2048]{1,0:T(8,128)(2,1)S(1)} %get-tuple-element.60), channel_id=1, source_target_pairs={{0,192},{64,128},{128,64},{192,0},{1,193},{65,129},{129,65},{193,1... | collective-permute-start | bytes 393224 | tf_op jit(solution)/shard_map/ppermute | solution.py:34
  30.2 2.4 %collective-permute-done.5 = bf16[32,1024]{1,0:T(8,128)(2,1)S(1)} collective-permute-done((bf16[32,1024]{1,0:T(8,128)(2,1)S(1)}, bf16[32,1024]{1,0:T(8,128)(2,1)S(1)}, u32[]{:S(2)}, u32[]{:S(2)}) %collective-permute-start.5) | collective-permute-done | bytes 65568 | tf_op jit(solution)/shard_map/ppermute | solution.py:34
  37.5 6.0 %collective-permute-done.6 = bf16[64,2048]{1,0:T(8,128)(2,1)S(1)} collective-permute-done((bf16[64,2048]{1,0:T(8,128)(2,1)S(1)}, bf16[64,2048]{1,0:T(8,128)(2,1)S(1)}, u32[]{:S(2)}, u32[]{:S(2)}) %collective-permute-start.6) | collective-permute-done | bytes 262176 | tf_op jit(solution)/shard_map/ppermute | solution.py:34
  44.8 3.1 %collective-permute-start.13 = (bf16[128,1024]{1,0:T(8,128)(2,1)S(1)}, bf16[128,1024]{1,0:T(8,128)(2,1)S(1)}, u32[]{:S(2)}, u32[]{:S(2)}) collective-permute-start(bf16[128,1024]{1,0:T(8,128)(2,1)S(1)} %get-tuple-element.134), channel_id=1, source_target_pairs={{0,192},{64,128},{128,64},{192,0},{1,193},{65,129},{129,65},{193,1... | collective-permute-start | bytes 786440 | tf_op jit(solution)/shard_map/ppermute | solution.py:34
  48.0 3.5 %collective-permute-start.12 = (bf16[128,1024]{1,0:T(8,128)(2,1)S(1)}, bf16[128,1024]{1,0:T(8,128)(2,1)S(1)}, u32[]{:S(2)}, u32[]{:S(2)}) collective-permute-start(bf16[128,1024]{1,0:T(8,128)(2,1)S(1)} %get-tuple-element.135), channel_id=1, source_target_pairs={{0,64},{64,0},{128,192},{192,128},{1,65},{65,1},{129,193},{193,129... | collective-permute-start | bytes 786440 | tf_op jit(solution)/shard_map/ppermute | solution.py:34
  53.7 6.8 %collective-permute-done.12 = bf16[128,1024]{1,0:T(8,128)(2,1)S(1)} collective-permute-done((bf16[128,1024]{1,0:T(8,128)(2,1)S(1)}, bf16[128,1024]{1,0:T(8,128)(2,1)S(1)}, u32[]{:S(2)}, u32[]{:S(2)}) %collective-permute-start.12) | collective-permute-done | bytes 262176 | tf_op jit(solution)/shard_map/ppermute | solution.py:34
  61.8 4.5 %collective-permute-done.17 = bf16[128,2048]{1,0:T(8,128)(2,1)S(1)} collective-permute-done((bf16[128,2048]{1,0:T(8,128)(2,1)S(1)}, bf16[128,2048]{1,0:T(8,128)(2,1)S(1)}, u32[]{:S(2)}, u32[]{:S(2)}) %collective-permute-start.17) | collective-permute-done | bytes 524320 | tf_op jit(solution)/shard_map/ppermute | solution.py:34
  69.0 15.2 %collective-permute-done.16.refs_5_ = bf16[256,1024]{1,0:T(8,128)(2,1)S(1)} collective-permute-done((bf16[256,1024]{1,0:T(8,128)(2,1)S(1)}, bf16[256,1024]{1,0:T(8,128)(2,1)S(1)}, u32[]{:S(2)}, u32[]{:S(2)}) %collective-permute-start.16) | collective-permute-done | bytes 524320 | tf_op jit(solution)/shard_map/ppermute | solution.py:34
  84.2 8.3 %collective-permute-done.15.refs_7_ = bf16[256,1024]{1,0:T(8,128)(2,1)S(1)} collective-permute-done((bf16[256,1024]{1,0:T(8,128)(2,1)S(1)}, bf16[256,1024]{1,0:T(8,128)(2,1)S(1)}, u32[]{:S(2)}, u32[]{:S(2)}) %collective-permute-start.15) | collective-permute-done | bytes 524320 | tf_op jit(solution)/shard_map/ppermute | solution.py:34
  92.5 9.0 %hidden.1 = bf16[512,512]{1,0:T(8,128)(2,1)S(1)} custom-call(bf16[256,2048]{1,0:T(8,128)(2,1)S(1)} %constant_dynamic-update-slice_fusion.28.refs_0_, bf16[256,2048]{1,0:T(8,128)(2,1)S(1)} %collective-permute-done.14.refs_1_, bf16[256,2048]{1,0:T(8,128)(2,1)S(1)} %constant_dynamic-update-slice_fusion.32.refs_2_, ...), custom_call_target="tpu_custom_call" | custom-call | flops 6442450944 | bytes 18874368 | tf_op jit(solution)/shard_map/hidden/pallas_call | solution.py:134
  109.2 2.2 %collective-permute-start.25 = (bf16[256,2048]{1,0:T(8,128)(2,1)S(1)}, bf16[256,2048]{1,0:T(8,128)(2,1)S(1)}, u32[]{:S(2)}, u32[]{:S(2)}) collective-permute-start(bf16[256,2048]{1,0:T(8,128)(2,1)S(1)} %get-tuple-element.89), channel_id=1, source_target_pairs={{0,6},{2,4},{4,2},{6,0},{1,7},{3,5},{5,3},{7,1},{8,14},{10,12},{12... | collective-permute-start | bytes 3145736 | tf_op jit(solution)/shard_map/ppermute | solution.py:34
  111.4 8.0 %collective-permute-done.21 = bf16[256,1024]{1,0:T(8,128)(2,1)S(1)} collective-permute-done((bf16[256,1024]{1,0:T(8,128)(2,1)S(1)}, bf16[256,1024]{1,0:T(8,128)(2,1)S(1)}, u32[]{:S(2)}, u32[]{:S(2)}) %collective-permute-start.21) | collective-permute-done | bytes 524320 | tf_op jit(solution)/shard_map/ppermute | solution.py:34
  119.6 10.4 %collective-permute-start.24 = (bf16[128,1024]{1,0:T(8,128)(2,1)S(1)}, bf16[128,1024]{1,0:T(8,128)(2,1)S(1)}, u32[]{:S(2)}, u32[]{:S(2)}) collective-permute-start(bf16[128,1024]{1,0:T(8,128)(2,1)S(1)} %get-tuple-element.108), channel_id=1, source_target_pairs={{0,192},{64,128},{128,64},{192,0},{1,193},{65,129},{129,65},{193,1... | collective-permute-start | bytes 786440 | tf_op jit(solution)/shard_map/ppermute | solution.py:34
  133.4 2.1 %collective-permute-done.25 = bf16[256,2048]{1,0:T(8,128)(2,1)S(1)} collective-permute-done((bf16[256,2048]{1,0:T(8,128)(2,1)S(1)}, bf16[256,2048]{1,0:T(8,128)(2,1)S(1)}, u32[]{:S(2)}, u32[]{:S(2)}) %collective-permute-start.25) | collective-permute-done | bytes 1048608 | tf_op jit(solution)/shard_map/ppermute | solution.py:34
  135.9 2.3 %collective-permute-start.29 = (bf16[128,2048]{1,0:T(8,128)(2,1)S(1)}, bf16[128,2048]{1,0:T(8,128)(2,1)S(1)}, u32[]{:S(2)}, u32[]{:S(2)}) collective-permute-start(bf16[128,2048]{1,0:T(8,128)(2,1)S(1)} %get-tuple-element.100), channel_id=1, source_target_pairs={{0,2},{2,0},{4,6},{6,4},{1,3},{3,1},{5,7},{7,5},{8,10},{10,8},{12,... | collective-permute-start | bytes 1572872 | tf_op jit(solution)/shard_map/ppermute | solution.py:34
  140.0 3.6 %collective-permute-done.23 = bf16[128,1024]{1,0:T(8,128)(2,1)S(1)} collective-permute-done((bf16[128,1024]{1,0:T(8,128)(2,1)S(1)}, bf16[128,1024]{1,0:T(8,128)(2,1)S(1)}, u32[]{:S(2)}, u32[]{:S(2)}) %collective-permute-start.23) | collective-permute-done | bytes 262176 | tf_op jit(solution)/shard_map/ppermute | solution.py:34
  147.6 2.6 %collective-permute-start.30 = (bf16[64,2048]{1,0:T(8,128)(2,1)S(1)}, bf16[64,2048]{1,0:T(8,128)(2,1)S(1)}, u32[]{:S(2)}, u32[]{:S(2)}) collective-permute-start(bf16[64,2048]{1,0:T(8,128)(2,1)S(1)} %get-tuple-element.104), channel_id=1, source_target_pairs={{0,64},{64,0},{128,192},{192,128},{1,65},{65,1},{129,193},{193,129... | collective-permute-start | bytes 786440 | tf_op jit(solution)/shard_map/ppermute | solution.py:34
  150.3 4.0 %collective-permute-done.26 = bf16[64,2048]{1,0:T(8,128)(2,1)S(1)} collective-permute-done((bf16[64,2048]{1,0:T(8,128)(2,1)S(1)}, bf16[64,2048]{1,0:T(8,128)(2,1)S(1)}, u32[]{:S(2)}, u32[]{:S(2)}) %collective-permute-start.26) | collective-permute-done | bytes 262176 | tf_op jit(solution)/shard_map/ppermute | solution.py:34
  154.4 5.6 %collective-permute-done.30 = bf16[64,2048]{1,0:T(8,128)(2,1)S(1)} collective-permute-done((bf16[64,2048]{1,0:T(8,128)(2,1)S(1)}, bf16[64,2048]{1,0:T(8,128)(2,1)S(1)}, u32[]{:S(2)}, u32[]{:S(2)}) %collective-permute-start.30) | collective-permute-done | bytes 262176 | tf_op jit(solution)/shard_map/ppermute | solution.py:34
  160.1 3.5 %collective-permute-start.31 = (bf16[32,2048]{1,0:T(8,128)(2,1)S(1)}, bf16[32,2048]{1,0:T(8,128)(2,1)S(1)}, u32[]{:S(2)}, u32[]{:S(2)}) collective-permute-start(bf16[32,2048]{1,0:T(8,128)(2,1)S(1)} %get-tuple-element.113), channel_id=1, source_target_pairs={{0,64},{64,0},{128,192},{192,128},{1,65},{65,1},{129,193},{193,129... | collective-permute-start | bytes 393224 | tf_op jit(solution)/shard_map/ppermute | solution.py:34
  164.9 2.5 %collective-permute-start.33 = (bf16[32,1024]{1,0:T(8,128)(2,1)S(1)}, bf16[32,1024]{1,0:T(8,128)(2,1)S(1)}, u32[]{:S(2)}, u32[]{:S(2)}) collective-permute-start(bf16[32,1024]{1,0:T(8,128)(2,1)S(1)} %get-tuple-element.122), channel_id=1, source_target_pairs={{0,2},{2,0},{4,6},{6,4},{1,3},{3,1},{5,7},{7,5},{8,10},{10,8},{12,... | collective-permute-start | bytes 196616 | tf_op jit(solution)/shard_map/ppermute | solution.py:34
  170.1 13.2 %all_to_all.11 = bf16[8,8,3072]{2,1,0:T(8,128)(2,1)S(1)} all-to-all(bf16[8,8,3072]{2,1,0:T(8,128)(2,1)S(1)} %bitcast.17), channel_id=1, replica_groups=mesh['dp'=4,'zl'=2,'y'=4,'x'=4,'c'=2] {'zl','y'}, dimensions={0} | all-to-all | bytes 786432 | tf_op jit(solution)/shard_map/all_to_all | solution.py:268
  (99 shorter events, 43.2 us)
Async XLA Ops:
  0.0 19.5 %collective-permute-start = (bf16[6144,256]{1,0:T(8,128)(2,1)}, bf16[6144,256]{1,0:T(8,128)(2,1)S(1)}, u32[]{:S(2)}, u32[]{:S(2)}) collective-permute-start(bf16[6144,256]{1,0:T(8,128)(2,1)} %bitcast.22), channel_id=1, source_target_pairs={{0,1},{1,0},{2,3},{3,2},{4,5},{5,4},{6,7},{7,6},{8,9},{9,8},{10,11... | collective-permute-start | bytes 9437192 | tf_op jit(solution)/shard_map/ppermute | solution.py:34
  0.0 19.5 %collective-permute-start.1 = (bf16[6144,256]{1,0:T(8,128)(2,1)}, bf16[6144,256]{1,0:T(8,128)(2,1)S(1)}, u32[]{:S(2)}, u32[]{:S(2)}) collective-permute-start(bf16[6144,256]{1,0:T(8,128)(2,1)} %bitcast.24), channel_id=1, source_target_pairs={{0,1},{1,0},{2,3},{3,2},{4,5},{5,4},{6,7},{7,6},{8,9},{9,8},{10,11... | collective-permute-start | bytes 9437192 | tf_op jit(solution)/shard_map/ppermute | solution.py:34
  0.5 19.0 %collective-permute-start.2 = (bf16[256,6144]{1,0:T(8,128)(2,1)}, bf16[256,6144]{1,0:T(8,128)(2,1)S(1)}, u32[]{:S(2)}, u32[]{:S(2)}) collective-permute-start(bf16[256,6144]{1,0:T(8,128)(2,1)} %bitcast.10), channel_id=1, source_target_pairs={{0,1},{1,0},{2,3},{3,2},{4,5},{5,4},{6,7},{7,6},{8,9},{9,8},{10,11... | collective-permute-start | bytes 9437192 | tf_op jit(solution)/shard_map/ppermute | solution.py:34
  19.8 12.9 %collective-permute-start.3 = (bf16[32,2048]{1,0:T(8,128)(2,1)S(1)}, bf16[32,2048]{1,0:T(8,128)(2,1)S(1)}, u32[]{:S(2)}, u32[]{:S(2)}) collective-permute-start(bf16[32,2048]{1,0:T(8,128)(2,1)S(1)} %get-tuple-element.55), channel_id=1, source_target_pairs={{0,64},{64,0},{128,192},{192,128},{1,65},{65,1},{129,193},{193,129... | collective-permute-start | bytes 393224 | tf_op jit(solution)/shard_map/ppermute | solution.py:34
  32.7 10.8 %collective-permute-start.6 = (bf16[64,2048]{1,0:T(8,128)(2,1)S(1)}, bf16[64,2048]{1,0:T(8,128)(2,1)S(1)}, u32[]{:S(2)}, u32[]{:S(2)}) collective-permute-start(bf16[64,2048]{1,0:T(8,128)(2,1)S(1)} %get-tuple-element.139), channel_id=1, source_target_pairs={{0,192},{64,128},{128,64},{192,0},{1,193},{65,129},{129,65},{193,1... | collective-permute-start | bytes 786440 | tf_op jit(solution)/shard_map/ppermute | solution.py:34
  33.4 11.3 %collective-permute-start.11 = (bf16[64,2048]{1,0:T(8,128)(2,1)S(1)}, bf16[64,2048]{1,0:T(8,128)(2,1)S(1)}, u32[]{:S(2)}, u32[]{:S(2)}) collective-permute-start(bf16[64,2048]{1,0:T(8,128)(2,1)S(1)} %get-tuple-element.129), channel_id=1, source_target_pairs={{0,64},{64,0},{128,192},{192,128},{1,65},{65,1},{129,193},{193,129... | collective-permute-start | bytes 786440 | tf_op jit(solution)/shard_map/ppermute | solution.py:34
  34.8 13.1 %collective-permute-start.9 = (bf16[64,1024]{1,0:T(8,128)(2,1)S(1)}, bf16[64,1024]{1,0:T(8,128)(2,1)S(1)}, u32[]{:S(2)}, u32[]{:S(2)}) collective-permute-start(bf16[64,1024]{1,0:T(8,128)(2,1)S(1)} %get-tuple-element.151), channel_id=1, source_target_pairs={{0,2},{2,0},{4,6},{6,4},{1,3},{3,1},{5,7},{7,5},{8,10},{10,8},{12,... | collective-permute-start | bytes 393224 | tf_op jit(solution)/shard_map/ppermute | solution.py:34
  43.6 17.0 %collective-permute-start.8 = (bf16[128,2048]{1,0:T(8,128)(2,1)S(1)}, bf16[128,2048]{1,0:T(8,128)(2,1)S(1)}, u32[]{:S(2)}, u32[]{:S(2)}) collective-permute-start(bf16[128,2048]{1,0:T(8,128)(2,1)S(1)} %get-tuple-element.125), channel_id=1, source_target_pairs={{0,6},{2,4},{4,2},{6,0},{1,7},{3,5},{5,3},{7,1},{8,14},{10,12},{12... | collective-permute-start | bytes 1572872 | tf_op jit(solution)/shard_map/ppermute | solution.py:34
  48.0 12.6 %collective-permute-start.12 = (bf16[128,1024]{1,0:T(8,128)(2,1)S(1)}, bf16[128,1024]{1,0:T(8,128)(2,1)S(1)}, u32[]{:S(2)}, u32[]{:S(2)}) collective-permute-start(bf16[128,1024]{1,0:T(8,128)(2,1)S(1)} %get-tuple-element.135), channel_id=1, source_target_pairs={{0,64},{64,0},{128,192},{192,128},{1,65},{65,1},{129,193},{193,129... | collective-permute-start | bytes 786440 | tf_op jit(solution)/shard_map/ppermute | solution.py:34
  51.4 14.9 %collective-permute-start.17 = (bf16[128,2048]{1,0:T(8,128)(2,1)S(1)}, bf16[128,2048]{1,0:T(8,128)(2,1)S(1)}, u32[]{:S(2)}, u32[]{:S(2)}) collective-permute-start(bf16[128,2048]{1,0:T(8,128)(2,1)S(1)} %get-tuple-element.124), channel_id=1, source_target_pairs={{0,2},{2,0},{4,6},{6,4},{1,3},{3,1},{5,7},{7,5},{8,10},{10,8},{12,... | collective-permute-start | bytes 1572872 | tf_op jit(solution)/shard_map/ppermute | solution.py:34
  60.7 31.8 %collective-permute-start.14 = (bf16[256,2048]{1,0:T(8,128)(2,1)S(1)}, bf16[256,2048]{1,0:T(8,128)(2,1)S(1)}, u32[]{:S(2)}, u32[]{:S(2)}) collective-permute-start(bf16[256,2048]{1,0:T(8,128)(2,1)S(1)} %constant_dynamic-update-slice_fusion.28.refs_0_), channel_id=1, source_target_pairs={{0,2},{2,0},{4,6},{6,4},{1,3},{3,1},{5,7},{7,5},{8,10},{10,8},{12,... | collective-permute-start | bytes 3145736 | tf_op jit(solution)/shard_map/ppermute | solution.py:34
  66.3 26.2 %collective-permute-start.18 = (bf16[256,2048]{1,0:T(8,128)(2,1)S(1)}, bf16[256,2048]{1,0:T(8,128)(2,1)S(1)}, u32[]{:S(2)}, u32[]{:S(2)}) collective-permute-start(bf16[256,2048]{1,0:T(8,128)(2,1)S(1)} %constant_dynamic-update-slice_fusion.32.refs_2_), channel_id=1, source_target_pairs={{0,6},{2,4},{4,2},{6,0},{1,7},{3,5},{5,3},{7,1},{8,14},{10,12},{12... | collective-permute-start | bytes 3145736 | tf_op jit(solution)/shard_map/ppermute | solution.py:34
  67.2 17.0 %collective-permute-start.16 = (bf16[256,1024]{1,0:T(8,128)(2,1)S(1)}, bf16[256,1024]{1,0:T(8,128)(2,1)S(1)}, u32[]{:S(2)}, u32[]{:S(2)}) collective-permute-start(bf16[256,1024]{1,0:T(8,128)(2,1)S(1)} %constant_dynamic-update-slice_fusion.20.refs_4_), channel_id=1, source_target_pairs={{0,64},{64,0},{128,192},{192,128},{1,65},{65,1},{129,193},{193,129... | collective-permute-start | bytes 1572872 | tf_op jit(solution)/shard_map/ppermute | solution.py:34
  67.2 25.3 %collective-permute-start.15 = (bf16[256,1024]{1,0:T(8,128)(2,1)S(1)}, bf16[256,1024]{1,0:T(8,128)(2,1)S(1)}, u32[]{:S(2)}, u32[]{:S(2)}) collective-permute-start(bf16[256,1024]{1,0:T(8,128)(2,1)S(1)} %constant_dynamic-update-slice_fusion.24.refs_6_), channel_id=1, source_target_pairs={{0,192},{64,128},{128,64},{192,0},{1,193},{65,129},{129,65},{193,1... | collective-permute-start | bytes 1572872 | tf_op jit(solution)/shard_map/ppermute | solution.py:34
  104.7 28.2 %collective-permute-start.19 = (bf16[256,2048]{1,0:T(8,128)(2,1)S(1)}, bf16[256,2048]{1,0:T(8,128)(2,1)S(1)}, u32[]{:S(2)}, u32[]{:S(2)}) collective-permute-start(bf16[256,2048]{1,0:T(8,128)(2,1)S(1)} %get-tuple-element.82), channel_id=1, source_target_pairs={{0,2},{2,0},{4,6},{6,4},{1,3},{3,1},{5,7},{7,5},{8,10},{10,8},{12,... | collective-permute-start | bytes 3145736 | tf_op jit(solution)/shard_map/ppermute | solution.py:34
  105.7 13.7 %collective-permute-start.21 = (bf16[256,1024]{1,0:T(8,128)(2,1)S(1)}, bf16[256,1024]{1,0:T(8,128)(2,1)S(1)}, u32[]{:S(2)}, u32[]{:S(2)}) collective-permute-start(bf16[256,1024]{1,0:T(8,128)(2,1)S(1)} %get-tuple-element.77), channel_id=1, source_target_pairs={{0,64},{64,0},{128,192},{192,128},{1,65},{65,1},{129,193},{193,129... | collective-permute-start | bytes 1572872 | tf_op jit(solution)/shard_map/ppermute | solution.py:34
  105.8 25.3 %collective-permute-start.20 = (bf16[256,1024]{1,0:T(8,128)(2,1)S(1)}, bf16[256,1024]{1,0:T(8,128)(2,1)S(1)}, u32[]{:S(2)}, u32[]{:S(2)}) collective-permute-start(bf16[256,1024]{1,0:T(8,128)(2,1)S(1)} %get-tuple-element.79), channel_id=1, source_target_pairs={{0,192},{64,128},{128,64},{192,0},{1,193},{65,129},{129,65},{193,1... | collective-permute-start | bytes 1572872 | tf_op jit(solution)/shard_map/ppermute | solution.py:34
  109.2 26.3 %collective-permute-start.25 = (bf16[256,2048]{1,0:T(8,128)(2,1)S(1)}, bf16[256,2048]{1,0:T(8,128)(2,1)S(1)}, u32[]{:S(2)}, u32[]{:S(2)}) collective-permute-start(bf16[256,2048]{1,0:T(8,128)(2,1)S(1)} %get-tuple-element.89), channel_id=1, source_target_pairs={{0,6},{2,4},{4,2},{6,0},{1,7},{3,5},{5,3},{7,1},{8,14},{10,12},{12... | collective-permute-start | bytes 3145736 | tf_op jit(solution)/shard_map/ppermute | solution.py:34
  119.6 20.2 %collective-permute-start.24 = (bf16[128,1024]{1,0:T(8,128)(2,1)S(1)}, bf16[128,1024]{1,0:T(8,128)(2,1)S(1)}, u32[]{:S(2)}, u32[]{:S(2)}) collective-permute-start(bf16[128,1024]{1,0:T(8,128)(2,1)S(1)} %get-tuple-element.108), channel_id=1, source_target_pairs={{0,192},{64,128},{128,64},{192,0},{1,193},{65,129},{129,65},{193,1... | collective-permute-start | bytes 786440 | tf_op jit(solution)/shard_map/ppermute | solution.py:34
  131.2 12.4 %collective-permute-start.23 = (bf16[128,1024]{1,0:T(8,128)(2,1)S(1)}, bf16[128,1024]{1,0:T(8,128)(2,1)S(1)}, u32[]{:S(2)}, u32[]{:S(2)}) collective-permute-start(bf16[128,1024]{1,0:T(8,128)(2,1)S(1)} %get-tuple-element.110), channel_id=1, source_target_pairs={{0,64},{64,0},{128,192},{192,128},{1,65},{65,1},{129,193},{193,129... | collective-permute-start | bytes 786440 | tf_op jit(solution)/shard_map/ppermute | solution.py:34
  133.3 12.0 %collective-permute-start.22 = (bf16[128,2048]{1,0:T(8,128)(2,1)S(1)}, bf16[128,2048]{1,0:T(8,128)(2,1)S(1)}, u32[]{:S(2)}, u32[]{:S(2)}) collective-permute-start(bf16[128,2048]{1,0:T(8,128)(2,1)S(1)} %get-tuple-element.101), channel_id=1, source_target_pairs={{0,6},{2,4},{4,2},{6,0},{1,7},{3,5},{5,3},{7,1},{8,14},{10,12},{12... | collective-permute-start | bytes 1572872 | tf_op jit(solution)/shard_map/ppermute | solution.py:34
  135.9 11.6 %collective-permute-start.29 = (bf16[128,2048]{1,0:T(8,128)(2,1)S(1)}, bf16[128,2048]{1,0:T(8,128)(2,1)S(1)}, u32[]{:S(2)}, u32[]{:S(2)}) collective-permute-start(bf16[128,2048]{1,0:T(8,128)(2,1)S(1)} %get-tuple-element.100), channel_id=1, source_target_pairs={{0,2},{2,0},{4,6},{6,4},{1,3},{3,1},{5,7},{7,5},{8,10},{10,8},{12,... | collective-permute-start | bytes 1572872 | tf_op jit(solution)/shard_map/ppermute | solution.py:34
  139.9 10.3 %collective-permute-start.28 = (bf16[64,1024]{1,0:T(8,128)(2,1)S(1)}, bf16[64,1024]{1,0:T(8,128)(2,1)S(1)}, u32[]{:S(2)}, u32[]{:S(2)}) collective-permute-start(bf16[64,1024]{1,0:T(8,128)(2,1)S(1)} %get-tuple-element.116), channel_id=1, source_target_pairs={{0,6},{2,4},{4,2},{6,0},{1,7},{3,5},{5,3},{7,1},{8,14},{10,12},{12... | collective-permute-start | bytes 393224 | tf_op jit(solution)/shard_map/ppermute | solution.py:34
  147.6 12.3 %collective-permute-start.30 = (bf16[64,2048]{1,0:T(8,128)(2,1)S(1)}, bf16[64,2048]{1,0:T(8,128)(2,1)S(1)}, u32[]{:S(2)}, u32[]{:S(2)}) collective-permute-start(bf16[64,2048]{1,0:T(8,128)(2,1)S(1)} %get-tuple-element.104), channel_id=1, source_target_pairs={{0,64},{64,0},{128,192},{192,128},{1,65},{65,1},{129,193},{193,129... | collective-permute-start | bytes 786440 | tf_op jit(solution)/shard_map/ppermute | solution.py:34
  (19 other events, 277.0 us)

commit v6 on v5

--- a/solution.py
+++ b/solution.py
@@ -18,6 +18,12 @@
     (3072, 2048, ("zb", "za", "xa", "xb")),
     (2048, 1024, ("xa", "xb", "zb", "za")),
     (5120, 1024, ("xb", "xa", "za", "zb")),
+)
+OUT_CHAINS = tuple(
+    (start, size, order)
+    for (start, size), (_, _, order) in zip(
+        ((0, 2304), (3072, 2304), (2304, 768), (5376, 768)), CHAINS
+    )
 )
 CANON = ("xa", "xb", "za", "zb")
 UNIT = 32
@@ -99,6 +105,7 @@
 
 
 PART = 1024
+OUT_PART = 768
 
 
 def pick(table, i):
@@ -140,8 +147,8 @@
         scratch_shapes=scratch,
         compiler_params=pltpu.CompilerParams(vmem_limit_bytes=32 << 20),
         cost_estimate=pl.CostEstimate(
-            flops=8 * count * depth * units,
-            bytes_accessed=8 * depth * units + 2 * count * depth,
+            flops=8 * count * depth * units if last else 0,
+            bytes_accessed=8 * depth * units + 2 * count * depth if last else 0,
             transcendentals=2 * count * units if last else 0,
         ),
         name="hidden",
@@ -149,17 +156,17 @@
 
 
 def expert_out(hidden, wd0, wd1, chain):
-    start, size, order = CHAINS[chain]
+    start, size, order = OUT_CHAINS[chain]
     units = wd0.shape[0]
-    low, count = start // PART, 2 * HALF
+    low, count = start // OUT_PART, 2 * HALF
     shape = jax.ShapeDtypeStruct((HALF, size), jnp.bfloat16)
     return pl.pallas_call(
         functools.partial(out_kernel, order),
-        grid=(size // PART,),
+        grid=(size // OUT_PART,),
         out_shape=[shape] * 2,
         in_specs=[pl.BlockSpec((count, 2 * units), lambda i: (0, 0))]
-        + [pl.BlockSpec((units, PART), lambda i: (0, low + i))] * 2,
-        out_specs=[pl.BlockSpec((HALF, PART), lambda i: (0, i))] * 2,
+        + [pl.BlockSpec((units, OUT_PART), lambda i: (0, low + i))] * 2,
+        out_specs=[pl.BlockSpec((HALF, OUT_PART), lambda i: (0, i))] * 2,
         compiler_params=pltpu.CompilerParams(vmem_limit_bytes=24 << 20),
         cost_estimate=pl.CostEstimate(
             flops=4 * count * size * units,
@@ -223,7 +230,7 @@
     held, came, folded = refs[:n], refs[n : 2 * n], refs[2 * n]
     half = folded.shape[1]
     f32 = jnp.float32
-    for c, (start, size, _) in enumerate(CHAINS):
+    for c, (start, size, _) in enumerate(OUT_CHAINS):
         total = (held[c][...].astype(f32) + came[c][...].astype(f32)).astype(folded.dtype)
         side = start // half
         give = onehot(2 * UNIT, UNIT, lambda r, c: r == (c // 4) * 8 + c % 4 + 4 * side)
@@ -296,18 +303,21 @@
         came = [trade(h, order[step]) for h, (_, _, order) in zip(held, CHAINS)]
         if step == 3:
             break
-        for j in (0, 1, 2, 3) if step == 1 else (2, 3, 0, 1):
+        for j in (2, 3, 0, 1):
             if last is not None:
                 came[j] = after(came[j], last)
             held[j] = last = jnp.concatenate([held[j], came[j]], axis=0)
-    for j in (2, 3, 0, 1):
-        came[j] = last = after(came[j], last)
-    pieces = [piece for pair in zip(held, came) for piece in pair]
-    hidden = hidden_units(pieces, (wg0, wu0, wg1, wu1), (0, 1, 2, 3), None, True)
+    weights = (wg0, wu0, wg1, wu1)
+    came[0] = after(came[0], last)
+    came[1] = after(came[1], came[0])
+    sums = hidden_units((held[0], came[0], held[1], came[1]), weights, (0, 1), None, False)
+    came[2] = after(came[2], sums)
+    came[3] = after(came[3], came[2])
+    hidden = hidden_units((held[2], came[2], held[3], came[3]), weights, (2, 3), sums, True)
 
     held, away = [None] * 4, [None] * 4
     last = None
-    for j in (2, 3, 0, 1):
+    for j in range(4):
         held[j], away[j] = expert_out(hidden if last is None else after(hidden, last), wd0, wd1, j)
         last = away[j]
     last = None
@@ -316,7 +326,7 @@
         if not step:
             break
         half = held[0].shape[0] // 2
-        for j in (2, 3, 0, 1):
+        for j in range(4):
             got = came[j] if last is None else after(came[j], last)
             away[j] = last = add(held[j][half:], got[half:])
             held[j] = add(held[j][:half], got[:half])

time: 185 us -> 179 us (0.968)
  waiting for transfers between devices: 73.1 us -> 63.4 us
  starting transfers between devices: 61 us -> 66.2 us
    ppermute x35, waiting for transfers between devices: 73.1 us -> 63.4 us  [trade(): return lax.ppermute(value, axis, [(i, i ^ mask) for i in range(n)])]
    ppermute x35, starting transfers between devices: 61 us -> 66.2 us  [trade(): return lax.ppermute(value, axis, [(i, i ^ mask) for i in range(n)])]
    pallas_call x1 -> x2, Pallas kernels: 9 us -> 9.01 us  [hidden_units(): pl.pallas_call(functools.partial(hidden_kernel, chains, first, last), gri...]
  transfers between devices with their start and end apart: 35 -> 35, of which waited for: 16 -> 17; matrix products, arithmetic and copies ran while one was open for 1% -> 1% of each run, Pallas kernels for 1% -> 6%
where the time goes in v6:
time: 179 us; the launch traced here: 178 us
  starting transfers between devices  66.2 us (37%)
  waiting for transfers between devices  63.4 us (35%)
  blocking collectives  26.7 us (15%)
  Pallas kernels  17 us (9%)
  local copies, waits for them, and re-layouts  3.42 us (2%)
    ppermute x35, starting transfers between devices, trade(): return lax.ppermute(value, axis, [(i, i ^ mask) for i in range(n)])  66.2 us
    ppermute x35, waiting for transfers between devices, trade(): return lax.ppermute(value, axis, [(i, i ^ mask) for i in range(n)])  63.4 us
    all_to_all x2, blocking collectives, swap_experts(): lax.all_to_all(blocks, ('zl', 'y'), split_axis=0, concat_axis=0, tiled=True)  26.7 us
    pallas_call x2, Pallas kernels, hidden_units(): pl.pallas_call(functools.partial(hidden_kernel, chains, first, last), gri...  9.01 us
    pallas_call x4, Pallas kernels, expert_out(): pl.pallas_call(functools.partial(out_kernel, order), grid=(size // OUT_PA...  5.29 us
  transfers between devices with their start and end apart: 35, of which 17 were waited for; matrix products, arithmetic and copies ran while one was open for 1% of the time, Pallas kernels for 6%

profile of v6, /device:TPU:2, one launch (start us, length us, event | category | flops | bytes accessed | tf_op | source)
XLA Modules:
  0.0 178.3 jit_solution(6925749199931838404)
XLA Ops:
  4.5 15.0 %all_to_all.10 = bf16[8,8,3072]{2,1,0:T(8,128)(2,1)S(1)} all-to-all(bf16[8,8,3072]{2,1,0:T(8,128)(2,1)S(1)} %bitcast.24), channel_id=1, replica_groups=mesh['dp'=4,'zl'=2,'y'=4,'x'=4,'c'=2] {'zl','y'}, dimensions={0} | all-to-all | bytes 786432 | tf_op jit(solution)/shard_map/all_to_all | solution.py:275
  19.8 3.4 %collective-permute-start.6 = (bf16[32,2048]{1,0:T(8,128)(2,1)S(1)}, bf16[32,2048]{1,0:T(8,128)(2,1)S(1)}, u32[]{:S(2)}, u32[]{:S(2)}) collective-permute-start(bf16[32,2048]{1,0:T(8,128)(2,1)S(1)} %get-tuple-element.57), channel_id=1, source_target_pairs={{0,64},{64,0},{128,192},{192,128},{1,65},{65,1},{129,193},{193,129... | collective-permute-start | bytes 393224 | tf_op jit(solution)/shard_map/ppermute | solution.py:40
  23.2 3.7 %collective-permute-start.5 = (bf16[32,2048]{1,0:T(8,128)(2,1)S(1)}, bf16[32,2048]{1,0:T(8,128)(2,1)S(1)}, u32[]{:S(2)}, u32[]{:S(2)}) collective-permute-start(bf16[32,2048]{1,0:T(8,128)(2,1)S(1)} %get-tuple-element.56), channel_id=1, source_target_pairs={{0,192},{64,128},{128,64},{192,0},{1,193},{65,129},{129,65},{193,1... | collective-permute-start | bytes 393224 | tf_op jit(solution)/shard_map/ppermute | solution.py:40
  32.7 2.4 %collective-permute-start.11 = (bf16[64,1024]{1,0:T(8,128)(2,1)S(1)}, bf16[64,1024]{1,0:T(8,128)(2,1)S(1)}, u32[]{:S(2)}, u32[]{:S(2)}) collective-permute-start(bf16[64,1024]{1,0:T(8,128)(2,1)S(1)} %get-tuple-element.145), channel_id=1, source_target_pairs={{0,2},{2,0},{4,6},{6,4},{1,3},{3,1},{5,7},{7,5},{8,10},{10,8},{12,... | collective-permute-start | bytes 393224 | tf_op jit(solution)/shard_map/ppermute | solution.py:40
  37.0 4.1 %collective-permute-start.8 = (bf16[128,1024]{1,0:T(8,128)(2,1)S(1)}, bf16[128,1024]{1,0:T(8,128)(2,1)S(1)}, u32[]{:S(2)}, u32[]{:S(2)}) collective-permute-start(bf16[128,1024]{1,0:T(8,128)(2,1)S(1)} %get-tuple-element.141), channel_id=1, source_target_pairs={{0,192},{64,128},{128,64},{192,0},{1,193},{65,129},{129,65},{193,1... | collective-permute-start | bytes 786440 | tf_op jit(solution)/shard_map/ppermute | solution.py:40
  42.7 9.2 %collective-permute-done.10 = bf16[64,2048]{1,0:T(8,128)(2,1)S(1)} collective-permute-done((bf16[64,2048]{1,0:T(8,128)(2,1)S(1)}, bf16[64,2048]{1,0:T(8,128)(2,1)S(1)}, u32[]{:S(2)}, u32[]{:S(2)}) %collective-permute-start.10) | collective-permute-done | bytes 262176 | tf_op jit(solution)/shard_map/ppermute | solution.py:40
  52.8 4.4 %collective-permute-done.8 = bf16[128,1024]{1,0:T(8,128)(2,1)S(1)} collective-permute-done((bf16[128,1024]{1,0:T(8,128)(2,1)S(1)}, bf16[128,1024]{1,0:T(8,128)(2,1)S(1)}, u32[]{:S(2)}, u32[]{:S(2)}) %collective-permute-start.8) | collective-permute-done | bytes 262176 | tf_op jit(solution)/shard_map/ppermute | solution.py:40
  57.7 6.6 %collective-permute-done.13 = bf16[128,2048]{1,0:T(8,128)(2,1)S(1)} collective-permute-done((bf16[128,2048]{1,0:T(8,128)(2,1)S(1)}, bf16[128,2048]{1,0:T(8,128)(2,1)S(1)}, u32[]{:S(2)}, u32[]{:S(2)}) %collective-permute-start.13) | collective-permute-done | bytes 524320 | tf_op jit(solution)/shard_map/ppermute | solution.py:40
  66.0 5.0 %collective-permute-start.17 = (bf16[256,2048]{1,0:T(8,128)(2,1)S(1)}, bf16[256,2048]{1,0:T(8,128)(2,1)S(1)}, u32[]{:S(2)}, u32[]{:S(2)}) collective-permute-start(bf16[256,2048]{1,0:T(8,128)(2,1)S(1)} %constant_dynamic-update-slice_fusion.32.refs_2_), channel_id=1, source_target_pairs={{0,6},{2,4},{4,2},{6,0},{1,7},{3,5},{5,3},{7,1},{8,14},{10,12},{12... | collective-permute-start | bytes 3145736 | tf_op jit(solution)/shard_map/ppermute | solution.py:40
  74.1 10.1 %collective-permute-done.15.refs_1_ = bf16[256,2048]{1,0:T(8,128)(2,1)S(1)} collective-permute-done((bf16[256,2048]{1,0:T(8,128)(2,1)S(1)}, bf16[256,2048]{1,0:T(8,128)(2,1)S(1)}, u32[]{:S(2)}, u32[]{:S(2)}) %collective-permute-start.15) | collective-permute-done | bytes 1048608 | tf_op jit(solution)/shard_map/ppermute | solution.py:40
  84.3 5.9 %hidden.2.refs_8_ = f32[4,512,256]{2,1,0:T(8,128)S(1)} custom-call(bf16[256,2048]{1,0:T(8,128)(2,1)S(1)} %constant_dynamic-update-slice_fusion.28.refs_0_, bf16[256,2048]{1,0:T(8,128)(2,1)S(1)} %collective-permute-done.15.refs_1_, bf16[256,2048]{1,0:T(8,128)(2,1)S(1)} %constant_dynamic-update-slice_fusion.32.refs_2_, ...), custom_call_target="tpu_custom_call" | custom-call | tf_op jit(solution)/shard_map/hidden/pallas_call | solution.py:141
  90.2 3.1 %hidden.3 = bf16[512,512]{1,0:T(8,128)(2,1)S(1)} custom-call(bf16[256,1024]{1,0:T(8,128)(2,1)S(1)} %constant_dynamic-update-slice_fusion.20.refs_0_, bf16[256,1024]{1,0:T(8,128)(2,1)S(1)} %collective-permute-done.12.refs_1_, bf16[256,1024]{1,0:T(8,128)(2,1)S(1)} %constant_dynamic-update-slice_fusion.24.refs_2_, ...), custom_call_target="tpu_custom_call" | custom-call | flops 2147483648 | bytes 6291456 | tf_op jit(solution)/shard_map/hidden/pallas_call | solution.py:141
  98.5 2.9 %collective-permute-start.23 = (bf16[256,2304]{1,0:T(8,128)(2,1)S(1)}, bf16[256,2304]{1,0:T(8,128)(2,1)S(1)}, u32[]{:S(2)}, u32[]{:S(2)}) collective-permute-start(bf16[256,2304]{1,0:T(8,128)(2,1)S(1)} %get-tuple-element.80), channel_id=1, source_target_pairs={{0,6},{2,4},{4,2},{6,0},{1,7},{3,5},{5,3},{7,1},{8,14},{10,12},{12... | collective-permute-start | bytes 3538952 | tf_op jit(solution)/shard_map/ppermute | solution.py:40
  102.0 3.6 %collective-permute-start.22 = (bf16[256,768]{1,0:T(8,128)(2,1)S(1)}, bf16[256,768]{1,0:T(8,128)(2,1)S(1)}, u32[]{:S(2)}, u32[]{:S(2)}) collective-permute-start(bf16[256,768]{1,0:T(8,128)(2,1)S(1)} %get-tuple-element.82), channel_id=1, source_target_pairs={{0,64},{64,0},{128,192},{192,128},{1,65},{65,1},{129,193},{193,129... | collective-permute-start | bytes 1179656 | tf_op jit(solution)/shard_map/ppermute | solution.py:40
  107.0 10.2 %collective-permute-done.19 = bf16[256,2304]{1,0:T(8,128)(2,1)S(1)} collective-permute-done((bf16[256,2304]{1,0:T(8,128)(2,1)S(1)}, bf16[256,2304]{1,0:T(8,128)(2,1)S(1)}, u32[]{:S(2)}, u32[]{:S(2)}) %collective-permute-start.19) | collective-permute-done | bytes 1179680 | tf_op jit(solution)/shard_map/ppermute | solution.py:40
  117.5 4.5 %collective-permute-start.20 = (bf16[128,2304]{1,0:T(8,128)(2,1)S(1)}, bf16[128,2304]{1,0:T(8,128)(2,1)S(1)}, u32[]{:S(2)}, u32[]{:S(2)}) collective-permute-start(bf16[128,2304]{1,0:T(8,128)(2,1)S(1)} %get-tuple-element.101), channel_id=1, source_target_pairs={{0,6},{2,4},{4,2},{6,0},{1,7},{3,5},{5,3},{7,1},{8,14},{10,12},{12... | collective-permute-start | bytes 1769480 | tf_op jit(solution)/shard_map/ppermute | solution.py:40
  122.0 5.4 %collective-permute-done.23 = bf16[256,2304]{1,0:T(8,128)(2,1)S(1)} collective-permute-done((bf16[256,2304]{1,0:T(8,128)(2,1)S(1)}, bf16[256,2304]{1,0:T(8,128)(2,1)S(1)}, u32[]{:S(2)}, u32[]{:S(2)}) %collective-permute-start.23) | collective-permute-done | bytes 1179680 | tf_op jit(solution)/shard_map/ppermute | solution.py:40
  127.6 3.1 %collective-permute-start.27 = (bf16[128,2304]{1,0:T(8,128)(2,1)S(1)}, bf16[128,2304]{1,0:T(8,128)(2,1)S(1)}, u32[]{:S(2)}, u32[]{:S(2)}) collective-permute-start(bf16[128,2304]{1,0:T(8,128)(2,1)S(1)} %get-tuple-element.100), channel_id=1, source_target_pairs={{0,2},{2,0},{4,6},{6,4},{1,3},{3,1},{5,7},{7,5},{8,10},{10,8},{12,... | collective-permute-start | bytes 1769480 | tf_op jit(solution)/shard_map/ppermute | solution.py:40
  131.1 4.8 %collective-permute-start.25 = (bf16[128,768]{1,0:T(8,128)(2,1)S(1)}, bf16[128,768]{1,0:T(8,128)(2,1)S(1)}, u32[]{:S(2)}, u32[]{:S(2)}) collective-permute-start(bf16[128,768]{1,0:T(8,128)(2,1)S(1)} %get-tuple-element.110), channel_id=1, source_target_pairs={{0,64},{64,0},{128,192},{192,128},{1,65},{65,1},{129,193},{193,129... | collective-permute-start | bytes 589832 | tf_op jit(solution)/shard_map/ppermute | solution.py:40
  138.8 2.8 %collective-permute-start.28 = (bf16[64,2304]{1,0:T(8,128)(2,1)S(1)}, bf16[64,2304]{1,0:T(8,128)(2,1)S(1)}, u32[]{:S(2)}, u32[]{:S(2)}) collective-permute-start(bf16[64,2304]{1,0:T(8,128)(2,1)S(1)} %get-tuple-element.104), channel_id=1, source_target_pairs={{0,64},{64,0},{128,192},{192,128},{1,65},{65,1},{129,193},{193,129... | collective-permute-start | bytes 884744 | tf_op jit(solution)/shard_map/ppermute | solution.py:40
  144.2 5.3 %collective-permute-done.25 = bf16[128,768]{1,0:T(8,128)(2,1)S(1)} collective-permute-done((bf16[128,768]{1,0:T(8,128)(2,1)S(1)}, bf16[128,768]{1,0:T(8,128)(2,1)S(1)}, u32[]{:S(2)}, u32[]{:S(2)}) %collective-permute-start.25) | collective-permute-done | bytes 196640 | tf_op jit(solution)/shard_map/ppermute | solution.py:40
  150.8 3.4 %collective-permute-start.31 = (bf16[32,2304]{1,0:T(8,128)(2,1)S(1)}, bf16[32,2304]{1,0:T(8,128)(2,1)S(1)}, u32[]{:S(2)}, u32[]{:S(2)}) collective-permute-start(bf16[32,2304]{1,0:T(8,128)(2,1)S(1)} %get-tuple-element.113), channel_id=1, source_target_pairs={{0,64},{64,0},{128,192},{192,128},{1,65},{65,1},{129,193},{193,129... | collective-permute-start | bytes 442376 | tf_op jit(solution)/shard_map/ppermute | solution.py:40
  156.4 2.7 %collective-permute-start.32 = (bf16[32,2304]{1,0:T(8,128)(2,1)S(1)}, bf16[32,2304]{1,0:T(8,128)(2,1)S(1)}, u32[]{:S(2)}, u32[]{:S(2)}) collective-permute-start(bf16[32,2304]{1,0:T(8,128)(2,1)S(1)} %get-tuple-element.111), channel_id=1, source_target_pairs={{0,192},{64,128},{128,64},{192,0},{1,193},{65,129},{129,65},{193,1... | collective-permute-start | bytes 442376 | tf_op jit(solution)/shard_map/ppermute | solution.py:40
  165.5 11.7 %all_to_all.11 = bf16[8,8,3072]{2,1,0:T(8,128)(2,1)S(1)} all-to-all(bf16[8,8,3072]{2,1,0:T(8,128)(2,1)S(1)} %bitcast.23), channel_id=1, replica_groups=mesh['dp'=4,'zl'=2,'y'=4,'x'=4,'c'=2] {'zl','y'}, dimensions={0} | all-to-all | bytes 786432 | tf_op jit(solution)/shard_map/all_to_all | solution.py:275
  (100 shorter events, 44.6 us)
Async XLA Ops:
  0.0 19.5 %collective-permute-start.2 = (bf16[256,6144]{1,0:T(8,128)(2,1)}, bf16[256,6144]{1,0:T(8,128)(2,1)S(1)}, u32[]{:S(2)}, u32[]{:S(2)}) collective-permute-start(bf16[256,6144]{1,0:T(8,128)(2,1)} %bitcast.10), channel_id=1, source_target_pairs={{0,1},{1,0},{2,3},{3,2},{4,5},{5,4},{6,7},{7,6},{8,9},{9,8},{10,11... | collective-permute-start | bytes 9437192 | tf_op jit(solution)/shard_map/ppermute | solution.py:40
  0.0 19.5 %collective-permute-start = (bf16[6144,256]{1,0:T(8,128)(2,1)}, bf16[6144,256]{1,0:T(8,128)(2,1)S(1)}, u32[]{:S(2)}, u32[]{:S(2)}) collective-permute-start(bf16[6144,256]{1,0:T(8,128)(2,1)} %bitcast.15), channel_id=1, source_target_pairs={{0,1},{1,0},{2,3},{3,2},{4,5},{5,4},{6,7},{7,6},{8,9},{9,8},{10,11... | collective-permute-start | bytes 9437192 | tf_op jit(solution)/shard_map/ppermute | solution.py:40
  0.5 19.0 %collective-permute-start.1 = (bf16[6144,256]{1,0:T(8,128)(2,1)}, bf16[6144,256]{1,0:T(8,128)(2,1)S(1)}, u32[]{:S(2)}, u32[]{:S(2)}) collective-permute-start(bf16[6144,256]{1,0:T(8,128)(2,1)} %bitcast.18), channel_id=1, source_target_pairs={{0,1},{1,0},{2,3},{3,2},{4,5},{5,4},{6,7},{7,6},{8,9},{9,8},{10,11... | collective-permute-start | bytes 9437192 | tf_op jit(solution)/shard_map/ppermute | solution.py:40
  19.8 15.4 %collective-permute-start.6 = (bf16[32,2048]{1,0:T(8,128)(2,1)S(1)}, bf16[32,2048]{1,0:T(8,128)(2,1)S(1)}, u32[]{:S(2)}, u32[]{:S(2)}) collective-permute-start(bf16[32,2048]{1,0:T(8,128)(2,1)S(1)} %get-tuple-element.57), channel_id=1, source_target_pairs={{0,64},{64,0},{128,192},{192,128},{1,65},{65,1},{129,193},{193,129... | collective-permute-start | bytes 393224 | tf_op jit(solution)/shard_map/ppermute | solution.py:40
  35.2 16.7 %collective-permute-start.10 = (bf16[64,2048]{1,0:T(8,128)(2,1)S(1)}, bf16[64,2048]{1,0:T(8,128)(2,1)S(1)}, u32[]{:S(2)}, u32[]{:S(2)}) collective-permute-start(bf16[64,2048]{1,0:T(8,128)(2,1)S(1)} %get-tuple-element.137), channel_id=1, source_target_pairs={{0,192},{64,128},{128,64},{192,0},{1,193},{65,129},{129,65},{193,1... | collective-permute-start | bytes 786440 | tf_op jit(solution)/shard_map/ppermute | solution.py:40
  35.5 16.9 %collective-permute-start.9 = (bf16[64,2048]{1,0:T(8,128)(2,1)S(1)}, bf16[64,2048]{1,0:T(8,128)(2,1)S(1)}, u32[]{:S(2)}, u32[]{:S(2)}) collective-permute-start(bf16[64,2048]{1,0:T(8,128)(2,1)S(1)} %get-tuple-element.129), channel_id=1, source_target_pairs={{0,64},{64,0},{128,192},{192,128},{1,65},{65,1},{129,193},{193,129... | collective-permute-start | bytes 786440 | tf_op jit(solution)/shard_map/ppermute | solution.py:40
  37.0 20.2 %collective-permute-start.8 = (bf16[128,1024]{1,0:T(8,128)(2,1)S(1)}, bf16[128,1024]{1,0:T(8,128)(2,1)S(1)}, u32[]{:S(2)}, u32[]{:S(2)}) collective-permute-start(bf16[128,1024]{1,0:T(8,128)(2,1)S(1)} %get-tuple-element.141), channel_id=1, source_target_pairs={{0,192},{64,128},{128,64},{192,0},{1,193},{65,129},{129,65},{193,1... | collective-permute-start | bytes 786440 | tf_op jit(solution)/shard_map/ppermute | solution.py:40
  41.1 16.6 %collective-permute-start.14 = (bf16[128,1024]{1,0:T(8,128)(2,1)S(1)}, bf16[128,1024]{1,0:T(8,128)(2,1)S(1)}, u32[]{:S(2)}, u32[]{:S(2)}) collective-permute-start(bf16[128,1024]{1,0:T(8,128)(2,1)S(1)} %get-tuple-element.134), channel_id=1, source_target_pairs={{0,64},{64,0},{128,192},{192,128},{1,65},{65,1},{129,193},{193,129... | collective-permute-start | bytes 786440 | tf_op jit(solution)/shard_map/ppermute | solution.py:40
  52.5 13.4 %collective-permute-start.16 = (bf16[128,2048]{1,0:T(8,128)(2,1)S(1)}, bf16[128,2048]{1,0:T(8,128)(2,1)S(1)}, u32[]{:S(2)}, u32[]{:S(2)}) collective-permute-start(bf16[128,2048]{1,0:T(8,128)(2,1)S(1)} %get-tuple-element.120), channel_id=1, source_target_pairs={{0,2},{2,0},{4,6},{6,4},{1,3},{3,1},{5,7},{7,5},{8,10},{10,8},{12,... | collective-permute-start | bytes 1572872 | tf_op jit(solution)/shard_map/ppermute | solution.py:40
  64.3 19.9 %collective-permute-start.15 = (bf16[256,2048]{1,0:T(8,128)(2,1)S(1)}, bf16[256,2048]{1,0:T(8,128)(2,1)S(1)}, u32[]{:S(2)}, u32[]{:S(2)}) collective-permute-start(bf16[256,2048]{1,0:T(8,128)(2,1)S(1)} %constant_dynamic-update-slice_fusion.28.refs_0_), channel_id=1, source_target_pairs={{0,2},{2,0},{4,6},{6,4},{1,3},{3,1},{5,7},{7,5},{8,10},{10,8},{12,... | collective-permute-start | bytes 3145736 | tf_op jit(solution)/shard_map/ppermute | solution.py:40
  66.0 18.3 %collective-permute-start.17 = (bf16[256,2048]{1,0:T(8,128)(2,1)S(1)}, bf16[256,2048]{1,0:T(8,128)(2,1)S(1)}, u32[]{:S(2)}, u32[]{:S(2)}) collective-permute-start(bf16[256,2048]{1,0:T(8,128)(2,1)S(1)} %constant_dynamic-update-slice_fusion.32.refs_2_), channel_id=1, source_target_pairs={{0,6},{2,4},{4,2},{6,0},{1,7},{3,5},{5,3},{7,1},{8,14},{10,12},{12... | collective-permute-start | bytes 3145736 | tf_op jit(solution)/shard_map/ppermute | solution.py:40
  71.0 19.2 %collective-permute-start.12 = (bf16[256,1024]{1,0:T(8,128)(2,1)S(1)}, bf16[256,1024]{1,0:T(8,128)(2,1)S(1)}, u32[]{:S(2)}, u32[]{:S(2)}) collective-permute-start(bf16[256,1024]{1,0:T(8,128)(2,1)S(1)} %constant_dynamic-update-slice_fusion.20.refs_0_), channel_id=1, source_target_pairs={{0,64},{64,0},{128,192},{192,128},{1,65},{65,1},{129,193},{193,129... | collective-permute-start | bytes 1572872 | tf_op jit(solution)/shard_map/ppermute | solution.py:40
  73.3 16.9 %collective-permute-start.18 = (bf16[256,1024]{1,0:T(8,128)(2,1)S(1)}, bf16[256,1024]{1,0:T(8,128)(2,1)S(1)}, u32[]{:S(2)}, u32[]{:S(2)}) collective-permute-start(bf16[256,1024]{1,0:T(8,128)(2,1)S(1)} %constant_dynamic-update-slice_fusion.24.refs_2_), channel_id=1, source_target_pairs={{0,192},{64,128},{128,64},{192,0},{1,193},{65,129},{129,65},{193,1... | collective-permute-start | bytes 1572872 | tf_op jit(solution)/shard_map/ppermute | solution.py:40
  95.4 21.8 %collective-permute-start.19 = (bf16[256,2304]{1,0:T(8,128)(2,1)S(1)}, bf16[256,2304]{1,0:T(8,128)(2,1)S(1)}, u32[]{:S(2)}, u32[]{:S(2)}) collective-permute-start(bf16[256,2304]{1,0:T(8,128)(2,1)S(1)} %get-tuple-element.78), channel_id=1, source_target_pairs={{0,2},{2,0},{4,6},{6,4},{1,3},{3,1},{5,7},{7,5},{8,10},{10,8},{12,... | collective-permute-start | bytes 3538952 | tf_op jit(solution)/shard_map/ppermute | solution.py:40
  98.5 28.9 %collective-permute-start.23 = (bf16[256,2304]{1,0:T(8,128)(2,1)S(1)}, bf16[256,2304]{1,0:T(8,128)(2,1)S(1)}, u32[]{:S(2)}, u32[]{:S(2)}) collective-permute-start(bf16[256,2304]{1,0:T(8,128)(2,1)S(1)} %get-tuple-element.80), channel_id=1, source_target_pairs={{0,6},{2,4},{4,2},{6,0},{1,7},{3,5},{5,3},{7,1},{8,14},{10,12},{12... | collective-permute-start | bytes 3538952 | tf_op jit(solution)/shard_map/ppermute | solution.py:40
  102.0 28.8 %collective-permute-start.22 = (bf16[256,768]{1,0:T(8,128)(2,1)S(1)}, bf16[256,768]{1,0:T(8,128)(2,1)S(1)}, u32[]{:S(2)}, u32[]{:S(2)}) collective-permute-start(bf16[256,768]{1,0:T(8,128)(2,1)S(1)} %get-tuple-element.82), channel_id=1, source_target_pairs={{0,64},{64,0},{128,192},{192,128},{1,65},{65,1},{129,193},{193,129... | collective-permute-start | bytes 1179656 | tf_op jit(solution)/shard_map/ppermute | solution.py:40
  106.2 24.8 %collective-permute-start.21 = (bf16[256,768]{1,0:T(8,128)(2,1)S(1)}, bf16[256,768]{1,0:T(8,128)(2,1)S(1)}, u32[]{:S(2)}, u32[]{:S(2)}) collective-permute-start(bf16[256,768]{1,0:T(8,128)(2,1)S(1)} %get-tuple-element.85), channel_id=1, source_target_pairs={{0,192},{64,128},{128,64},{192,0},{1,193},{65,129},{129,65},{193,1... | collective-permute-start | bytes 1179656 | tf_op jit(solution)/shard_map/ppermute | solution.py:40
  117.5 18.4 %collective-permute-start.20 = (bf16[128,2304]{1,0:T(8,128)(2,1)S(1)}, bf16[128,2304]{1,0:T(8,128)(2,1)S(1)}, u32[]{:S(2)}, u32[]{:S(2)}) collective-permute-start(bf16[128,2304]{1,0:T(8,128)(2,1)S(1)} %get-tuple-element.101), channel_id=1, source_target_pairs={{0,6},{2,4},{4,2},{6,0},{1,7},{3,5},{5,3},{7,1},{8,14},{10,12},{12... | collective-permute-start | bytes 1769480 | tf_op jit(solution)/shard_map/ppermute | solution.py:40
  130.9 12.4 %collective-permute-start.26 = (bf16[128,768]{1,0:T(8,128)(2,1)S(1)}, bf16[128,768]{1,0:T(8,128)(2,1)S(1)}, u32[]{:S(2)}, u32[]{:S(2)}) collective-permute-start(bf16[128,768]{1,0:T(8,128)(2,1)S(1)} %get-tuple-element.108), channel_id=1, source_target_pairs={{0,192},{64,128},{128,64},{192,0},{1,193},{65,129},{129,65},{193,1... | collective-permute-start | bytes 589832 | tf_op jit(solution)/shard_map/ppermute | solution.py:40
  131.1 18.4 %collective-permute-start.25 = (bf16[128,768]{1,0:T(8,128)(2,1)S(1)}, bf16[128,768]{1,0:T(8,128)(2,1)S(1)}, u32[]{:S(2)}, u32[]{:S(2)}) collective-permute-start(bf16[128,768]{1,0:T(8,128)(2,1)S(1)} %get-tuple-element.110), channel_id=1, source_target_pairs={{0,64},{64,0},{128,192},{192,128},{1,65},{65,1},{129,193},{193,129... | collective-permute-start | bytes 589832 | tf_op jit(solution)/shard_map/ppermute | solution.py:40
  136.1 14.7 %collective-permute-start.24 = (bf16[64,2304]{1,0:T(8,128)(2,1)S(1)}, bf16[64,2304]{1,0:T(8,128)(2,1)S(1)}, u32[]{:S(2)}, u32[]{:S(2)}) collective-permute-start(bf16[64,2304]{1,0:T(8,128)(2,1)S(1)} %get-tuple-element.105), channel_id=1, source_target_pairs={{0,192},{64,128},{128,64},{192,0},{1,193},{65,129},{129,65},{193,1... | collective-permute-start | bytes 884744 | tf_op jit(solution)/shard_map/ppermute | solution.py:40
  138.8 17.6 %collective-permute-start.28 = (bf16[64,2304]{1,0:T(8,128)(2,1)S(1)}, bf16[64,2304]{1,0:T(8,128)(2,1)S(1)}, u32[]{:S(2)}, u32[]{:S(2)}) collective-permute-start(bf16[64,2304]{1,0:T(8,128)(2,1)S(1)} %get-tuple-element.104), channel_id=1, source_target_pairs={{0,64},{64,0},{128,192},{192,128},{1,65},{65,1},{129,193},{193,129... | collective-permute-start | bytes 884744 | tf_op jit(solution)/shard_map/ppermute | solution.py:40
  143.4 15.7 %collective-permute-start.29 = (bf16[64,768]{1,0:T(8,128)(2,1)S(1)}, bf16[64,768]{1,0:T(8,128)(2,1)S(1)}, u32[]{:S(2)}, u32[]{:S(2)}) collective-permute-start(bf16[64,768]{1,0:T(8,128)(2,1)S(1)} %get-tuple-element.118), channel_id=1, source_target_pairs={{0,6},{2,4},{4,2},{6,0},{1,7},{3,5},{5,3},{7,1},{8,14},{10,12},{12... | collective-permute-start | bytes 294920 | tf_op jit(solution)/shard_map/ppermute | solution.py:40
  150.8 14.3 %collective-permute-start.31 = (bf16[32,2304]{1,0:T(8,128)(2,1)S(1)}, bf16[32,2304]{1,0:T(8,128)(2,1)S(1)}, u32[]{:S(2)}, u32[]{:S(2)}) collective-permute-start(bf16[32,2304]{1,0:T(8,128)(2,1)S(1)} %get-tuple-element.113), channel_id=1, source_target_pairs={{0,64},{64,0},{128,192},{192,128},{1,65},{65,1},{129,193},{193,129... | collective-permute-start | bytes 442376 | tf_op jit(solution)/shard_map/ppermute | solution.py:40
  (19 other events, 186.5 us)

commit v7 on v6

--- a/solution.py
+++ b/solution.py
@@ -22,7 +22,7 @@
 OUT_CHAINS = tuple(
     (start, size, order)
     for (start, size), (_, _, order) in zip(
-        ((0, 2304), (3072, 2304), (2304, 768), (5376, 768)), CHAINS
+        ((0, 2048), (3072, 2048), (2048, 1024), (5120, 1024)), CHAINS
     )
 )
 CANON = ("xa", "xb", "za", "zb")
@@ -105,7 +105,7 @@
 
 
 PART = 1024
-OUT_PART = 768
+OUT_PART = 1024
 
 
 def pick(table, i):
@@ -183,7 +183,14 @@
     return hit(row, column).astype(jnp.bfloat16)
 
 
-def place_kernel(routes, weights, tokens, gain, folded, combine):
+def place_kernel(*refs):
+    folded, combine = refs[4:6]
+    routes, weights, tokens, gain = refs[6:10]
+    copies = [pltpu.make_async_copy(refs[i], refs[6 + i], refs[10].at[i]) for i in range(4)]
+    for copy in copies:
+        copy.start()
+    for copy in copies:
+        copy.wait()
     f32 = jnp.float32
     count, width = tokens.shape
     half = width // 2
@@ -258,14 +265,15 @@
         out[:, columns] = total.astype(out.dtype)
 
 
-def small(kernel, out_shape, *args, scalars=0, name):
-    vmem, smem = pl.BlockSpec(memory_space=pltpu.VMEM), pl.BlockSpec(memory_space=pltpu.SMEM)
+def small(kernel, out_shape, *args, space=pltpu.VMEM, scratch=(), limit=16, name):
+    vmem = pl.BlockSpec(memory_space=pltpu.VMEM)
     return pl.pallas_call(
         kernel,
         out_shape=out_shape,
-        in_specs=[smem] * scalars + [vmem] * (len(args) - scalars),
+        in_specs=[pl.BlockSpec(memory_space=space)] * len(args),
         out_specs=jax.tree.map(lambda _: vmem, out_shape),
-        compiler_params=pltpu.CompilerParams(vmem_limit_bytes=16 << 20),
+        scratch_shapes=scratch,
+        compiler_params=pltpu.CompilerParams(vmem_limit_bytes=limit << 20),
         name=name,
     )(*args)
 
@@ -290,7 +298,15 @@
         route_weights.T,
         tokens,
         norm_gain.reshape(1, width),
-        scalars=2,
+        space=pltpu.HBM,
+        scratch=[
+            pltpu.SMEM((2, count), jnp.int32),
+            pltpu.SMEM((2, count), jnp.float32),
+            pltpu.VMEM((count, width), bf16),
+            pltpu.VMEM((1, width), jnp.float32),
+            pltpu.SemaphoreType.DMA((4,)),
+        ],
+        limit=60,
         name="place",
     )
     folded = swap_experts(folded)

time: 179 us -> 183 us (1.022)
  blocking collectives: 26.7 us -> 34.9 us
  starting transfers between devices: 66.2 us -> 61 us
  Pallas kernels: 17 us -> 20.2 us
  local copies, waits for them, and re-layouts: 3.42 us -> 0.43 us
    all_to_all x2, blocking collectives: 26.7 us -> 34.9 us  [swap_experts(): lax.all_to_all(blocks, ('zl', 'y'), split_axis=0, concat_axis=0, tiled=True)]
    ppermute x35, starting transfers between devices: 66.2 us -> 61 us  [trade(): return lax.ppermute(value, axis, [(i, i ^ mask) for i in range(n)])]
    unnamed x25 -> x19, local copies, waits for them, and re-layouts: 3.29 us -> 0.29 us
    pallas_call x2, Pallas kernels: 9.01 us -> 11.6 us  [hidden_units(): pl.pallas_call(functools.partial(hidden_kernel, chains, first, last), gri...]
  transfers between devices with their start and end apart: 35 -> 35, of which waited for: 17 -> 16; matrix products, arithmetic and copies ran while one was open for 1% -> 1% of each run, Pallas kernels for 6% -> 7%
where the time goes in v7:
time: 183 us; the launch traced here: 182 us
  waiting for transfers between devices  63.7 us (35%)
  starting transfers between devices  61 us (33%)
  blocking collectives  34.9 us (19%)
  Pallas kernels  20.2 us (11%)
    ppermute x35, waiting for transfers between devices, trade(): return lax.ppermute(value, axis, [(i, i ^ mask) for i in range(n)])  63.7 us
    ppermute x35, starting transfers between devices, trade(): return lax.ppermute(value, axis, [(i, i ^ mask) for i in range(n)])  61 us
    all_to_all x2, blocking collectives, swap_experts(): lax.all_to_all(blocks, ('zl', 'y'), split_axis=0, concat_axis=0, tiled=True)  34.9 us
    pallas_call x2, Pallas kernels, hidden_units(): pl.pallas_call(functools.partial(hidden_kernel, chains, first, last), gri...  11.6 us
    pallas_call x4, Pallas kernels, expert_out(): pl.pallas_call(functools.partial(out_kernel, order), grid=(size // OUT_PA...  4.88 us
    pallas_call x4, Pallas kernels, small(): pl.pallas_call(kernel, out_shape=out_shape, in_specs=[pl.BlockSpec(memory...  3.79 us
  transfers between devices with their start and end apart: 35, of which 16 were waited for; matrix products, arithmetic and copies ran while one was open for 1% of the time, Pallas kernels for 7%

profile of v7, /device:TPU:2, one launch (start us, length us, event | category | flops | bytes accessed | tf_op | source)
XLA Modules:
  0.0 182.4 jit_solution(11569806790009544304)
XLA Ops:
  2.6 15.2 %all_to_all.10 = bf16[8,8,3072]{2,1,0:T(8,128)(2,1)S(1)} all-to-all(bf16[8,8,3072]{2,1,0:T(8,128)(2,1)} %bitcast.24), channel_id=1, replica_groups=mesh['dp'=4,'zl'=2,'y'=4,'x'=4,'c'=2] {'zl','y'}, dimensions={0} | all-to-all | bytes 786432 | tf_op jit(solution)/shard_map/all_to_all | solution.py:283
  18.1 3.3 %collective-permute-start.6 = (bf16[32,2048]{1,0:T(8,128)(2,1)S(1)}, bf16[32,2048]{1,0:T(8,128)(2,1)S(1)}, u32[]{:S(2)}, u32[]{:S(2)}) collective-permute-start(bf16[32,2048]{1,0:T(8,128)(2,1)S(1)} %get-tuple-element.57), channel_id=1, source_target_pairs={{0,64},{64,0},{128,192},{192,128},{1,65},{65,1},{129,193},{193,129... | collective-permute-start | bytes 393224 | tf_op jit(solution)/shard_map/ppermute | solution.py:40
  21.5 3.7 %collective-permute-start.5 = (bf16[32,2048]{1,0:T(8,128)(2,1)S(1)}, bf16[32,2048]{1,0:T(8,128)(2,1)S(1)}, u32[]{:S(2)}, u32[]{:S(2)}) collective-permute-start(bf16[32,2048]{1,0:T(8,128)(2,1)S(1)} %get-tuple-element.56), channel_id=1, source_target_pairs={{0,192},{64,128},{128,64},{192,0},{1,193},{65,129},{129,65},{193,1... | collective-permute-start | bytes 393224 | tf_op jit(solution)/shard_map/ppermute | solution.py:40
  35.3 4.1 %collective-permute-start.8 = (bf16[128,1024]{1,0:T(8,128)(2,1)S(1)}, bf16[128,1024]{1,0:T(8,128)(2,1)S(1)}, u32[]{:S(2)}, u32[]{:S(2)}) collective-permute-start(bf16[128,1024]{1,0:T(8,128)(2,1)S(1)} %get-tuple-element.141), channel_id=1, source_target_pairs={{0,192},{64,128},{128,64},{192,0},{1,193},{65,129},{129,65},{193,1... | collective-permute-start | bytes 786440 | tf_op jit(solution)/shard_map/ppermute | solution.py:40
  41.0 9.2 %collective-permute-done.10 = bf16[64,2048]{1,0:T(8,128)(2,1)S(1)} collective-permute-done((bf16[64,2048]{1,0:T(8,128)(2,1)S(1)}, bf16[64,2048]{1,0:T(8,128)(2,1)S(1)}, u32[]{:S(2)}, u32[]{:S(2)}) %collective-permute-start.10) | collective-permute-done | bytes 262176 | tf_op jit(solution)/shard_map/ppermute | solution.py:40
  52.1 3.4 %collective-permute-done.8 = bf16[128,1024]{1,0:T(8,128)(2,1)S(1)} collective-permute-done((bf16[128,1024]{1,0:T(8,128)(2,1)S(1)}, bf16[128,1024]{1,0:T(8,128)(2,1)S(1)}, u32[]{:S(2)}, u32[]{:S(2)}) %collective-permute-start.8) | collective-permute-done | bytes 262176 | tf_op jit(solution)/shard_map/ppermute | solution.py:40
  56.0 6.5 %collective-permute-done.13 = bf16[128,2048]{1,0:T(8,128)(2,1)S(1)} collective-permute-done((bf16[128,2048]{1,0:T(8,128)(2,1)S(1)}, bf16[128,2048]{1,0:T(8,128)(2,1)S(1)}, u32[]{:S(2)}, u32[]{:S(2)}) %collective-permute-start.13) | collective-permute-done | bytes 524320 | tf_op jit(solution)/shard_map/ppermute | solution.py:40
  62.8 3.8 %collective-permute-done.16 = bf16[128,2048]{1,0:T(8,128)(2,1)S(1)} collective-permute-done((bf16[128,2048]{1,0:T(8,128)(2,1)S(1)}, bf16[128,2048]{1,0:T(8,128)(2,1)S(1)}, u32[]{:S(2)}, u32[]{:S(2)}) %collective-permute-start.16) | collective-permute-done | bytes 524320 | tf_op jit(solution)/shard_map/ppermute | solution.py:40
  66.7 2.5 %collective-permute-start.17 = (bf16[256,2048]{1,0:T(8,128)(2,1)S(1)}, bf16[256,2048]{1,0:T(8,128)(2,1)S(1)}, u32[]{:S(2)}, u32[]{:S(2)}) collective-permute-start(bf16[256,2048]{1,0:T(8,128)(2,1)S(1)} %constant_dynamic-update-slice_fusion.32.refs_2_), channel_id=1, source_target_pairs={{0,6},{2,4},{4,2},{6,0},{1,7},{3,5},{5,3},{7,1},{8,14},{10,12},{12... | collective-permute-start | bytes 3145736 | tf_op jit(solution)/shard_map/ppermute | solution.py:40
  69.2 2.5 %collective-permute-start.12 = (bf16[256,1024]{1,0:T(8,128)(2,1)S(1)}, bf16[256,1024]{1,0:T(8,128)(2,1)S(1)}, u32[]{:S(2)}, u32[]{:S(2)}) collective-permute-start(bf16[256,1024]{1,0:T(8,128)(2,1)S(1)} %constant_dynamic-update-slice_fusion.20.refs_0_), channel_id=1, source_target_pairs={{0,64},{64,0},{128,192},{192,128},{1,65},{65,1},{129,193},{193,129... | collective-permute-start | bytes 1572872 | tf_op jit(solution)/shard_map/ppermute | solution.py:40
  72.4 11.3 %collective-permute-done.15.refs_1_ = bf16[256,2048]{1,0:T(8,128)(2,1)S(1)} collective-permute-done((bf16[256,2048]{1,0:T(8,128)(2,1)S(1)}, bf16[256,2048]{1,0:T(8,128)(2,1)S(1)}, u32[]{:S(2)}, u32[]{:S(2)}) %collective-permute-start.15) | collective-permute-done | bytes 1048608 | tf_op jit(solution)/shard_map/ppermute | solution.py:40
  83.7 7.1 %hidden.2.refs_8_ = f32[4,512,256]{2,1,0:T(8,128)S(1)} custom-call(bf16[256,2048]{1,0:T(8,128)(2,1)S(1)} %constant_dynamic-update-slice_fusion.28.refs_0_, bf16[256,2048]{1,0:T(8,128)(2,1)S(1)} %collective-permute-done.15.refs_1_, bf16[256,2048]{1,0:T(8,128)(2,1)S(1)} %constant_dynamic-update-slice_fusion.32.refs_2_, ...), custom_call_target="tpu_custom_call" | custom-call | tf_op jit(solution)/shard_map/hidden/pallas_call | solution.py:141
  90.9 4.5 %hidden.3 = bf16[512,512]{1,0:T(8,128)(2,1)S(1)} custom-call(bf16[256,1024]{1,0:T(8,128)(2,1)S(1)} %constant_dynamic-update-slice_fusion.20.refs_0_, bf16[256,1024]{1,0:T(8,128)(2,1)S(1)} %collective-permute-done.12.refs_1_, bf16[256,1024]{1,0:T(8,128)(2,1)S(1)} %constant_dynamic-update-slice_fusion.24.refs_2_, ...), custom_call_target="tpu_custom_call" | custom-call | flops 2147483648 | bytes 6291456 | tf_op jit(solution)/shard_map/hidden/pallas_call | solution.py:141
  98.9 2.7 %collective-permute-start.23 = (bf16[256,2048]{1,0:T(8,128)(2,1)S(1)}, bf16[256,2048]{1,0:T(8,128)(2,1)S(1)}, u32[]{:S(2)}, u32[]{:S(2)}) collective-permute-start(bf16[256,2048]{1,0:T(8,128)(2,1)S(1)} %get-tuple-element.80), channel_id=1, source_target_pairs={{0,6},{2,4},{4,2},{6,0},{1,7},{3,5},{5,3},{7,1},{8,14},{10,12},{12... | collective-permute-start | bytes 3145736 | tf_op jit(solution)/shard_map/ppermute | solution.py:40
  102.4 3.7 %collective-permute-start.22 = (bf16[256,1024]{1,0:T(8,128)(2,1)S(1)}, bf16[256,1024]{1,0:T(8,128)(2,1)S(1)}, u32[]{:S(2)}, u32[]{:S(2)}) collective-permute-start(bf16[256,1024]{1,0:T(8,128)(2,1)S(1)} %get-tuple-element.82), channel_id=1, source_target_pairs={{0,64},{64,0},{128,192},{192,128},{1,65},{65,1},{129,193},{193,129... | collective-permute-start | bytes 1572872 | tf_op jit(solution)/shard_map/ppermute | solution.py:40
  107.5 9.8 %collective-permute-done.19 = bf16[256,2048]{1,0:T(8,128)(2,1)S(1)} collective-permute-done((bf16[256,2048]{1,0:T(8,128)(2,1)S(1)}, bf16[256,2048]{1,0:T(8,128)(2,1)S(1)}, u32[]{:S(2)}, u32[]{:S(2)}) %collective-permute-start.19) | collective-permute-done | bytes 1048608 | tf_op jit(solution)/shard_map/ppermute | solution.py:40
  120.0 4.2 %collective-permute-done.23 = bf16[256,2048]{1,0:T(8,128)(2,1)S(1)} collective-permute-done((bf16[256,2048]{1,0:T(8,128)(2,1)S(1)}, bf16[256,2048]{1,0:T(8,128)(2,1)S(1)}, u32[]{:S(2)}, u32[]{:S(2)}) %collective-permute-start.23) | collective-permute-done | bytes 1048608 | tf_op jit(solution)/shard_map/ppermute | solution.py:40
  124.6 3.2 %collective-permute-start.27 = (bf16[128,2048]{1,0:T(8,128)(2,1)S(1)}, bf16[128,2048]{1,0:T(8,128)(2,1)S(1)}, u32[]{:S(2)}, u32[]{:S(2)}) collective-permute-start(bf16[128,2048]{1,0:T(8,128)(2,1)S(1)} %get-tuple-element.100), channel_id=1, source_target_pairs={{0,2},{2,0},{4,6},{6,4},{1,3},{3,1},{5,7},{7,5},{8,10},{10,8},{12,... | collective-permute-start | bytes 1572872 | tf_op jit(solution)/shard_map/ppermute | solution.py:40
  129.9 3.5 %collective-permute-start.25 = (bf16[128,1024]{1,0:T(8,128)(2,1)S(1)}, bf16[128,1024]{1,0:T(8,128)(2,1)S(1)}, u32[]{:S(2)}, u32[]{:S(2)}) collective-permute-start(bf16[128,1024]{1,0:T(8,128)(2,1)S(1)} %get-tuple-element.108), channel_id=1, source_target_pairs={{0,64},{64,0},{128,192},{192,128},{1,65},{65,1},{129,193},{193,129... | collective-permute-start | bytes 786440 | tf_op jit(solution)/shard_map/ppermute | solution.py:40
  136.8 6.4 %collective-permute-done.26 = bf16[128,1024]{1,0:T(8,128)(2,1)S(1)} collective-permute-done((bf16[128,1024]{1,0:T(8,128)(2,1)S(1)}, bf16[128,1024]{1,0:T(8,128)(2,1)S(1)}, u32[]{:S(2)}, u32[]{:S(2)}) %collective-permute-start.26) | collective-permute-done | bytes 262176 | tf_op jit(solution)/shard_map/ppermute | solution.py:40
  143.3 3.7 %collective-permute-start.29 = (bf16[64,1024]{1,0:T(8,128)(2,1)S(1)}, bf16[64,1024]{1,0:T(8,128)(2,1)S(1)}, u32[]{:S(2)}, u32[]{:S(2)}) collective-permute-start(bf16[64,1024]{1,0:T(8,128)(2,1)S(1)} %get-tuple-element.116), channel_id=1, source_target_pairs={{0,6},{2,4},{4,2},{6,0},{1,7},{3,5},{5,3},{7,1},{8,14},{10,12},{12... | collective-permute-start | bytes 393224 | tf_op jit(solution)/shard_map/ppermute | solution.py:40
  147.8 3.7 %collective-permute-start.31 = (bf16[32,2048]{1,0:T(8,128)(2,1)S(1)}, bf16[32,2048]{1,0:T(8,128)(2,1)S(1)}, u32[]{:S(2)}, u32[]{:S(2)}) collective-permute-start(bf16[32,2048]{1,0:T(8,128)(2,1)S(1)} %get-tuple-element.117), channel_id=1, source_target_pairs={{0,64},{64,0},{128,192},{192,128},{1,65},{65,1},{129,193},{193,129... | collective-permute-start | bytes 393224 | tf_op jit(solution)/shard_map/ppermute | solution.py:40
  153.5 2.8 %collective-permute-start.32 = (bf16[32,2048]{1,0:T(8,128)(2,1)S(1)}, bf16[32,2048]{1,0:T(8,128)(2,1)S(1)}, u32[]{:S(2)}, u32[]{:S(2)}) collective-permute-start(bf16[32,2048]{1,0:T(8,128)(2,1)S(1)} %get-tuple-element.113), channel_id=1, source_target_pairs={{0,192},{64,128},{128,64},{192,0},{1,193},{65,129},{129,65},{193,1... | collective-permute-start | bytes 393224 | tf_op jit(solution)/shard_map/ppermute | solution.py:40
  161.6 19.8 %all_to_all.11 = bf16[8,8,3072]{2,1,0:T(8,128)(2,1)S(1)} all-to-all(bf16[8,8,3072]{2,1,0:T(8,128)(2,1)S(1)} %bitcast.23), channel_id=1, replica_groups=mesh['dp'=4,'zl'=2,'y'=4,'x'=4,'c'=2] {'zl','y'}, dimensions={0} | all-to-all | bytes 786432 | tf_op jit(solution)/shard_map/all_to_all | solution.py:283
  (94 shorter events, 41.4 us)
Async XLA Ops:
  0.0 17.8 %collective-permute-start.2 = (bf16[256,6144]{1,0:T(8,128)(2,1)}, bf16[256,6144]{1,0:T(8,128)(2,1)S(1)}, u32[]{:S(2)}, u32[]{:S(2)}) collective-permute-start(bf16[256,6144]{1,0:T(8,128)(2,1)} %bitcast.10), channel_id=1, source_target_pairs={{0,1},{1,0},{2,3},{3,2},{4,5},{5,4},{6,7},{7,6},{8,9},{9,8},{10,11... | collective-permute-start | bytes 9437192 | tf_op jit(solution)/shard_map/ppermute | solution.py:40
  0.0 17.8 %collective-permute-start = (bf16[6144,256]{1,0:T(8,128)(2,1)}, bf16[6144,256]{1,0:T(8,128)(2,1)}, u32[]{:S(2)}, u32[]{:S(2)}) collective-permute-start(bf16[6144,256]{1,0:T(8,128)(2,1)} %bitcast.15), channel_id=1, source_target_pairs={{0,1},{1,0},{2,3},{3,2},{4,5},{5,4},{6,7},{7,6},{8,9},{9,8},{10,11... | collective-permute-start | bytes 9437192 | tf_op jit(solution)/shard_map/ppermute | solution.py:40
  0.5 17.3 %collective-permute-start.1 = (bf16[6144,256]{1,0:T(8,128)(2,1)}, bf16[6144,256]{1,0:T(8,128)(2,1)}, u32[]{:S(2)}, u32[]{:S(2)}) collective-permute-start(bf16[6144,256]{1,0:T(8,128)(2,1)} %bitcast.18), channel_id=1, source_target_pairs={{0,1},{1,0},{2,3},{3,2},{4,5},{5,4},{6,7},{7,6},{8,9},{9,8},{10,11... | collective-permute-start | bytes 9437192 | tf_op jit(solution)/shard_map/ppermute | solution.py:40
  18.1 15.3 %collective-permute-start.6 = (bf16[32,2048]{1,0:T(8,128)(2,1)S(1)}, bf16[32,2048]{1,0:T(8,128)(2,1)S(1)}, u32[]{:S(2)}, u32[]{:S(2)}) collective-permute-start(bf16[32,2048]{1,0:T(8,128)(2,1)S(1)} %get-tuple-element.57), channel_id=1, source_target_pairs={{0,64},{64,0},{128,192},{192,128},{1,65},{65,1},{129,193},{193,129... | collective-permute-start | bytes 393224 | tf_op jit(solution)/shard_map/ppermute | solution.py:40
  33.5 16.7 %collective-permute-start.10 = (bf16[64,2048]{1,0:T(8,128)(2,1)S(1)}, bf16[64,2048]{1,0:T(8,128)(2,1)S(1)}, u32[]{:S(2)}, u32[]{:S(2)}) collective-permute-start(bf16[64,2048]{1,0:T(8,128)(2,1)S(1)} %get-tuple-element.137), channel_id=1, source_target_pairs={{0,192},{64,128},{128,64},{192,0},{1,193},{65,129},{129,65},{193,1... | collective-permute-start | bytes 786440 | tf_op jit(solution)/shard_map/ppermute | solution.py:40
  33.9 18.1 %collective-permute-start.9 = (bf16[64,2048]{1,0:T(8,128)(2,1)S(1)}, bf16[64,2048]{1,0:T(8,128)(2,1)S(1)}, u32[]{:S(2)}, u32[]{:S(2)}) collective-permute-start(bf16[64,2048]{1,0:T(8,128)(2,1)S(1)} %get-tuple-element.129), channel_id=1, source_target_pairs={{0,64},{64,0},{128,192},{192,128},{1,65},{65,1},{129,193},{193,129... | collective-permute-start | bytes 786440 | tf_op jit(solution)/shard_map/ppermute | solution.py:40
  35.3 20.2 %collective-permute-start.8 = (bf16[128,1024]{1,0:T(8,128)(2,1)S(1)}, bf16[128,1024]{1,0:T(8,128)(2,1)S(1)}, u32[]{:S(2)}, u32[]{:S(2)}) collective-permute-start(bf16[128,1024]{1,0:T(8,128)(2,1)S(1)} %get-tuple-element.141), channel_id=1, source_target_pairs={{0,192},{64,128},{128,64},{192,0},{1,193},{65,129},{129,65},{193,1... | collective-permute-start | bytes 786440 | tf_op jit(solution)/shard_map/ppermute | solution.py:40
  39.5 16.6 %collective-permute-start.14 = (bf16[128,1024]{1,0:T(8,128)(2,1)S(1)}, bf16[128,1024]{1,0:T(8,128)(2,1)S(1)}, u32[]{:S(2)}, u32[]{:S(2)}) collective-permute-start(bf16[128,1024]{1,0:T(8,128)(2,1)S(1)} %get-tuple-element.134), channel_id=1, source_target_pairs={{0,64},{64,0},{128,192},{192,128},{1,65},{65,1},{129,193},{193,129... | collective-permute-start | bytes 786440 | tf_op jit(solution)/shard_map/ppermute | solution.py:40
  52.0 14.6 %collective-permute-start.16 = (bf16[128,2048]{1,0:T(8,128)(2,1)S(1)}, bf16[128,2048]{1,0:T(8,128)(2,1)S(1)}, u32[]{:S(2)}, u32[]{:S(2)}) collective-permute-start(bf16[128,2048]{1,0:T(8,128)(2,1)S(1)} %get-tuple-element.124), channel_id=1, source_target_pairs={{0,2},{2,0},{4,6},{6,4},{1,3},{3,1},{5,7},{7,5},{8,10},{10,8},{12,... | collective-permute-start | bytes 1572872 | tf_op jit(solution)/shard_map/ppermute | solution.py:40
  62.6 21.1 %collective-permute-start.15 = (bf16[256,2048]{1,0:T(8,128)(2,1)S(1)}, bf16[256,2048]{1,0:T(8,128)(2,1)S(1)}, u32[]{:S(2)}, u32[]{:S(2)}) collective-permute-start(bf16[256,2048]{1,0:T(8,128)(2,1)S(1)} %constant_dynamic-update-slice_fusion.28.refs_0_), channel_id=1, source_target_pairs={{0,2},{2,0},{4,6},{6,4},{1,3},{3,1},{5,7},{7,5},{8,10},{10,8},{12,... | collective-permute-start | bytes 3145736 | tf_op jit(solution)/shard_map/ppermute | solution.py:40
  66.7 17.1 %collective-permute-start.17 = (bf16[256,2048]{1,0:T(8,128)(2,1)S(1)}, bf16[256,2048]{1,0:T(8,128)(2,1)S(1)}, u32[]{:S(2)}, u32[]{:S(2)}) collective-permute-start(bf16[256,2048]{1,0:T(8,128)(2,1)S(1)} %constant_dynamic-update-slice_fusion.32.refs_2_), channel_id=1, source_target_pairs={{0,6},{2,4},{4,2},{6,0},{1,7},{3,5},{5,3},{7,1},{8,14},{10,12},{12... | collective-permute-start | bytes 3145736 | tf_op jit(solution)/shard_map/ppermute | solution.py:40
  69.2 21.7 %collective-permute-start.12 = (bf16[256,1024]{1,0:T(8,128)(2,1)S(1)}, bf16[256,1024]{1,0:T(8,128)(2,1)S(1)}, u32[]{:S(2)}, u32[]{:S(2)}) collective-permute-start(bf16[256,1024]{1,0:T(8,128)(2,1)S(1)} %constant_dynamic-update-slice_fusion.20.refs_0_), channel_id=1, source_target_pairs={{0,64},{64,0},{128,192},{192,128},{1,65},{65,1},{129,193},{193,129... | collective-permute-start | bytes 1572872 | tf_op jit(solution)/shard_map/ppermute | solution.py:40
  71.7 19.2 %collective-permute-start.18 = (bf16[256,1024]{1,0:T(8,128)(2,1)S(1)}, bf16[256,1024]{1,0:T(8,128)(2,1)S(1)}, u32[]{:S(2)}, u32[]{:S(2)}) collective-permute-start(bf16[256,1024]{1,0:T(8,128)(2,1)S(1)} %constant_dynamic-update-slice_fusion.24.refs_2_), channel_id=1, source_target_pairs={{0,192},{64,128},{128,64},{192,0},{1,193},{65,129},{129,65},{193,1... | collective-permute-start | bytes 1572872 | tf_op jit(solution)/shard_map/ppermute | solution.py:40
  97.1 20.2 %collective-permute-start.19 = (bf16[256,2048]{1,0:T(8,128)(2,1)S(1)}, bf16[256,2048]{1,0:T(8,128)(2,1)S(1)}, u32[]{:S(2)}, u32[]{:S(2)}) collective-permute-start(bf16[256,2048]{1,0:T(8,128)(2,1)S(1)} %get-tuple-element.78), channel_id=1, source_target_pairs={{0,2},{2,0},{4,6},{6,4},{1,3},{3,1},{5,7},{7,5},{8,10},{10,8},{12,... | collective-permute-start | bytes 3145736 | tf_op jit(solution)/shard_map/ppermute | solution.py:40
  98.9 25.3 %collective-permute-start.23 = (bf16[256,2048]{1,0:T(8,128)(2,1)S(1)}, bf16[256,2048]{1,0:T(8,128)(2,1)S(1)}, u32[]{:S(2)}, u32[]{:S(2)}) collective-permute-start(bf16[256,2048]{1,0:T(8,128)(2,1)S(1)} %get-tuple-element.80), channel_id=1, source_target_pairs={{0,6},{2,4},{4,2},{6,0},{1,7},{3,5},{5,3},{7,1},{8,14},{10,12},{12... | collective-permute-start | bytes 3145736 | tf_op jit(solution)/shard_map/ppermute | solution.py:40
  102.4 25.5 %collective-permute-start.22 = (bf16[256,1024]{1,0:T(8,128)(2,1)S(1)}, bf16[256,1024]{1,0:T(8,128)(2,1)S(1)}, u32[]{:S(2)}, u32[]{:S(2)}) collective-permute-start(bf16[256,1024]{1,0:T(8,128)(2,1)S(1)} %get-tuple-element.82), channel_id=1, source_target_pairs={{0,64},{64,0},{128,192},{192,128},{1,65},{65,1},{129,193},{193,129... | collective-permute-start | bytes 1572872 | tf_op jit(solution)/shard_map/ppermute | solution.py:40
  106.7 22.9 %collective-permute-start.21 = (bf16[256,1024]{1,0:T(8,128)(2,1)S(1)}, bf16[256,1024]{1,0:T(8,128)(2,1)S(1)}, u32[]{:S(2)}, u32[]{:S(2)}) collective-permute-start(bf16[256,1024]{1,0:T(8,128)(2,1)S(1)} %get-tuple-element.85), channel_id=1, source_target_pairs={{0,192},{64,128},{128,64},{192,0},{1,193},{65,129},{129,65},{193,1... | collective-permute-start | bytes 1572872 | tf_op jit(solution)/shard_map/ppermute | solution.py:40
  117.7 15.7 %collective-permute-start.20 = (bf16[128,2048]{1,0:T(8,128)(2,1)S(1)}, bf16[128,2048]{1,0:T(8,128)(2,1)S(1)}, u32[]{:S(2)}, u32[]{:S(2)}) collective-permute-start(bf16[128,2048]{1,0:T(8,128)(2,1)S(1)} %get-tuple-element.101), channel_id=1, source_target_pairs={{0,6},{2,4},{4,2},{6,0},{1,7},{3,5},{5,3},{7,1},{8,14},{10,12},{12... | collective-permute-start | bytes 1572872 | tf_op jit(solution)/shard_map/ppermute | solution.py:40
  128.1 15.1 %collective-permute-start.26 = (bf16[128,1024]{1,0:T(8,128)(2,1)S(1)}, bf16[128,1024]{1,0:T(8,128)(2,1)S(1)}, u32[]{:S(2)}, u32[]{:S(2)}) collective-permute-start(bf16[128,1024]{1,0:T(8,128)(2,1)S(1)} %get-tuple-element.106), channel_id=1, source_target_pairs={{0,192},{64,128},{128,64},{192,0},{1,193},{65,129},{129,65},{193,1... | collective-permute-start | bytes 786440 | tf_op jit(solution)/shard_map/ppermute | solution.py:40
  129.9 17.6 %collective-permute-start.25 = (bf16[128,1024]{1,0:T(8,128)(2,1)S(1)}, bf16[128,1024]{1,0:T(8,128)(2,1)S(1)}, u32[]{:S(2)}, u32[]{:S(2)}) collective-permute-start(bf16[128,1024]{1,0:T(8,128)(2,1)S(1)} %get-tuple-element.108), channel_id=1, source_target_pairs={{0,64},{64,0},{128,192},{192,128},{1,65},{65,1},{129,193},{193,129... | collective-permute-start | bytes 786440 | tf_op jit(solution)/shard_map/ppermute | solution.py:40
  133.5 14.2 %collective-permute-start.24 = (bf16[64,2048]{1,0:T(8,128)(2,1)S(1)}, bf16[64,2048]{1,0:T(8,128)(2,1)S(1)}, u32[]{:S(2)}, u32[]{:S(2)}) collective-permute-start(bf16[64,2048]{1,0:T(8,128)(2,1)S(1)} %get-tuple-element.109), channel_id=1, source_target_pairs={{0,192},{64,128},{128,64},{192,0},{1,193},{65,129},{129,65},{193,1... | collective-permute-start | bytes 786440 | tf_op jit(solution)/shard_map/ppermute | solution.py:40
  135.2 18.3 %collective-permute-start.28 = (bf16[64,2048]{1,0:T(8,128)(2,1)S(1)}, bf16[64,2048]{1,0:T(8,128)(2,1)S(1)}, u32[]{:S(2)}, u32[]{:S(2)}) collective-permute-start(bf16[64,2048]{1,0:T(8,128)(2,1)S(1)} %get-tuple-element.104), channel_id=1, source_target_pairs={{0,64},{64,0},{128,192},{192,128},{1,65},{65,1},{129,193},{193,129... | collective-permute-start | bytes 786440 | tf_op jit(solution)/shard_map/ppermute | solution.py:40
  143.3 13.0 %collective-permute-start.29 = (bf16[64,1024]{1,0:T(8,128)(2,1)S(1)}, bf16[64,1024]{1,0:T(8,128)(2,1)S(1)}, u32[]{:S(2)}, u32[]{:S(2)}) collective-permute-start(bf16[64,1024]{1,0:T(8,128)(2,1)S(1)} %get-tuple-element.116), channel_id=1, source_target_pairs={{0,6},{2,4},{4,2},{6,0},{1,7},{3,5},{5,3},{7,1},{8,14},{10,12},{12... | collective-permute-start | bytes 393224 | tf_op jit(solution)/shard_map/ppermute | solution.py:40
  147.8 13.4 %collective-permute-start.31 = (bf16[32,2048]{1,0:T(8,128)(2,1)S(1)}, bf16[32,2048]{1,0:T(8,128)(2,1)S(1)}, u32[]{:S(2)}, u32[]{:S(2)}) collective-permute-start(bf16[32,2048]{1,0:T(8,128)(2,1)S(1)} %get-tuple-element.117), channel_id=1, source_target_pairs={{0,64},{64,0},{128,192},{192,128},{1,65},{65,1},{129,193},{193,129... | collective-permute-start | bytes 393224 | tf_op jit(solution)/shard_map/ppermute | solution.py:40
  (16 other events, 281.5 us)

commit v8 on v7

--- a/solution.py
+++ b/solution.py
@@ -17,14 +17,9 @@
     (0, 2048, ("za", "zb", "xb", "xa")),
     (3072, 2048, ("zb", "za", "xa", "xb")),
     (2048, 1024, ("xa", "xb", "zb", "za")),
-    (5120, 1024, ("xb", "xa", "za", "zb")),
+    (5120, 1024, ("xa", "xb", "za", "zb")),
 )
-OUT_CHAINS = tuple(
-    (start, size, order)
-    for (start, size), (_, _, order) in zip(
-        ((0, 2048), (3072, 2048), (2048, 1024), (5120, 1024)), CHAINS
-    )
-)
+JOINED = ((0,), (1,), (2, 3))
 CANON = ("xa", "xb", "za", "zb")
 UNIT = 32
 HALF = 8 * UNIT
@@ -105,7 +100,6 @@
 
 
 PART = 1024
-OUT_PART = 1024
 
 
 def pick(table, i):
@@ -156,17 +150,17 @@
 
 
 def expert_out(hidden, wd0, wd1, chain):
-    start, size, order = OUT_CHAINS[chain]
+    start, size, order = CHAINS[chain]
     units = wd0.shape[0]
-    low, count = start // OUT_PART, 2 * HALF
+    low, count = start // PART, 2 * HALF
     shape = jax.ShapeDtypeStruct((HALF, size), jnp.bfloat16)
     return pl.pallas_call(
         functools.partial(out_kernel, order),
-        grid=(size // OUT_PART,),
+        grid=(size // PART,),
         out_shape=[shape] * 2,
         in_specs=[pl.BlockSpec((count, 2 * units), lambda i: (0, 0))]
-        + [pl.BlockSpec((units, OUT_PART), lambda i: (0, low + i))] * 2,
-        out_specs=[pl.BlockSpec((HALF, OUT_PART), lambda i: (0, i))] * 2,
+        + [pl.BlockSpec((units, PART), lambda i: (0, low + i))] * 2,
+        out_specs=[pl.BlockSpec((HALF, PART), lambda i: (0, i))] * 2,
         compiler_params=pltpu.CompilerParams(vmem_limit_bytes=24 << 20),
         cost_estimate=pl.CostEstimate(
             flops=4 * count * size * units,
@@ -224,12 +218,18 @@
 
 def unfold_kernel(folded, *outs):
     half = folded.shape[1]
+    sides = []
     for side in range(2):
         take = onehot(UNIT, 2 * UNIT, lambda r, c: c == (r // 4) * 8 + r % 4 + 4 * side)
         rows = jnp.dot(take, folded[...], preferred_element_type=jnp.float32)
-        for out, (start, size, _) in zip(outs, CHAINS):
-            if start // half == side:
-                out[...] = rows[:, start - side * half : start - side * half + size].astype(out.dtype)
+        sides.append(rows.astype(folded.dtype))
+    for out, joined in zip(outs, JOINED):
+        at = 0
+        for c in joined:
+            start, size, _ = CHAINS[c]
+            low = start % half
+            out[:, at : at + size] = sides[start // half][:, low : low + size]
+            at += size
 
 
 def fold_kernel(*refs):
@@ -237,7 +237,7 @@
     held, came, folded = refs[:n], refs[n : 2 * n], refs[2 * n]
     half = folded.shape[1]
     f32 = jnp.float32
-    for c, (start, size, _) in enumerate(OUT_CHAINS):
+    for c, (start, size, _) in enumerate(CHAINS):
         total = (held[c][...].astype(f32) + came[c][...].astype(f32)).astype(folded.dtype)
         side = start // half
         give = onehot(2 * UNIT, UNIT, lambda r, c: r == (c // 4) * 8 + c % 4 + 4 * side)
@@ -288,7 +288,6 @@
     bf16 = jnp.bfloat16
     count, width = tokens.shape
     wg0, wu0, wd0 = w_gate[0], w_up[0], w_down[0]
-    wg1, wu1, wd1 = (trade(w, "c") for w in (wg0, wu0, wd0))
 
     folded_shape = jax.ShapeDtypeStruct((64, width // 2), bf16)
     folded, combine = small(
@@ -309,20 +308,37 @@
         limit=60,
         name="place",
     )
+    wg1, wu1, wd1 = (trade(after(w, folded), "c") for w in (wg0, wu0, wd0))
     folded = swap_experts(folded)
-    folded, wg1, wu1, wd1 = lax.optimization_barrier((folded, wg1, wu1, wd1))
-    heads = [jax.ShapeDtypeStruct((UNIT, size), bf16) for _, size, _ in CHAINS]
+    folded, wg1, wu1 = lax.optimization_barrier((folded, wg1, wu1))
+    heads = [
+        jax.ShapeDtypeStruct((UNIT, sum(CHAINS[c][1] for c in joined)), bf16) for joined in JOINED
+    ]
     held = list(small(unfold_kernel, heads, folded, name="unfold"))
 
     last = None
-    for step in range(4):
-        came = [trade(h, order[step]) for h, (_, _, order) in zip(held, CHAINS)]
-        if step == 3:
-            break
-        for j in (2, 3, 0, 1):
+    for step in range(2):
+        came = [trade(h, CHAINS[joined[0]][2][step]) for h, joined in zip(held, JOINED)]
+        for k in (2, 0, 1):
             if last is not None:
-                came[j] = after(came[j], last)
-            held[j] = last = jnp.concatenate([held[j], came[j]], axis=0)
+                came[k] = after(came[k], last)
+            if (step, k) == (0, 1):
+                came[k], wd1 = lax.optimization_barrier((came[k], wd1))
+            if (step, k) == (1, 2):
+                size = CHAINS[2][1]
+                both = [
+                    jnp.concatenate([held[k][:, at], came[k][:, at]], axis=0)
+                    for at in (slice(0, size), slice(size, 2 * size))
+                ]
+                last = both[1]
+            else:
+                held[k] = last = jnp.concatenate([held[k], came[k]], axis=0)
+    held = held[:2] + both
+    came = [trade(h, order[2]) for h, (_, _, order) in zip(held, CHAINS)]
+    for j in (2, 3, 0, 1):
+        came[j] = after(came[j], last)
+        held[j] = last = jnp.concatenate([held[j], came[j]], axis=0)
+    came = [trade(h, order[3]) for h, (_, _, order) in zip(held, CHAINS)]
     weights = (wg0, wu0, wg1, wu1)
     came[0] = after(came[0], last)
     came[1] = after(came[1], came[0])
@@ -337,15 +353,26 @@
         held[j], away[j] = expert_out(hidden if last is None else after(hidden, last), wd0, wd1, j)
         last = away[j]
     last = None
-    for step in (3, 2, 1, 0):
+    for step in (3, 2):
         came = [trade(a, order[step]) for a, (_, _, order) in zip(away, CHAINS)]
-        if not step:
-            break
         half = held[0].shape[0] // 2
         for j in range(4):
             got = came[j] if last is None else after(came[j], last)
             away[j] = last = add(held[j][half:], got[half:])
             held[j] = add(held[j][:half], got[:half])
+    join = lambda values: values[:2] + [jnp.concatenate(values[2:], axis=1)]
+    held, away = join(held), join(away)
+    last = None
+    came = [trade(a, CHAINS[joined[0]][2][1]) for a, joined in zip(away, JOINED)]
+    half = held[0].shape[0] // 2
+    for k in range(3):
+        got = came[k] if last is None else after(came[k], last)
+        away[k] = last = add(held[k][half:], got[half:])
+        held[k] = add(held[k][:half], got[:half])
+    size = CHAINS[2][1]
+    part = lambda values: values[:2] + [values[2][:, :size], values[2][:, size:]]
+    held, away = part(held), part(away)
+    came = [trade(a, order[0]) for a, (_, _, order) in zip(away, CHAINS)]
 
     folded = small(fold_kernel, folded_shape, *held, *came, name="fold")
     back = swap_experts(folded)

time: 183 us -> 176 us (0.962)
  blocking collectives: 34.9 us -> 26.8 us
  waiting for transfers between devices: 63.7 us -> 66.7 us
  Pallas kernels: 20.2 us -> 17.7 us
    all_to_all x2, blocking collectives: 34.9 us -> 26.8 us  [swap_experts(): lax.all_to_all(blocks, ('zl', 'y'), split_axis=0, concat_axis=0, tiled=True)]
    ppermute x35 -> x32, waiting for transfers between devices: 63.7 us -> 66.7 us  [trade(): return lax.ppermute(value, axis, [(i, i ^ mask) for i in range(n)])]
    pallas_call x2, Pallas kernels: 11.6 us -> 9.01 us  [hidden_units(): pl.pallas_call(functools.partial(hidden_kernel, chains, first, last), gri...]
    ppermute x35 -> x32, starting transfers between devices: 61 us -> 61.8 us  [trade(): return lax.ppermute(value, axis, [(i, i ^ mask) for i in range(n)])]
  transfers between devices with their start and end apart: 35 -> 32, of which waited for: 16 -> 15; matrix products, arithmetic and copies ran while one was open for 1% -> 1% of each run, Pallas kernels for 7% -> 5%
where the time goes in v8:
time: 176 us
  waiting for transfers between devices  66.7 us (38%)
  starting transfers between devices  61.8 us (35%)
  blocking collectives  26.8 us (15%)
  Pallas kernels  17.7 us (10%)
  other arithmetic  1.82 us (1%)
    ppermute x32, waiting for transfers between devices, trade(): return lax.ppermute(value, axis, [(i, i ^ mask) for i in range(n)])  66.7 us
    ppermute x32, starting transfers between devices, trade(): return lax.ppermute(value, axis, [(i, i ^ mask) for i in range(n)])  61.8 us
    all_to_all x2, blocking collectives, swap_experts(): lax.all_to_all(blocks, ('zl', 'y'), split_axis=0, concat_axis=0, tiled=True)  26.8 us
    pallas_call x2, Pallas kernels, hidden_units(): pl.pallas_call(functools.partial(hidden_kernel, chains, first, last), gri...  9.01 us
    pallas_call x4, Pallas kernels, expert_out(): pl.pallas_call(functools.partial(out_kernel, order), grid=(size // PART,)...  4.87 us
    pallas_call x4, Pallas kernels, small(): pl.pallas_call(kernel, out_shape=out_shape, in_specs=[pl.BlockSpec(memory...  3.8 us
  transfers between devices with their start and end apart: 32, of which 15 were waited for; matrix products, arithmetic and copies ran while one was open for 1% of the time, Pallas kernels for 5%

profile of v8, /device:TPU:2, one launch (start us, length us, event | category | flops | bytes accessed | tf_op | source)
XLA Modules:
  0.0 175.6 jit_solution(198521282878212139)
XLA Ops:
  2.8 15.1 %all_to_all.10 = bf16[8,8,3072]{2,1,0:T(8,128)(2,1)S(1)} all-to-all(bf16[8,8,3072]{2,1,0:T(8,128)(2,1)} %bitcast.24), channel_id=1, replica_groups=mesh['dp'=4,'zl'=2,'y'=4,'x'=4,'c'=2] {'zl','y'}, dimensions={0} | all-to-all | bytes 786432 | tf_op jit(solution)/shard_map/all_to_all | solution.py:283
  18.8 3.3 %collective-permute-start.5 = (bf16[32,2048]{1,0:T(8,128)(2,1)S(1)}, bf16[32,2048]{1,0:T(8,128)(2,1)S(1)}, u32[]{:S(2)}, u32[]{:S(2)}) collective-permute-start(bf16[32,2048]{1,0:T(8,128)(2,1)S(1)} %get-tuple-element.58), channel_id=1, source_target_pairs={{0,64},{64,0},{128,192},{192,128},{1,65},{65,1},{129,193},{193,129... | collective-permute-start | bytes 393224 | tf_op jit(solution)/shard_map/ppermute | solution.py:35
  22.1 3.6 %collective-permute-start.4 = (bf16[32,2048]{1,0:T(8,128)(2,1)S(1)}, bf16[32,2048]{1,0:T(8,128)(2,1)S(1)}, u32[]{:S(2)}, u32[]{:S(2)}) collective-permute-start(bf16[32,2048]{1,0:T(8,128)(2,1)S(1)} %get-tuple-element.57), channel_id=1, source_target_pairs={{0,192},{64,128},{128,64},{192,0},{1,193},{65,129},{129,65},{193,1... | collective-permute-start | bytes 393224 | tf_op jit(solution)/shard_map/ppermute | solution.py:35
  28.1 3.5 %collective-permute-start.9 = (bf16[64,2048]{1,0:T(8,128)(2,1)S(1)}, bf16[64,2048]{1,0:T(8,128)(2,1)S(1)}, u32[]{:S(2)}, u32[]{:S(2)}) collective-permute-start(bf16[64,2048]{1,0:T(8,128)(2,1)S(1)} %get-tuple-element.139), channel_id=1, source_target_pairs={{0,192},{64,128},{128,64},{192,0},{1,193},{65,129},{129,65},{193,1... | collective-permute-start | bytes 786440 | tf_op jit(solution)/shard_map/ppermute | solution.py:35
  35.5 4.4 %collective-permute-done.9 = bf16[64,2048]{1,0:T(8,128)(2,1)S(1)} collective-permute-done((bf16[64,2048]{1,0:T(8,128)(2,1)S(1)}, bf16[64,2048]{1,0:T(8,128)(2,1)S(1)}, u32[]{:S(2)}, u32[]{:S(2)}) %collective-permute-start.9) | collective-permute-done | bytes 262176 | tf_op jit(solution)/shard_map/ppermute | solution.py:35
  42.3 10.2 %collective-permute-done.8 = bf16[64,2048]{1,0:T(8,128)(2,1)S(1)} collective-permute-done((bf16[64,2048]{1,0:T(8,128)(2,1)S(1)}, bf16[64,2048]{1,0:T(8,128)(2,1)S(1)}, u32[]{:S(2)}, u32[]{:S(2)}) %collective-permute-start.8) | collective-permute-done | bytes 262176 | tf_op jit(solution)/shard_map/ppermute | solution.py:35
  54.1 7.4 %collective-permute-done.7 = bf16[128,1024]{1,0:T(8,128)(2,1)S(1)} collective-permute-done((bf16[128,1024]{1,0:T(8,128)(2,1)S(1)}, bf16[128,1024]{1,0:T(8,128)(2,1)S(1)}, u32[]{:S(2)}, u32[]{:S(2)}) %collective-permute-start.7) | collective-permute-done | bytes 262176 | tf_op jit(solution)/shard_map/ppermute | solution.py:35
  63.1 4.3 %collective-permute-done.14 = bf16[128,2048]{1,0:T(8,128)(2,1)S(1)} collective-permute-done((bf16[128,2048]{1,0:T(8,128)(2,1)S(1)}, bf16[128,2048]{1,0:T(8,128)(2,1)S(1)}, u32[]{:S(2)}, u32[]{:S(2)}) %collective-permute-start.14) | collective-permute-done | bytes 524320 | tf_op jit(solution)/shard_map/ppermute | solution.py:35
  68.7 4.2 %collective-permute-start.16 = (bf16[256,1024]{1,0:T(8,128)(2,1)S(1)}, bf16[256,1024]{1,0:T(8,128)(2,1)S(1)}, u32[]{:S(2)}, u32[]{:S(2)}) collective-permute-start(bf16[256,1024]{1,0:T(8,128)(2,1)S(1)} %pad_maximum_fusion.1.refs_2_), channel_id=1, source_target_pairs={{0,192},{64,128},{128,64},{192,0},{1,193},{65,129},{129,65},{193,1... | collective-permute-start | bytes 1572872 | tf_op jit(solution)/shard_map/ppermute | solution.py:35
  72.9 10.1 %collective-permute-done.13.refs_1_ = bf16[256,2048]{1,0:T(8,128)(2,1)S(1)} collective-permute-done((bf16[256,2048]{1,0:T(8,128)(2,1)S(1)}, bf16[256,2048]{1,0:T(8,128)(2,1)S(1)}, u32[]{:S(2)}, u32[]{:S(2)}) %collective-permute-start.13) | collective-permute-done | bytes 1048608 | tf_op jit(solution)/shard_map/ppermute | solution.py:35
  83.0 5.9 %hidden.2.refs_8_ = f32[4,512,256]{2,1,0:T(8,128)S(1)} custom-call(bf16[256,2048]{1,0:T(8,128)(2,1)S(1)} %constant_dynamic-update-slice_fusion.12.refs_0_, bf16[256,2048]{1,0:T(8,128)(2,1)S(1)} %collective-permute-done.13.refs_1_, bf16[256,2048]{1,0:T(8,128)(2,1)S(1)} %constant_dynamic-update-slice_fusion.16.refs_2_, ...), custom_call_target="tpu_custom_call" | custom-call | tf_op jit(solution)/shard_map/hidden/pallas_call | solution.py:135
  89.0 3.1 %hidden.3 = bf16[512,512]{1,0:T(8,128)(2,1)S(1)} custom-call(bf16[256,1024]{1,0:T(8,128)(2,1)S(1)} %pad_maximum_fusion.refs_0_, bf16[256,1024]{1,0:T(8,128)(2,1)S(1)} %collective-permute-done.10.refs_1_, bf16[256,1024]{1,0:T(8,128)(2,1)S(1)} %pad_maximum_fusion.1.refs_2_, bf16[256,1024]{1,0:T(8,128)(2,1)S(1)} %collective-permute-done.16.refs_3_, ...), custom_call_target="tpu_custom_call" | custom-call | flops 2147483648 | bytes 6291456 | tf_op jit(solution)/shard_map/hidden/pallas_call | solution.py:135
  99.8 2.8 %collective-permute-start.20 = (bf16[256,1024]{1,0:T(8,128)(2,1)S(1)}, bf16[256,1024]{1,0:T(8,128)(2,1)S(1)}, u32[]{:S(2)}, u32[]{:S(2)}) collective-permute-start(bf16[256,1024]{1,0:T(8,128)(2,1)S(1)} %get-tuple-element.82), channel_id=1, source_target_pairs={{0,64},{64,0},{128,192},{192,128},{1,65},{65,1},{129,193},{193,129... | collective-permute-start | bytes 1572872 | tf_op jit(solution)/shard_map/ppermute | solution.py:35
  103.3 3.6 %collective-permute-start.19 = (bf16[256,1024]{1,0:T(8,128)(2,1)S(1)}, bf16[256,1024]{1,0:T(8,128)(2,1)S(1)}, u32[]{:S(2)}, u32[]{:S(2)}) collective-permute-start(bf16[256,1024]{1,0:T(8,128)(2,1)S(1)} %get-tuple-element.85), channel_id=1, source_target_pairs={{0,192},{64,128},{128,64},{192,0},{1,193},{65,129},{129,65},{193,1... | collective-permute-start | bytes 1572872 | tf_op jit(solution)/shard_map/ppermute | solution.py:35
  106.9 7.1 %collective-permute-done.17 = bf16[256,2048]{1,0:T(8,128)(2,1)S(1)} collective-permute-done((bf16[256,2048]{1,0:T(8,128)(2,1)S(1)}, bf16[256,2048]{1,0:T(8,128)(2,1)S(1)}, u32[]{:S(2)}, u32[]{:S(2)}) %collective-permute-start.17) | collective-permute-done | bytes 1048608 | tf_op jit(solution)/shard_map/ppermute | solution.py:35
  115.8 5.1 %collective-permute-done.21 = bf16[256,2048]{1,0:T(8,128)(2,1)S(1)} collective-permute-done((bf16[256,2048]{1,0:T(8,128)(2,1)S(1)}, bf16[256,2048]{1,0:T(8,128)(2,1)S(1)}, u32[]{:S(2)}, u32[]{:S(2)}) %collective-permute-start.21) | collective-permute-done | bytes 1048608 | tf_op jit(solution)/shard_map/ppermute | solution.py:35
  123.3 2.4 %collective-permute-start.25 = (bf16[128,1024]{1,0:T(8,128)(2,1)S(1)}, bf16[128,1024]{1,0:T(8,128)(2,1)S(1)}, u32[]{:S(2)}, u32[]{:S(2)}) collective-permute-start(bf16[128,1024]{1,0:T(8,128)(2,1)S(1)} %get-tuple-element.104), channel_id=1, source_target_pairs={{0,192},{64,128},{128,64},{192,0},{1,193},{65,129},{129,65},{193,1... | collective-permute-start | bytes 786440 | tf_op jit(solution)/shard_map/ppermute | solution.py:35
  125.7 4.1 %collective-permute-done.19 = bf16[256,1024]{1,0:T(8,128)(2,1)S(1)} collective-permute-done((bf16[256,1024]{1,0:T(8,128)(2,1)S(1)}, bf16[256,1024]{1,0:T(8,128)(2,1)S(1)}, u32[]{:S(2)}, u32[]{:S(2)}) %collective-permute-start.19) | collective-permute-done | bytes 524320 | tf_op jit(solution)/shard_map/ppermute | solution.py:35
  130.0 2.3 %collective-permute-start.26 = (bf16[128,1024]{1,0:T(8,128)(2,1)S(1)}, bf16[128,1024]{1,0:T(8,128)(2,1)S(1)}, u32[]{:S(2)}, u32[]{:S(2)}) collective-permute-start(bf16[128,1024]{1,0:T(8,128)(2,1)S(1)} %get-tuple-element.102), channel_id=1, source_target_pairs={{0,64},{64,0},{128,192},{192,128},{1,65},{65,1},{129,193},{193,129... | collective-permute-start | bytes 786440 | tf_op jit(solution)/shard_map/ppermute | solution.py:35
  134.0 6.0 %collective-permute-start.24 = (bf16[64,2048]{1,0:T(8,128)(2,1)S(1)}, bf16[64,2048]{1,0:T(8,128)(2,1)S(1)}, u32[]{:S(2)}, u32[]{:S(2)}) collective-permute-start(bf16[64,2048]{1,0:T(8,128)(2,1)S(1)} %get-tuple-element.105), channel_id=1, source_target_pairs={{0,64},{64,0},{128,192},{192,128},{1,65},{65,1},{129,193},{193,129... | collective-permute-start | bytes 786440 | tf_op jit(solution)/shard_map/ppermute | solution.py:35
  141.5 4.7 %collective-permute-done.26 = bf16[128,1024]{1,0:T(8,128)(2,1)S(1)} collective-permute-done((bf16[128,1024]{1,0:T(8,128)(2,1)S(1)}, bf16[128,1024]{1,0:T(8,128)(2,1)S(1)}, u32[]{:S(2)}, u32[]{:S(2)}) %collective-permute-start.26) | collective-permute-done | bytes 262176 | tf_op jit(solution)/shard_map/ppermute | solution.py:35
  148.7 2.9 %collective-permute-start.28 = (bf16[32,2048]{1,0:T(8,128)(2,1)S(1)}, bf16[32,2048]{1,0:T(8,128)(2,1)S(1)}, u32[]{:S(2)}, u32[]{:S(2)}) collective-permute-start(bf16[32,2048]{1,0:T(8,128)(2,1)S(1)} %get-tuple-element.117), channel_id=1, source_target_pairs={{0,64},{64,0},{128,192},{192,128},{1,65},{65,1},{129,193},{193,129... | collective-permute-start | bytes 393224 | tf_op jit(solution)/shard_map/ppermute | solution.py:35
  153.0 3.3 %collective-permute-start.29 = (bf16[32,2048]{1,0:T(8,128)(2,1)S(1)}, bf16[32,2048]{1,0:T(8,128)(2,1)S(1)}, u32[]{:S(2)}, u32[]{:S(2)}) collective-permute-start(bf16[32,2048]{1,0:T(8,128)(2,1)S(1)} %get-tuple-element.111), channel_id=1, source_target_pairs={{0,192},{64,128},{128,64},{192,0},{1,193},{65,129},{129,65},{193,1... | collective-permute-start | bytes 393224 | tf_op jit(solution)/shard_map/ppermute | solution.py:35
  162.8 11.7 %all_to_all.11 = bf16[8,8,3072]{2,1,0:T(8,128)(2,1)S(1)} all-to-all(bf16[8,8,3072]{2,1,0:T(8,128)(2,1)S(1)} %bitcast.23), channel_id=1, replica_groups=mesh['dp'=4,'zl'=2,'y'=4,'x'=4,'c'=2] {'zl','y'}, dimensions={0} | all-to-all | bytes 786432 | tf_op jit(solution)/shard_map/all_to_all | solution.py:283
  (92 shorter events, 44.2 us)
Async XLA Ops:
  2.1 15.8 %collective-permute-start = (bf16[6144,256]{1,0:T(8,128)(2,1)}, bf16[6144,256]{1,0:T(8,128)(2,1)S(1)}, u32[]{:S(2)}, u32[]{:S(2)}) collective-permute-start(bf16[6144,256]{1,0:T(8,128)(2,1)} %bitcast.15), channel_id=1, source_target_pairs={{0,1},{1,0},{2,3},{3,2},{4,5},{5,4},{6,7},{7,6},{8,9},{9,8},{10,11... | collective-permute-start | bytes 9437192 | tf_op jit(solution)/shard_map/ppermute | solution.py:35
  2.2 15.7 %collective-permute-start.1 = (bf16[6144,256]{1,0:T(8,128)(2,1)}, bf16[6144,256]{1,0:T(8,128)(2,1)S(1)}, u32[]{:S(2)}, u32[]{:S(2)}) collective-permute-start(bf16[6144,256]{1,0:T(8,128)(2,1)} %bitcast.18), channel_id=1, source_target_pairs={{0,1},{1,0},{2,3},{3,2},{4,5},{5,4},{6,7},{7,6},{8,9},{9,8},{10,11... | collective-permute-start | bytes 9437192 | tf_op jit(solution)/shard_map/ppermute | solution.py:35
  2.7 29.6 %collective-permute-start.6 = (bf16[256,6144]{1,0:T(8,128)(2,1)}, bf16[256,6144]{1,0:T(8,128)(2,1)S(1)}, u32[]{:S(2)}, u32[]{:S(2)}) collective-permute-start(bf16[256,6144]{1,0:T(8,128)(2,1)} %bitcast.10), channel_id=1, source_target_pairs={{0,1},{1,0},{2,3},{3,2},{4,5},{5,4},{6,7},{7,6},{8,9},{9,8},{10,11... | collective-permute-start | bytes 9437192 | tf_op jit(solution)/shard_map/ppermute | solution.py:35
  22.1 10.2 %collective-permute-start.4 = (bf16[32,2048]{1,0:T(8,128)(2,1)S(1)}, bf16[32,2048]{1,0:T(8,128)(2,1)S(1)}, u32[]{:S(2)}, u32[]{:S(2)}) collective-permute-start(bf16[32,2048]{1,0:T(8,128)(2,1)S(1)} %get-tuple-element.57), channel_id=1, source_target_pairs={{0,192},{64,128},{128,64},{192,0},{1,193},{65,129},{129,65},{193,1... | collective-permute-start | bytes 393224 | tf_op jit(solution)/shard_map/ppermute | solution.py:35
  28.1 11.9 %collective-permute-start.9 = (bf16[64,2048]{1,0:T(8,128)(2,1)S(1)}, bf16[64,2048]{1,0:T(8,128)(2,1)S(1)}, u32[]{:S(2)}, u32[]{:S(2)}) collective-permute-start(bf16[64,2048]{1,0:T(8,128)(2,1)S(1)} %get-tuple-element.139), channel_id=1, source_target_pairs={{0,192},{64,128},{128,64},{192,0},{1,193},{65,129},{129,65},{193,1... | collective-permute-start | bytes 786440 | tf_op jit(solution)/shard_map/ppermute | solution.py:35
  32.3 20.1 %collective-permute-start.8 = (bf16[64,2048]{1,0:T(8,128)(2,1)S(1)}, bf16[64,2048]{1,0:T(8,128)(2,1)S(1)}, u32[]{:S(2)}, u32[]{:S(2)}) collective-permute-start(bf16[64,2048]{1,0:T(8,128)(2,1)S(1)} %get-tuple-element.133), channel_id=1, source_target_pairs={{0,64},{64,0},{128,192},{192,128},{1,65},{65,1},{129,193},{193,129... | collective-permute-start | bytes 786440 | tf_op jit(solution)/shard_map/ppermute | solution.py:35
  33.7 27.8 %collective-permute-start.12 = (bf16[128,1024]{1,0:T(8,128)(2,1)S(1)}, bf16[128,1024]{1,0:T(8,128)(2,1)S(1)}, u32[]{:S(2)}, u32[]{:S(2)}) collective-permute-start(bf16[128,1024]{1,0:T(8,128)(2,1)S(1)} %pad_maximum_fusion.3), channel_id=1, source_target_pairs={{0,64},{64,0},{128,192},{192,128},{1,65},{65,1},{129,193},{193,129... | collective-permute-start | bytes 786440 | tf_op jit(solution)/shard_map/ppermute | solution.py:35
  40.0 21.5 %collective-permute-start.11 = (bf16[128,2048]{1,0:T(8,128)(2,1)S(1)}, bf16[128,2048]{1,0:T(8,128)(2,1)S(1)}, u32[]{:S(2)}, u32[]{:S(2)}) collective-permute-start(bf16[128,2048]{1,0:T(8,128)(2,1)S(1)} %get-tuple-element.122), channel_id=1, source_target_pairs={{0,6},{2,4},{4,2},{6,0},{1,7},{3,5},{5,3},{7,1},{8,14},{10,12},{12... | collective-permute-start | bytes 1572872 | tf_op jit(solution)/shard_map/ppermute | solution.py:35
  52.5 14.9 %collective-permute-start.14 = (bf16[128,2048]{1,0:T(8,128)(2,1)S(1)}, bf16[128,2048]{1,0:T(8,128)(2,1)S(1)}, u32[]{:S(2)}, u32[]{:S(2)}) collective-permute-start(bf16[128,2048]{1,0:T(8,128)(2,1)S(1)} %get-tuple-element.120), channel_id=1, source_target_pairs={{0,2},{2,0},{4,6},{6,4},{1,3},{3,1},{5,7},{7,5},{8,10},{10,8},{12,... | collective-permute-start | bytes 1572872 | tf_op jit(solution)/shard_map/ppermute | solution.py:35
  61.6 21.4 %collective-permute-start.13 = (bf16[256,2048]{1,0:T(8,128)(2,1)S(1)}, bf16[256,2048]{1,0:T(8,128)(2,1)S(1)}, u32[]{:S(2)}, u32[]{:S(2)}) collective-permute-start(bf16[256,2048]{1,0:T(8,128)(2,1)S(1)} %constant_dynamic-update-slice_fusion.12.refs_0_), channel_id=1, source_target_pairs={{0,2},{2,0},{4,6},{6,4},{1,3},{3,1},{5,7},{7,5},{8,10},{10,8},{12,... | collective-permute-start | bytes 3145736 | tf_op jit(solution)/shard_map/ppermute | solution.py:35
  67.4 15.6 %collective-permute-start.15 = (bf16[256,2048]{1,0:T(8,128)(2,1)S(1)}, bf16[256,2048]{1,0:T(8,128)(2,1)S(1)}, u32[]{:S(2)}, u32[]{:S(2)}) collective-permute-start(bf16[256,2048]{1,0:T(8,128)(2,1)S(1)} %constant_dynamic-update-slice_fusion.16.refs_2_), channel_id=1, source_target_pairs={{0,6},{2,4},{4,2},{6,0},{1,7},{3,5},{5,3},{7,1},{8,14},{10,12},{12... | collective-permute-start | bytes 3145736 | tf_op jit(solution)/shard_map/ppermute | solution.py:35
  68.7 20.2 %collective-permute-start.10 = (bf16[256,1024]{1,0:T(8,128)(2,1)S(1)}, bf16[256,1024]{1,0:T(8,128)(2,1)S(1)}, u32[]{:S(2)}, u32[]{:S(2)}) collective-permute-start(bf16[256,1024]{1,0:T(8,128)(2,1)S(1)} %pad_maximum_fusion.refs_0_), channel_id=1, source_target_pairs={{0,64},{64,0},{128,192},{192,128},{1,65},{65,1},{129,193},{193,129... | collective-permute-start | bytes 1572872 | tf_op jit(solution)/shard_map/ppermute | solution.py:35
  68.7 20.2 %collective-permute-start.16 = (bf16[256,1024]{1,0:T(8,128)(2,1)S(1)}, bf16[256,1024]{1,0:T(8,128)(2,1)S(1)}, u32[]{:S(2)}, u32[]{:S(2)}) collective-permute-start(bf16[256,1024]{1,0:T(8,128)(2,1)S(1)} %pad_maximum_fusion.1.refs_2_), channel_id=1, source_target_pairs={{0,192},{64,128},{128,64},{192,0},{1,193},{65,129},{129,65},{193,1... | collective-permute-start | bytes 1572872 | tf_op jit(solution)/shard_map/ppermute | solution.py:35
  93.8 20.2 %collective-permute-start.17 = (bf16[256,2048]{1,0:T(8,128)(2,1)S(1)}, bf16[256,2048]{1,0:T(8,128)(2,1)S(1)}, u32[]{:S(2)}, u32[]{:S(2)}) collective-permute-start(bf16[256,2048]{1,0:T(8,128)(2,1)S(1)} %get-tuple-element.78), channel_id=1, source_target_pairs={{0,2},{2,0},{4,6},{6,4},{1,3},{3,1},{5,7},{7,5},{8,10},{10,8},{12,... | collective-permute-start | bytes 3145736 | tf_op jit(solution)/shard_map/ppermute | solution.py:35
  97.7 23.3 %collective-permute-start.21 = (bf16[256,2048]{1,0:T(8,128)(2,1)S(1)}, bf16[256,2048]{1,0:T(8,128)(2,1)S(1)}, u32[]{:S(2)}, u32[]{:S(2)}) collective-permute-start(bf16[256,2048]{1,0:T(8,128)(2,1)S(1)} %get-tuple-element.80), channel_id=1, source_target_pairs={{0,6},{2,4},{4,2},{6,0},{1,7},{3,5},{5,3},{7,1},{8,14},{10,12},{12... | collective-permute-start | bytes 3145736 | tf_op jit(solution)/shard_map/ppermute | solution.py:35
  99.8 23.3 %collective-permute-start.20 = (bf16[256,1024]{1,0:T(8,128)(2,1)S(1)}, bf16[256,1024]{1,0:T(8,128)(2,1)S(1)}, u32[]{:S(2)}, u32[]{:S(2)}) collective-permute-start(bf16[256,1024]{1,0:T(8,128)(2,1)S(1)} %get-tuple-element.82), channel_id=1, source_target_pairs={{0,64},{64,0},{128,192},{192,128},{1,65},{65,1},{129,193},{193,129... | collective-permute-start | bytes 1572872 | tf_op jit(solution)/shard_map/ppermute | solution.py:35
  103.3 26.5 %collective-permute-start.19 = (bf16[256,1024]{1,0:T(8,128)(2,1)S(1)}, bf16[256,1024]{1,0:T(8,128)(2,1)S(1)}, u32[]{:S(2)}, u32[]{:S(2)}) collective-permute-start(bf16[256,1024]{1,0:T(8,128)(2,1)S(1)} %get-tuple-element.85), channel_id=1, source_target_pairs={{0,192},{64,128},{128,64},{192,0},{1,193},{65,129},{129,65},{193,1... | collective-permute-start | bytes 1572872 | tf_op jit(solution)/shard_map/ppermute | solution.py:35
  114.4 17.9 %collective-permute-start.18 = (bf16[128,2048]{1,0:T(8,128)(2,1)S(1)}, bf16[128,2048]{1,0:T(8,128)(2,1)S(1)}, u32[]{:S(2)}, u32[]{:S(2)}) collective-permute-start(bf16[128,2048]{1,0:T(8,128)(2,1)S(1)} %get-tuple-element.99), channel_id=1, source_target_pairs={{0,6},{2,4},{4,2},{6,0},{1,7},{3,5},{5,3},{7,1},{8,14},{10,12},{12... | collective-permute-start | bytes 1572872 | tf_op jit(solution)/shard_map/ppermute | solution.py:35
  121.3 12.5 %collective-permute-start.23 = (bf16[128,2048]{1,0:T(8,128)(2,1)S(1)}, bf16[128,2048]{1,0:T(8,128)(2,1)S(1)}, u32[]{:S(2)}, u32[]{:S(2)}) collective-permute-start(bf16[128,2048]{1,0:T(8,128)(2,1)S(1)} %get-tuple-element.98), channel_id=1, source_target_pairs={{0,2},{2,0},{4,6},{6,4},{1,3},{3,1},{5,7},{7,5},{8,10},{10,8},{12,... | collective-permute-start | bytes 1572872 | tf_op jit(solution)/shard_map/ppermute | solution.py:35
  123.3 18.1 %collective-permute-start.25 = (bf16[128,1024]{1,0:T(8,128)(2,1)S(1)}, bf16[128,1024]{1,0:T(8,128)(2,1)S(1)}, u32[]{:S(2)}, u32[]{:S(2)}) collective-permute-start(bf16[128,1024]{1,0:T(8,128)(2,1)S(1)} %get-tuple-element.104), channel_id=1, source_target_pairs={{0,192},{64,128},{128,64},{192,0},{1,193},{65,129},{129,65},{193,1... | collective-permute-start | bytes 786440 | tf_op jit(solution)/shard_map/ppermute | solution.py:35
  130.0 16.2 %collective-permute-start.26 = (bf16[128,1024]{1,0:T(8,128)(2,1)S(1)}, bf16[128,1024]{1,0:T(8,128)(2,1)S(1)}, u32[]{:S(2)}, u32[]{:S(2)}) collective-permute-start(bf16[128,1024]{1,0:T(8,128)(2,1)S(1)} %get-tuple-element.102), channel_id=1, source_target_pairs={{0,64},{64,0},{128,192},{192,128},{1,65},{65,1},{129,193},{193,129... | collective-permute-start | bytes 786440 | tf_op jit(solution)/shard_map/ppermute | solution.py:35
  132.4 16.2 %collective-permute-start.22 = (bf16[64,2048]{1,0:T(8,128)(2,1)S(1)}, bf16[64,2048]{1,0:T(8,128)(2,1)S(1)}, u32[]{:S(2)}, u32[]{:S(2)}) collective-permute-start(bf16[64,2048]{1,0:T(8,128)(2,1)S(1)} %get-tuple-element.108), channel_id=1, source_target_pairs={{0,192},{64,128},{128,64},{192,0},{1,193},{65,129},{129,65},{193,1... | collective-permute-start | bytes 786440 | tf_op jit(solution)/shard_map/ppermute | solution.py:35
  134.0 18.9 %collective-permute-start.24 = (bf16[64,2048]{1,0:T(8,128)(2,1)S(1)}, bf16[64,2048]{1,0:T(8,128)(2,1)S(1)}, u32[]{:S(2)}, u32[]{:S(2)}) collective-permute-start(bf16[64,2048]{1,0:T(8,128)(2,1)S(1)} %get-tuple-element.105), channel_id=1, source_target_pairs={{0,64},{64,0},{128,192},{192,128},{1,65},{65,1},{129,193},{193,129... | collective-permute-start | bytes 786440 | tf_op jit(solution)/shard_map/ppermute | solution.py:35
  148.7 13.7 %collective-permute-start.28 = (bf16[32,2048]{1,0:T(8,128)(2,1)S(1)}, bf16[32,2048]{1,0:T(8,128)(2,1)S(1)}, u32[]{:S(2)}, u32[]{:S(2)}) collective-permute-start(bf16[32,2048]{1,0:T(8,128)(2,1)S(1)} %get-tuple-element.117), channel_id=1, source_target_pairs={{0,64},{64,0},{128,192},{192,128},{1,65},{65,1},{129,193},{193,129... | collective-permute-start | bytes 393224 | tf_op jit(solution)/shard_map/ppermute | solution.py:35
  (13 other events, 216.9 us)

commit v9 on v8

--- a/solution.py
+++ b/solution.py
@@ -86,17 +86,15 @@
                 total[:, i * units : (i + 1) * units] = value.astype(total.dtype)
 
 
-def out_kernel(order, hidden, wd0, wd1, keep, away):
+def out_kernel(order, sent, hidden, wd0, wd1, out):
     units = wd0.shape[0]
     f32 = jnp.float32
-    total = jnp.dot(hidden[:, :units], wd0[...], preferred_element_type=f32) + jnp.dot(
-        hidden[:, units:], wd1[...], preferred_element_type=f32
+    blocks = [canon_block(order, index + 8 * sent) * UNIT for index in range(8)]
+    rows = jnp.concatenate([hidden[row : row + UNIT, :] for row in blocks], axis=0)
+    total = jnp.dot(rows[:, :units], wd0[...], preferred_element_type=f32) + jnp.dot(
+        rows[:, units:], wd1[...], preferred_element_type=f32
     )
-    total = total.astype(jnp.bfloat16)
-    for index in range(16):
-        row = canon_block(order, index) * UNIT
-        to = (index % 8) * UNIT
-        (keep, away)[index // 8][to : to + UNIT, :] = total[row : row + UNIT]
+    out[...] = total.astype(out.dtype)
 
 
 PART = 1024
@@ -149,22 +147,21 @@
     )(*pieces, *weights, *(() if first else (before,)))
 
 
-def expert_out(hidden, wd0, wd1, chain):
+def expert_out(hidden, wd0, wd1, chain, sent):
     start, size, order = CHAINS[chain]
     units = wd0.shape[0]
     low, count = start // PART, 2 * HALF
-    shape = jax.ShapeDtypeStruct((HALF, size), jnp.bfloat16)
     return pl.pallas_call(
-        functools.partial(out_kernel, order),
+        functools.partial(out_kernel, order, int(sent)),
         grid=(size // PART,),
-        out_shape=[shape] * 2,
+        out_shape=jax.ShapeDtypeStruct((HALF, size), jnp.bfloat16),
         in_specs=[pl.BlockSpec((count, 2 * units), lambda i: (0, 0))]
         + [pl.BlockSpec((units, PART), lambda i: (0, low + i))] * 2,
-        out_specs=[pl.BlockSpec((HALF, PART), lambda i: (0, i))] * 2,
+        out_specs=pl.BlockSpec((HALF, PART), lambda i: (0, i)),
         compiler_params=pltpu.CompilerParams(vmem_limit_bytes=24 << 20),
         cost_estimate=pl.CostEstimate(
-            flops=4 * count * size * units,
-            bytes_accessed=4 * size * units + 2 * count * size,
+            flops=2 * count * size * units,
+            bytes_accessed=4 * size * units + count * size,
             transcendentals=0,
         ),
         name="out",
@@ -321,7 +318,7 @@
         came = [trade(h, CHAINS[joined[0]][2][step]) for h, joined in zip(held, JOINED)]
         for k in (2, 0, 1):
             if last is not None:
-                came[k] = after(came[k], last)
+                came[k] = after(came[k], *(last if isinstance(last, list) else (last,)))
             if (step, k) == (0, 1):
                 came[k], wd1 = lax.optimization_barrier((came[k], wd1))
             if (step, k) == (1, 2):
@@ -330,7 +327,7 @@
                     jnp.concatenate([held[k][:, at], came[k][:, at]], axis=0)
                     for at in (slice(0, size), slice(size, 2 * size))
                 ]
-                last = both[1]
+                last = both
             else:
                 held[k] = last = jnp.concatenate([held[k], came[k]], axis=0)
     held = held[:2] + both
@@ -347,11 +344,13 @@
     came[3] = after(came[3], came[2])
     hidden = hidden_units((held[2], came[2], held[3], came[3]), weights, (2, 3), sums, True)
 
-    held, away = [None] * 4, [None] * 4
-    last = None
+    held, away = [], []
     for j in range(4):
-        held[j], away[j] = expert_out(hidden if last is None else after(hidden, last), wd0, wd1, j)
-        last = away[j]
+        given = after(hidden, away[-1]) if away else hidden
+        away.append(expert_out(given, wd0, wd1, j, True))
+    for j in range(4):
+        given = after(hidden, away[-1], *held[-1:])
+        held.append(expert_out(given, wd0, wd1, j, False))
     last = None
     for step in (3, 2):
         came = [trade(a, order[step]) for a, (_, _, order) in zip(away, CHAINS)]

time: 176 us -> 173 us (0.983)
  waiting for transfers between devices: 66.7 us -> 43.5 us
  starting transfers between devices: 61.8 us -> 79 us
  blocking collectives: 26.8 us -> 28.6 us
    ppermute x32, waiting for transfers between devices: 66.7 us -> 43.5 us  [trade(): return lax.ppermute(value, axis, [(i, i ^ mask) for i in range(n)])]
    ppermute x32, starting transfers between devices: 61.8 us -> 79 us  [trade(): return lax.ppermute(value, axis, [(i, i ^ mask) for i in range(n)])]
    all_to_all x2, blocking collectives: 26.8 us -> 28.6 us  [swap_experts(): lax.all_to_all(blocks, ('zl', 'y'), split_axis=0, concat_axis=0, tiled=True)]
    pallas_call x4 -> x8, Pallas kernels: 4.87 us -> 6.21 us  [expert_out(): pl.pallas_call(functools.partial(out_kernel, order, int(sent)), grid=(siz...]
  transfers between devices with their start and end apart: 32 -> 32, of which waited for: 15 -> 13; matrix products, arithmetic and copies ran while one was open for 1% -> 1% of each run, Pallas kernels for 5% -> 7%
where the time goes in v9:
time: 173 us
  starting transfers between devices  79 us (46%)
  waiting for transfers between devices  43.5 us (25%)
  blocking collectives  28.6 us (17%)
  Pallas kernels  19 us (11%)
  other arithmetic  1.82 us (1%)
    ppermute x32, starting transfers between devices, trade(): return lax.ppermute(value, axis, [(i, i ^ mask) for i in range(n)])  79 us
    ppermute x32, waiting for transfers between devices, trade(): return lax.ppermute(value, axis, [(i, i ^ mask) for i in range(n)])  43.5 us
    all_to_all x2, blocking collectives, swap_experts(): lax.all_to_all(blocks, ('zl', 'y'), split_axis=0, concat_axis=0, tiled=True)  28.6 us
    pallas_call x2, Pallas kernels, hidden_units(): pl.pallas_call(functools.partial(hidden_kernel, chains, first, last), gri...  9.01 us
    pallas_call x8, Pallas kernels, expert_out(): pl.pallas_call(functools.partial(out_kernel, order, int(sent)), grid=(siz...  6.21 us
    pallas_call x4, Pallas kernels, small(): pl.pallas_call(kernel, out_shape=out_shape, in_specs=[pl.BlockSpec(memory...  3.82 us
  transfers between devices with their start and end apart: 32, of which 13 were waited for; matrix products, arithmetic and copies ran while one was open for 1% of the time, Pallas kernels for 7%

profile of v9, /device:TPU:2, one launch (start us, length us, event | category | flops | bytes accessed | tf_op | source)
XLA Modules:
  0.0 172.8 jit_solution(4506891930865393165)
XLA Ops:
  2.8 15.1 %all_to_all.10 = bf16[8,8,3072]{2,1,0:T(8,128)(2,1)S(1)} all-to-all(bf16[8,8,3072]{2,1,0:T(8,128)(2,1)} %bitcast.28), channel_id=1, replica_groups=mesh['dp'=4,'zl'=2,'y'=4,'x'=4,'c'=2] {'zl','y'}, dimensions={0} | all-to-all | bytes 786432 | tf_op jit(solution)/shard_map/all_to_all | solution.py:280
  18.8 3.3 %collective-permute-start.5 = (bf16[32,2048]{1,0:T(8,128)(2,1)S(1)}, bf16[32,2048]{1,0:T(8,128)(2,1)S(1)}, u32[]{:S(2)}, u32[]{:S(2)}) collective-permute-start(bf16[32,2048]{1,0:T(8,128)(2,1)S(1)} %get-tuple-element.54), channel_id=1, source_target_pairs={{0,64},{64,0},{128,192},{192,128},{1,65},{65,1},{129,193},{193,129... | collective-permute-start | bytes 393224 | tf_op jit(solution)/shard_map/ppermute | solution.py:35
  22.1 3.6 %collective-permute-start.4 = (bf16[32,2048]{1,0:T(8,128)(2,1)S(1)}, bf16[32,2048]{1,0:T(8,128)(2,1)S(1)}, u32[]{:S(2)}, u32[]{:S(2)}) collective-permute-start(bf16[32,2048]{1,0:T(8,128)(2,1)S(1)} %get-tuple-element.53), channel_id=1, source_target_pairs={{0,192},{64,128},{128,64},{192,0},{1,193},{65,129},{129,65},{193,1... | collective-permute-start | bytes 393224 | tf_op jit(solution)/shard_map/ppermute | solution.py:35
  28.1 3.5 %collective-permute-start.9 = (bf16[64,2048]{1,0:T(8,128)(2,1)S(1)}, bf16[64,2048]{1,0:T(8,128)(2,1)S(1)}, u32[]{:S(2)}, u32[]{:S(2)}) collective-permute-start(bf16[64,2048]{1,0:T(8,128)(2,1)S(1)} %get-tuple-element.131), channel_id=1, source_target_pairs={{0,192},{64,128},{128,64},{192,0},{1,193},{65,129},{129,65},{193,1... | collective-permute-start | bytes 786440 | tf_op jit(solution)/shard_map/ppermute | solution.py:35
  33.7 3.8 %collective-permute-start.7 = (bf16[128,1024]{1,0:T(8,128)(2,1)S(1)}, bf16[128,1024]{1,0:T(8,128)(2,1)S(1)}, u32[]{:S(2)}, u32[]{:S(2)}) collective-permute-start(bf16[128,1024]{1,0:T(8,128)(2,1)S(1)} %pad_maximum_fusion.2), channel_id=1, source_target_pairs={{0,192},{64,128},{128,64},{192,0},{1,193},{65,129},{129,65},{193,1... | collective-permute-start | bytes 786440 | tf_op jit(solution)/shard_map/ppermute | solution.py:35
  37.5 3.0 %collective-permute-start.12 = (bf16[128,1024]{1,0:T(8,128)(2,1)S(1)}, bf16[128,1024]{1,0:T(8,128)(2,1)S(1)}, u32[]{:S(2)}, u32[]{:S(2)}) collective-permute-start(bf16[128,1024]{1,0:T(8,128)(2,1)S(1)} %pad_maximum_fusion.3), channel_id=1, source_target_pairs={{0,64},{64,0},{128,192},{192,128},{1,65},{65,1},{129,193},{193,129... | collective-permute-start | bytes 786440 | tf_op jit(solution)/shard_map/ppermute | solution.py:35
  48.8 3.8 %collective-permute-done.7 = bf16[128,1024]{1,0:T(8,128)(2,1)S(1)} collective-permute-done((bf16[128,1024]{1,0:T(8,128)(2,1)S(1)}, bf16[128,1024]{1,0:T(8,128)(2,1)S(1)}, u32[]{:S(2)}, u32[]{:S(2)}) %collective-permute-start.7) | collective-permute-done | bytes 262176 | tf_op jit(solution)/shard_map/ppermute | solution.py:35
  56.3 5.0 %collective-permute-done.14 = bf16[128,2048]{1,0:T(8,128)(2,1)S(1)} collective-permute-done((bf16[128,2048]{1,0:T(8,128)(2,1)S(1)}, bf16[128,2048]{1,0:T(8,128)(2,1)S(1)}, u32[]{:S(2)}, u32[]{:S(2)}) %collective-permute-start.14) | collective-permute-done | bytes 524320 | tf_op jit(solution)/shard_map/ppermute | solution.py:35
  65.8 5.4 %collective-permute-start.16 = (bf16[256,1024]{1,0:T(8,128)(2,1)S(1)}, bf16[256,1024]{1,0:T(8,128)(2,1)S(1)}, u32[]{:S(2)}, u32[]{:S(2)}) collective-permute-start(bf16[256,1024]{1,0:T(8,128)(2,1)S(1)} %pad_maximum_fusion.1.refs_2_), channel_id=1, source_target_pairs={{0,192},{64,128},{128,64},{192,0},{1,193},{65,129},{129,65},{193,1... | collective-permute-start | bytes 1572872 | tf_op jit(solution)/shard_map/ppermute | solution.py:35
  71.2 7.7 %collective-permute-done.13.refs_1_ = bf16[256,2048]{1,0:T(8,128)(2,1)S(1)} collective-permute-done((bf16[256,2048]{1,0:T(8,128)(2,1)S(1)}, bf16[256,2048]{1,0:T(8,128)(2,1)S(1)}, u32[]{:S(2)}, u32[]{:S(2)}) %collective-permute-start.13) | collective-permute-done | bytes 1048608 | tf_op jit(solution)/shard_map/ppermute | solution.py:35
  78.9 5.9 %hidden.2.refs_8_ = f32[4,512,256]{2,1,0:T(8,128)S(1)} custom-call(bf16[256,2048]{1,0:T(8,128)(2,1)S(1)} %constant_dynamic-update-slice_fusion.12.refs_0_, bf16[256,2048]{1,0:T(8,128)(2,1)S(1)} %collective-permute-done.13.refs_1_, bf16[256,2048]{1,0:T(8,128)(2,1)S(1)} %constant_dynamic-update-slice_fusion.16.refs_2_, ...), custom_call_target="tpu_custom_call" | custom-call | tf_op jit(solution)/shard_map/hidden/pallas_call | solution.py:133
  84.9 3.1 %hidden.3 = bf16[512,512]{1,0:T(8,128)(2,1)S(1)} custom-call(bf16[256,1024]{1,0:T(8,128)(2,1)S(1)} %pad_maximum_fusion.refs_0_, bf16[256,1024]{1,0:T(8,128)(2,1)S(1)} %collective-permute-done.10.refs_1_, bf16[256,1024]{1,0:T(8,128)(2,1)S(1)} %pad_maximum_fusion.1.refs_2_, bf16[256,1024]{1,0:T(8,128)(2,1)S(1)} %collective-permute-done.16.refs_3_, ...), custom_call_target="tpu_custom_call" | custom-call | flops 2147483648 | bytes 6291456 | tf_op jit(solution)/shard_map/hidden/pallas_call | solution.py:133
  93.8 3.6 %collective-permute-start.20 = (bf16[256,1024]{1,0:T(8,128)(2,1)S(1)}, bf16[256,1024]{1,0:T(8,128)(2,1)S(1)}, u32[]{:S(2)}, u32[]{:S(2)}) collective-permute-start(bf16[256,1024]{1,0:T(8,128)(2,1)S(1)} %out.10), channel_id=1, source_target_pairs={{0,64},{64,0},{128,192},{192,128},{1,65},{65,1},{129,193},{193,129... | collective-permute-start | bytes 1572872 | tf_op jit(solution)/shard_map/ppermute | solution.py:35
  97.9 3.6 %collective-permute-start.19 = (bf16[256,1024]{1,0:T(8,128)(2,1)S(1)}, bf16[256,1024]{1,0:T(8,128)(2,1)S(1)}, u32[]{:S(2)}, u32[]{:S(2)}) collective-permute-start(bf16[256,1024]{1,0:T(8,128)(2,1)S(1)} %out.11), channel_id=1, source_target_pairs={{0,192},{64,128},{128,64},{192,0},{1,193},{65,129},{129,65},{193,1... | collective-permute-start | bytes 1572872 | tf_op jit(solution)/shard_map/ppermute | solution.py:35
  104.6 5.1 %collective-permute-done.17 = bf16[256,2048]{1,0:T(8,128)(2,1)S(1)} collective-permute-done((bf16[256,2048]{1,0:T(8,128)(2,1)S(1)}, bf16[256,2048]{1,0:T(8,128)(2,1)S(1)}, u32[]{:S(2)}, u32[]{:S(2)}) %collective-permute-start.17) | collective-permute-done | bytes 1048608 | tf_op jit(solution)/shard_map/ppermute | solution.py:35
  112.6 4.0 %collective-permute-done.21 = bf16[256,2048]{1,0:T(8,128)(2,1)S(1)} collective-permute-done((bf16[256,2048]{1,0:T(8,128)(2,1)S(1)}, bf16[256,2048]{1,0:T(8,128)(2,1)S(1)}, u32[]{:S(2)}, u32[]{:S(2)}) %collective-permute-start.21) | collective-permute-done | bytes 1048608 | tf_op jit(solution)/shard_map/ppermute | solution.py:35
  118.4 5.9 %collective-permute-start.25 = (bf16[128,1024]{1,0:T(8,128)(2,1)S(1)}, bf16[128,1024]{1,0:T(8,128)(2,1)S(1)}, u32[]{:S(2)}, u32[]{:S(2)}) collective-permute-start(bf16[128,1024]{1,0:T(8,128)(2,1)S(1)} %get-tuple-element.96), channel_id=1, source_target_pairs={{0,192},{64,128},{128,64},{192,0},{1,193},{65,129},{129,65},{193,1... | collective-permute-start | bytes 786440 | tf_op jit(solution)/shard_map/ppermute | solution.py:35
  127.9 5.2 %collective-permute-start.24 = (bf16[64,2048]{1,0:T(8,128)(2,1)S(1)}, bf16[64,2048]{1,0:T(8,128)(2,1)S(1)}, u32[]{:S(2)}, u32[]{:S(2)}) collective-permute-start(bf16[64,2048]{1,0:T(8,128)(2,1)S(1)} %get-tuple-element.97), channel_id=1, source_target_pairs={{0,64},{64,0},{128,192},{192,128},{1,65},{65,1},{129,193},{193,129... | collective-permute-start | bytes 786440 | tf_op jit(solution)/shard_map/ppermute | solution.py:35
  133.1 3.2 %collective-permute-done.25 = bf16[128,1024]{1,0:T(8,128)(2,1)S(1)} collective-permute-done((bf16[128,1024]{1,0:T(8,128)(2,1)S(1)}, bf16[128,1024]{1,0:T(8,128)(2,1)S(1)}, u32[]{:S(2)}, u32[]{:S(2)}) %collective-permute-start.25) | collective-permute-done | bytes 262176 | tf_op jit(solution)/shard_map/ppermute | solution.py:35
  136.3 4.2 %collective-permute-done.26 = bf16[128,1024]{1,0:T(8,128)(2,1)S(1)} collective-permute-done((bf16[128,1024]{1,0:T(8,128)(2,1)S(1)}, bf16[128,1024]{1,0:T(8,128)(2,1)S(1)}, u32[]{:S(2)}, u32[]{:S(2)}) %collective-permute-start.26) | collective-permute-done | bytes 262176 | tf_op jit(solution)/shard_map/ppermute | solution.py:35
  140.7 3.5 %collective-permute-start.27 = (bf16[64,2048]{1,0:T(8,128)(2,1)S(1)}, bf16[64,2048]{1,0:T(8,128)(2,1)S(1)}, u32[]{:S(2)}, u32[]{:S(2)}) collective-permute-start(bf16[64,2048]{1,0:T(8,128)(2,1)S(1)} %pad_maximum_fusion.4), channel_id=1, source_target_pairs={{0,6},{2,4},{4,2},{6,0},{1,7},{3,5},{5,3},{7,1},{8,14},{10,12},{12... | collective-permute-start | bytes 786440 | tf_op jit(solution)/shard_map/ppermute | solution.py:35
  144.2 3.6 %collective-permute-start.28 = (bf16[32,2048]{1,0:T(8,128)(2,1)S(1)}, bf16[32,2048]{1,0:T(8,128)(2,1)S(1)}, u32[]{:S(2)}, u32[]{:S(2)}) collective-permute-start(bf16[32,2048]{1,0:T(8,128)(2,1)S(1)} %get-tuple-element.109), channel_id=1, source_target_pairs={{0,64},{64,0},{128,192},{192,128},{1,65},{65,1},{129,193},{193,129... | collective-permute-start | bytes 393224 | tf_op jit(solution)/shard_map/ppermute | solution.py:35
  147.8 3.6 %collective-permute-start.29 = (bf16[32,2048]{1,0:T(8,128)(2,1)S(1)}, bf16[32,2048]{1,0:T(8,128)(2,1)S(1)}, u32[]{:S(2)}, u32[]{:S(2)}) collective-permute-start(bf16[32,2048]{1,0:T(8,128)(2,1)S(1)} %get-tuple-element.103), channel_id=1, source_target_pairs={{0,192},{64,128},{128,64},{192,0},{1,193},{65,129},{129,65},{193,1... | collective-permute-start | bytes 393224 | tf_op jit(solution)/shard_map/ppermute | solution.py:35
  158.1 13.5 %all_to_all.11 = bf16[8,8,3072]{2,1,0:T(8,128)(2,1)S(1)} all-to-all(bf16[8,8,3072]{2,1,0:T(8,128)(2,1)S(1)} %bitcast.27), channel_id=1, replica_groups=mesh['dp'=4,'zl'=2,'y'=4,'x'=4,'c'=2] {'zl','y'}, dimensions={0} | all-to-all | bytes 786432 | tf_op jit(solution)/shard_map/all_to_all | solution.py:280
  (96 shorter events, 50.2 us)
Async XLA Ops:
  2.1 15.8 %collective-permute-start = (bf16[6144,256]{1,0:T(8,128)(2,1)}, bf16[6144,256]{1,0:T(8,128)(2,1)S(1)}, u32[]{:S(2)}, u32[]{:S(2)}) collective-permute-start(bf16[6144,256]{1,0:T(8,128)(2,1)} %bitcast.19), channel_id=1, source_target_pairs={{0,1},{1,0},{2,3},{3,2},{4,5},{5,4},{6,7},{7,6},{8,9},{9,8},{10,11... | collective-permute-start | bytes 9437192 | tf_op jit(solution)/shard_map/ppermute | solution.py:35
  2.2 15.7 %collective-permute-start.1 = (bf16[6144,256]{1,0:T(8,128)(2,1)}, bf16[6144,256]{1,0:T(8,128)(2,1)S(1)}, u32[]{:S(2)}, u32[]{:S(2)}) collective-permute-start(bf16[6144,256]{1,0:T(8,128)(2,1)} %bitcast.22), channel_id=1, source_target_pairs={{0,1},{1,0},{2,3},{3,2},{4,5},{5,4},{6,7},{7,6},{8,9},{9,8},{10,11... | collective-permute-start | bytes 9437192 | tf_op jit(solution)/shard_map/ppermute | solution.py:35
  2.7 29.6 %collective-permute-start.6 = (bf16[256,6144]{1,0:T(8,128)(2,1)}, bf16[256,6144]{1,0:T(8,128)(2,1)S(1)}, u32[]{:S(2)}, u32[]{:S(2)}) collective-permute-start(bf16[256,6144]{1,0:T(8,128)(2,1)} %bitcast.10), channel_id=1, source_target_pairs={{0,1},{1,0},{2,3},{3,2},{4,5},{5,4},{6,7},{7,6},{8,9},{9,8},{10,11... | collective-permute-start | bytes 9437192 | tf_op jit(solution)/shard_map/ppermute | solution.py:35
  28.1 15.3 %collective-permute-start.9 = (bf16[64,2048]{1,0:T(8,128)(2,1)S(1)}, bf16[64,2048]{1,0:T(8,128)(2,1)S(1)}, u32[]{:S(2)}, u32[]{:S(2)}) collective-permute-start(bf16[64,2048]{1,0:T(8,128)(2,1)S(1)} %get-tuple-element.131), channel_id=1, source_target_pairs={{0,192},{64,128},{128,64},{192,0},{1,193},{65,129},{129,65},{193,1... | collective-permute-start | bytes 786440 | tf_op jit(solution)/shard_map/ppermute | solution.py:35
  32.3 14.8 %collective-permute-start.8 = (bf16[64,2048]{1,0:T(8,128)(2,1)S(1)}, bf16[64,2048]{1,0:T(8,128)(2,1)S(1)}, u32[]{:S(2)}, u32[]{:S(2)}) collective-permute-start(bf16[64,2048]{1,0:T(8,128)(2,1)S(1)} %get-tuple-element.125), channel_id=1, source_target_pairs={{0,64},{64,0},{128,192},{192,128},{1,65},{65,1},{129,193},{193,129... | collective-permute-start | bytes 786440 | tf_op jit(solution)/shard_map/ppermute | solution.py:35
  33.7 18.9 %collective-permute-start.7 = (bf16[128,1024]{1,0:T(8,128)(2,1)S(1)}, bf16[128,1024]{1,0:T(8,128)(2,1)S(1)}, u32[]{:S(2)}, u32[]{:S(2)}) collective-permute-start(bf16[128,1024]{1,0:T(8,128)(2,1)S(1)} %pad_maximum_fusion.2), channel_id=1, source_target_pairs={{0,192},{64,128},{128,64},{192,0},{1,193},{65,129},{129,65},{193,1... | collective-permute-start | bytes 786440 | tf_op jit(solution)/shard_map/ppermute | solution.py:35
  37.5 16.5 %collective-permute-start.12 = (bf16[128,1024]{1,0:T(8,128)(2,1)S(1)}, bf16[128,1024]{1,0:T(8,128)(2,1)S(1)}, u32[]{:S(2)}, u32[]{:S(2)}) collective-permute-start(bf16[128,1024]{1,0:T(8,128)(2,1)S(1)} %pad_maximum_fusion.3), channel_id=1, source_target_pairs={{0,64},{64,0},{128,192},{192,128},{1,65},{65,1},{129,193},{193,129... | collective-permute-start | bytes 786440 | tf_op jit(solution)/shard_map/ppermute | solution.py:35
  47.2 14.2 %collective-permute-start.14 = (bf16[128,2048]{1,0:T(8,128)(2,1)S(1)}, bf16[128,2048]{1,0:T(8,128)(2,1)S(1)}, u32[]{:S(2)}, u32[]{:S(2)}) collective-permute-start(bf16[128,2048]{1,0:T(8,128)(2,1)S(1)} %get-tuple-element.112), channel_id=1, source_target_pairs={{0,2},{2,0},{4,6},{6,4},{1,3},{3,1},{5,7},{7,5},{8,10},{10,8},{12,... | collective-permute-start | bytes 1572872 | tf_op jit(solution)/shard_map/ppermute | solution.py:35
  54.0 24.9 %collective-permute-start.13 = (bf16[256,2048]{1,0:T(8,128)(2,1)S(1)}, bf16[256,2048]{1,0:T(8,128)(2,1)S(1)}, u32[]{:S(2)}, u32[]{:S(2)}) collective-permute-start(bf16[256,2048]{1,0:T(8,128)(2,1)S(1)} %constant_dynamic-update-slice_fusion.12.refs_0_), channel_id=1, source_target_pairs={{0,2},{2,0},{4,6},{6,4},{1,3},{3,1},{5,7},{7,5},{8,10},{10,8},{12,... | collective-permute-start | bytes 3145736 | tf_op jit(solution)/shard_map/ppermute | solution.py:35
  61.4 17.5 %collective-permute-start.15 = (bf16[256,2048]{1,0:T(8,128)(2,1)S(1)}, bf16[256,2048]{1,0:T(8,128)(2,1)S(1)}, u32[]{:S(2)}, u32[]{:S(2)}) collective-permute-start(bf16[256,2048]{1,0:T(8,128)(2,1)S(1)} %constant_dynamic-update-slice_fusion.16.refs_2_), channel_id=1, source_target_pairs={{0,6},{2,4},{4,2},{6,0},{1,7},{3,5},{5,3},{7,1},{8,14},{10,12},{12... | collective-permute-start | bytes 3145736 | tf_op jit(solution)/shard_map/ppermute | solution.py:35
  63.7 21.1 %collective-permute-start.10 = (bf16[256,1024]{1,0:T(8,128)(2,1)S(1)}, bf16[256,1024]{1,0:T(8,128)(2,1)S(1)}, u32[]{:S(2)}, u32[]{:S(2)}) collective-permute-start(bf16[256,1024]{1,0:T(8,128)(2,1)S(1)} %pad_maximum_fusion.refs_0_), channel_id=1, source_target_pairs={{0,64},{64,0},{128,192},{192,128},{1,65},{65,1},{129,193},{193,129... | collective-permute-start | bytes 1572872 | tf_op jit(solution)/shard_map/ppermute | solution.py:35
  65.8 19.1 %collective-permute-start.16 = (bf16[256,1024]{1,0:T(8,128)(2,1)S(1)}, bf16[256,1024]{1,0:T(8,128)(2,1)S(1)}, u32[]{:S(2)}, u32[]{:S(2)}) collective-permute-start(bf16[256,1024]{1,0:T(8,128)(2,1)S(1)} %pad_maximum_fusion.1.refs_2_), channel_id=1, source_target_pairs={{0,192},{64,128},{128,64},{192,0},{1,193},{65,129},{129,65},{193,1... | collective-permute-start | bytes 1572872 | tf_op jit(solution)/shard_map/ppermute | solution.py:35
  89.1 20.6 %collective-permute-start.17 = (bf16[256,2048]{1,0:T(8,128)(2,1)S(1)}, bf16[256,2048]{1,0:T(8,128)(2,1)S(1)}, u32[]{:S(2)}, u32[]{:S(2)}) collective-permute-start(bf16[256,2048]{1,0:T(8,128)(2,1)S(1)} %out.8), channel_id=1, source_target_pairs={{0,2},{2,0},{4,6},{6,4},{1,3},{3,1},{5,7},{7,5},{8,10},{10,8},{12,... | collective-permute-start | bytes 3145736 | tf_op jit(solution)/shard_map/ppermute | solution.py:35
  91.9 24.7 %collective-permute-start.21 = (bf16[256,2048]{1,0:T(8,128)(2,1)S(1)}, bf16[256,2048]{1,0:T(8,128)(2,1)S(1)}, u32[]{:S(2)}, u32[]{:S(2)}) collective-permute-start(bf16[256,2048]{1,0:T(8,128)(2,1)S(1)} %out.9), channel_id=1, source_target_pairs={{0,6},{2,4},{4,2},{6,0},{1,7},{3,5},{5,3},{7,1},{8,14},{10,12},{12... | collective-permute-start | bytes 3145736 | tf_op jit(solution)/shard_map/ppermute | solution.py:35
  93.8 24.4 %collective-permute-start.20 = (bf16[256,1024]{1,0:T(8,128)(2,1)S(1)}, bf16[256,1024]{1,0:T(8,128)(2,1)S(1)}, u32[]{:S(2)}, u32[]{:S(2)}) collective-permute-start(bf16[256,1024]{1,0:T(8,128)(2,1)S(1)} %out.10), channel_id=1, source_target_pairs={{0,64},{64,0},{128,192},{192,128},{1,65},{65,1},{129,193},{193,129... | collective-permute-start | bytes 1572872 | tf_op jit(solution)/shard_map/ppermute | solution.py:35
  97.9 26.4 %collective-permute-start.19 = (bf16[256,1024]{1,0:T(8,128)(2,1)S(1)}, bf16[256,1024]{1,0:T(8,128)(2,1)S(1)}, u32[]{:S(2)}, u32[]{:S(2)}) collective-permute-start(bf16[256,1024]{1,0:T(8,128)(2,1)S(1)} %out.11), channel_id=1, source_target_pairs={{0,192},{64,128},{128,64},{192,0},{1,193},{65,129},{129,65},{193,1... | collective-permute-start | bytes 1572872 | tf_op jit(solution)/shard_map/ppermute | solution.py:35
  110.1 16.1 %collective-permute-start.18 = (bf16[128,2048]{1,0:T(8,128)(2,1)S(1)}, bf16[128,2048]{1,0:T(8,128)(2,1)S(1)}, u32[]{:S(2)}, u32[]{:S(2)}) collective-permute-start(bf16[128,2048]{1,0:T(8,128)(2,1)S(1)} %get-tuple-element.91), channel_id=1, source_target_pairs={{0,6},{2,4},{4,2},{6,0},{1,7},{3,5},{5,3},{7,1},{8,14},{10,12},{12... | collective-permute-start | bytes 1572872 | tf_op jit(solution)/shard_map/ppermute | solution.py:35
  116.9 10.8 %collective-permute-start.23 = (bf16[128,2048]{1,0:T(8,128)(2,1)S(1)}, bf16[128,2048]{1,0:T(8,128)(2,1)S(1)}, u32[]{:S(2)}, u32[]{:S(2)}) collective-permute-start(bf16[128,2048]{1,0:T(8,128)(2,1)S(1)} %get-tuple-element.90), channel_id=1, source_target_pairs={{0,2},{2,0},{4,6},{6,4},{1,3},{3,1},{5,7},{7,5},{8,10},{10,8},{12,... | collective-permute-start | bytes 1572872 | tf_op jit(solution)/shard_map/ppermute | solution.py:35
  118.4 17.8 %collective-permute-start.25 = (bf16[128,1024]{1,0:T(8,128)(2,1)S(1)}, bf16[128,1024]{1,0:T(8,128)(2,1)S(1)}, u32[]{:S(2)}, u32[]{:S(2)}) collective-permute-start(bf16[128,1024]{1,0:T(8,128)(2,1)S(1)} %get-tuple-element.96), channel_id=1, source_target_pairs={{0,192},{64,128},{128,64},{192,0},{1,193},{65,129},{129,65},{193,1... | collective-permute-start | bytes 786440 | tf_op jit(solution)/shard_map/ppermute | solution.py:35
  124.5 16.0 %collective-permute-start.26 = (bf16[128,1024]{1,0:T(8,128)(2,1)S(1)}, bf16[128,1024]{1,0:T(8,128)(2,1)S(1)}, u32[]{:S(2)}, u32[]{:S(2)}) collective-permute-start(bf16[128,1024]{1,0:T(8,128)(2,1)S(1)} %get-tuple-element.94), channel_id=1, source_target_pairs={{0,64},{64,0},{128,192},{192,128},{1,65},{65,1},{129,193},{193,129... | collective-permute-start | bytes 786440 | tf_op jit(solution)/shard_map/ppermute | solution.py:35
  126.3 17.8 %collective-permute-start.22 = (bf16[64,2048]{1,0:T(8,128)(2,1)S(1)}, bf16[64,2048]{1,0:T(8,128)(2,1)S(1)}, u32[]{:S(2)}, u32[]{:S(2)}) collective-permute-start(bf16[64,2048]{1,0:T(8,128)(2,1)S(1)} %get-tuple-element.100), channel_id=1, source_target_pairs={{0,192},{64,128},{128,64},{192,0},{1,193},{65,129},{129,65},{193,1... | collective-permute-start | bytes 786440 | tf_op jit(solution)/shard_map/ppermute | solution.py:35
  127.9 19.9 %collective-permute-start.24 = (bf16[64,2048]{1,0:T(8,128)(2,1)S(1)}, bf16[64,2048]{1,0:T(8,128)(2,1)S(1)}, u32[]{:S(2)}, u32[]{:S(2)}) collective-permute-start(bf16[64,2048]{1,0:T(8,128)(2,1)S(1)} %get-tuple-element.97), channel_id=1, source_target_pairs={{0,64},{64,0},{128,192},{192,128},{1,65},{65,1},{129,193},{193,129... | collective-permute-start | bytes 786440 | tf_op jit(solution)/shard_map/ppermute | solution.py:35
  140.7 10.8 %collective-permute-start.27 = (bf16[64,2048]{1,0:T(8,128)(2,1)S(1)}, bf16[64,2048]{1,0:T(8,128)(2,1)S(1)}, u32[]{:S(2)}, u32[]{:S(2)}) collective-permute-start(bf16[64,2048]{1,0:T(8,128)(2,1)S(1)} %pad_maximum_fusion.4), channel_id=1, source_target_pairs={{0,6},{2,4},{4,2},{6,0},{1,7},{3,5},{5,3},{7,1},{8,14},{10,12},{12... | collective-permute-start | bytes 786440 | tf_op jit(solution)/shard_map/ppermute | solution.py:35
  144.2 13.6 %collective-permute-start.28 = (bf16[32,2048]{1,0:T(8,128)(2,1)S(1)}, bf16[32,2048]{1,0:T(8,128)(2,1)S(1)}, u32[]{:S(2)}, u32[]{:S(2)}) collective-permute-start(bf16[32,2048]{1,0:T(8,128)(2,1)S(1)} %get-tuple-element.109), channel_id=1, source_target_pairs={{0,64},{64,0},{128,192},{192,128},{1,65},{65,1},{129,193},{193,129... | collective-permute-start | bytes 393224 | tf_op jit(solution)/shard_map/ppermute | solution.py:35
  (13 other events, 220.7 us)

commit v10 on v9

--- a/solution.py
+++ b/solution.py
@@ -43,38 +43,37 @@
     return lax.optimization_barrier((value, *others))[0]
 
 
-def hidden_kernel(chains, first, last, *refs):
-    n = len(chains)
-    ins = refs[: 2 * n]
-    wg0, wu0, wg1, wu1 = refs[2 * n : 2 * n + 4]
-    refs = refs[2 * n + 4 :]
+def hidden_kernel(pieces, first, last, *refs):
+    n = len(pieces)
+    ins = refs[:n]
+    wg0, wu0, wg1, wu1 = refs[n : n + 4]
+    refs = refs[n + 4 :]
     before = None if first else refs[0]
     refs = refs if first else refs[1:]
-    total, part = refs[0], refs[1]
-    acc = refs[2] if last else total
+    total = refs[0]
+    acc = refs[1] if last else total
     step = pl.program_id(0)
     units = wg0.shape[1]
     f32 = jnp.float32
-    at = 0
-    for k, c in enumerate(chains):
-        _, width, order = CHAINS[c]
-        steps = width // PART
-
-        @pl.when((step >= at) & (step < at + steps))
-        def _(k=k, order=order):
-            for index in range(16):
-                to = canon_block(order, index) * UNIT
-                row = (index % 8) * UNIT
-                part[to : to + UNIT, :] = ins[2 * k + index // 8][row : row + UNIT, :]
-
-        at += steps
 
     @pl.when(step == 0)
     def _():
         acc[...] = jnp.zeros_like(acc) if first else before[...]
 
-    for i, w in enumerate((wg0, wu0, wg1, wu1)):
-        acc[i] += jnp.dot(part[...], w[...], preferred_element_type=f32)
+    at = 0
+    for k, (c, came) in enumerate(pieces):
+        _, width, order = CHAINS[c]
+        steps = width // PART
+
+        @pl.when((step >= at) & (step < at + steps))
+        def _(k=k, order=order, came=came):
+            for i, w in enumerate((wg0, wu0, wg1, wu1)):
+                product = jnp.dot(ins[k][...], w[...], preferred_element_type=f32)
+                for index in range(8):
+                    to = canon_block(order, index + 8 * came) * UNIT
+                    acc[i, to : to + UNIT, :] += product[index * UNIT : (index + 1) * UNIT]
+
+        at += steps
 
     if last:
 
@@ -107,31 +106,30 @@
     return value
 
 
-def hidden_units(pieces, weights, chains, before, last):
+def hidden_units(pieces, weights, before, last):
     width, units = weights[0].shape
     count = 2 * HALF
     first = before is None
     in_specs, parts = [], []
-    for c in chains:
+    for c, _ in pieces:
         start, size, _ = CHAINS[c]
         low, steps = len(parts), size // PART
         to = lambda i, low=low, steps=steps: (0, jnp.clip(i - low, 0, steps - 1))
-        in_specs += [pl.BlockSpec((HALF, PART), to)] * 2
+        in_specs.append(pl.BlockSpec((HALF, PART), to))
         parts += [start // PART + k for k in range(steps)]
     whole = lambda *shape: pl.BlockSpec(shape, lambda i: (0,) * len(shape))
     in_specs += [pl.BlockSpec((PART, units), lambda i: (pick(parts, i), 0))] * 4
     sums = (4, count, units)
     if not first:
         in_specs.append(whole(*sums))
-    scratch = [pltpu.VMEM((count, PART), jnp.bfloat16)]
     if last:
         out, out_spec = jax.ShapeDtypeStruct((count, 2 * units), jnp.bfloat16), whole(count, 2 * units)
-        scratch.append(pltpu.VMEM(sums, jnp.float32))
+        scratch = [pltpu.VMEM(sums, jnp.float32)]
     else:
-        out, out_spec = jax.ShapeDtypeStruct(sums, jnp.float32), whole(*sums)
+        out, out_spec, scratch = jax.ShapeDtypeStruct(sums, jnp.float32), whole(*sums), []
     depth = len(parts) * PART
     return pl.pallas_call(
-        functools.partial(hidden_kernel, chains, first, last),
+        functools.partial(hidden_kernel, tuple(pieces), first, last),
         grid=(len(parts),),
         out_shape=out,
         in_specs=in_specs,
@@ -139,12 +137,12 @@
         scratch_shapes=scratch,
         compiler_params=pltpu.CompilerParams(vmem_limit_bytes=32 << 20),
         cost_estimate=pl.CostEstimate(
-            flops=8 * count * depth * units if last else 0,
-            bytes_accessed=8 * depth * units + 2 * count * depth if last else 0,
+            flops=8 * HALF * depth * units if last else 0,
+            bytes_accessed=8 * depth * units + 2 * HALF * depth if last else 0,
             transcendentals=2 * count * units if last else 0,
         ),
         name="hidden",
-    )(*pieces, *weights, *(() if first else (before,)))
+    )(*pieces.values(), *weights, *(() if first else (before,)))
 
 
 def expert_out(hidden, wd0, wd1, chain, sent):
@@ -337,12 +335,13 @@
         held[j] = last = jnp.concatenate([held[j], came[j]], axis=0)
     came = [trade(h, order[3]) for h, (_, _, order) in zip(held, CHAINS)]
     weights = (wg0, wu0, wg1, wu1)
-    came[0] = after(came[0], last)
+    sums = hidden_units({(j, False): held[j] for j in range(4)}, weights, None, False)
+    came[0] = after(came[0], last, sums)
     came[1] = after(came[1], came[0])
-    sums = hidden_units((held[0], came[0], held[1], came[1]), weights, (0, 1), None, False)
+    sums = hidden_units({(j, True): came[j] for j in (0, 1)}, weights, sums, False)
     came[2] = after(came[2], sums)
     came[3] = after(came[3], came[2])
-    hidden = hidden_units((held[2], came[2], held[3], came[3]), weights, (2, 3), sums, True)
+    hidden = hidden_units({(j, True): came[j] for j in (2, 3)}, weights, sums, True)
 
     held, away = [], []
     for j in range(4):

time: 173 us -> 170 us (0.983)
  starting transfers between devices: 79 us -> 51.3 us
  waiting for transfers between devices: 43.5 us -> 69.5 us
  blocking collectives: 28.6 us -> 26.3 us
    ppermute x32, starting transfers between devices: 79 us -> 51.3 us  [trade(): return lax.ppermute(value, axis, [(i, i ^ mask) for i in range(n)])]
    ppermute x32, waiting for transfers between devices: 43.5 us -> 69.5 us  [trade(): return lax.ppermute(value, axis, [(i, i ^ mask) for i in range(n)])]
    all_to_all x2, blocking collectives: 28.6 us -> 26.3 us  [swap_experts(): lax.all_to_all(blocks, ('zl', 'y'), split_axis=0, concat_axis=0, tiled=True)]
    pallas_call x2 -> x3, Pallas kernels: 9.01 us -> 9.99 us  [hidden_units(): pl.pallas_call(functools.partial(hidden_kernel, tuple(pieces), first, las...]
  transfers between devices with their start and end apart: 32 -> 32, of which waited for: 13 -> 17; matrix products, arithmetic and copies ran while one was open for 1% -> 1% of each run, Pallas kernels for 7% -> 8%
where the time goes in v10:
time: 170 us
  waiting for transfers between devices  69.5 us (41%)
  starting transfers between devices  51.3 us (30%)
  blocking collectives  26.3 us (15%)
  Pallas kernels  20 us (12%)
  other arithmetic  1.82 us (1%)
    ppermute x32, waiting for transfers between devices, trade(): return lax.ppermute(value, axis, [(i, i ^ mask) for i in range(n)])  69.5 us
    ppermute x32, starting transfers between devices, trade(): return lax.ppermute(value, axis, [(i, i ^ mask) for i in range(n)])  51.3 us
    all_to_all x2, blocking collectives, swap_experts(): lax.all_to_all(blocks, ('zl', 'y'), split_axis=0, concat_axis=0, tiled=True)  26.3 us
    pallas_call x3, Pallas kernels, hidden_units(): pl.pallas_call(functools.partial(hidden_kernel, tuple(pieces), first, las...  9.99 us
    pallas_call x8, Pallas kernels, expert_out(): pl.pallas_call(functools.partial(out_kernel, order, int(sent)), grid=(siz...  6.21 us
    pallas_call x4, Pallas kernels, small(): pl.pallas_call(kernel, out_shape=out_shape, in_specs=[pl.BlockSpec(memory...  3.81 us
  transfers between devices with their start and end apart: 32, of which 17 were waited for; matrix products, arithmetic and copies ran while one was open for 1% of the time, Pallas kernels for 8%

profile of v10, /device:TPU:2, one launch (start us, length us, event | category | flops | bytes accessed | tf_op | source)
XLA Modules:
  0.0 169.8 jit_solution(2118547225081139488)
XLA Ops:
  0.0 2.1 %place.1 = (bf16[64,3072]{1,0:T(8,128)(2,1)}, f32[16,64]{1,0:T(8,128)}) custom-call(s32[2,8]{1,0:T(2,128)} %bitcast.32, f32[2,8]{1,0:T(2,128)} %bitcast.33, bf16[8,6144]{1,0:T(8,128)(2,1)} %tokens.1, f32[1,6144]{1,0:T(1,128)} %bitcast.31), custom_call_target="tpu_custom_call" | custom-call | tf_op jit(solution)/shard_map/place/pallas_call | solution.py:265
  2.8 15.1 %all_to_all.10 = bf16[8,8,3072]{2,1,0:T(8,128)(2,1)S(1)} all-to-all(bf16[8,8,3072]{2,1,0:T(8,128)(2,1)} %bitcast.30), channel_id=1, replica_groups=mesh['dp'=4,'zl'=2,'y'=4,'x'=4,'c'=2] {'zl','y'}, dimensions={0} | all-to-all | bytes 786432 | tf_op jit(solution)/shard_map/all_to_all | solution.py:278
  18.8 5.4 %collective-permute-start.4 = (bf16[32,2048]{1,0:T(8,128)(2,1)S(1)}, bf16[32,2048]{1,0:T(8,128)(2,1)S(1)}, u32[]{:S(2)}, u32[]{:S(2)}) collective-permute-start(bf16[32,2048]{1,0:T(8,128)(2,1)S(1)} %get-tuple-element.53), channel_id=1, source_target_pairs={{0,192},{64,128},{128,64},{192,0},{1,193},{65,129},{129,65},{193,1... | collective-permute-start | bytes 393224 | tf_op jit(solution)/shard_map/ppermute | solution.py:35
  25.8 2.2 %collective-permute-start.3 = (bf16[64,2048]{1,0:T(8,128)(2,1)S(1)}, bf16[64,2048]{1,0:T(8,128)(2,1)S(1)}, u32[]{:S(2)}, u32[]{:S(2)}) collective-permute-start(bf16[64,2048]{1,0:T(8,128)(2,1)S(1)} %constant_dynamic-update-slice_fusion), channel_id=1, source_target_pairs={{0,6},{2,4},{4,2},{6,0},{1,7},{3,5},{5,3},{7,1},{8,14},{10,12},{12... | collective-permute-start | bytes 786440 | tf_op jit(solution)/shard_map/ppermute | solution.py:35
  28.0 2.2 %collective-permute-done.5 = bf16[32,2048]{1,0:T(8,128)(2,1)S(1)} collective-permute-done((bf16[32,2048]{1,0:T(8,128)(2,1)S(1)}, bf16[32,2048]{1,0:T(8,128)(2,1)S(1)}, u32[]{:S(2)}, u32[]{:S(2)}) %collective-permute-start.5) | collective-permute-done | bytes 131104 | tf_op jit(solution)/shard_map/ppermute | solution.py:35
  33.8 3.3 %collective-permute-start.7 = (bf16[128,1024]{1,0:T(8,128)(2,1)S(1)}, bf16[128,1024]{1,0:T(8,128)(2,1)S(1)}, u32[]{:S(2)}, u32[]{:S(2)}) collective-permute-start(bf16[128,1024]{1,0:T(8,128)(2,1)S(1)} %pad_maximum_fusion.2), channel_id=1, source_target_pairs={{0,192},{64,128},{128,64},{192,0},{1,193},{65,129},{129,65},{193,1... | collective-permute-start | bytes 786440 | tf_op jit(solution)/shard_map/ppermute | solution.py:35
  37.9 9.5 %collective-permute-done.9 = bf16[64,2048]{1,0:T(8,128)(2,1)S(1)} collective-permute-done((bf16[64,2048]{1,0:T(8,128)(2,1)S(1)}, bf16[64,2048]{1,0:T(8,128)(2,1)S(1)}, u32[]{:S(2)}, u32[]{:S(2)}) %collective-permute-start.9) | collective-permute-done | bytes 262176 | tf_op jit(solution)/shard_map/ppermute | solution.py:35
  47.4 2.2 %collective-permute-start.11 = (bf16[128,2048]{1,0:T(8,128)(2,1)S(1)}, bf16[128,2048]{1,0:T(8,128)(2,1)S(1)}, u32[]{:S(2)}, u32[]{:S(2)}) collective-permute-start(bf16[128,2048]{1,0:T(8,128)(2,1)S(1)} %get-tuple-element.114), channel_id=1, source_target_pairs={{0,6},{2,4},{4,2},{6,0},{1,7},{3,5},{5,3},{7,1},{8,14},{10,12},{12... | collective-permute-start | bytes 1572872 | tf_op jit(solution)/shard_map/ppermute | solution.py:35
  51.2 5.1 %collective-permute-done.7 = bf16[128,1024]{1,0:T(8,128)(2,1)S(1)} collective-permute-done((bf16[128,1024]{1,0:T(8,128)(2,1)S(1)}, bf16[128,1024]{1,0:T(8,128)(2,1)S(1)}, u32[]{:S(2)}, u32[]{:S(2)}) %collective-permute-start.7) | collective-permute-done | bytes 262176 | tf_op jit(solution)/shard_map/ppermute | solution.py:35
  56.9 2.6 %collective-permute-start.13 = (bf16[256,2048]{1,0:T(8,128)(2,1)S(1)}, bf16[256,2048]{1,0:T(8,128)(2,1)S(1)}, u32[]{:S(2)}, u32[]{:S(2)}) collective-permute-start(bf16[256,2048]{1,0:T(8,128)(2,1)S(1)} %constant_dynamic-update-slice_fusion.12.refs_0_), channel_id=1, source_target_pairs={{0,2},{2,0},{4,6},{6,4},{1,3},{3,1},{5,7},{7,5},{8,10},{10,8},{12,... | collective-permute-start | bytes 3145736 | tf_op jit(solution)/shard_map/ppermute | solution.py:35
  63.1 3.1 %collective-permute-start.16 = (bf16[256,1024]{1,0:T(8,128)(2,1)S(1)}, bf16[256,1024]{1,0:T(8,128)(2,1)S(1)}, u32[]{:S(2)}, u32[]{:S(2)}) collective-permute-start(bf16[256,1024]{1,0:T(8,128)(2,1)S(1)} %pad_maximum_fusion.1.refs_3_), channel_id=1, source_target_pairs={{0,192},{64,128},{128,64},{192,0},{1,193},{65,129},{129,65},{193,1... | collective-permute-start | bytes 1572872 | tf_op jit(solution)/shard_map/ppermute | solution.py:35
  66.3 4.8 %hidden.3.refs_6_ = f32[4,512,256]{2,1,0:T(8,128)S(1)} custom-call(bf16[256,2048]{1,0:T(8,128)(2,1)S(1)} %constant_dynamic-update-slice_fusion.12.refs_0_, bf16[256,2048]{1,0:T(8,128)(2,1)S(1)} %constant_dynamic-update-slice_fusion.16.refs_1_, bf16[256,1024]{1,0:T(8,128)(2,1)S(1)} %pad_maximum_fusion.refs_2_, ...), custom_call_target="tpu_custom_call" | custom-call | tf_op jit(solution)/shard_map/hidden/pallas_call | solution.py:131
  71.1 10.3 %collective-permute-done.13.refs_0_ = bf16[256,2048]{1,0:T(8,128)(2,1)S(1)} collective-permute-done((bf16[256,2048]{1,0:T(8,128)(2,1)S(1)}, bf16[256,2048]{1,0:T(8,128)(2,1)S(1)}, u32[]{:S(2)}, u32[]{:S(2)}) %collective-permute-start.13) | collective-permute-done | bytes 1048608 | tf_op jit(solution)/shard_map/ppermute | solution.py:35
  81.5 3.3 %hidden.4.refs_6_ = f32[4,512,256]{2,1,0:T(8,128)S(1)} custom-call(bf16[256,2048]{1,0:T(8,128)(2,1)S(1)} %collective-permute-done.13.refs_0_, bf16[256,2048]{1,0:T(8,128)(2,1)S(1)} %collective-permute-done.15.refs_1_, bf16[6144,256]{1,0:T(8,128)(2,1)S(1)} %bitcast.21, bf16[6144,256]{1,0:T(8,128)(2,1)S(1)} %bitcast.25, ...), custom_call_target="tpu_custom_call" | custom-call | tf_op jit(solution)/shard_map/hidden/pallas_call | solution.py:131
  94.1 4.0 %collective-permute-start.19 = (bf16[256,1024]{1,0:T(8,128)(2,1)S(1)}, bf16[256,1024]{1,0:T(8,128)(2,1)S(1)}, u32[]{:S(2)}, u32[]{:S(2)}) collective-permute-start(bf16[256,1024]{1,0:T(8,128)(2,1)S(1)} %out.11), channel_id=1, source_target_pairs={{0,192},{64,128},{128,64},{192,0},{1,193},{65,129},{129,65},{193,1... | collective-permute-start | bytes 1572872 | tf_op jit(solution)/shard_map/ppermute | solution.py:35
  101.2 9.7 %collective-permute-done.17 = bf16[256,2048]{1,0:T(8,128)(2,1)S(1)} collective-permute-done((bf16[256,2048]{1,0:T(8,128)(2,1)S(1)}, bf16[256,2048]{1,0:T(8,128)(2,1)S(1)}, u32[]{:S(2)}, u32[]{:S(2)}) %collective-permute-start.17) | collective-permute-done | bytes 1048608 | tf_op jit(solution)/shard_map/ppermute | solution.py:35
  112.9 3.5 %collective-permute-done.21 = bf16[256,2048]{1,0:T(8,128)(2,1)S(1)} collective-permute-done((bf16[256,2048]{1,0:T(8,128)(2,1)S(1)}, bf16[256,2048]{1,0:T(8,128)(2,1)S(1)}, u32[]{:S(2)}, u32[]{:S(2)}) %collective-permute-start.21) | collective-permute-done | bytes 1048608 | tf_op jit(solution)/shard_map/ppermute | solution.py:35
  118.3 3.1 %collective-permute-done.20 = bf16[256,1024]{1,0:T(8,128)(2,1)S(1)} collective-permute-done((bf16[256,1024]{1,0:T(8,128)(2,1)S(1)}, bf16[256,1024]{1,0:T(8,128)(2,1)S(1)}, u32[]{:S(2)}, u32[]{:S(2)}) %collective-permute-start.20) | collective-permute-done | bytes 524320 | tf_op jit(solution)/shard_map/ppermute | solution.py:35
  126.7 3.0 %collective-permute-start.24 = (bf16[64,2048]{1,0:T(8,128)(2,1)S(1)}, bf16[64,2048]{1,0:T(8,128)(2,1)S(1)}, u32[]{:S(2)}, u32[]{:S(2)}) collective-permute-start(bf16[64,2048]{1,0:T(8,128)(2,1)S(1)} %get-tuple-element.97), channel_id=1, source_target_pairs={{0,64},{64,0},{128,192},{192,128},{1,65},{65,1},{129,193},{193,129... | collective-permute-start | bytes 786440 | tf_op jit(solution)/shard_map/ppermute | solution.py:35
  129.7 6.2 %collective-permute-done.25 = bf16[128,1024]{1,0:T(8,128)(2,1)S(1)} collective-permute-done((bf16[128,1024]{1,0:T(8,128)(2,1)S(1)}, bf16[128,1024]{1,0:T(8,128)(2,1)S(1)}, u32[]{:S(2)}, u32[]{:S(2)}) %collective-permute-start.25) | collective-permute-done | bytes 262176 | tf_op jit(solution)/shard_map/ppermute | solution.py:35
  136.2 11.5 %collective-permute-done.22 = bf16[64,2048]{1,0:T(8,128)(2,1)S(1)} collective-permute-done((bf16[64,2048]{1,0:T(8,128)(2,1)S(1)}, bf16[64,2048]{1,0:T(8,128)(2,1)S(1)}, u32[]{:S(2)}, u32[]{:S(2)}) %collective-permute-start.22) | collective-permute-done | bytes 262176 | tf_op jit(solution)/shard_map/ppermute | solution.py:35
  148.0 2.7 %collective-permute-start.29 = (bf16[32,2048]{1,0:T(8,128)(2,1)S(1)}, bf16[32,2048]{1,0:T(8,128)(2,1)S(1)}, u32[]{:S(2)}, u32[]{:S(2)}) collective-permute-start(bf16[32,2048]{1,0:T(8,128)(2,1)S(1)} %get-tuple-element.103), channel_id=1, source_target_pairs={{0,192},{64,128},{128,64},{192,0},{1,193},{65,129},{129,65},{193,1... | collective-permute-start | bytes 393224 | tf_op jit(solution)/shard_map/ppermute | solution.py:35
  152.9 2.2 %collective-permute-done.30.refs_6_ = bf16[32,1024]{1,0:T(8,128)(2,1)S(1)} collective-permute-done((bf16[32,1024]{1,0:T(8,128)(2,1)S(1)}, bf16[32,1024]{1,0:T(8,128)(2,1)S(1)}, u32[]{:S(2)}, u32[]{:S(2)}) %collective-permute-start.30) | collective-permute-done | bytes 65568 | tf_op jit(solution)/shard_map/ppermute | solution.py:35
  157.4 11.2 %all_to_all.11 = bf16[8,8,3072]{2,1,0:T(8,128)(2,1)S(1)} all-to-all(bf16[8,8,3072]{2,1,0:T(8,128)(2,1)S(1)} %bitcast.29), channel_id=1, replica_groups=mesh['dp'=4,'zl'=2,'y'=4,'x'=4,'c'=2] {'zl','y'}, dimensions={0} | all-to-all | bytes 786432 | tf_op jit(solution)/shard_map/all_to_all | solution.py:278
  (97 shorter events, 40.7 us)
Async XLA Ops:
  2.1 15.8 %collective-permute-start = (bf16[6144,256]{1,0:T(8,128)(2,1)}, bf16[6144,256]{1,0:T(8,128)(2,1)S(1)}, u32[]{:S(2)}, u32[]{:S(2)}) collective-permute-start(bf16[6144,256]{1,0:T(8,128)(2,1)} %bitcast.19), channel_id=1, source_target_pairs={{0,1},{1,0},{2,3},{3,2},{4,5},{5,4},{6,7},{7,6},{8,9},{9,8},{10,11... | collective-permute-start | bytes 9437192 | tf_op jit(solution)/shard_map/ppermute | solution.py:35
  2.2 15.7 %collective-permute-start.1 = (bf16[6144,256]{1,0:T(8,128)(2,1)}, bf16[6144,256]{1,0:T(8,128)(2,1)S(1)}, u32[]{:S(2)}, u32[]{:S(2)}) collective-permute-start(bf16[6144,256]{1,0:T(8,128)(2,1)} %bitcast.23), channel_id=1, source_target_pairs={{0,1},{1,0},{2,3},{3,2},{4,5},{5,4},{6,7},{7,6},{8,9},{9,8},{10,11... | collective-permute-start | bytes 9437192 | tf_op jit(solution)/shard_map/ppermute | solution.py:35
  2.7 29.1 %collective-permute-start.6 = (bf16[256,6144]{1,0:T(8,128)(2,1)}, bf16[256,6144]{1,0:T(8,128)(2,1)S(1)}, u32[]{:S(2)}, u32[]{:S(2)}) collective-permute-start(bf16[256,6144]{1,0:T(8,128)(2,1)} %bitcast.10), channel_id=1, source_target_pairs={{0,1},{1,0},{2,3},{3,2},{4,5},{5,4},{6,7},{7,6},{8,9},{9,8},{10,11... | collective-permute-start | bytes 9437192 | tf_op jit(solution)/shard_map/ppermute | solution.py:35
  18.8 13.0 %collective-permute-start.4 = (bf16[32,2048]{1,0:T(8,128)(2,1)S(1)}, bf16[32,2048]{1,0:T(8,128)(2,1)S(1)}, u32[]{:S(2)}, u32[]{:S(2)}) collective-permute-start(bf16[32,2048]{1,0:T(8,128)(2,1)S(1)} %get-tuple-element.53), channel_id=1, source_target_pairs={{0,192},{64,128},{128,64},{192,0},{1,193},{65,129},{129,65},{193,1... | collective-permute-start | bytes 393224 | tf_op jit(solution)/shard_map/ppermute | solution.py:35
  30.3 17.1 %collective-permute-start.9 = (bf16[64,2048]{1,0:T(8,128)(2,1)S(1)}, bf16[64,2048]{1,0:T(8,128)(2,1)S(1)}, u32[]{:S(2)}, u32[]{:S(2)}) collective-permute-start(bf16[64,2048]{1,0:T(8,128)(2,1)S(1)} %get-tuple-element.131), channel_id=1, source_target_pairs={{0,192},{64,128},{128,64},{192,0},{1,193},{65,129},{129,65},{193,1... | collective-permute-start | bytes 786440 | tf_op jit(solution)/shard_map/ppermute | solution.py:35
  31.8 17.8 %collective-permute-start.8 = (bf16[64,2048]{1,0:T(8,128)(2,1)S(1)}, bf16[64,2048]{1,0:T(8,128)(2,1)S(1)}, u32[]{:S(2)}, u32[]{:S(2)}) collective-permute-start(bf16[64,2048]{1,0:T(8,128)(2,1)S(1)} %get-tuple-element.125), channel_id=1, source_target_pairs={{0,64},{64,0},{128,192},{192,128},{1,65},{65,1},{129,193},{193,129... | collective-permute-start | bytes 786440 | tf_op jit(solution)/shard_map/ppermute | solution.py:35
  33.8 22.6 %collective-permute-start.7 = (bf16[128,1024]{1,0:T(8,128)(2,1)S(1)}, bf16[128,1024]{1,0:T(8,128)(2,1)S(1)}, u32[]{:S(2)}, u32[]{:S(2)}) collective-permute-start(bf16[128,1024]{1,0:T(8,128)(2,1)S(1)} %pad_maximum_fusion.2), channel_id=1, source_target_pairs={{0,192},{64,128},{128,64},{192,0},{1,193},{65,129},{129,65},{193,1... | collective-permute-start | bytes 786440 | tf_op jit(solution)/shard_map/ppermute | solution.py:35
  37.1 19.3 %collective-permute-start.12 = (bf16[128,1024]{1,0:T(8,128)(2,1)S(1)}, bf16[128,1024]{1,0:T(8,128)(2,1)S(1)}, u32[]{:S(2)}, u32[]{:S(2)}) collective-permute-start(bf16[128,1024]{1,0:T(8,128)(2,1)S(1)} %pad_maximum_fusion.3), channel_id=1, source_target_pairs={{0,64},{64,0},{128,192},{192,128},{1,65},{65,1},{129,193},{193,129... | collective-permute-start | bytes 786440 | tf_op jit(solution)/shard_map/ppermute | solution.py:35
  49.7 10.4 %collective-permute-start.14 = (bf16[128,2048]{1,0:T(8,128)(2,1)S(1)}, bf16[128,2048]{1,0:T(8,128)(2,1)S(1)}, u32[]{:S(2)}, u32[]{:S(2)}) collective-permute-start(bf16[128,2048]{1,0:T(8,128)(2,1)S(1)} %get-tuple-element.112), channel_id=1, source_target_pairs={{0,2},{2,0},{4,6},{6,4},{1,3},{3,1},{5,7},{7,5},{8,10},{10,8},{12,... | collective-permute-start | bytes 1572872 | tf_op jit(solution)/shard_map/ppermute | solution.py:35
  56.9 24.6 %collective-permute-start.13 = (bf16[256,2048]{1,0:T(8,128)(2,1)S(1)}, bf16[256,2048]{1,0:T(8,128)(2,1)S(1)}, u32[]{:S(2)}, u32[]{:S(2)}) collective-permute-start(bf16[256,2048]{1,0:T(8,128)(2,1)S(1)} %constant_dynamic-update-slice_fusion.12.refs_0_), channel_id=1, source_target_pairs={{0,2},{2,0},{4,6},{6,4},{1,3},{3,1},{5,7},{7,5},{8,10},{10,8},{12,... | collective-permute-start | bytes 3145736 | tf_op jit(solution)/shard_map/ppermute | solution.py:35
  60.1 21.4 %collective-permute-start.15 = (bf16[256,2048]{1,0:T(8,128)(2,1)S(1)}, bf16[256,2048]{1,0:T(8,128)(2,1)S(1)}, u32[]{:S(2)}, u32[]{:S(2)}) collective-permute-start(bf16[256,2048]{1,0:T(8,128)(2,1)S(1)} %constant_dynamic-update-slice_fusion.16.refs_1_), channel_id=1, source_target_pairs={{0,6},{2,4},{4,2},{6,0},{1,7},{3,5},{5,3},{7,1},{8,14},{10,12},{12... | collective-permute-start | bytes 3145736 | tf_op jit(solution)/shard_map/ppermute | solution.py:35
  61.1 23.7 %collective-permute-start.10 = (bf16[256,1024]{1,0:T(8,128)(2,1)S(1)}, bf16[256,1024]{1,0:T(8,128)(2,1)S(1)}, u32[]{:S(2)}, u32[]{:S(2)}) collective-permute-start(bf16[256,1024]{1,0:T(8,128)(2,1)S(1)} %pad_maximum_fusion.refs_2_), channel_id=1, source_target_pairs={{0,64},{64,0},{128,192},{192,128},{1,65},{65,1},{129,193},{193,129... | collective-permute-start | bytes 1572872 | tf_op jit(solution)/shard_map/ppermute | solution.py:35
  63.1 22.6 %collective-permute-start.16 = (bf16[256,1024]{1,0:T(8,128)(2,1)S(1)}, bf16[256,1024]{1,0:T(8,128)(2,1)S(1)}, u32[]{:S(2)}, u32[]{:S(2)}) collective-permute-start(bf16[256,1024]{1,0:T(8,128)(2,1)S(1)} %pad_maximum_fusion.1.refs_3_), channel_id=1, source_target_pairs={{0,192},{64,128},{128,64},{192,0},{1,193},{65,129},{129,65},{193,1... | collective-permute-start | bytes 1572872 | tf_op jit(solution)/shard_map/ppermute | solution.py:35
  88.7 22.2 %collective-permute-start.17 = (bf16[256,2048]{1,0:T(8,128)(2,1)S(1)}, bf16[256,2048]{1,0:T(8,128)(2,1)S(1)}, u32[]{:S(2)}, u32[]{:S(2)}) collective-permute-start(bf16[256,2048]{1,0:T(8,128)(2,1)S(1)} %out.8), channel_id=1, source_target_pairs={{0,2},{2,0},{4,6},{6,4},{1,3},{3,1},{5,7},{7,5},{8,10},{10,8},{12,... | collective-permute-start | bytes 3145736 | tf_op jit(solution)/shard_map/ppermute | solution.py:35
  91.4 25.1 %collective-permute-start.21 = (bf16[256,2048]{1,0:T(8,128)(2,1)S(1)}, bf16[256,2048]{1,0:T(8,128)(2,1)S(1)}, u32[]{:S(2)}, u32[]{:S(2)}) collective-permute-start(bf16[256,2048]{1,0:T(8,128)(2,1)S(1)} %out.9), channel_id=1, source_target_pairs={{0,6},{2,4},{4,2},{6,0},{1,7},{3,5},{5,3},{7,1},{8,14},{10,12},{12... | collective-permute-start | bytes 3145736 | tf_op jit(solution)/shard_map/ppermute | solution.py:35
  94.1 28.2 %collective-permute-start.19 = (bf16[256,1024]{1,0:T(8,128)(2,1)S(1)}, bf16[256,1024]{1,0:T(8,128)(2,1)S(1)}, u32[]{:S(2)}, u32[]{:S(2)}) collective-permute-start(bf16[256,1024]{1,0:T(8,128)(2,1)S(1)} %out.11), channel_id=1, source_target_pairs={{0,192},{64,128},{128,64},{192,0},{1,193},{65,129},{129,65},{193,1... | collective-permute-start | bytes 1572872 | tf_op jit(solution)/shard_map/ppermute | solution.py:35
  98.1 23.3 %collective-permute-start.20 = (bf16[256,1024]{1,0:T(8,128)(2,1)S(1)}, bf16[256,1024]{1,0:T(8,128)(2,1)S(1)}, u32[]{:S(2)}, u32[]{:S(2)}) collective-permute-start(bf16[256,1024]{1,0:T(8,128)(2,1)S(1)} %out.10), channel_id=1, source_target_pairs={{0,64},{64,0},{128,192},{192,128},{1,65},{65,1},{129,193},{193,129... | collective-permute-start | bytes 1572872 | tf_op jit(solution)/shard_map/ppermute | solution.py:35
  111.3 13.3 %collective-permute-start.18 = (bf16[128,2048]{1,0:T(8,128)(2,1)S(1)}, bf16[128,2048]{1,0:T(8,128)(2,1)S(1)}, u32[]{:S(2)}, u32[]{:S(2)}) collective-permute-start(bf16[128,2048]{1,0:T(8,128)(2,1)S(1)} %get-tuple-element.91), channel_id=1, source_target_pairs={{0,6},{2,4},{4,2},{6,0},{1,7},{3,5},{5,3},{7,1},{8,14},{10,12},{12... | collective-permute-start | bytes 1572872 | tf_op jit(solution)/shard_map/ppermute | solution.py:35
  116.8 9.8 %collective-permute-start.23 = (bf16[128,2048]{1,0:T(8,128)(2,1)S(1)}, bf16[128,2048]{1,0:T(8,128)(2,1)S(1)}, u32[]{:S(2)}, u32[]{:S(2)}) collective-permute-start(bf16[128,2048]{1,0:T(8,128)(2,1)S(1)} %get-tuple-element.90), channel_id=1, source_target_pairs={{0,2},{2,0},{4,6},{6,4},{1,3},{3,1},{5,7},{7,5},{8,10},{10,8},{12,... | collective-permute-start | bytes 1572872 | tf_op jit(solution)/shard_map/ppermute | solution.py:35
  121.6 14.3 %collective-permute-start.25 = (bf16[128,1024]{1,0:T(8,128)(2,1)S(1)}, bf16[128,1024]{1,0:T(8,128)(2,1)S(1)}, u32[]{:S(2)}, u32[]{:S(2)}) collective-permute-start(bf16[128,1024]{1,0:T(8,128)(2,1)S(1)} %get-tuple-element.96), channel_id=1, source_target_pairs={{0,192},{64,128},{128,64},{192,0},{1,193},{65,129},{129,65},{193,1... | collective-permute-start | bytes 786440 | tf_op jit(solution)/shard_map/ppermute | solution.py:35
  122.4 13.6 %collective-permute-start.26 = (bf16[128,1024]{1,0:T(8,128)(2,1)S(1)}, bf16[128,1024]{1,0:T(8,128)(2,1)S(1)}, u32[]{:S(2)}, u32[]{:S(2)}) collective-permute-start(bf16[128,1024]{1,0:T(8,128)(2,1)S(1)} %get-tuple-element.94), channel_id=1, source_target_pairs={{0,64},{64,0},{128,192},{192,128},{1,65},{65,1},{129,193},{193,129... | collective-permute-start | bytes 786440 | tf_op jit(solution)/shard_map/ppermute | solution.py:35
  124.7 23.0 %collective-permute-start.22 = (bf16[64,2048]{1,0:T(8,128)(2,1)S(1)}, bf16[64,2048]{1,0:T(8,128)(2,1)S(1)}, u32[]{:S(2)}, u32[]{:S(2)}) collective-permute-start(bf16[64,2048]{1,0:T(8,128)(2,1)S(1)} %get-tuple-element.100), channel_id=1, source_target_pairs={{0,192},{64,128},{128,64},{192,0},{1,193},{65,129},{129,65},{193,1... | collective-permute-start | bytes 786440 | tf_op jit(solution)/shard_map/ppermute | solution.py:35
  126.7 21.2 %collective-permute-start.24 = (bf16[64,2048]{1,0:T(8,128)(2,1)S(1)}, bf16[64,2048]{1,0:T(8,128)(2,1)S(1)}, u32[]{:S(2)}, u32[]{:S(2)}) collective-permute-start(bf16[64,2048]{1,0:T(8,128)(2,1)S(1)} %get-tuple-element.97), channel_id=1, source_target_pairs={{0,64},{64,0},{128,192},{192,128},{1,65},{65,1},{129,193},{193,129... | collective-permute-start | bytes 786440 | tf_op jit(solution)/shard_map/ppermute | solution.py:35
  136.1 14.6 %collective-permute-start.27 = (bf16[64,2048]{1,0:T(8,128)(2,1)S(1)}, bf16[64,2048]{1,0:T(8,128)(2,1)S(1)}, u32[]{:S(2)}, u32[]{:S(2)}) collective-permute-start(bf16[64,2048]{1,0:T(8,128)(2,1)S(1)} %pad_maximum_fusion.4), channel_id=1, source_target_pairs={{0,6},{2,4},{4,2},{6,0},{1,7},{3,5},{5,3},{7,1},{8,14},{10,12},{12... | collective-permute-start | bytes 786440 | tf_op jit(solution)/shard_map/ppermute | solution.py:35
  (13 other events, 183.9 us)

commit v11 on v10

--- a/solution.py
+++ b/solution.py
@@ -14,11 +14,18 @@
 
 DIMS = {"xa": ("x", 1), "xb": ("x", 3), "za": ("dp", 1), "zb": ("dp", 3), "c": ("c", 1)}
 CHAINS = (
-    (0, 2048, ("za", "zb", "xb", "xa")),
-    (3072, 2048, ("zb", "za", "xa", "xb")),
-    (2048, 1024, ("xa", "xb", "zb", "za")),
-    (5120, 1024, ("xa", "xb", "za", "zb")),
+    (0, 1792, ("za", "zb", "xb", "xa")),
+    (3072, 1792, ("zb", "za", "xa", "xb")),
+    (1792, 1280, ("xa", "xb", "zb", "za")),
+    (4864, 1280, ("xa", "xb", "za", "zb")),
 )
+OUT_CHAINS = tuple(
+    (start, size, order)
+    for (start, size), (_, _, order) in zip(
+        ((0, 2048), (3072, 2048), (2048, 1024), (5120, 1024)), CHAINS
+    )
+)
+DEPTHS = (896, 896, 1280, 1280)
 JOINED = ((0,), (1,), (2, 3))
 CANON = ("xa", "xb", "za", "zb")
 UNIT = 32
@@ -43,17 +50,22 @@
     return lax.optimization_barrier((value, *others))[0]
 
 
+def depths_of(pieces):
+    return sorted({DEPTHS[c] for c, _ in pieces})
+
+
 def hidden_kernel(pieces, first, last, *refs):
     n = len(pieces)
     ins = refs[:n]
-    wg0, wu0, wg1, wu1 = refs[n : n + 4]
-    refs = refs[n + 4 :]
+    depths = depths_of(pieces)
+    weights = [refs[n + 4 * k : n + 4 * k + 4] for k in range(len(depths))]
+    refs = refs[n + 4 * len(depths) :]
     before = None if first else refs[0]
     refs = refs if first else refs[1:]
     total = refs[0]
     acc = refs[1] if last else total
     step = pl.program_id(0)
-    units = wg0.shape[1]
+    units = weights[0][0].shape[1]
     f32 = jnp.float32
 
     @pl.when(step == 0)
@@ -63,11 +75,11 @@
     at = 0
     for k, (c, came) in enumerate(pieces):
         _, width, order = CHAINS[c]
-        steps = width // PART
+        steps = width // DEPTHS[c]
 
         @pl.when((step >= at) & (step < at + steps))
-        def _(k=k, order=order, came=came):
-            for i, w in enumerate((wg0, wu0, wg1, wu1)):
+        def _(k=k, order=order, came=came, ws=weights[depths.index(DEPTHS[c])]):
+            for i, w in enumerate(ws):
                 product = jnp.dot(ins[k][...], w[...], preferred_element_type=f32)
                 for index in range(8):
                     to = canon_block(order, index + 8 * came) * UNIT
@@ -100,9 +112,9 @@
 
 
 def pick(table, i):
-    value = table[0]
-    for k, entry in enumerate(table[1:], 1):
-        value = jnp.where(i >= k, entry, value)
+    value = table[0][1]
+    for step, entry in table[1:]:
+        value = jnp.where(i >= step, entry, value)
     return value
 
 
@@ -110,15 +122,21 @@
     width, units = weights[0].shape
     count = 2 * HALF
     first = before is None
-    in_specs, parts = [], []
+    in_specs, tables, steps = [], {}, 0
     for c, _ in pieces:
         start, size, _ = CHAINS[c]
-        low, steps = len(parts), size // PART
-        to = lambda i, low=low, steps=steps: (0, jnp.clip(i - low, 0, steps - 1))
-        in_specs.append(pl.BlockSpec((HALF, PART), to))
-        parts += [start // PART + k for k in range(steps)]
+        depth = DEPTHS[c]
+        more = size // depth
+        to = lambda i, low=steps, more=more: (0, jnp.clip(i - low, 0, more - 1))
+        in_specs.append(pl.BlockSpec((HALF, depth), to))
+        tables.setdefault(depth, []).extend(
+            (steps + k, start + k * depth) for k in range(more)
+        )
+        steps += more
     whole = lambda *shape: pl.BlockSpec(shape, lambda i: (0,) * len(shape))
-    in_specs += [pl.BlockSpec((PART, units), lambda i: (pick(parts, i), 0))] * 4
+    for depth in depths_of(pieces):
+        at = lambda i, table=tables[depth]: (pl.multiple_of(pick(table, i), 128), 0)
+        in_specs += [pl.BlockSpec((pl.Element(depth), pl.Element(units)), at)] * 4
     sums = (4, count, units)
     if not first:
         in_specs.append(whole(*sums))
@@ -127,10 +145,10 @@
         scratch = [pltpu.VMEM(sums, jnp.float32)]
     else:
         out, out_spec, scratch = jax.ShapeDtypeStruct(sums, jnp.float32), whole(*sums), []
-    depth = len(parts) * PART
+    depth = sum(CHAINS[c][1] for c, _ in pieces)
     return pl.pallas_call(
         functools.partial(hidden_kernel, tuple(pieces), first, last),
-        grid=(len(parts),),
+        grid=(steps,),
         out_shape=out,
         in_specs=in_specs,
         out_specs=out_spec,
@@ -142,11 +160,11 @@
             transcendentals=2 * count * units if last else 0,
         ),
         name="hidden",
-    )(*pieces.values(), *weights, *(() if first else (before,)))
+    )(*pieces.values(), *weights * len(tables), *(() if first else (before,)))
 
 
 def expert_out(hidden, wd0, wd1, chain, sent):
-    start, size, order = CHAINS[chain]
+    start, size, order = OUT_CHAINS[chain]
     units = wd0.shape[0]
     low, count = start // PART, 2 * HALF
     return pl.pallas_call(
@@ -232,7 +250,7 @@
     held, came, folded = refs[:n], refs[n : 2 * n], refs[2 * n]
     half = folded.shape[1]
     f32 = jnp.float32
-    for c, (start, size, _) in enumerate(CHAINS):
+    for c, (start, size, _) in enumerate(OUT_CHAINS):
         total = (held[c][...].astype(f32) + came[c][...].astype(f32)).astype(folded.dtype)
         side = start // half
         give = onehot(2 * UNIT, UNIT, lambda r, c: r == (c // 4) * 8 + c % 4 + 4 * side)
@@ -367,7 +385,7 @@
         got = came[k] if last is None else after(came[k], last)
         away[k] = last = add(held[k][half:], got[half:])
         held[k] = add(held[k][:half], got[:half])
-    size = CHAINS[2][1]
+    size = OUT_CHAINS[2][1]
     part = lambda values: values[:2] + [values[2][:, :size], values[2][:, size:]]
     held, away = part(held), part(away)
     came = [trade(a, order[0]) for a, (_, _, order) in zip(away, CHAINS)]

time: 170 us -> 172 us (1.012)
  starting transfers between devices: 51.3 us -> 58.4 us
  waiting for transfers between devices: 69.5 us -> 62.7 us
    ppermute x32, starting transfers between devices: 51.3 us -> 58.4 us  [trade(): return lax.ppermute(value, axis, [(i, i ^ mask) for i in range(n)])]
    ppermute x32, waiting for transfers between devices: 69.5 us -> 62.7 us  [trade(): return lax.ppermute(value, axis, [(i, i ^ mask) for i in range(n)])]
  transfers between devices with their start and end apart: 32 -> 32, of which waited for: 17 -> 15; matrix products, arithmetic and copies ran while one was open for 1% -> 1% of each run, Pallas kernels for 8% -> 8%
where the time goes in v11:
time: 172 us; the launch traced here: 171 us
  waiting for transfers between devices  62.7 us (36%)
  starting transfers between devices  58.4 us (34%)
  blocking collectives  26.9 us (16%)
  Pallas kernels  20.7 us (12%)
  other arithmetic  1.85 us (1%)
    ppermute x32, waiting for transfers between devices, trade(): return lax.ppermute(value, axis, [(i, i ^ mask) for i in range(n)])  62.7 us
    ppermute x32, starting transfers between devices, trade(): return lax.ppermute(value, axis, [(i, i ^ mask) for i in range(n)])  58.4 us
    all_to_all x2, blocking collectives, swap_experts(): lax.all_to_all(blocks, ('zl', 'y'), split_axis=0, concat_axis=0, tiled=True)  26.9 us
    pallas_call x3, Pallas kernels, hidden_units(): pl.pallas_call(functools.partial(hidden_kernel, tuple(pieces), first, las...  10.6 us
    pallas_call x8, Pallas kernels, expert_out(): pl.pallas_call(functools.partial(out_kernel, order, int(sent)), grid=(siz...  6.21 us
    pallas_call x4, Pallas kernels, small(): pl.pallas_call(kernel, out_shape=out_shape, in_specs=[pl.BlockSpec(memory...  3.81 us
  transfers between devices with their start and end apart: 32, of which 15 were waited for; matrix products, arithmetic and copies ran while one was open for 1% of the time, Pallas kernels for 8%

profile of v11, /device:TPU:2, one launch (start us, length us, event | category | flops | bytes accessed | tf_op | source)
XLA Modules:
  0.0 171.3 jit_solution(7841739844398633920)
XLA Ops:
  2.8 15.1 %all_to_all.10 = bf16[8,8,3072]{2,1,0:T(8,128)(2,1)S(1)} all-to-all(bf16[8,8,3072]{2,1,0:T(8,128)(2,1)} %bitcast.32), channel_id=1, replica_groups=mesh['dp'=4,'zl'=2,'y'=4,'x'=4,'c'=2] {'zl','y'}, dimensions={0} | all-to-all | bytes 786432 | tf_op jit(solution)/shard_map/all_to_all | solution.py:296
  18.8 5.4 %collective-permute-start.4 = (bf16[32,1792]{1,0:T(8,128)(2,1)S(1)}, bf16[32,1792]{1,0:T(8,128)(2,1)S(1)}, u32[]{:S(2)}, u32[]{:S(2)}) collective-permute-start(bf16[32,1792]{1,0:T(8,128)(2,1)S(1)} %get-tuple-element.53), channel_id=1, source_target_pairs={{0,192},{64,128},{128,64},{192,0},{1,193},{65,129},{129,65},{193,1... | collective-permute-start | bytes 344072 | tf_op jit(solution)/shard_map/ppermute | solution.py:42
  25.8 2.2 %collective-permute-start.3 = (bf16[64,2560]{1,0:T(8,128)(2,1)S(1)}, bf16[64,2560]{1,0:T(8,128)(2,1)S(1)}, u32[]{:S(2)}, u32[]{:S(2)}) collective-permute-start(bf16[64,2560]{1,0:T(8,128)(2,1)S(1)} %constant_dynamic-update-slice_fusion), channel_id=1, source_target_pairs={{0,6},{2,4},{4,2},{6,0},{1,7},{3,5},{5,3},{7,1},{8,14},{10,12},{12... | collective-permute-start | bytes 983048 | tf_op jit(solution)/shard_map/ppermute | solution.py:42
  28.0 3.2 %collective-permute-done.5 = bf16[32,1792]{1,0:T(8,128)(2,1)S(1)} collective-permute-done((bf16[32,1792]{1,0:T(8,128)(2,1)S(1)}, bf16[32,1792]{1,0:T(8,128)(2,1)S(1)}, u32[]{:S(2)}, u32[]{:S(2)}) %collective-permute-start.5) | collective-permute-done | bytes 114720 | tf_op jit(solution)/shard_map/ppermute | solution.py:42
  33.9 2.6 %collective-permute-start.7 = (bf16[128,1280]{1,0:T(8,128)(2,1)S(1)}, bf16[128,1280]{1,0:T(8,128)(2,1)S(1)}, u32[]{:S(2)}, u32[]{:S(2)}) collective-permute-start(bf16[128,1280]{1,0:T(8,128)(2,1)S(1)} %pad_maximum_fusion.2), channel_id=1, source_target_pairs={{0,192},{64,128},{128,64},{192,0},{1,193},{65,129},{129,65},{193,1... | collective-permute-start | bytes 983048 | tf_op jit(solution)/shard_map/ppermute | solution.py:42
  36.5 2.3 %collective-permute-start.12 = (bf16[128,1280]{1,0:T(8,128)(2,1)S(1)}, bf16[128,1280]{1,0:T(8,128)(2,1)S(1)}, u32[]{:S(2)}, u32[]{:S(2)}) collective-permute-start(bf16[128,1280]{1,0:T(8,128)(2,1)S(1)} %pad_maximum_fusion.3), channel_id=1, source_target_pairs={{0,64},{64,0},{128,192},{192,128},{1,65},{65,1},{129,193},{193,129... | collective-permute-start | bytes 983048 | tf_op jit(solution)/shard_map/ppermute | solution.py:42
  38.8 8.0 %collective-permute-done.9 = bf16[64,1792]{1,0:T(8,128)(2,1)S(1)} collective-permute-done((bf16[64,1792]{1,0:T(8,128)(2,1)S(1)}, bf16[64,1792]{1,0:T(8,128)(2,1)S(1)}, u32[]{:S(2)}, u32[]{:S(2)}) %collective-permute-start.9) | collective-permute-done | bytes 229408 | tf_op jit(solution)/shard_map/ppermute | solution.py:42
  47.7 8.5 %collective-permute-start.14 = (bf16[128,1792]{1,0:T(8,128)(2,1)S(1)}, bf16[128,1792]{1,0:T(8,128)(2,1)S(1)}, u32[]{:S(2)}, u32[]{:S(2)}) collective-permute-start(bf16[128,1792]{1,0:T(8,128)(2,1)S(1)} %get-tuple-element.116), channel_id=1, source_target_pairs={{0,2},{2,0},{4,6},{6,4},{1,3},{3,1},{5,7},{7,5},{8,10},{10,8},{12,... | collective-permute-start | bytes 1376264 | tf_op jit(solution)/shard_map/ppermute | solution.py:42
  56.4 11.7 %collective-permute-start.13 = (bf16[256,1792]{1,0:T(8,128)(2,1)S(1)}, bf16[256,1792]{1,0:T(8,128)(2,1)S(1)}, u32[]{:S(2)}, u32[]{:S(2)}) collective-permute-start(bf16[256,1792]{1,0:T(8,128)(2,1)S(1)} %constant_dynamic-update-slice_fusion.12.refs_0_), channel_id=1, source_target_pairs={{0,2},{2,0},{4,6},{6,4},{1,3},{3,1},{5,7},{7,5},{8,10},{10,8},{12,... | collective-permute-start | bytes 2752520 | tf_op jit(solution)/shard_map/ppermute | solution.py:42
  69.4 5.2 %hidden.3.refs_6_ = f32[4,512,256]{2,1,0:T(8,128)S(1)} custom-call(bf16[256,1792]{1,0:T(8,128)(2,1)S(1)} %constant_dynamic-update-slice_fusion.12.refs_0_, bf16[256,1792]{1,0:T(8,128)(2,1)S(1)} %constant_dynamic-update-slice_fusion.16.refs_1_, bf16[256,1280]{1,0:T(8,128)(2,1)S(1)} %pad_maximum_fusion.refs_2_, ...), custom_call_target="tpu_custom_call" | custom-call | tf_op jit(solution)/shard_map/hidden/pallas_call | solution.py:149
  74.6 6.4 %collective-permute-done.13.refs_0_ = bf16[256,1792]{1,0:T(8,128)(2,1)S(1)} collective-permute-done((bf16[256,1792]{1,0:T(8,128)(2,1)S(1)}, bf16[256,1792]{1,0:T(8,128)(2,1)S(1)}, u32[]{:S(2)}, u32[]{:S(2)}) %collective-permute-start.13) | collective-permute-done | bytes 917536 | tf_op jit(solution)/shard_map/ppermute | solution.py:42
  81.6 3.3 %hidden.4.refs_6_ = f32[4,512,256]{2,1,0:T(8,128)S(1)} custom-call(bf16[256,1792]{1,0:T(8,128)(2,1)S(1)} %collective-permute-done.13.refs_0_, bf16[256,1792]{1,0:T(8,128)(2,1)S(1)} %collective-permute-done.15.refs_1_, bf16[6144,256]{1,0:T(8,128)(2,1)S(1)} %bitcast.22, bf16[6144,256]{1,0:T(8,128)(2,1)S(1)} %bitcast.27, ...), custom_call_target="tpu_custom_call" | custom-call | tf_op jit(solution)/shard_map/hidden/pallas_call | solution.py:149
  84.9 5.0 %collective-permute-done.10.refs_0_ = bf16[256,1280]{1,0:T(8,128)(2,1)S(1)} collective-permute-done((bf16[256,1280]{1,0:T(8,128)(2,1)S(1)}, bf16[256,1280]{1,0:T(8,128)(2,1)S(1)}, u32[]{:S(2)}, u32[]{:S(2)}) %collective-permute-start.10) | collective-permute-done | bytes 655392 | tf_op jit(solution)/shard_map/ppermute | solution.py:42
  95.4 2.3 %collective-permute-start.17 = (bf16[256,2048]{1,0:T(8,128)(2,1)S(1)}, bf16[256,2048]{1,0:T(8,128)(2,1)S(1)}, u32[]{:S(2)}, u32[]{:S(2)}) collective-permute-start(bf16[256,2048]{1,0:T(8,128)(2,1)S(1)} %out.8), channel_id=1, source_target_pairs={{0,2},{2,0},{4,6},{6,4},{1,3},{3,1},{5,7},{7,5},{8,10},{10,8},{12,... | collective-permute-start | bytes 3145736 | tf_op jit(solution)/shard_map/ppermute | solution.py:42
  99.7 2.5 %collective-permute-start.19 = (bf16[256,1024]{1,0:T(8,128)(2,1)S(1)}, bf16[256,1024]{1,0:T(8,128)(2,1)S(1)}, u32[]{:S(2)}, u32[]{:S(2)}) collective-permute-start(bf16[256,1024]{1,0:T(8,128)(2,1)S(1)} %out.11), channel_id=1, source_target_pairs={{0,192},{64,128},{128,64},{192,0},{1,193},{65,129},{129,65},{193,1... | collective-permute-start | bytes 1572872 | tf_op jit(solution)/shard_map/ppermute | solution.py:42
  105.8 10.5 %collective-permute-done.17 = bf16[256,2048]{1,0:T(8,128)(2,1)S(1)} collective-permute-done((bf16[256,2048]{1,0:T(8,128)(2,1)S(1)}, bf16[256,2048]{1,0:T(8,128)(2,1)S(1)}, u32[]{:S(2)}, u32[]{:S(2)}) %collective-permute-start.17) | collective-permute-done | bytes 1048608 | tf_op jit(solution)/shard_map/ppermute | solution.py:42
  116.8 5.8 %collective-permute-done.21 = bf16[256,2048]{1,0:T(8,128)(2,1)S(1)} collective-permute-done((bf16[256,2048]{1,0:T(8,128)(2,1)S(1)}, bf16[256,2048]{1,0:T(8,128)(2,1)S(1)}, u32[]{:S(2)}, u32[]{:S(2)}) %collective-permute-start.21) | collective-permute-done | bytes 1048608 | tf_op jit(solution)/shard_map/ppermute | solution.py:42
  124.9 2.8 %collective-permute-start.25 = (bf16[128,1024]{1,0:T(8,128)(2,1)S(1)}, bf16[128,1024]{1,0:T(8,128)(2,1)S(1)}, u32[]{:S(2)}, u32[]{:S(2)}) collective-permute-start(bf16[128,1024]{1,0:T(8,128)(2,1)S(1)} %get-tuple-element.96), channel_id=1, source_target_pairs={{0,192},{64,128},{128,64},{192,0},{1,193},{65,129},{129,65},{193,1... | collective-permute-start | bytes 786440 | tf_op jit(solution)/shard_map/ppermute | solution.py:42
  129.7 3.3 %collective-permute-start.22 = (bf16[64,2048]{1,0:T(8,128)(2,1)S(1)}, bf16[64,2048]{1,0:T(8,128)(2,1)S(1)}, u32[]{:S(2)}, u32[]{:S(2)}) collective-permute-start(bf16[64,2048]{1,0:T(8,128)(2,1)S(1)} %get-tuple-element.100), channel_id=1, source_target_pairs={{0,192},{64,128},{128,64},{192,0},{1,193},{65,129},{129,65},{193,1... | collective-permute-start | bytes 786440 | tf_op jit(solution)/shard_map/ppermute | solution.py:42
  133.3 5.1 %collective-permute-done.25 = bf16[128,1024]{1,0:T(8,128)(2,1)S(1)} collective-permute-done((bf16[128,1024]{1,0:T(8,128)(2,1)S(1)}, bf16[128,1024]{1,0:T(8,128)(2,1)S(1)}, u32[]{:S(2)}, u32[]{:S(2)}) %collective-permute-start.25) | collective-permute-done | bytes 262176 | tf_op jit(solution)/shard_map/ppermute | solution.py:42
  140.1 6.4 %collective-permute-done.22 = bf16[64,2048]{1,0:T(8,128)(2,1)S(1)} collective-permute-done((bf16[64,2048]{1,0:T(8,128)(2,1)S(1)}, bf16[64,2048]{1,0:T(8,128)(2,1)S(1)}, u32[]{:S(2)}, u32[]{:S(2)}) %collective-permute-start.22) | collective-permute-done | bytes 262176 | tf_op jit(solution)/shard_map/ppermute | solution.py:42
  146.7 3.7 %collective-permute-done.24 = bf16[64,2048]{1,0:T(8,128)(2,1)S(1)} collective-permute-done((bf16[64,2048]{1,0:T(8,128)(2,1)S(1)}, bf16[64,2048]{1,0:T(8,128)(2,1)S(1)}, u32[]{:S(2)}, u32[]{:S(2)}) %collective-permute-start.24) | collective-permute-done | bytes 262176 | tf_op jit(solution)/shard_map/ppermute | solution.py:42
  154.5 2.2 %collective-permute-done.30.refs_6_ = bf16[32,1024]{1,0:T(8,128)(2,1)S(1)} collective-permute-done((bf16[32,1024]{1,0:T(8,128)(2,1)S(1)}, bf16[32,1024]{1,0:T(8,128)(2,1)S(1)}, u32[]{:S(2)}, u32[]{:S(2)}) %collective-permute-start.30) | collective-permute-done | bytes 65568 | tf_op jit(solution)/shard_map/ppermute | solution.py:42
  158.3 11.8 %all_to_all.11 = bf16[8,8,3072]{2,1,0:T(8,128)(2,1)S(1)} all-to-all(bf16[8,8,3072]{2,1,0:T(8,128)(2,1)S(1)} %bitcast.31), channel_id=1, replica_groups=mesh['dp'=4,'zl'=2,'y'=4,'x'=4,'c'=2] {'zl','y'}, dimensions={0} | all-to-all | bytes 786432 | tf_op jit(solution)/shard_map/all_to_all | solution.py:296
  (97 shorter events, 35.5 us)
Async XLA Ops:
  2.1 15.8 %collective-permute-start = (bf16[6144,256]{1,0:T(8,128)(2,1)}, bf16[6144,256]{1,0:T(8,128)(2,1)S(1)}, u32[]{:S(2)}, u32[]{:S(2)}) collective-permute-start(bf16[6144,256]{1,0:T(8,128)(2,1)} %bitcast.19), channel_id=1, source_target_pairs={{0,1},{1,0},{2,3},{3,2},{4,5},{5,4},{6,7},{7,6},{8,9},{9,8},{10,11... | collective-permute-start | bytes 9437192 | tf_op jit(solution)/shard_map/ppermute | solution.py:42
  2.2 15.7 %collective-permute-start.1 = (bf16[6144,256]{1,0:T(8,128)(2,1)}, bf16[6144,256]{1,0:T(8,128)(2,1)S(1)}, u32[]{:S(2)}, u32[]{:S(2)}) collective-permute-start(bf16[6144,256]{1,0:T(8,128)(2,1)} %bitcast.24), channel_id=1, source_target_pairs={{0,1},{1,0},{2,3},{3,2},{4,5},{5,4},{6,7},{7,6},{8,9},{9,8},{10,11... | collective-permute-start | bytes 9437192 | tf_op jit(solution)/shard_map/ppermute | solution.py:42
  2.7 28.9 %collective-permute-start.6 = (bf16[256,6144]{1,0:T(8,128)(2,1)}, bf16[256,6144]{1,0:T(8,128)(2,1)S(1)}, u32[]{:S(2)}, u32[]{:S(2)}) collective-permute-start(bf16[256,6144]{1,0:T(8,128)(2,1)} %bitcast.10), channel_id=1, source_target_pairs={{0,1},{1,0},{2,3},{3,2},{4,5},{5,4},{6,7},{7,6},{8,9},{9,8},{10,11... | collective-permute-start | bytes 9437192 | tf_op jit(solution)/shard_map/ppermute | solution.py:42
  18.8 12.8 %collective-permute-start.4 = (bf16[32,1792]{1,0:T(8,128)(2,1)S(1)}, bf16[32,1792]{1,0:T(8,128)(2,1)S(1)}, u32[]{:S(2)}, u32[]{:S(2)}) collective-permute-start(bf16[32,1792]{1,0:T(8,128)(2,1)S(1)} %get-tuple-element.53), channel_id=1, source_target_pairs={{0,192},{64,128},{128,64},{192,0},{1,193},{65,129},{129,65},{193,1... | collective-permute-start | bytes 344072 | tf_op jit(solution)/shard_map/ppermute | solution.py:42
  31.3 15.5 %collective-permute-start.9 = (bf16[64,1792]{1,0:T(8,128)(2,1)S(1)}, bf16[64,1792]{1,0:T(8,128)(2,1)S(1)}, u32[]{:S(2)}, u32[]{:S(2)}) collective-permute-start(bf16[64,1792]{1,0:T(8,128)(2,1)S(1)} %get-tuple-element.131), channel_id=1, source_target_pairs={{0,192},{64,128},{128,64},{192,0},{1,193},{65,129},{129,65},{193,1... | collective-permute-start | bytes 688136 | tf_op jit(solution)/shard_map/ppermute | solution.py:42
  31.7 16.0 %collective-permute-start.8 = (bf16[64,1792]{1,0:T(8,128)(2,1)S(1)}, bf16[64,1792]{1,0:T(8,128)(2,1)S(1)}, u32[]{:S(2)}, u32[]{:S(2)}) collective-permute-start(bf16[64,1792]{1,0:T(8,128)(2,1)S(1)} %get-tuple-element.125), channel_id=1, source_target_pairs={{0,64},{64,0},{128,192},{192,128},{1,65},{65,1},{129,193},{193,129... | collective-permute-start | bytes 688136 | tf_op jit(solution)/shard_map/ppermute | solution.py:42
  33.9 22.3 %collective-permute-start.7 = (bf16[128,1280]{1,0:T(8,128)(2,1)S(1)}, bf16[128,1280]{1,0:T(8,128)(2,1)S(1)}, u32[]{:S(2)}, u32[]{:S(2)}) collective-permute-start(bf16[128,1280]{1,0:T(8,128)(2,1)S(1)} %pad_maximum_fusion.2), channel_id=1, source_target_pairs={{0,192},{64,128},{128,64},{192,0},{1,193},{65,129},{129,65},{193,1... | collective-permute-start | bytes 983048 | tf_op jit(solution)/shard_map/ppermute | solution.py:42
  36.5 19.8 %collective-permute-start.12 = (bf16[128,1280]{1,0:T(8,128)(2,1)S(1)}, bf16[128,1280]{1,0:T(8,128)(2,1)S(1)}, u32[]{:S(2)}, u32[]{:S(2)}) collective-permute-start(bf16[128,1280]{1,0:T(8,128)(2,1)S(1)} %pad_maximum_fusion.3), channel_id=1, source_target_pairs={{0,64},{64,0},{128,192},{192,128},{1,65},{65,1},{129,193},{193,129... | collective-permute-start | bytes 983048 | tf_op jit(solution)/shard_map/ppermute | solution.py:42
  47.7 20.3 %collective-permute-start.14 = (bf16[128,1792]{1,0:T(8,128)(2,1)S(1)}, bf16[128,1792]{1,0:T(8,128)(2,1)S(1)}, u32[]{:S(2)}, u32[]{:S(2)}) collective-permute-start(bf16[128,1792]{1,0:T(8,128)(2,1)S(1)} %get-tuple-element.116), channel_id=1, source_target_pairs={{0,2},{2,0},{4,6},{6,4},{1,3},{3,1},{5,7},{7,5},{8,10},{10,8},{12,... | collective-permute-start | bytes 1376264 | tf_op jit(solution)/shard_map/ppermute | solution.py:42
  56.4 24.6 %collective-permute-start.13 = (bf16[256,1792]{1,0:T(8,128)(2,1)S(1)}, bf16[256,1792]{1,0:T(8,128)(2,1)S(1)}, u32[]{:S(2)}, u32[]{:S(2)}) collective-permute-start(bf16[256,1792]{1,0:T(8,128)(2,1)S(1)} %constant_dynamic-update-slice_fusion.12.refs_0_), channel_id=1, source_target_pairs={{0,2},{2,0},{4,6},{6,4},{1,3},{3,1},{5,7},{7,5},{8,10},{10,8},{12,... | collective-permute-start | bytes 2752520 | tf_op jit(solution)/shard_map/ppermute | solution.py:42
  68.1 13.5 %collective-permute-start.15 = (bf16[256,1792]{1,0:T(8,128)(2,1)S(1)}, bf16[256,1792]{1,0:T(8,128)(2,1)S(1)}, u32[]{:S(2)}, u32[]{:S(2)}) collective-permute-start(bf16[256,1792]{1,0:T(8,128)(2,1)S(1)} %constant_dynamic-update-slice_fusion.16.refs_1_), channel_id=1, source_target_pairs={{0,6},{2,4},{4,2},{6,0},{1,7},{3,5},{5,3},{7,1},{8,14},{10,12},{12... | collective-permute-start | bytes 2752520 | tf_op jit(solution)/shard_map/ppermute | solution.py:42
  69.3 20.5 %collective-permute-start.10 = (bf16[256,1280]{1,0:T(8,128)(2,1)S(1)}, bf16[256,1280]{1,0:T(8,128)(2,1)S(1)}, u32[]{:S(2)}, u32[]{:S(2)}) collective-permute-start(bf16[256,1280]{1,0:T(8,128)(2,1)S(1)} %pad_maximum_fusion.refs_2_), channel_id=1, source_target_pairs={{0,64},{64,0},{128,192},{192,128},{1,65},{65,1},{129,193},{193,129... | collective-permute-start | bytes 1966088 | tf_op jit(solution)/shard_map/ppermute | solution.py:42
  69.3 22.7 %collective-permute-start.16 = (bf16[256,1280]{1,0:T(8,128)(2,1)S(1)}, bf16[256,1280]{1,0:T(8,128)(2,1)S(1)}, u32[]{:S(2)}, u32[]{:S(2)}) collective-permute-start(bf16[256,1280]{1,0:T(8,128)(2,1)S(1)} %pad_maximum_fusion.1.refs_3_), channel_id=1, source_target_pairs={{0,192},{64,128},{128,64},{192,0},{1,193},{65,129},{129,65},{193,1... | collective-permute-start | bytes 1966088 | tf_op jit(solution)/shard_map/ppermute | solution.py:42
  95.4 20.9 %collective-permute-start.17 = (bf16[256,2048]{1,0:T(8,128)(2,1)S(1)}, bf16[256,2048]{1,0:T(8,128)(2,1)S(1)}, u32[]{:S(2)}, u32[]{:S(2)}) collective-permute-start(bf16[256,2048]{1,0:T(8,128)(2,1)S(1)} %out.8), channel_id=1, source_target_pairs={{0,2},{2,0},{4,6},{6,4},{1,3},{3,1},{5,7},{7,5},{8,10},{10,8},{12,... | collective-permute-start | bytes 3145736 | tf_op jit(solution)/shard_map/ppermute | solution.py:42
  98.8 23.9 %collective-permute-start.21 = (bf16[256,2048]{1,0:T(8,128)(2,1)S(1)}, bf16[256,2048]{1,0:T(8,128)(2,1)S(1)}, u32[]{:S(2)}, u32[]{:S(2)}) collective-permute-start(bf16[256,2048]{1,0:T(8,128)(2,1)S(1)} %out.9), channel_id=1, source_target_pairs={{0,6},{2,4},{4,2},{6,0},{1,7},{3,5},{5,3},{7,1},{8,14},{10,12},{12... | collective-permute-start | bytes 3145736 | tf_op jit(solution)/shard_map/ppermute | solution.py:42
  99.7 27.9 %collective-permute-start.19 = (bf16[256,1024]{1,0:T(8,128)(2,1)S(1)}, bf16[256,1024]{1,0:T(8,128)(2,1)S(1)}, u32[]{:S(2)}, u32[]{:S(2)}) collective-permute-start(bf16[256,1024]{1,0:T(8,128)(2,1)S(1)} %out.11), channel_id=1, source_target_pairs={{0,192},{64,128},{128,64},{192,0},{1,193},{65,129},{129,65},{193,1... | collective-permute-start | bytes 1572872 | tf_op jit(solution)/shard_map/ppermute | solution.py:42
  102.3 22.4 %collective-permute-start.20 = (bf16[256,1024]{1,0:T(8,128)(2,1)S(1)}, bf16[256,1024]{1,0:T(8,128)(2,1)S(1)}, u32[]{:S(2)}, u32[]{:S(2)}) collective-permute-start(bf16[256,1024]{1,0:T(8,128)(2,1)S(1)} %out.10), channel_id=1, source_target_pairs={{0,64},{64,0},{128,192},{192,128},{1,65},{65,1},{129,193},{193,129... | collective-permute-start | bytes 1572872 | tf_op jit(solution)/shard_map/ppermute | solution.py:42
  116.7 12.9 %collective-permute-start.18 = (bf16[128,2048]{1,0:T(8,128)(2,1)S(1)}, bf16[128,2048]{1,0:T(8,128)(2,1)S(1)}, u32[]{:S(2)}, u32[]{:S(2)}) collective-permute-start(bf16[128,2048]{1,0:T(8,128)(2,1)S(1)} %get-tuple-element.91), channel_id=1, source_target_pairs={{0,6},{2,4},{4,2},{6,0},{1,7},{3,5},{5,3},{7,1},{8,14},{10,12},{12... | collective-permute-start | bytes 1572872 | tf_op jit(solution)/shard_map/ppermute | solution.py:42
  124.9 13.5 %collective-permute-start.25 = (bf16[128,1024]{1,0:T(8,128)(2,1)S(1)}, bf16[128,1024]{1,0:T(8,128)(2,1)S(1)}, u32[]{:S(2)}, u32[]{:S(2)}) collective-permute-start(bf16[128,1024]{1,0:T(8,128)(2,1)S(1)} %get-tuple-element.96), channel_id=1, source_target_pairs={{0,192},{64,128},{128,64},{192,0},{1,193},{65,129},{129,65},{193,1... | collective-permute-start | bytes 786440 | tf_op jit(solution)/shard_map/ppermute | solution.py:42
  127.8 12.1 %collective-permute-start.26 = (bf16[128,1024]{1,0:T(8,128)(2,1)S(1)}, bf16[128,1024]{1,0:T(8,128)(2,1)S(1)}, u32[]{:S(2)}, u32[]{:S(2)}) collective-permute-start(bf16[128,1024]{1,0:T(8,128)(2,1)S(1)} %get-tuple-element.94), channel_id=1, source_target_pairs={{0,64},{64,0},{128,192},{192,128},{1,65},{65,1},{129,193},{193,129... | collective-permute-start | bytes 786440 | tf_op jit(solution)/shard_map/ppermute | solution.py:42
  129.7 16.8 %collective-permute-start.22 = (bf16[64,2048]{1,0:T(8,128)(2,1)S(1)}, bf16[64,2048]{1,0:T(8,128)(2,1)S(1)}, u32[]{:S(2)}, u32[]{:S(2)}) collective-permute-start(bf16[64,2048]{1,0:T(8,128)(2,1)S(1)} %get-tuple-element.100), channel_id=1, source_target_pairs={{0,192},{64,128},{128,64},{192,0},{1,193},{65,129},{129,65},{193,1... | collective-permute-start | bytes 786440 | tf_op jit(solution)/shard_map/ppermute | solution.py:42
  133.2 17.2 %collective-permute-start.24 = (bf16[64,2048]{1,0:T(8,128)(2,1)S(1)}, bf16[64,2048]{1,0:T(8,128)(2,1)S(1)}, u32[]{:S(2)}, u32[]{:S(2)}) collective-permute-start(bf16[64,2048]{1,0:T(8,128)(2,1)S(1)} %get-tuple-element.97), channel_id=1, source_target_pairs={{0,64},{64,0},{128,192},{192,128},{1,65},{65,1},{129,193},{193,129... | collective-permute-start | bytes 786440 | tf_op jit(solution)/shard_map/ppermute | solution.py:42
  140.0 12.2 %collective-permute-start.27 = (bf16[64,2048]{1,0:T(8,128)(2,1)S(1)}, bf16[64,2048]{1,0:T(8,128)(2,1)S(1)}, u32[]{:S(2)}, u32[]{:S(2)}) collective-permute-start(bf16[64,2048]{1,0:T(8,128)(2,1)S(1)} %pad_maximum_fusion.4), channel_id=1, source_target_pairs={{0,6},{2,4},{4,2},{6,0},{1,7},{3,5},{5,3},{7,1},{8,14},{10,12},{12... | collective-permute-start | bytes 786440 | tf_op jit(solution)/shard_map/ppermute | solution.py:42
  146.6 11.4 %collective-permute-start.28 = (bf16[32,2048]{1,0:T(8,128)(2,1)S(1)}, bf16[32,2048]{1,0:T(8,128)(2,1)S(1)}, u32[]{:S(2)}, u32[]{:S(2)}) collective-permute-start(bf16[32,2048]{1,0:T(8,128)(2,1)S(1)} %get-tuple-element.109), channel_id=1, source_target_pairs={{0,64},{64,0},{128,192},{192,128},{1,65},{65,1},{129,193},{193,129... | collective-permute-start | bytes 393224 | tf_op jit(solution)/shard_map/ppermute | solution.py:42
  (13 other events, 142.2 us)

commit v12 on v10

--- a/solution.py
+++ b/solution.py
@@ -43,13 +43,14 @@
     return lax.optimization_barrier((value, *others))[0]
 
 
-def hidden_kernel(pieces, first, last, *refs):
+def hidden_kernel(pieces, first, last, more, *refs):
     n = len(pieces)
     ins = refs[:n]
     wg0, wu0, wg1, wu1 = refs[n : n + 4]
     refs = refs[n + 4 :]
     before = None if first else refs[0]
     refs = refs if first else refs[1:]
+    extra, refs = refs[:more], refs[more:]
     total = refs[0]
     acc = refs[1] if last else total
     step = pl.program_id(0)
@@ -59,6 +60,10 @@
     @pl.when(step == 0)
     def _():
         acc[...] = jnp.zeros_like(acc) if first else before[...]
+        for k, product in enumerate(extra):
+            for index in range(8):
+                to = canon_block(CHAINS[2 + k // 4][2], index + 8) * UNIT
+                acc[k % 4, to : to + UNIT, :] += product[index * UNIT : (index + 1) * UNIT, :]
 
     at = 0
     for k, (c, came) in enumerate(pieces):
@@ -106,7 +111,7 @@
     return value
 
 
-def hidden_units(pieces, weights, before, last):
+def hidden_units(pieces, weights, before, last, extra=()):
     width, units = weights[0].shape
     count = 2 * HALF
     first = before is None
@@ -122,6 +127,7 @@
     sums = (4, count, units)
     if not first:
         in_specs.append(whole(*sums))
+    in_specs += [whole(HALF, units)] * len(extra)
     if last:
         out, out_spec = jax.ShapeDtypeStruct((count, 2 * units), jnp.bfloat16), whole(count, 2 * units)
         scratch = [pltpu.VMEM(sums, jnp.float32)]
@@ -129,7 +135,7 @@
         out, out_spec, scratch = jax.ShapeDtypeStruct(sums, jnp.float32), whole(*sums), []
     depth = len(parts) * PART
     return pl.pallas_call(
-        functools.partial(hidden_kernel, tuple(pieces), first, last),
+        functools.partial(hidden_kernel, tuple(pieces), first, last, len(extra)),
         grid=(len(parts),),
         out_shape=out,
         in_specs=in_specs,
@@ -142,7 +148,7 @@
             transcendentals=2 * count * units if last else 0,
         ),
         name="hidden",
-    )(*pieces.values(), *weights, *(() if first else (before,)))
+    )(*pieces.values(), *weights, *(() if first else (before,)), *extra)
 
 
 def expert_out(hidden, wd0, wd1, chain, sent):
@@ -336,12 +342,17 @@
     came = [trade(h, order[3]) for h, (_, _, order) in zip(held, CHAINS)]
     weights = (wg0, wu0, wg1, wu1)
     sums = hidden_units({(j, False): held[j] for j in range(4)}, weights, None, False)
-    came[0] = after(came[0], last, sums)
+    came[2] = after(came[2], last, sums)
+    came[3] = after(came[3], came[2])
+    extra = []
+    for j in (2, 3):
+        start, size, _ = CHAINS[j]
+        for w in weights:
+            product = jnp.dot(came[j], w[start : start + size], preferred_element_type=jnp.float32)
+            extra.append(product)
+    came[0] = after(came[0], *extra)
     came[1] = after(came[1], came[0])
-    sums = hidden_units({(j, True): came[j] for j in (0, 1)}, weights, sums, False)
-    came[2] = after(came[2], sums)
-    came[3] = after(came[3], came[2])
-    hidden = hidden_units({(j, True): came[j] for j in (2, 3)}, weights, sums, True)
+    hidden = hidden_units({(j, True): came[j] for j in (0, 1)}, weights, sums, True, extra)
 
     held, away = [], []
     for j in range(4):

time: 170 us -> 171 us (level)
  waiting for transfers between devices: 69.5 us -> 39.6 us
  starting transfers between devices: 51.3 us -> 79.2 us
  matrix products: 0 us -> 2.4 us
    ppermute x32, waiting for transfers between devices: 69.5 us -> 39.6 us  [trade(): return lax.ppermute(value, axis, [(i, i ^ mask) for i in range(n)])]
    ppermute x32, starting transfers between devices: 51.3 us -> 79.2 us  [trade(): return lax.ppermute(value, axis, [(i, i ^ mask) for i in range(n)])]
    dot_general x0 -> x8, matrix products: none -> 2.4 us  [per_device(): jnp.dot(came[j], w[start:start + size], preferred_element_type=jnp.float32)]
    pallas_call x3 -> x2, Pallas kernels: 9.99 us -> 8.66 us  [hidden_units(): pl.pallas_call(functools.partial(hidden_kernel, tuple(pieces), first, las...]
  transfers between devices with their start and end apart: 32 -> 32, of which waited for: 17 -> 15; matrix products, arithmetic and copies ran while one was open for 1% -> 3% of each run, Pallas kernels for 8% -> 6%
where the time goes in v12:
time: 171 us; the launch traced here: 170 us
  starting transfers between devices  79.2 us (46%)
  waiting for transfers between devices  39.6 us (23%)
  blocking collectives  27.9 us (16%)
  Pallas kernels  18.7 us (11%)
  matrix products  2.4 us (1%)
  other arithmetic  1.82 us (1%)
    ppermute x32, starting transfers between devices, trade(): return lax.ppermute(value, axis, [(i, i ^ mask) for i in range(n)])  79.2 us
    ppermute x32, waiting for transfers between devices, trade(): return lax.ppermute(value, axis, [(i, i ^ mask) for i in range(n)])  39.6 us
    all_to_all x2, blocking collectives, swap_experts(): lax.all_to_all(blocks, ('zl', 'y'), split_axis=0, concat_axis=0, tiled=True)  27.9 us
    pallas_call x2, Pallas kernels, hidden_units(): pl.pallas_call(functools.partial(hidden_kernel, tuple(pieces), first, las...  8.66 us
    pallas_call x8, Pallas kernels, expert_out(): pl.pallas_call(functools.partial(out_kernel, order, int(sent)), grid=(siz...  6.21 us
    pallas_call x4, Pallas kernels, small(): pl.pallas_call(kernel, out_shape=out_shape, in_specs=[pl.BlockSpec(memory...  3.82 us
  transfers between devices with their start and end apart: 32, of which 15 were waited for; matrix products, arithmetic and copies ran while one was open for 3% of the time, Pallas kernels for 6%

profile of v12, /device:TPU:2, one launch (start us, length us, event | category | flops | bytes accessed | tf_op | source)
XLA Modules:
  0.0 170.5 jit_solution(2229648483598476670)
XLA Ops:
  2.8 15.1 %all_to_all.10 = bf16[8,8,3072]{2,1,0:T(8,128)(2,1)S(1)} all-to-all(bf16[8,8,3072]{2,1,0:T(8,128)(2,1)} %bitcast.48), channel_id=1, replica_groups=mesh['dp'=4,'zl'=2,'y'=4,'x'=4,'c'=2] {'zl','y'}, dimensions={0} | all-to-all | bytes 786432 | tf_op jit(solution)/shard_map/all_to_all | solution.py:284
  18.2 3.4 %collective-permute-start.2 = (bf16[32,2048]{1,0:T(8,128)(2,1)S(1)}, bf16[32,2048]{1,0:T(8,128)(2,1)S(1)}, u32[]{:S(2)}, u32[]{:S(2)}) collective-permute-start(bf16[32,2048]{1,0:T(8,128)(2,1)S(1)} %get-tuple-element.52), channel_id=1, source_target_pairs={{0,64},{64,0},{128,192},{192,128},{1,65},{65,1},{129,193},{193,129... | collective-permute-start | bytes 393224 | tf_op jit(solution)/shard_map/ppermute | solution.py:35
  22.1 3.6 %collective-permute-start.6 = (bf16[32,2048]{1,0:T(8,128)(2,1)S(1)}, bf16[32,2048]{1,0:T(8,128)(2,1)S(1)}, u32[]{:S(2)}, u32[]{:S(2)}) collective-permute-start(bf16[32,2048]{1,0:T(8,128)(2,1)S(1)} %get-tuple-element.55), channel_id=1, source_target_pairs={{0,192},{64,128},{128,64},{192,0},{1,193},{65,129},{129,65},{193,1... | collective-permute-start | bytes 393224 | tf_op jit(solution)/shard_map/ppermute | solution.py:35
  28.1 3.7 %collective-permute-start.4 = (bf16[64,2048]{1,0:T(8,128)(2,1)S(1)}, bf16[64,2048]{1,0:T(8,128)(2,1)S(1)}, u32[]{:S(2)}, u32[]{:S(2)}) collective-permute-start(bf16[64,2048]{1,0:T(8,128)(2,1)S(1)} %get-tuple-element.131), channel_id=1, source_target_pairs={{0,192},{64,128},{128,64},{192,0},{1,193},{65,129},{129,65},{193,1... | collective-permute-start | bytes 786440 | tf_op jit(solution)/shard_map/ppermute | solution.py:35
  33.5 3.2 %collective-permute-start.10 = (bf16[128,1024]{1,0:T(8,128)(2,1)S(1)}, bf16[128,1024]{1,0:T(8,128)(2,1)S(1)}, u32[]{:S(2)}, u32[]{:S(2)}) collective-permute-start(bf16[128,1024]{1,0:T(8,128)(2,1)S(1)} %pad_maximum_fusion.2), channel_id=1, source_target_pairs={{0,192},{64,128},{128,64},{192,0},{1,193},{65,129},{129,65},{193,1... | collective-permute-start | bytes 786440 | tf_op jit(solution)/shard_map/ppermute | solution.py:35
  38.9 8.6 %collective-permute-done.4 = bf16[64,2048]{1,0:T(8,128)(2,1)S(1)} collective-permute-done((bf16[64,2048]{1,0:T(8,128)(2,1)S(1)}, bf16[64,2048]{1,0:T(8,128)(2,1)S(1)}, u32[]{:S(2)}, u32[]{:S(2)}) %collective-permute-start.4) | collective-permute-done | bytes 262176 | tf_op jit(solution)/shard_map/ppermute | solution.py:35
  47.6 4.0 %collective-permute-start.8 = (bf16[128,2048]{1,0:T(8,128)(2,1)S(1)}, bf16[128,2048]{1,0:T(8,128)(2,1)S(1)}, u32[]{:S(2)}, u32[]{:S(2)}) collective-permute-start(bf16[128,2048]{1,0:T(8,128)(2,1)S(1)} %get-tuple-element.113), channel_id=1, source_target_pairs={{0,6},{2,4},{4,2},{6,0},{1,7},{3,5},{5,3},{7,1},{8,14},{10,12},{12... | collective-permute-start | bytes 1572872 | tf_op jit(solution)/shard_map/ppermute | solution.py:35
  55.3 4.7 %collective-permute-start.15 = (bf16[256,1024]{1,0:T(8,128)(2,1)S(1)}, bf16[256,1024]{1,0:T(8,128)(2,1)S(1)}, u32[]{:S(2)}, u32[]{:S(2)}) collective-permute-start(bf16[256,1024]{1,0:T(8,128)(2,1)S(1)} %pad_maximum_fusion.1.refs_3_), channel_id=1, source_target_pairs={{0,192},{64,128},{128,64},{192,0},{1,193},{65,129},{129,65},{193,1... | collective-permute-start | bytes 1572872 | tf_op jit(solution)/shard_map/ppermute | solution.py:35
  61.4 3.5 %collective-permute-start.16 = (bf16[256,2048]{1,0:T(8,128)(2,1)S(1)}, bf16[256,2048]{1,0:T(8,128)(2,1)S(1)}, u32[]{:S(2)}, u32[]{:S(2)}) collective-permute-start(bf16[256,2048]{1,0:T(8,128)(2,1)S(1)} %constant_dynamic-update-slice_fusion.16.refs_1_), channel_id=1, source_target_pairs={{0,6},{2,4},{4,2},{6,0},{1,7},{3,5},{5,3},{7,1},{8,14},{10,12},{12... | collective-permute-start | bytes 3145736 | tf_op jit(solution)/shard_map/ppermute | solution.py:35
  64.9 4.8 %hidden.2.refs_6_ = f32[4,512,256]{2,1,0:T(8,128)S(1)} custom-call(bf16[256,2048]{1,0:T(8,128)(2,1)S(1)} %constant_dynamic-update-slice_fusion.12.refs_0_, bf16[256,2048]{1,0:T(8,128)(2,1)S(1)} %constant_dynamic-update-slice_fusion.16.refs_1_, bf16[256,1024]{1,0:T(8,128)(2,1)S(1)} %pad_maximum_fusion.refs_2_, ...), custom_call_target="tpu_custom_call" | custom-call | tf_op jit(solution)/shard_map/hidden/pallas_call | solution.py:137
  69.8 9.6 %collective-permute-done.13 = bf16[256,1024]{1,0:T(8,128)(2,1)S(1)} collective-permute-done((bf16[256,1024]{1,0:T(8,128)(2,1)S(1)}, bf16[256,1024]{1,0:T(8,128)(2,1)S(1)}, u32[]{:S(2)}, u32[]{:S(2)}) %collective-permute-start.13) | collective-permute-done | bytes 524320 | tf_op jit(solution)/shard_map/ppermute | solution.py:35
  79.4 2.8 %collective-permute-done.15 = bf16[256,1024]{1,0:T(8,128)(2,1)S(1)} collective-permute-done((bf16[256,1024]{1,0:T(8,128)(2,1)S(1)}, bf16[256,1024]{1,0:T(8,128)(2,1)S(1)}, u32[]{:S(2)}, u32[]{:S(2)}) %collective-permute-start.15) | collective-permute-done | bytes 524320 | tf_op jit(solution)/shard_map/ppermute | solution.py:35
  84.8 3.8 %hidden.3 = bf16[512,512]{1,0:T(8,128)(2,1)S(1)} custom-call(bf16[256,2048]{1,0:T(8,128)(2,1)S(1)} %collective-permute-done.12.refs_0_, bf16[256,2048]{1,0:T(8,128)(2,1)S(1)} %collective-permute-done.16.refs_1_, bf16[6144,256]{1,0:T(8,128)(2,1)S(1)} %bitcast.41, bf16[6144,256]{1,0:T(8,128)(2,1)S(1)} %bitcast.44, ...), custom_call_target="tpu_custom_call" | custom-call | flops 2147483648 | bytes 10485760 | tf_op jit(solution)/shard_map/hidden/pallas_call | solution.py:137
  89.7 2.7 %collective-permute-start.17 = (bf16[256,2048]{1,0:T(8,128)(2,1)S(1)}, bf16[256,2048]{1,0:T(8,128)(2,1)S(1)}, u32[]{:S(2)}, u32[]{:S(2)}) collective-permute-start(bf16[256,2048]{1,0:T(8,128)(2,1)S(1)} %out.8), channel_id=1, source_target_pairs={{0,2},{2,0},{4,6},{6,4},{1,3},{3,1},{5,7},{7,5},{8,10},{10,8},{12,... | collective-permute-start | bytes 3145736 | tf_op jit(solution)/shard_map/ppermute | solution.py:35
  98.2 4.4 %collective-permute-start.20 = (bf16[256,1024]{1,0:T(8,128)(2,1)S(1)}, bf16[256,1024]{1,0:T(8,128)(2,1)S(1)}, u32[]{:S(2)}, u32[]{:S(2)}) collective-permute-start(bf16[256,1024]{1,0:T(8,128)(2,1)S(1)} %out.10), channel_id=1, source_target_pairs={{0,64},{64,0},{128,192},{192,128},{1,65},{65,1},{129,193},{193,129... | collective-permute-start | bytes 1572872 | tf_op jit(solution)/shard_map/ppermute | solution.py:35
  105.7 6.3 %collective-permute-done.17 = bf16[256,2048]{1,0:T(8,128)(2,1)S(1)} collective-permute-done((bf16[256,2048]{1,0:T(8,128)(2,1)S(1)}, bf16[256,2048]{1,0:T(8,128)(2,1)S(1)}, u32[]{:S(2)}, u32[]{:S(2)}) %collective-permute-start.17) | collective-permute-done | bytes 1048608 | tf_op jit(solution)/shard_map/ppermute | solution.py:35
  112.4 3.2 %collective-permute-start.18 = (bf16[128,2048]{1,0:T(8,128)(2,1)S(1)}, bf16[128,2048]{1,0:T(8,128)(2,1)S(1)}, u32[]{:S(2)}, u32[]{:S(2)}) collective-permute-start(bf16[128,2048]{1,0:T(8,128)(2,1)S(1)} %get-tuple-element.91), channel_id=1, source_target_pairs={{0,6},{2,4},{4,2},{6,0},{1,7},{3,5},{5,3},{7,1},{8,14},{10,12},{12... | collective-permute-start | bytes 1572872 | tf_op jit(solution)/shard_map/ppermute | solution.py:35
  115.6 3.4 %collective-permute-done.21 = bf16[256,2048]{1,0:T(8,128)(2,1)S(1)} collective-permute-done((bf16[256,2048]{1,0:T(8,128)(2,1)S(1)}, bf16[256,2048]{1,0:T(8,128)(2,1)S(1)}, u32[]{:S(2)}, u32[]{:S(2)}) %collective-permute-start.21) | collective-permute-done | bytes 1048608 | tf_op jit(solution)/shard_map/ppermute | solution.py:35
  123.9 2.7 %collective-permute-start.26 = (bf16[128,1024]{1,0:T(8,128)(2,1)S(1)}, bf16[128,1024]{1,0:T(8,128)(2,1)S(1)}, u32[]{:S(2)}, u32[]{:S(2)}) collective-permute-start(bf16[128,1024]{1,0:T(8,128)(2,1)S(1)} %get-tuple-element.94), channel_id=1, source_target_pairs={{0,64},{64,0},{128,192},{192,128},{1,65},{65,1},{129,193},{193,129... | collective-permute-start | bytes 786440 | tf_op jit(solution)/shard_map/ppermute | solution.py:35
  127.3 4.7 %collective-permute-start.22 = (bf16[64,2048]{1,0:T(8,128)(2,1)S(1)}, bf16[64,2048]{1,0:T(8,128)(2,1)S(1)}, u32[]{:S(2)}, u32[]{:S(2)}) collective-permute-start(bf16[64,2048]{1,0:T(8,128)(2,1)S(1)} %get-tuple-element.100), channel_id=1, source_target_pairs={{0,192},{64,128},{128,64},{192,0},{1,193},{65,129},{129,65},{193,1... | collective-permute-start | bytes 786440 | tf_op jit(solution)/shard_map/ppermute | solution.py:35
  134.0 10.4 %collective-permute-start.27 = (bf16[64,2048]{1,0:T(8,128)(2,1)S(1)}, bf16[64,2048]{1,0:T(8,128)(2,1)S(1)}, u32[]{:S(2)}, u32[]{:S(2)}) collective-permute-start(bf16[64,2048]{1,0:T(8,128)(2,1)S(1)} %pad_maximum_fusion.4), channel_id=1, source_target_pairs={{0,6},{2,4},{4,2},{6,0},{1,7},{3,5},{5,3},{7,1},{8,14},{10,12},{12... | collective-permute-start | bytes 786440 | tf_op jit(solution)/shard_map/ppermute | solution.py:35
  144.5 2.8 %collective-permute-start.28 = (bf16[32,2048]{1,0:T(8,128)(2,1)S(1)}, bf16[32,2048]{1,0:T(8,128)(2,1)S(1)}, u32[]{:S(2)}, u32[]{:S(2)}) collective-permute-start(bf16[32,2048]{1,0:T(8,128)(2,1)S(1)} %get-tuple-element.109), channel_id=1, source_target_pairs={{0,64},{64,0},{128,192},{192,128},{1,65},{65,1},{129,193},{193,129... | collective-permute-start | bytes 393224 | tf_op jit(solution)/shard_map/ppermute | solution.py:35
  147.4 2.8 %collective-permute-start.29 = (bf16[32,2048]{1,0:T(8,128)(2,1)S(1)}, bf16[32,2048]{1,0:T(8,128)(2,1)S(1)}, u32[]{:S(2)}, u32[]{:S(2)}) collective-permute-start(bf16[32,2048]{1,0:T(8,128)(2,1)S(1)} %get-tuple-element.103), channel_id=1, source_target_pairs={{0,192},{64,128},{128,64},{192,0},{1,193},{65,129},{129,65},{193,1... | collective-permute-start | bytes 393224 | tf_op jit(solution)/shard_map/ppermute | solution.py:35
  156.5 12.8 %all_to_all.11 = bf16[8,8,3072]{2,1,0:T(8,128)(2,1)S(1)} all-to-all(bf16[8,8,3072]{2,1,0:T(8,128)(2,1)S(1)} %bitcast.47), channel_id=1, replica_groups=mesh['dp'=4,'zl'=2,'y'=4,'x'=4,'c'=2] {'zl','y'}, dimensions={0} | all-to-all | bytes 786432 | tf_op jit(solution)/shard_map/all_to_all | solution.py:284
  (104 shorter events, 42.9 us)
Async XLA Ops:
  2.1 15.8 %collective-permute-start = (bf16[6144,256]{1,0:T(8,128)(2,1)}, bf16[6144,256]{1,0:T(8,128)(2,1)S(1)}, u32[]{:S(2)}, u32[]{:S(2)}) collective-permute-start(bf16[6144,256]{1,0:T(8,128)(2,1)} %bitcast.39), channel_id=1, source_target_pairs={{0,1},{1,0},{2,3},{3,2},{4,5},{5,4},{6,7},{7,6},{8,9},{9,8},{10,11... | collective-permute-start | bytes 9437192 | tf_op jit(solution)/shard_map/ppermute | solution.py:35
  2.2 15.7 %collective-permute-start.1 = (bf16[6144,256]{1,0:T(8,128)(2,1)}, bf16[6144,256]{1,0:T(8,128)(2,1)S(1)}, u32[]{:S(2)}, u32[]{:S(2)}) collective-permute-start(bf16[6144,256]{1,0:T(8,128)(2,1)} %bitcast.42), channel_id=1, source_target_pairs={{0,1},{1,0},{2,3},{3,2},{4,5},{5,4},{6,7},{7,6},{8,9},{9,8},{10,11... | collective-permute-start | bytes 9437192 | tf_op jit(solution)/shard_map/ppermute | solution.py:35
  2.7 29.1 %collective-permute-start.7 = (bf16[256,6144]{1,0:T(8,128)(2,1)}, bf16[256,6144]{1,0:T(8,128)(2,1)S(1)}, u32[]{:S(2)}, u32[]{:S(2)}) collective-permute-start(bf16[256,6144]{1,0:T(8,128)(2,1)} %bitcast.30), channel_id=1, source_target_pairs={{0,1},{1,0},{2,3},{3,2},{4,5},{5,4},{6,7},{7,6},{8,9},{9,8},{10,11... | collective-permute-start | bytes 9437192 | tf_op jit(solution)/shard_map/ppermute | solution.py:35
  28.1 19.4 %collective-permute-start.4 = (bf16[64,2048]{1,0:T(8,128)(2,1)S(1)}, bf16[64,2048]{1,0:T(8,128)(2,1)S(1)}, u32[]{:S(2)}, u32[]{:S(2)}) collective-permute-start(bf16[64,2048]{1,0:T(8,128)(2,1)S(1)} %get-tuple-element.131), channel_id=1, source_target_pairs={{0,192},{64,128},{128,64},{192,0},{1,193},{65,129},{129,65},{193,1... | collective-permute-start | bytes 786440 | tf_op jit(solution)/shard_map/ppermute | solution.py:35
  31.9 19.7 %collective-permute-start.11 = (bf16[64,2048]{1,0:T(8,128)(2,1)S(1)}, bf16[64,2048]{1,0:T(8,128)(2,1)S(1)}, u32[]{:S(2)}, u32[]{:S(2)}) collective-permute-start(bf16[64,2048]{1,0:T(8,128)(2,1)S(1)} %get-tuple-element.125), channel_id=1, source_target_pairs={{0,64},{64,0},{128,192},{192,128},{1,65},{65,1},{129,193},{193,129... | collective-permute-start | bytes 786440 | tf_op jit(solution)/shard_map/ppermute | solution.py:35
  33.5 20.2 %collective-permute-start.10 = (bf16[128,1024]{1,0:T(8,128)(2,1)S(1)}, bf16[128,1024]{1,0:T(8,128)(2,1)S(1)}, u32[]{:S(2)}, u32[]{:S(2)}) collective-permute-start(bf16[128,1024]{1,0:T(8,128)(2,1)S(1)} %pad_maximum_fusion.2), channel_id=1, source_target_pairs={{0,192},{64,128},{128,64},{192,0},{1,193},{65,129},{129,65},{193,1... | collective-permute-start | bytes 786440 | tf_op jit(solution)/shard_map/ppermute | solution.py:35
  36.7 18.5 %collective-permute-start.9 = (bf16[128,1024]{1,0:T(8,128)(2,1)S(1)}, bf16[128,1024]{1,0:T(8,128)(2,1)S(1)}, u32[]{:S(2)}, u32[]{:S(2)}) collective-permute-start(bf16[128,1024]{1,0:T(8,128)(2,1)S(1)} %pad_maximum_fusion.3), channel_id=1, source_target_pairs={{0,64},{64,0},{128,192},{192,128},{1,65},{65,1},{129,193},{193,129... | collective-permute-start | bytes 786440 | tf_op jit(solution)/shard_map/ppermute | solution.py:35
  47.6 12.4 %collective-permute-start.8 = (bf16[128,2048]{1,0:T(8,128)(2,1)S(1)}, bf16[128,2048]{1,0:T(8,128)(2,1)S(1)}, u32[]{:S(2)}, u32[]{:S(2)}) collective-permute-start(bf16[128,2048]{1,0:T(8,128)(2,1)S(1)} %get-tuple-element.113), channel_id=1, source_target_pairs={{0,6},{2,4},{4,2},{6,0},{1,7},{3,5},{5,3},{7,1},{8,14},{10,12},{12... | collective-permute-start | bytes 1572872 | tf_op jit(solution)/shard_map/ppermute | solution.py:35
  53.7 25.7 %collective-permute-start.13 = (bf16[256,1024]{1,0:T(8,128)(2,1)S(1)}, bf16[256,1024]{1,0:T(8,128)(2,1)S(1)}, u32[]{:S(2)}, u32[]{:S(2)}) collective-permute-start(bf16[256,1024]{1,0:T(8,128)(2,1)S(1)} %pad_maximum_fusion.refs_2_), channel_id=1, source_target_pairs={{0,64},{64,0},{128,192},{192,128},{1,65},{65,1},{129,193},{193,129... | collective-permute-start | bytes 1572872 | tf_op jit(solution)/shard_map/ppermute | solution.py:35
  55.3 26.9 %collective-permute-start.15 = (bf16[256,1024]{1,0:T(8,128)(2,1)S(1)}, bf16[256,1024]{1,0:T(8,128)(2,1)S(1)}, u32[]{:S(2)}, u32[]{:S(2)}) collective-permute-start(bf16[256,1024]{1,0:T(8,128)(2,1)S(1)} %pad_maximum_fusion.1.refs_3_), channel_id=1, source_target_pairs={{0,192},{64,128},{128,64},{192,0},{1,193},{65,129},{129,65},{193,1... | collective-permute-start | bytes 1572872 | tf_op jit(solution)/shard_map/ppermute | solution.py:35
  60.0 24.7 %collective-permute-start.12 = (bf16[256,2048]{1,0:T(8,128)(2,1)S(1)}, bf16[256,2048]{1,0:T(8,128)(2,1)S(1)}, u32[]{:S(2)}, u32[]{:S(2)}) collective-permute-start(bf16[256,2048]{1,0:T(8,128)(2,1)S(1)} %constant_dynamic-update-slice_fusion.12.refs_0_), channel_id=1, source_target_pairs={{0,2},{2,0},{4,6},{6,4},{1,3},{3,1},{5,7},{7,5},{8,10},{10,8},{12,... | collective-permute-start | bytes 3145736 | tf_op jit(solution)/shard_map/ppermute | solution.py:35
  61.4 23.3 %collective-permute-start.16 = (bf16[256,2048]{1,0:T(8,128)(2,1)S(1)}, bf16[256,2048]{1,0:T(8,128)(2,1)S(1)}, u32[]{:S(2)}, u32[]{:S(2)}) collective-permute-start(bf16[256,2048]{1,0:T(8,128)(2,1)S(1)} %constant_dynamic-update-slice_fusion.16.refs_1_), channel_id=1, source_target_pairs={{0,6},{2,4},{4,2},{6,0},{1,7},{3,5},{5,3},{7,1},{8,14},{10,12},{12... | collective-permute-start | bytes 3145736 | tf_op jit(solution)/shard_map/ppermute | solution.py:35
  89.7 22.3 %collective-permute-start.17 = (bf16[256,2048]{1,0:T(8,128)(2,1)S(1)}, bf16[256,2048]{1,0:T(8,128)(2,1)S(1)}, u32[]{:S(2)}, u32[]{:S(2)}) collective-permute-start(bf16[256,2048]{1,0:T(8,128)(2,1)S(1)} %out.8), channel_id=1, source_target_pairs={{0,2},{2,0},{4,6},{6,4},{1,3},{3,1},{5,7},{7,5},{8,10},{10,8},{12,... | collective-permute-start | bytes 3145736 | tf_op jit(solution)/shard_map/ppermute | solution.py:35
  93.5 25.4 %collective-permute-start.21 = (bf16[256,2048]{1,0:T(8,128)(2,1)S(1)}, bf16[256,2048]{1,0:T(8,128)(2,1)S(1)}, u32[]{:S(2)}, u32[]{:S(2)}) collective-permute-start(bf16[256,2048]{1,0:T(8,128)(2,1)S(1)} %out.9), channel_id=1, source_target_pairs={{0,6},{2,4},{4,2},{6,0},{1,7},{3,5},{5,3},{7,1},{8,14},{10,12},{12... | collective-permute-start | bytes 3145736 | tf_op jit(solution)/shard_map/ppermute | solution.py:35
  96.9 26.9 %collective-permute-start.19 = (bf16[256,1024]{1,0:T(8,128)(2,1)S(1)}, bf16[256,1024]{1,0:T(8,128)(2,1)S(1)}, u32[]{:S(2)}, u32[]{:S(2)}) collective-permute-start(bf16[256,1024]{1,0:T(8,128)(2,1)S(1)} %out.11), channel_id=1, source_target_pairs={{0,192},{64,128},{128,64},{192,0},{1,193},{65,129},{129,65},{193,1... | collective-permute-start | bytes 1572872 | tf_op jit(solution)/shard_map/ppermute | solution.py:35
  98.2 23.8 %collective-permute-start.20 = (bf16[256,1024]{1,0:T(8,128)(2,1)S(1)}, bf16[256,1024]{1,0:T(8,128)(2,1)S(1)}, u32[]{:S(2)}, u32[]{:S(2)}) collective-permute-start(bf16[256,1024]{1,0:T(8,128)(2,1)S(1)} %out.10), channel_id=1, source_target_pairs={{0,64},{64,0},{128,192},{192,128},{1,65},{65,1},{129,193},{193,129... | collective-permute-start | bytes 1572872 | tf_op jit(solution)/shard_map/ppermute | solution.py:35
  112.4 14.8 %collective-permute-start.18 = (bf16[128,2048]{1,0:T(8,128)(2,1)S(1)}, bf16[128,2048]{1,0:T(8,128)(2,1)S(1)}, u32[]{:S(2)}, u32[]{:S(2)}) collective-permute-start(bf16[128,2048]{1,0:T(8,128)(2,1)S(1)} %get-tuple-element.91), channel_id=1, source_target_pairs={{0,6},{2,4},{4,2},{6,0},{1,7},{3,5},{5,3},{7,1},{8,14},{10,12},{12... | collective-permute-start | bytes 1572872 | tf_op jit(solution)/shard_map/ppermute | solution.py:35
  119.4 12.6 %collective-permute-start.23 = (bf16[128,2048]{1,0:T(8,128)(2,1)S(1)}, bf16[128,2048]{1,0:T(8,128)(2,1)S(1)}, u32[]{:S(2)}, u32[]{:S(2)}) collective-permute-start(bf16[128,2048]{1,0:T(8,128)(2,1)S(1)} %get-tuple-element.90), channel_id=1, source_target_pairs={{0,2},{2,0},{4,6},{6,4},{1,3},{3,1},{5,7},{7,5},{8,10},{10,8},{12,... | collective-permute-start | bytes 1572872 | tf_op jit(solution)/shard_map/ppermute | solution.py:35
  122.3 11.5 %collective-permute-start.25 = (bf16[128,1024]{1,0:T(8,128)(2,1)S(1)}, bf16[128,1024]{1,0:T(8,128)(2,1)S(1)}, u32[]{:S(2)}, u32[]{:S(2)}) collective-permute-start(bf16[128,1024]{1,0:T(8,128)(2,1)S(1)} %get-tuple-element.96), channel_id=1, source_target_pairs={{0,192},{64,128},{128,64},{192,0},{1,193},{65,129},{129,65},{193,1... | collective-permute-start | bytes 786440 | tf_op jit(solution)/shard_map/ppermute | solution.py:35
  123.9 9.9 %collective-permute-start.26 = (bf16[128,1024]{1,0:T(8,128)(2,1)S(1)}, bf16[128,1024]{1,0:T(8,128)(2,1)S(1)}, u32[]{:S(2)}, u32[]{:S(2)}) collective-permute-start(bf16[128,1024]{1,0:T(8,128)(2,1)S(1)} %get-tuple-element.94), channel_id=1, source_target_pairs={{0,64},{64,0},{128,192},{192,128},{1,65},{65,1},{129,193},{193,129... | collective-permute-start | bytes 786440 | tf_op jit(solution)/shard_map/ppermute | solution.py:35
  127.3 17.1 %collective-permute-start.22 = (bf16[64,2048]{1,0:T(8,128)(2,1)S(1)}, bf16[64,2048]{1,0:T(8,128)(2,1)S(1)}, u32[]{:S(2)}, u32[]{:S(2)}) collective-permute-start(bf16[64,2048]{1,0:T(8,128)(2,1)S(1)} %get-tuple-element.100), channel_id=1, source_target_pairs={{0,192},{64,128},{128,64},{192,0},{1,193},{65,129},{129,65},{193,1... | collective-permute-start | bytes 786440 | tf_op jit(solution)/shard_map/ppermute | solution.py:35
  132.1 15.1 %collective-permute-start.24 = (bf16[64,2048]{1,0:T(8,128)(2,1)S(1)}, bf16[64,2048]{1,0:T(8,128)(2,1)S(1)}, u32[]{:S(2)}, u32[]{:S(2)}) collective-permute-start(bf16[64,2048]{1,0:T(8,128)(2,1)S(1)} %get-tuple-element.97), channel_id=1, source_target_pairs={{0,64},{64,0},{128,192},{192,128},{1,65},{65,1},{129,193},{193,129... | collective-permute-start | bytes 786440 | tf_op jit(solution)/shard_map/ppermute | solution.py:35
  134.0 16.5 %collective-permute-start.27 = (bf16[64,2048]{1,0:T(8,128)(2,1)S(1)}, bf16[64,2048]{1,0:T(8,128)(2,1)S(1)}, u32[]{:S(2)}, u32[]{:S(2)}) collective-permute-start(bf16[64,2048]{1,0:T(8,128)(2,1)S(1)} %pad_maximum_fusion.4), channel_id=1, source_target_pairs={{0,6},{2,4},{4,2},{6,0},{1,7},{3,5},{5,3},{7,1},{8,14},{10,12},{12... | collective-permute-start | bytes 786440 | tf_op jit(solution)/shard_map/ppermute | solution.py:35
  144.5 11.7 %collective-permute-start.28 = (bf16[32,2048]{1,0:T(8,128)(2,1)S(1)}, bf16[32,2048]{1,0:T(8,128)(2,1)S(1)}, u32[]{:S(2)}, u32[]{:S(2)}) collective-permute-start(bf16[32,2048]{1,0:T(8,128)(2,1)S(1)} %get-tuple-element.109), channel_id=1, source_target_pairs={{0,64},{64,0},{128,192},{192,128},{1,65},{65,1},{129,193},{193,129... | collective-permute-start | bytes 393224 | tf_op jit(solution)/shard_map/ppermute | solution.py:35
  (13 other events, 190.6 us)

commit v13 on v10

--- a/solution.py
+++ b/solution.py
@@ -35,8 +35,8 @@
     return lax.ppermute(value, axis, [(i, i ^ mask) for i in range(n)])
 
 
-def add(a, b):
-    return (a.astype(jnp.float32) + b.astype(jnp.float32)).astype(a.dtype)
+def add(values):
+    return sum(v.astype(jnp.float32) for v in values)
 
 
 def after(value, *others):
@@ -350,27 +350,28 @@
     for j in range(4):
         given = after(hidden, away[-1], *held[-1:])
         held.append(expert_out(given, wd0, wd1, j, False))
+    parts = [[h] for h in held]
     last = None
     for step in (3, 2):
         came = [trade(a, order[step]) for a, (_, _, order) in zip(away, CHAINS)]
-        half = held[0].shape[0] // 2
+        half = away[0].shape[0] // 2
         for j in range(4):
-            got = came[j] if last is None else after(came[j], last)
-            away[j] = last = add(held[j][half:], got[half:])
-            held[j] = add(held[j][:half], got[:half])
-    join = lambda values: values[:2] + [jnp.concatenate(values[2:], axis=1)]
-    held, away = join(held), join(away)
+            parts[j].append(came[j] if last is None else after(came[j], last))
+            away[j] = last = add([p[half:] for p in parts[j]]).astype(bf16)
+            parts[j] = [p[:half] for p in parts[j]]
+    size = CHAINS[2][1]
+    joined = away[:2] + [jnp.concatenate(away[2:], axis=1)]
+    came = [trade(a, CHAINS[j][2][1]) for j, a in enumerate(joined)]
+    half = away[0].shape[0] // 2
     last = None
-    came = [trade(a, CHAINS[joined[0]][2][1]) for a, joined in zip(away, JOINED)]
-    half = held[0].shape[0] // 2
     for k in range(3):
         got = came[k] if last is None else after(came[k], last)
-        away[k] = last = add(held[k][half:], got[half:])
-        held[k] = add(held[k][:half], got[:half])
-    size = CHAINS[2][1]
-    part = lambda values: values[:2] + [values[2][:, :size], values[2][:, size:]]
-    held, away = part(held), part(away)
+        for j, piece in ((k, got),) if k < 2 else ((2, got[:, :size]), (3, got[:, size:])):
+            parts[j].append(piece)
+            away[j] = last = add([p[half:] for p in parts[j]]).astype(bf16)
+            parts[j] = [p[:half] for p in parts[j]]
     came = [trade(a, order[0]) for a, (_, _, order) in zip(away, CHAINS)]
+    held = [add(p) for p in parts]
 
     folded = small(fold_kernel, folded_shape, *held, *came, name="fold")
     back = swap_experts(folded)

time: 170 us -> 171 us (level)
  no operation moved by 1% of the time
where the time goes in v13:
time: 171 us; the launch traced here: 170 us
  waiting for transfers between devices  69.5 us (41%)
  starting transfers between devices  51.4 us (30%)
  blocking collectives  27.5 us (16%)
  Pallas kernels  20 us (12%)
    ppermute x32, waiting for transfers between devices, trade(): return lax.ppermute(value, axis, [(i, i ^ mask) for i in range(n)])  69.5 us
    ppermute x32, starting transfers between devices, trade(): return lax.ppermute(value, axis, [(i, i ^ mask) for i in range(n)])  51.4 us
    all_to_all x2, blocking collectives, swap_experts(): lax.all_to_all(blocks, ('zl', 'y'), split_axis=0, concat_axis=0, tiled=True)  27.5 us
    pallas_call x3, Pallas kernels, hidden_units(): pl.pallas_call(functools.partial(hidden_kernel, tuple(pieces), first, las...  9.99 us
    pallas_call x8, Pallas kernels, expert_out(): pl.pallas_call(functools.partial(out_kernel, order, int(sent)), grid=(siz...  6.21 us
    pallas_call x4, Pallas kernels, small(): pl.pallas_call(kernel, out_shape=out_shape, in_specs=[pl.BlockSpec(memory...  3.78 us
  transfers between devices with their start and end apart: 32, of which 17 were waited for; matrix products, arithmetic and copies ran while one was open for 1% of the time, Pallas kernels for 8%

profile of v13, /device:TPU:2, one launch (start us, length us, event | category | flops | bytes accessed | tf_op | source)
XLA Modules:
  0.0 170.5 jit_solution(2883731499350624853)
XLA Ops:
  0.0 2.1 %place.1 = (bf16[64,3072]{1,0:T(8,128)(2,1)}, f32[16,64]{1,0:T(8,128)}) custom-call(s32[2,8]{1,0:T(2,128)} %bitcast.32, f32[2,8]{1,0:T(2,128)} %bitcast.33, bf16[8,6144]{1,0:T(8,128)(2,1)} %tokens.1, f32[1,6144]{1,0:T(1,128)} %bitcast.31), custom_call_target="tpu_custom_call" | custom-call | tf_op jit(solution)/shard_map/place/pallas_call | solution.py:265
  2.8 15.1 %all_to_all.10 = bf16[8,8,3072]{2,1,0:T(8,128)(2,1)S(1)} all-to-all(bf16[8,8,3072]{2,1,0:T(8,128)(2,1)} %bitcast.30), channel_id=1, replica_groups=mesh['dp'=4,'zl'=2,'y'=4,'x'=4,'c'=2] {'zl','y'}, dimensions={0} | all-to-all | bytes 786432 | tf_op jit(solution)/shard_map/all_to_all | solution.py:278
  18.8 5.4 %collective-permute-start.4 = (bf16[32,2048]{1,0:T(8,128)(2,1)S(1)}, bf16[32,2048]{1,0:T(8,128)(2,1)S(1)}, u32[]{:S(2)}, u32[]{:S(2)}) collective-permute-start(bf16[32,2048]{1,0:T(8,128)(2,1)S(1)} %get-tuple-element.53), channel_id=1, source_target_pairs={{0,192},{64,128},{128,64},{192,0},{1,193},{65,129},{129,65},{193,1... | collective-permute-start | bytes 393224 | tf_op jit(solution)/shard_map/ppermute | solution.py:35
  25.8 2.2 %collective-permute-start.3 = (bf16[64,2048]{1,0:T(8,128)(2,1)S(1)}, bf16[64,2048]{1,0:T(8,128)(2,1)S(1)}, u32[]{:S(2)}, u32[]{:S(2)}) collective-permute-start(bf16[64,2048]{1,0:T(8,128)(2,1)S(1)} %constant_dynamic-update-slice_fusion), channel_id=1, source_target_pairs={{0,6},{2,4},{4,2},{6,0},{1,7},{3,5},{5,3},{7,1},{8,14},{10,12},{12... | collective-permute-start | bytes 786440 | tf_op jit(solution)/shard_map/ppermute | solution.py:35
  28.0 2.2 %collective-permute-done.5 = bf16[32,2048]{1,0:T(8,128)(2,1)S(1)} collective-permute-done((bf16[32,2048]{1,0:T(8,128)(2,1)S(1)}, bf16[32,2048]{1,0:T(8,128)(2,1)S(1)}, u32[]{:S(2)}, u32[]{:S(2)}) %collective-permute-start.5) | collective-permute-done | bytes 131104 | tf_op jit(solution)/shard_map/ppermute | solution.py:35
  33.8 3.3 %collective-permute-start.7 = (bf16[128,1024]{1,0:T(8,128)(2,1)S(1)}, bf16[128,1024]{1,0:T(8,128)(2,1)S(1)}, u32[]{:S(2)}, u32[]{:S(2)}) collective-permute-start(bf16[128,1024]{1,0:T(8,128)(2,1)S(1)} %pad_maximum_fusion.2), channel_id=1, source_target_pairs={{0,192},{64,128},{128,64},{192,0},{1,193},{65,129},{129,65},{193,1... | collective-permute-start | bytes 786440 | tf_op jit(solution)/shard_map/ppermute | solution.py:35
  37.9 9.5 %collective-permute-done.9 = bf16[64,2048]{1,0:T(8,128)(2,1)S(1)} collective-permute-done((bf16[64,2048]{1,0:T(8,128)(2,1)S(1)}, bf16[64,2048]{1,0:T(8,128)(2,1)S(1)}, u32[]{:S(2)}, u32[]{:S(2)}) %collective-permute-start.9) | collective-permute-done | bytes 262176 | tf_op jit(solution)/shard_map/ppermute | solution.py:35
  47.4 2.2 %collective-permute-start.11 = (bf16[128,2048]{1,0:T(8,128)(2,1)S(1)}, bf16[128,2048]{1,0:T(8,128)(2,1)S(1)}, u32[]{:S(2)}, u32[]{:S(2)}) collective-permute-start(bf16[128,2048]{1,0:T(8,128)(2,1)S(1)} %get-tuple-element.102), channel_id=1, source_target_pairs={{0,6},{2,4},{4,2},{6,0},{1,7},{3,5},{5,3},{7,1},{8,14},{10,12},{12... | collective-permute-start | bytes 1572872 | tf_op jit(solution)/shard_map/ppermute | solution.py:35
  51.2 5.2 %collective-permute-done.7 = bf16[128,1024]{1,0:T(8,128)(2,1)S(1)} collective-permute-done((bf16[128,1024]{1,0:T(8,128)(2,1)S(1)}, bf16[128,1024]{1,0:T(8,128)(2,1)S(1)}, u32[]{:S(2)}, u32[]{:S(2)}) %collective-permute-start.7) | collective-permute-done | bytes 262176 | tf_op jit(solution)/shard_map/ppermute | solution.py:35
  56.9 2.6 %collective-permute-start.13 = (bf16[256,2048]{1,0:T(8,128)(2,1)S(1)}, bf16[256,2048]{1,0:T(8,128)(2,1)S(1)}, u32[]{:S(2)}, u32[]{:S(2)}) collective-permute-start(bf16[256,2048]{1,0:T(8,128)(2,1)S(1)} %constant_dynamic-update-slice_fusion.12.refs_0_), channel_id=1, source_target_pairs={{0,2},{2,0},{4,6},{6,4},{1,3},{3,1},{5,7},{7,5},{8,10},{10,8},{12,... | collective-permute-start | bytes 3145736 | tf_op jit(solution)/shard_map/ppermute | solution.py:35
  63.1 3.2 %collective-permute-start.16 = (bf16[256,1024]{1,0:T(8,128)(2,1)S(1)}, bf16[256,1024]{1,0:T(8,128)(2,1)S(1)}, u32[]{:S(2)}, u32[]{:S(2)}) collective-permute-start(bf16[256,1024]{1,0:T(8,128)(2,1)S(1)} %pad_maximum_fusion.1.refs_3_), channel_id=1, source_target_pairs={{0,192},{64,128},{128,64},{192,0},{1,193},{65,129},{129,65},{193,1... | collective-permute-start | bytes 1572872 | tf_op jit(solution)/shard_map/ppermute | solution.py:35
  66.3 4.8 %hidden.3.refs_6_ = f32[4,512,256]{2,1,0:T(8,128)S(1)} custom-call(bf16[256,2048]{1,0:T(8,128)(2,1)S(1)} %constant_dynamic-update-slice_fusion.12.refs_0_, bf16[256,2048]{1,0:T(8,128)(2,1)S(1)} %constant_dynamic-update-slice_fusion.16.refs_1_, bf16[256,1024]{1,0:T(8,128)(2,1)S(1)} %pad_maximum_fusion.refs_2_, ...), custom_call_target="tpu_custom_call" | custom-call | tf_op jit(solution)/shard_map/hidden/pallas_call | solution.py:131
  71.2 10.3 %collective-permute-done.13.refs_0_ = bf16[256,2048]{1,0:T(8,128)(2,1)S(1)} collective-permute-done((bf16[256,2048]{1,0:T(8,128)(2,1)S(1)}, bf16[256,2048]{1,0:T(8,128)(2,1)S(1)}, u32[]{:S(2)}, u32[]{:S(2)}) %collective-permute-start.13) | collective-permute-done | bytes 1048608 | tf_op jit(solution)/shard_map/ppermute | solution.py:35
  81.5 3.3 %hidden.4.refs_6_ = f32[4,512,256]{2,1,0:T(8,128)S(1)} custom-call(bf16[256,2048]{1,0:T(8,128)(2,1)S(1)} %collective-permute-done.13.refs_0_, bf16[256,2048]{1,0:T(8,128)(2,1)S(1)} %collective-permute-done.15.refs_1_, bf16[6144,256]{1,0:T(8,128)(2,1)S(1)} %bitcast.21, bf16[6144,256]{1,0:T(8,128)(2,1)S(1)} %bitcast.25, ...), custom_call_target="tpu_custom_call" | custom-call | tf_op jit(solution)/shard_map/hidden/pallas_call | solution.py:131
  94.0 3.9 %collective-permute-start.19 = (bf16[256,1024]{1,0:T(8,128)(2,1)S(1)}, bf16[256,1024]{1,0:T(8,128)(2,1)S(1)}, u32[]{:S(2)}, u32[]{:S(2)}) collective-permute-start(bf16[256,1024]{1,0:T(8,128)(2,1)S(1)} %out.11), channel_id=1, source_target_pairs={{0,192},{64,128},{128,64},{192,0},{1,193},{65,129},{129,65},{193,1... | collective-permute-start | bytes 1572872 | tf_op jit(solution)/shard_map/ppermute | solution.py:35
  101.1 9.8 %collective-permute-done.17 = bf16[256,2048]{1,0:T(8,128)(2,1)S(1)} collective-permute-done((bf16[256,2048]{1,0:T(8,128)(2,1)S(1)}, bf16[256,2048]{1,0:T(8,128)(2,1)S(1)}, u32[]{:S(2)}, u32[]{:S(2)}) %collective-permute-start.17) | collective-permute-done | bytes 1048608 | tf_op jit(solution)/shard_map/ppermute | solution.py:35
  112.7 4.0 %collective-permute-done.21 = bf16[256,2048]{1,0:T(8,128)(2,1)S(1)} collective-permute-done((bf16[256,2048]{1,0:T(8,128)(2,1)S(1)}, bf16[256,2048]{1,0:T(8,128)(2,1)S(1)}, u32[]{:S(2)}, u32[]{:S(2)}) %collective-permute-start.21) | collective-permute-done | bytes 1048608 | tf_op jit(solution)/shard_map/ppermute | solution.py:35
  118.3 2.9 %collective-permute-done.20 = bf16[256,1024]{1,0:T(8,128)(2,1)S(1)} collective-permute-done((bf16[256,1024]{1,0:T(8,128)(2,1)S(1)}, bf16[256,1024]{1,0:T(8,128)(2,1)S(1)}, u32[]{:S(2)}, u32[]{:S(2)}) %collective-permute-start.20) | collective-permute-done | bytes 524320 | tf_op jit(solution)/shard_map/ppermute | solution.py:35
  126.2 3.0 %collective-permute-start.24 = (bf16[64,2048]{1,0:T(8,128)(2,1)S(1)}, bf16[64,2048]{1,0:T(8,128)(2,1)S(1)}, u32[]{:S(2)}, u32[]{:S(2)}) collective-permute-start(bf16[64,2048]{1,0:T(8,128)(2,1)S(1)} %add_convert_fusion.2), channel_id=1, source_target_pairs={{0,64},{64,0},{128,192},{192,128},{1,65},{65,1},{129,193},{193,129... | collective-permute-start | bytes 786440 | tf_op jit(solution)/shard_map/ppermute | solution.py:35
  129.2 6.6 %collective-permute-done.25 = bf16[128,1024]{1,0:T(8,128)(2,1)S(1)} collective-permute-done((bf16[128,1024]{1,0:T(8,128)(2,1)S(1)}, bf16[128,1024]{1,0:T(8,128)(2,1)S(1)}, u32[]{:S(2)}, u32[]{:S(2)}) %collective-permute-start.25) | collective-permute-done | bytes 262176 | tf_op jit(solution)/shard_map/ppermute | solution.py:35
  136.0 11.2 %collective-permute-done.22 = bf16[64,2048]{1,0:T(8,128)(2,1)S(1)} collective-permute-done((bf16[64,2048]{1,0:T(8,128)(2,1)S(1)}, bf16[64,2048]{1,0:T(8,128)(2,1)S(1)}, u32[]{:S(2)}, u32[]{:S(2)}) %collective-permute-start.22) | collective-permute-done | bytes 262176 | tf_op jit(solution)/shard_map/ppermute | solution.py:35
  147.6 2.4 %collective-permute-start.29 = (bf16[32,2048]{1,0:T(8,128)(2,1)S(1)}, bf16[32,2048]{1,0:T(8,128)(2,1)S(1)}, u32[]{:S(2)}, u32[]{:S(2)}) collective-permute-start(bf16[32,2048]{1,0:T(8,128)(2,1)S(1)} %get-tuple-element.89), channel_id=1, source_target_pairs={{0,192},{64,128},{128,64},{192,0},{1,193},{65,129},{129,65},{193,1... | collective-permute-start | bytes 393224 | tf_op jit(solution)/shard_map/ppermute | solution.py:35
  152.3 2.2 %collective-permute-done.30.refs_6_ = bf16[32,1024]{1,0:T(8,128)(2,1)S(1)} collective-permute-done((bf16[32,1024]{1,0:T(8,128)(2,1)S(1)}, bf16[32,1024]{1,0:T(8,128)(2,1)S(1)}, u32[]{:S(2)}, u32[]{:S(2)}) %collective-permute-start.30) | collective-permute-done | bytes 65568 | tf_op jit(solution)/shard_map/ppermute | solution.py:35
  157.0 12.4 %all_to_all.11 = bf16[8,8,3072]{2,1,0:T(8,128)(2,1)S(1)} all-to-all(bf16[8,8,3072]{2,1,0:T(8,128)(2,1)S(1)} %bitcast.29), channel_id=1, replica_groups=mesh['dp'=4,'zl'=2,'y'=4,'x'=4,'c'=2] {'zl','y'}, dimensions={0} | all-to-all | bytes 786432 | tf_op jit(solution)/shard_map/all_to_all | solution.py:278
  (95 shorter events, 40.2 us)
Async XLA Ops:
  2.1 15.8 %collective-permute-start = (bf16[6144,256]{1,0:T(8,128)(2,1)}, bf16[6144,256]{1,0:T(8,128)(2,1)S(1)}, u32[]{:S(2)}, u32[]{:S(2)}) collective-permute-start(bf16[6144,256]{1,0:T(8,128)(2,1)} %bitcast.19), channel_id=1, source_target_pairs={{0,1},{1,0},{2,3},{3,2},{4,5},{5,4},{6,7},{7,6},{8,9},{9,8},{10,11... | collective-permute-start | bytes 9437192 | tf_op jit(solution)/shard_map/ppermute | solution.py:35
  2.2 15.7 %collective-permute-start.1 = (bf16[6144,256]{1,0:T(8,128)(2,1)}, bf16[6144,256]{1,0:T(8,128)(2,1)S(1)}, u32[]{:S(2)}, u32[]{:S(2)}) collective-permute-start(bf16[6144,256]{1,0:T(8,128)(2,1)} %bitcast.23), channel_id=1, source_target_pairs={{0,1},{1,0},{2,3},{3,2},{4,5},{5,4},{6,7},{7,6},{8,9},{9,8},{10,11... | collective-permute-start | bytes 9437192 | tf_op jit(solution)/shard_map/ppermute | solution.py:35
  2.7 29.1 %collective-permute-start.6 = (bf16[256,6144]{1,0:T(8,128)(2,1)}, bf16[256,6144]{1,0:T(8,128)(2,1)S(1)}, u32[]{:S(2)}, u32[]{:S(2)}) collective-permute-start(bf16[256,6144]{1,0:T(8,128)(2,1)} %bitcast.10), channel_id=1, source_target_pairs={{0,1},{1,0},{2,3},{3,2},{4,5},{5,4},{6,7},{7,6},{8,9},{9,8},{10,11... | collective-permute-start | bytes 9437192 | tf_op jit(solution)/shard_map/ppermute | solution.py:35
  18.8 13.0 %collective-permute-start.4 = (bf16[32,2048]{1,0:T(8,128)(2,1)S(1)}, bf16[32,2048]{1,0:T(8,128)(2,1)S(1)}, u32[]{:S(2)}, u32[]{:S(2)}) collective-permute-start(bf16[32,2048]{1,0:T(8,128)(2,1)S(1)} %get-tuple-element.53), channel_id=1, source_target_pairs={{0,192},{64,128},{128,64},{192,0},{1,193},{65,129},{129,65},{193,1... | collective-permute-start | bytes 393224 | tf_op jit(solution)/shard_map/ppermute | solution.py:35
  30.3 17.1 %collective-permute-start.9 = (bf16[64,2048]{1,0:T(8,128)(2,1)S(1)}, bf16[64,2048]{1,0:T(8,128)(2,1)S(1)}, u32[]{:S(2)}, u32[]{:S(2)}) collective-permute-start(bf16[64,2048]{1,0:T(8,128)(2,1)S(1)} %get-tuple-element.115), channel_id=1, source_target_pairs={{0,192},{64,128},{128,64},{192,0},{1,193},{65,129},{129,65},{193,1... | collective-permute-start | bytes 786440 | tf_op jit(solution)/shard_map/ppermute | solution.py:35
  31.8 17.8 %collective-permute-start.8 = (bf16[64,2048]{1,0:T(8,128)(2,1)S(1)}, bf16[64,2048]{1,0:T(8,128)(2,1)S(1)}, u32[]{:S(2)}, u32[]{:S(2)}) collective-permute-start(bf16[64,2048]{1,0:T(8,128)(2,1)S(1)} %get-tuple-element.109), channel_id=1, source_target_pairs={{0,64},{64,0},{128,192},{192,128},{1,65},{65,1},{129,193},{193,129... | collective-permute-start | bytes 786440 | tf_op jit(solution)/shard_map/ppermute | solution.py:35
  33.8 22.6 %collective-permute-start.7 = (bf16[128,1024]{1,0:T(8,128)(2,1)S(1)}, bf16[128,1024]{1,0:T(8,128)(2,1)S(1)}, u32[]{:S(2)}, u32[]{:S(2)}) collective-permute-start(bf16[128,1024]{1,0:T(8,128)(2,1)S(1)} %pad_maximum_fusion.2), channel_id=1, source_target_pairs={{0,192},{64,128},{128,64},{192,0},{1,193},{65,129},{129,65},{193,1... | collective-permute-start | bytes 786440 | tf_op jit(solution)/shard_map/ppermute | solution.py:35
  37.1 19.3 %collective-permute-start.12 = (bf16[128,1024]{1,0:T(8,128)(2,1)S(1)}, bf16[128,1024]{1,0:T(8,128)(2,1)S(1)}, u32[]{:S(2)}, u32[]{:S(2)}) collective-permute-start(bf16[128,1024]{1,0:T(8,128)(2,1)S(1)} %pad_maximum_fusion.3), channel_id=1, source_target_pairs={{0,64},{64,0},{128,192},{192,128},{1,65},{65,1},{129,193},{193,129... | collective-permute-start | bytes 786440 | tf_op jit(solution)/shard_map/ppermute | solution.py:35
  47.4 9.4 %collective-permute-start.11 = (bf16[128,2048]{1,0:T(8,128)(2,1)S(1)}, bf16[128,2048]{1,0:T(8,128)(2,1)S(1)}, u32[]{:S(2)}, u32[]{:S(2)}) collective-permute-start(bf16[128,2048]{1,0:T(8,128)(2,1)S(1)} %get-tuple-element.102), channel_id=1, source_target_pairs={{0,6},{2,4},{4,2},{6,0},{1,7},{3,5},{5,3},{7,1},{8,14},{10,12},{12... | collective-permute-start | bytes 1572872 | tf_op jit(solution)/shard_map/ppermute | solution.py:35
  49.7 10.4 %collective-permute-start.14 = (bf16[128,2048]{1,0:T(8,128)(2,1)S(1)}, bf16[128,2048]{1,0:T(8,128)(2,1)S(1)}, u32[]{:S(2)}, u32[]{:S(2)}) collective-permute-start(bf16[128,2048]{1,0:T(8,128)(2,1)S(1)} %get-tuple-element.100), channel_id=1, source_target_pairs={{0,2},{2,0},{4,6},{6,4},{1,3},{3,1},{5,7},{7,5},{8,10},{10,8},{12,... | collective-permute-start | bytes 1572872 | tf_op jit(solution)/shard_map/ppermute | solution.py:35
  56.9 24.6 %collective-permute-start.13 = (bf16[256,2048]{1,0:T(8,128)(2,1)S(1)}, bf16[256,2048]{1,0:T(8,128)(2,1)S(1)}, u32[]{:S(2)}, u32[]{:S(2)}) collective-permute-start(bf16[256,2048]{1,0:T(8,128)(2,1)S(1)} %constant_dynamic-update-slice_fusion.12.refs_0_), channel_id=1, source_target_pairs={{0,2},{2,0},{4,6},{6,4},{1,3},{3,1},{5,7},{7,5},{8,10},{10,8},{12,... | collective-permute-start | bytes 3145736 | tf_op jit(solution)/shard_map/ppermute | solution.py:35
  60.1 21.4 %collective-permute-start.15 = (bf16[256,2048]{1,0:T(8,128)(2,1)S(1)}, bf16[256,2048]{1,0:T(8,128)(2,1)S(1)}, u32[]{:S(2)}, u32[]{:S(2)}) collective-permute-start(bf16[256,2048]{1,0:T(8,128)(2,1)S(1)} %constant_dynamic-update-slice_fusion.16.refs_1_), channel_id=1, source_target_pairs={{0,6},{2,4},{4,2},{6,0},{1,7},{3,5},{5,3},{7,1},{8,14},{10,12},{12... | collective-permute-start | bytes 3145736 | tf_op jit(solution)/shard_map/ppermute | solution.py:35
  61.1 23.7 %collective-permute-start.10 = (bf16[256,1024]{1,0:T(8,128)(2,1)S(1)}, bf16[256,1024]{1,0:T(8,128)(2,1)S(1)}, u32[]{:S(2)}, u32[]{:S(2)}) collective-permute-start(bf16[256,1024]{1,0:T(8,128)(2,1)S(1)} %pad_maximum_fusion.refs_2_), channel_id=1, source_target_pairs={{0,64},{64,0},{128,192},{192,128},{1,65},{65,1},{129,193},{193,129... | collective-permute-start | bytes 1572872 | tf_op jit(solution)/shard_map/ppermute | solution.py:35
  63.1 22.6 %collective-permute-start.16 = (bf16[256,1024]{1,0:T(8,128)(2,1)S(1)}, bf16[256,1024]{1,0:T(8,128)(2,1)S(1)}, u32[]{:S(2)}, u32[]{:S(2)}) collective-permute-start(bf16[256,1024]{1,0:T(8,128)(2,1)S(1)} %pad_maximum_fusion.1.refs_3_), channel_id=1, source_target_pairs={{0,192},{64,128},{128,64},{192,0},{1,193},{65,129},{129,65},{193,1... | collective-permute-start | bytes 1572872 | tf_op jit(solution)/shard_map/ppermute | solution.py:35
  88.7 22.2 %collective-permute-start.17 = (bf16[256,2048]{1,0:T(8,128)(2,1)S(1)}, bf16[256,2048]{1,0:T(8,128)(2,1)S(1)}, u32[]{:S(2)}, u32[]{:S(2)}) collective-permute-start(bf16[256,2048]{1,0:T(8,128)(2,1)S(1)} %out.8), channel_id=1, source_target_pairs={{0,2},{2,0},{4,6},{6,4},{1,3},{3,1},{5,7},{7,5},{8,10},{10,8},{12,... | collective-permute-start | bytes 3145736 | tf_op jit(solution)/shard_map/ppermute | solution.py:35
  91.4 25.3 %collective-permute-start.21 = (bf16[256,2048]{1,0:T(8,128)(2,1)S(1)}, bf16[256,2048]{1,0:T(8,128)(2,1)S(1)}, u32[]{:S(2)}, u32[]{:S(2)}) collective-permute-start(bf16[256,2048]{1,0:T(8,128)(2,1)S(1)} %out.9), channel_id=1, source_target_pairs={{0,6},{2,4},{4,2},{6,0},{1,7},{3,5},{5,3},{7,1},{8,14},{10,12},{12... | collective-permute-start | bytes 3145736 | tf_op jit(solution)/shard_map/ppermute | solution.py:35
  94.0 28.6 %collective-permute-start.19 = (bf16[256,1024]{1,0:T(8,128)(2,1)S(1)}, bf16[256,1024]{1,0:T(8,128)(2,1)S(1)}, u32[]{:S(2)}, u32[]{:S(2)}) collective-permute-start(bf16[256,1024]{1,0:T(8,128)(2,1)S(1)} %out.11), channel_id=1, source_target_pairs={{0,192},{64,128},{128,64},{192,0},{1,193},{65,129},{129,65},{193,1... | collective-permute-start | bytes 1572872 | tf_op jit(solution)/shard_map/ppermute | solution.py:35
  98.0 23.2 %collective-permute-start.20 = (bf16[256,1024]{1,0:T(8,128)(2,1)S(1)}, bf16[256,1024]{1,0:T(8,128)(2,1)S(1)}, u32[]{:S(2)}, u32[]{:S(2)}) collective-permute-start(bf16[256,1024]{1,0:T(8,128)(2,1)S(1)} %out.10), channel_id=1, source_target_pairs={{0,64},{64,0},{128,192},{192,128},{1,65},{65,1},{129,193},{193,129... | collective-permute-start | bytes 1572872 | tf_op jit(solution)/shard_map/ppermute | solution.py:35
  111.1 13.5 %collective-permute-start.18 = (bf16[128,2048]{1,0:T(8,128)(2,1)S(1)}, bf16[128,2048]{1,0:T(8,128)(2,1)S(1)}, u32[]{:S(2)}, u32[]{:S(2)}) collective-permute-start(bf16[128,2048]{1,0:T(8,128)(2,1)S(1)} %add_convert_fusion.1), channel_id=1, source_target_pairs={{0,6},{2,4},{4,2},{6,0},{1,7},{3,5},{5,3},{7,1},{8,14},{10,12},{12... | collective-permute-start | bytes 1572872 | tf_op jit(solution)/shard_map/ppermute | solution.py:35
  121.3 14.5 %collective-permute-start.25 = (bf16[128,1024]{1,0:T(8,128)(2,1)S(1)}, bf16[128,1024]{1,0:T(8,128)(2,1)S(1)}, u32[]{:S(2)}, u32[]{:S(2)}) collective-permute-start(bf16[128,1024]{1,0:T(8,128)(2,1)S(1)} %add_convert_fusion.5), channel_id=1, source_target_pairs={{0,192},{64,128},{128,64},{192,0},{1,193},{65,129},{129,65},{193,1... | collective-permute-start | bytes 786440 | tf_op jit(solution)/shard_map/ppermute | solution.py:35
  122.7 13.1 %collective-permute-start.26 = (bf16[128,1024]{1,0:T(8,128)(2,1)S(1)}, bf16[128,1024]{1,0:T(8,128)(2,1)S(1)}, u32[]{:S(2)}, u32[]{:S(2)}) collective-permute-start(bf16[128,1024]{1,0:T(8,128)(2,1)S(1)} %add_convert_fusion.4), channel_id=1, source_target_pairs={{0,64},{64,0},{128,192},{192,128},{1,65},{65,1},{129,193},{193,129... | collective-permute-start | bytes 786440 | tf_op jit(solution)/shard_map/ppermute | solution.py:35
  124.7 22.5 %collective-permute-start.22 = (bf16[64,2048]{1,0:T(8,128)(2,1)S(1)}, bf16[64,2048]{1,0:T(8,128)(2,1)S(1)}, u32[]{:S(2)}, u32[]{:S(2)}) collective-permute-start(bf16[64,2048]{1,0:T(8,128)(2,1)S(1)} %add_convert_fusion.3), channel_id=1, source_target_pairs={{0,192},{64,128},{128,64},{192,0},{1,193},{65,129},{129,65},{193,1... | collective-permute-start | bytes 786440 | tf_op jit(solution)/shard_map/ppermute | solution.py:35
  126.2 21.3 %collective-permute-start.24 = (bf16[64,2048]{1,0:T(8,128)(2,1)S(1)}, bf16[64,2048]{1,0:T(8,128)(2,1)S(1)}, u32[]{:S(2)}, u32[]{:S(2)}) collective-permute-start(bf16[64,2048]{1,0:T(8,128)(2,1)S(1)} %add_convert_fusion.2), channel_id=1, source_target_pairs={{0,64},{64,0},{128,192},{192,128},{1,65},{65,1},{129,193},{193,129... | collective-permute-start | bytes 786440 | tf_op jit(solution)/shard_map/ppermute | solution.py:35
  135.9 14.1 %collective-permute-start.27 = (bf16[64,2048]{1,0:T(8,128)(2,1)S(1)}, bf16[64,2048]{1,0:T(8,128)(2,1)S(1)}, u32[]{:S(2)}, u32[]{:S(2)}) collective-permute-start(bf16[64,2048]{1,0:T(8,128)(2,1)S(1)} %pad_maximum_fusion.4), channel_id=1, source_target_pairs={{0,6},{2,4},{4,2},{6,0},{1,7},{3,5},{5,3},{7,1},{8,14},{10,12},{12... | collective-permute-start | bytes 786440 | tf_op jit(solution)/shard_map/ppermute | solution.py:35
  (13 other events, 185.3 us)

commit v14 on v13

--- a/solution.py
+++ b/solution.py
@@ -43,13 +43,14 @@
     return lax.optimization_barrier((value, *others))[0]
 
 
-def hidden_kernel(pieces, first, last, *refs):
+def hidden_kernel(pieces, first, last, more, *refs):
     n = len(pieces)
     ins = refs[:n]
     wg0, wu0, wg1, wu1 = refs[n : n + 4]
     refs = refs[n + 4 :]
     before = None if first else refs[0]
     refs = refs if first else refs[1:]
+    extra, refs = refs[:more], refs[more:]
     total = refs[0]
     acc = refs[1] if last else total
     step = pl.program_id(0)
@@ -59,6 +60,10 @@
     @pl.when(step == 0)
     def _():
         acc[...] = jnp.zeros_like(acc) if first else before[...]
+        for k, product in enumerate(extra):
+            for index in range(8):
+                to = canon_block(CHAINS[2 + k // 4][2], index + 8) * UNIT
+                acc[k % 4, to : to + UNIT, :] += product[index * UNIT : (index + 1) * UNIT, :]
 
     at = 0
     for k, (c, came) in enumerate(pieces):
@@ -106,7 +111,7 @@
     return value
 
 
-def hidden_units(pieces, weights, before, last):
+def hidden_units(pieces, weights, before, last, extra=()):
     width, units = weights[0].shape
     count = 2 * HALF
     first = before is None
@@ -122,6 +127,7 @@
     sums = (4, count, units)
     if not first:
         in_specs.append(whole(*sums))
+    in_specs += [whole(HALF, units)] * len(extra)
     if last:
         out, out_spec = jax.ShapeDtypeStruct((count, 2 * units), jnp.bfloat16), whole(count, 2 * units)
         scratch = [pltpu.VMEM(sums, jnp.float32)]
@@ -129,7 +135,7 @@
         out, out_spec, scratch = jax.ShapeDtypeStruct(sums, jnp.float32), whole(*sums), []
     depth = len(parts) * PART
     return pl.pallas_call(
-        functools.partial(hidden_kernel, tuple(pieces), first, last),
+        functools.partial(hidden_kernel, tuple(pieces), first, last, len(extra)),
         grid=(len(parts),),
         out_shape=out,
         in_specs=in_specs,
@@ -142,7 +148,7 @@
             transcendentals=2 * count * units if last else 0,
         ),
         name="hidden",
-    )(*pieces.values(), *weights, *(() if first else (before,)))
+    )(*pieces.values(), *weights, *(() if first else (before,)), *extra)
 
 
 def expert_out(hidden, wd0, wd1, chain, sent):
@@ -336,12 +342,17 @@
     came = [trade(h, order[3]) for h, (_, _, order) in zip(held, CHAINS)]
     weights = (wg0, wu0, wg1, wu1)
     sums = hidden_units({(j, False): held[j] for j in range(4)}, weights, None, False)
-    came[0] = after(came[0], last, sums)
+    came[2] = after(came[2], last, sums)
+    came[3] = after(came[3], came[2])
+    extra = []
+    for j in (2, 3):
+        start, size, _ = CHAINS[j]
+        for w in weights:
+            product = jnp.dot(came[j], w[start : start + size], preferred_element_type=jnp.float32)
+            extra.append(product)
+    came[0] = after(came[0], *extra)
     came[1] = after(came[1], came[0])
-    sums = hidden_units({(j, True): came[j] for j in (0, 1)}, weights, sums, False)
-    came[2] = after(came[2], sums)
-    came[3] = after(came[3], came[2])
-    hidden = hidden_units({(j, True): came[j] for j in (2, 3)}, weights, sums, True)
+    hidden = hidden_units({(j, True): came[j] for j in (0, 1)}, weights, sums, True, extra)
 
     held, away = [], []
     for j in range(4):

time: 171 us -> 173 us (1.012)
  waiting for transfers between devices: 69.5 us -> 41.5 us
  starting transfers between devices: 51.4 us -> 78.1 us
  matrix products: 0 us -> 2.4 us
    ppermute x32, waiting for transfers between devices: 69.5 us -> 41.5 us  [trade(): return lax.ppermute(value, axis, [(i, i ^ mask) for i in range(n)])]
    ppermute x32, starting transfers between devices: 51.4 us -> 78.1 us  [trade(): return lax.ppermute(value, axis, [(i, i ^ mask) for i in range(n)])]
    dot_general x0 -> x8, matrix products: none -> 2.4 us  [per_device(): jnp.dot(came[j], w[start:start + size], preferred_element_type=jnp.float32)]
    pallas_call x3 -> x2, Pallas kernels: 9.99 us -> 8.67 us  [hidden_units(): pl.pallas_call(functools.partial(hidden_kernel, tuple(pieces), first, las...]
  transfers between devices with their start and end apart: 32 -> 32, of which waited for: 17 -> 14; matrix products, arithmetic and copies ran while one was open for 1% -> 2% of each run, Pallas kernels for 8% -> 6%
where the time goes in v14:
time: 173 us; the launch traced here: 171 us
  starting transfers between devices  78.1 us (45%)
  waiting for transfers between devices  41.5 us (24%)
  blocking collectives  28 us (16%)
  Pallas kernels  18.7 us (11%)
  matrix products  2.4 us (1%)
    ppermute x32, starting transfers between devices, trade(): return lax.ppermute(value, axis, [(i, i ^ mask) for i in range(n)])  78.1 us
    ppermute x32, waiting for transfers between devices, trade(): return lax.ppermute(value, axis, [(i, i ^ mask) for i in range(n)])  41.5 us
    all_to_all x2, blocking collectives, swap_experts(): lax.all_to_all(blocks, ('zl', 'y'), split_axis=0, concat_axis=0, tiled=True)  28 us
    pallas_call x2, Pallas kernels, hidden_units(): pl.pallas_call(functools.partial(hidden_kernel, tuple(pieces), first, las...  8.67 us
    pallas_call x8, Pallas kernels, expert_out(): pl.pallas_call(functools.partial(out_kernel, order, int(sent)), grid=(siz...  6.21 us
    pallas_call x4, Pallas kernels, small(): pl.pallas_call(kernel, out_shape=out_shape, in_specs=[pl.BlockSpec(memory...  3.78 us
  transfers between devices with their start and end apart: 32, of which 14 were waited for; matrix products, arithmetic and copies ran while one was open for 2% of the time, Pallas kernels for 6%

profile of v14, /device:TPU:2, one launch (start us, length us, event | category | flops | bytes accessed | tf_op | source)
XLA Modules:
  0.0 170.8 jit_solution(13150093010242997261)
XLA Ops:
  2.8 15.1 %all_to_all.10 = bf16[8,8,3072]{2,1,0:T(8,128)(2,1)S(1)} all-to-all(bf16[8,8,3072]{2,1,0:T(8,128)(2,1)} %bitcast.48), channel_id=1, replica_groups=mesh['dp'=4,'zl'=2,'y'=4,'x'=4,'c'=2] {'zl','y'}, dimensions={0} | all-to-all | bytes 786432 | tf_op jit(solution)/shard_map/all_to_all | solution.py:284
  18.2 3.4 %collective-permute-start.2 = (bf16[32,2048]{1,0:T(8,128)(2,1)S(1)}, bf16[32,2048]{1,0:T(8,128)(2,1)S(1)}, u32[]{:S(2)}, u32[]{:S(2)}) collective-permute-start(bf16[32,2048]{1,0:T(8,128)(2,1)S(1)} %get-tuple-element.52), channel_id=1, source_target_pairs={{0,64},{64,0},{128,192},{192,128},{1,65},{65,1},{129,193},{193,129... | collective-permute-start | bytes 393224 | tf_op jit(solution)/shard_map/ppermute | solution.py:35
  22.1 3.6 %collective-permute-start.6 = (bf16[32,2048]{1,0:T(8,128)(2,1)S(1)}, bf16[32,2048]{1,0:T(8,128)(2,1)S(1)}, u32[]{:S(2)}, u32[]{:S(2)}) collective-permute-start(bf16[32,2048]{1,0:T(8,128)(2,1)S(1)} %get-tuple-element.55), channel_id=1, source_target_pairs={{0,192},{64,128},{128,64},{192,0},{1,193},{65,129},{129,65},{193,1... | collective-permute-start | bytes 393224 | tf_op jit(solution)/shard_map/ppermute | solution.py:35
  28.1 3.7 %collective-permute-start.4 = (bf16[64,2048]{1,0:T(8,128)(2,1)S(1)}, bf16[64,2048]{1,0:T(8,128)(2,1)S(1)}, u32[]{:S(2)}, u32[]{:S(2)}) collective-permute-start(bf16[64,2048]{1,0:T(8,128)(2,1)S(1)} %get-tuple-element.115), channel_id=1, source_target_pairs={{0,192},{64,128},{128,64},{192,0},{1,193},{65,129},{129,65},{193,1... | collective-permute-start | bytes 786440 | tf_op jit(solution)/shard_map/ppermute | solution.py:35
  33.5 3.2 %collective-permute-start.10 = (bf16[128,1024]{1,0:T(8,128)(2,1)S(1)}, bf16[128,1024]{1,0:T(8,128)(2,1)S(1)}, u32[]{:S(2)}, u32[]{:S(2)}) collective-permute-start(bf16[128,1024]{1,0:T(8,128)(2,1)S(1)} %pad_maximum_fusion.2), channel_id=1, source_target_pairs={{0,192},{64,128},{128,64},{192,0},{1,193},{65,129},{129,65},{193,1... | collective-permute-start | bytes 786440 | tf_op jit(solution)/shard_map/ppermute | solution.py:35
  38.8 8.7 %collective-permute-done.4 = bf16[64,2048]{1,0:T(8,128)(2,1)S(1)} collective-permute-done((bf16[64,2048]{1,0:T(8,128)(2,1)S(1)}, bf16[64,2048]{1,0:T(8,128)(2,1)S(1)}, u32[]{:S(2)}, u32[]{:S(2)}) %collective-permute-start.4) | collective-permute-done | bytes 262176 | tf_op jit(solution)/shard_map/ppermute | solution.py:35
  47.6 3.9 %collective-permute-start.8 = (bf16[128,2048]{1,0:T(8,128)(2,1)S(1)}, bf16[128,2048]{1,0:T(8,128)(2,1)S(1)}, u32[]{:S(2)}, u32[]{:S(2)}) collective-permute-start(bf16[128,2048]{1,0:T(8,128)(2,1)S(1)} %get-tuple-element.101), channel_id=1, source_target_pairs={{0,6},{2,4},{4,2},{6,0},{1,7},{3,5},{5,3},{7,1},{8,14},{10,12},{12... | collective-permute-start | bytes 1572872 | tf_op jit(solution)/shard_map/ppermute | solution.py:35
  55.3 4.7 %collective-permute-start.15 = (bf16[256,1024]{1,0:T(8,128)(2,1)S(1)}, bf16[256,1024]{1,0:T(8,128)(2,1)S(1)}, u32[]{:S(2)}, u32[]{:S(2)}) collective-permute-start(bf16[256,1024]{1,0:T(8,128)(2,1)S(1)} %pad_maximum_fusion.1.refs_3_), channel_id=1, source_target_pairs={{0,192},{64,128},{128,64},{192,0},{1,193},{65,129},{129,65},{193,1... | collective-permute-start | bytes 1572872 | tf_op jit(solution)/shard_map/ppermute | solution.py:35
  61.4 3.4 %collective-permute-start.16 = (bf16[256,2048]{1,0:T(8,128)(2,1)S(1)}, bf16[256,2048]{1,0:T(8,128)(2,1)S(1)}, u32[]{:S(2)}, u32[]{:S(2)}) collective-permute-start(bf16[256,2048]{1,0:T(8,128)(2,1)S(1)} %constant_dynamic-update-slice_fusion.16.refs_1_), channel_id=1, source_target_pairs={{0,6},{2,4},{4,2},{6,0},{1,7},{3,5},{5,3},{7,1},{8,14},{10,12},{12... | collective-permute-start | bytes 3145736 | tf_op jit(solution)/shard_map/ppermute | solution.py:35
  64.9 4.8 %hidden.2.refs_6_ = f32[4,512,256]{2,1,0:T(8,128)S(1)} custom-call(bf16[256,2048]{1,0:T(8,128)(2,1)S(1)} %constant_dynamic-update-slice_fusion.12.refs_0_, bf16[256,2048]{1,0:T(8,128)(2,1)S(1)} %constant_dynamic-update-slice_fusion.16.refs_1_, bf16[256,1024]{1,0:T(8,128)(2,1)S(1)} %pad_maximum_fusion.refs_2_, ...), custom_call_target="tpu_custom_call" | custom-call | tf_op jit(solution)/shard_map/hidden/pallas_call | solution.py:137
  69.7 9.7 %collective-permute-done.13 = bf16[256,1024]{1,0:T(8,128)(2,1)S(1)} collective-permute-done((bf16[256,1024]{1,0:T(8,128)(2,1)S(1)}, bf16[256,1024]{1,0:T(8,128)(2,1)S(1)}, u32[]{:S(2)}, u32[]{:S(2)}) %collective-permute-start.13) | collective-permute-done | bytes 524320 | tf_op jit(solution)/shard_map/ppermute | solution.py:35
  79.4 2.8 %collective-permute-done.15 = bf16[256,1024]{1,0:T(8,128)(2,1)S(1)} collective-permute-done((bf16[256,1024]{1,0:T(8,128)(2,1)S(1)}, bf16[256,1024]{1,0:T(8,128)(2,1)S(1)}, u32[]{:S(2)}, u32[]{:S(2)}) %collective-permute-start.15) | collective-permute-done | bytes 524320 | tf_op jit(solution)/shard_map/ppermute | solution.py:35
  84.7 3.8 %hidden.3 = bf16[512,512]{1,0:T(8,128)(2,1)S(1)} custom-call(bf16[256,2048]{1,0:T(8,128)(2,1)S(1)} %collective-permute-done.12.refs_0_, bf16[256,2048]{1,0:T(8,128)(2,1)S(1)} %collective-permute-done.16.refs_1_, bf16[6144,256]{1,0:T(8,128)(2,1)S(1)} %bitcast.41, bf16[6144,256]{1,0:T(8,128)(2,1)S(1)} %bitcast.44, ...), custom_call_target="tpu_custom_call" | custom-call | flops 2147483648 | bytes 10485760 | tf_op jit(solution)/shard_map/hidden/pallas_call | solution.py:137
  89.7 2.7 %collective-permute-start.17 = (bf16[256,2048]{1,0:T(8,128)(2,1)S(1)}, bf16[256,2048]{1,0:T(8,128)(2,1)S(1)}, u32[]{:S(2)}, u32[]{:S(2)}) collective-permute-start(bf16[256,2048]{1,0:T(8,128)(2,1)S(1)} %out.8), channel_id=1, source_target_pairs={{0,2},{2,0},{4,6},{6,4},{1,3},{3,1},{5,7},{7,5},{8,10},{10,8},{12,... | collective-permute-start | bytes 3145736 | tf_op jit(solution)/shard_map/ppermute | solution.py:35
  98.2 4.3 %collective-permute-start.20 = (bf16[256,1024]{1,0:T(8,128)(2,1)S(1)}, bf16[256,1024]{1,0:T(8,128)(2,1)S(1)}, u32[]{:S(2)}, u32[]{:S(2)}) collective-permute-start(bf16[256,1024]{1,0:T(8,128)(2,1)S(1)} %out.10), channel_id=1, source_target_pairs={{0,64},{64,0},{128,192},{192,128},{1,65},{65,1},{129,193},{193,129... | collective-permute-start | bytes 1572872 | tf_op jit(solution)/shard_map/ppermute | solution.py:35
  105.7 6.4 %collective-permute-done.17 = bf16[256,2048]{1,0:T(8,128)(2,1)S(1)} collective-permute-done((bf16[256,2048]{1,0:T(8,128)(2,1)S(1)}, bf16[256,2048]{1,0:T(8,128)(2,1)S(1)}, u32[]{:S(2)}, u32[]{:S(2)}) %collective-permute-start.17) | collective-permute-done | bytes 1048608 | tf_op jit(solution)/shard_map/ppermute | solution.py:35
  112.2 3.1 %collective-permute-start.18 = (bf16[128,2048]{1,0:T(8,128)(2,1)S(1)}, bf16[128,2048]{1,0:T(8,128)(2,1)S(1)}, u32[]{:S(2)}, u32[]{:S(2)}) collective-permute-start(bf16[128,2048]{1,0:T(8,128)(2,1)S(1)} %add_convert_fusion.1), channel_id=1, source_target_pairs={{0,6},{2,4},{4,2},{6,0},{1,7},{3,5},{5,3},{7,1},{8,14},{10,12},{12... | collective-permute-start | bytes 1572872 | tf_op jit(solution)/shard_map/ppermute | solution.py:35
  115.3 3.7 %collective-permute-done.21 = bf16[256,2048]{1,0:T(8,128)(2,1)S(1)} collective-permute-done((bf16[256,2048]{1,0:T(8,128)(2,1)S(1)}, bf16[256,2048]{1,0:T(8,128)(2,1)S(1)}, u32[]{:S(2)}, u32[]{:S(2)}) %collective-permute-start.21) | collective-permute-done | bytes 1048608 | tf_op jit(solution)/shard_map/ppermute | solution.py:35
  123.6 2.7 %collective-permute-start.26 = (bf16[128,1024]{1,0:T(8,128)(2,1)S(1)}, bf16[128,1024]{1,0:T(8,128)(2,1)S(1)}, u32[]{:S(2)}, u32[]{:S(2)}) collective-permute-start(bf16[128,1024]{1,0:T(8,128)(2,1)S(1)} %add_convert_fusion.4), channel_id=1, source_target_pairs={{0,64},{64,0},{128,192},{192,128},{1,65},{65,1},{129,193},{193,129... | collective-permute-start | bytes 786440 | tf_op jit(solution)/shard_map/ppermute | solution.py:35
  127.2 4.5 %collective-permute-start.22 = (bf16[64,2048]{1,0:T(8,128)(2,1)S(1)}, bf16[64,2048]{1,0:T(8,128)(2,1)S(1)}, u32[]{:S(2)}, u32[]{:S(2)}) collective-permute-start(bf16[64,2048]{1,0:T(8,128)(2,1)S(1)} %add_convert_fusion.3), channel_id=1, source_target_pairs={{0,192},{64,128},{128,64},{192,0},{1,193},{65,129},{129,65},{193,1... | collective-permute-start | bytes 786440 | tf_op jit(solution)/shard_map/ppermute | solution.py:35
  134.0 10.5 %collective-permute-start.27 = (bf16[64,2048]{1,0:T(8,128)(2,1)S(1)}, bf16[64,2048]{1,0:T(8,128)(2,1)S(1)}, u32[]{:S(2)}, u32[]{:S(2)}) collective-permute-start(bf16[64,2048]{1,0:T(8,128)(2,1)S(1)} %pad_maximum_fusion.4), channel_id=1, source_target_pairs={{0,6},{2,4},{4,2},{6,0},{1,7},{3,5},{5,3},{7,1},{8,14},{10,12},{12... | collective-permute-start | bytes 786440 | tf_op jit(solution)/shard_map/ppermute | solution.py:35
  149.0 3.1 %collective-permute-start.31 = (bf16[32,1024]{1,0:T(8,128)(2,1)S(1)}, bf16[32,1024]{1,0:T(8,128)(2,1)S(1)}, u32[]{:S(2)}, u32[]{:S(2)}) collective-permute-start(bf16[32,1024]{1,0:T(8,128)(2,1)S(1)} %get-tuple-element.93), channel_id=1, source_target_pairs={{0,2},{2,0},{4,6},{6,4},{1,3},{3,1},{5,7},{7,5},{8,10},{10,8},{12,... | collective-permute-start | bytes 196616 | tf_op jit(solution)/shard_map/ppermute | solution.py:35
  152.2 2.4 %collective-permute-done.31.refs_7_ = bf16[32,1024]{1,0:T(8,128)(2,1)S(1)} collective-permute-done((bf16[32,1024]{1,0:T(8,128)(2,1)S(1)}, bf16[32,1024]{1,0:T(8,128)(2,1)S(1)}, u32[]{:S(2)}, u32[]{:S(2)}) %collective-permute-start.31) | collective-permute-done | bytes 65568 | tf_op jit(solution)/shard_map/ppermute | solution.py:35
  156.8 13.0 %all_to_all.11 = bf16[8,8,3072]{2,1,0:T(8,128)(2,1)S(1)} all-to-all(bf16[8,8,3072]{2,1,0:T(8,128)(2,1)S(1)} %bitcast.47), channel_id=1, replica_groups=mesh['dp'=4,'zl'=2,'y'=4,'x'=4,'c'=2] {'zl','y'}, dimensions={0} | all-to-all | bytes 786432 | tf_op jit(solution)/shard_map/all_to_all | solution.py:284
  (102 shorter events, 43.0 us)
Async XLA Ops:
  2.1 15.8 %collective-permute-start = (bf16[6144,256]{1,0:T(8,128)(2,1)}, bf16[6144,256]{1,0:T(8,128)(2,1)S(1)}, u32[]{:S(2)}, u32[]{:S(2)}) collective-permute-start(bf16[6144,256]{1,0:T(8,128)(2,1)} %bitcast.39), channel_id=1, source_target_pairs={{0,1},{1,0},{2,3},{3,2},{4,5},{5,4},{6,7},{7,6},{8,9},{9,8},{10,11... | collective-permute-start | bytes 9437192 | tf_op jit(solution)/shard_map/ppermute | solution.py:35
  2.2 15.7 %collective-permute-start.1 = (bf16[6144,256]{1,0:T(8,128)(2,1)}, bf16[6144,256]{1,0:T(8,128)(2,1)S(1)}, u32[]{:S(2)}, u32[]{:S(2)}) collective-permute-start(bf16[6144,256]{1,0:T(8,128)(2,1)} %bitcast.42), channel_id=1, source_target_pairs={{0,1},{1,0},{2,3},{3,2},{4,5},{5,4},{6,7},{7,6},{8,9},{9,8},{10,11... | collective-permute-start | bytes 9437192 | tf_op jit(solution)/shard_map/ppermute | solution.py:35
  2.7 29.1 %collective-permute-start.7 = (bf16[256,6144]{1,0:T(8,128)(2,1)}, bf16[256,6144]{1,0:T(8,128)(2,1)S(1)}, u32[]{:S(2)}, u32[]{:S(2)}) collective-permute-start(bf16[256,6144]{1,0:T(8,128)(2,1)} %bitcast.30), channel_id=1, source_target_pairs={{0,1},{1,0},{2,3},{3,2},{4,5},{5,4},{6,7},{7,6},{8,9},{9,8},{10,11... | collective-permute-start | bytes 9437192 | tf_op jit(solution)/shard_map/ppermute | solution.py:35
  28.1 19.4 %collective-permute-start.4 = (bf16[64,2048]{1,0:T(8,128)(2,1)S(1)}, bf16[64,2048]{1,0:T(8,128)(2,1)S(1)}, u32[]{:S(2)}, u32[]{:S(2)}) collective-permute-start(bf16[64,2048]{1,0:T(8,128)(2,1)S(1)} %get-tuple-element.115), channel_id=1, source_target_pairs={{0,192},{64,128},{128,64},{192,0},{1,193},{65,129},{129,65},{193,1... | collective-permute-start | bytes 786440 | tf_op jit(solution)/shard_map/ppermute | solution.py:35
  31.8 19.7 %collective-permute-start.11 = (bf16[64,2048]{1,0:T(8,128)(2,1)S(1)}, bf16[64,2048]{1,0:T(8,128)(2,1)S(1)}, u32[]{:S(2)}, u32[]{:S(2)}) collective-permute-start(bf16[64,2048]{1,0:T(8,128)(2,1)S(1)} %get-tuple-element.109), channel_id=1, source_target_pairs={{0,64},{64,0},{128,192},{192,128},{1,65},{65,1},{129,193},{193,129... | collective-permute-start | bytes 786440 | tf_op jit(solution)/shard_map/ppermute | solution.py:35
  33.5 20.2 %collective-permute-start.10 = (bf16[128,1024]{1,0:T(8,128)(2,1)S(1)}, bf16[128,1024]{1,0:T(8,128)(2,1)S(1)}, u32[]{:S(2)}, u32[]{:S(2)}) collective-permute-start(bf16[128,1024]{1,0:T(8,128)(2,1)S(1)} %pad_maximum_fusion.2), channel_id=1, source_target_pairs={{0,192},{64,128},{128,64},{192,0},{1,193},{65,129},{129,65},{193,1... | collective-permute-start | bytes 786440 | tf_op jit(solution)/shard_map/ppermute | solution.py:35
  36.7 18.5 %collective-permute-start.9 = (bf16[128,1024]{1,0:T(8,128)(2,1)S(1)}, bf16[128,1024]{1,0:T(8,128)(2,1)S(1)}, u32[]{:S(2)}, u32[]{:S(2)}) collective-permute-start(bf16[128,1024]{1,0:T(8,128)(2,1)S(1)} %pad_maximum_fusion.3), channel_id=1, source_target_pairs={{0,64},{64,0},{128,192},{192,128},{1,65},{65,1},{129,193},{193,129... | collective-permute-start | bytes 786440 | tf_op jit(solution)/shard_map/ppermute | solution.py:35
  47.6 12.4 %collective-permute-start.8 = (bf16[128,2048]{1,0:T(8,128)(2,1)S(1)}, bf16[128,2048]{1,0:T(8,128)(2,1)S(1)}, u32[]{:S(2)}, u32[]{:S(2)}) collective-permute-start(bf16[128,2048]{1,0:T(8,128)(2,1)S(1)} %get-tuple-element.101), channel_id=1, source_target_pairs={{0,6},{2,4},{4,2},{6,0},{1,7},{3,5},{5,3},{7,1},{8,14},{10,12},{12... | collective-permute-start | bytes 1572872 | tf_op jit(solution)/shard_map/ppermute | solution.py:35
  53.7 25.7 %collective-permute-start.13 = (bf16[256,1024]{1,0:T(8,128)(2,1)S(1)}, bf16[256,1024]{1,0:T(8,128)(2,1)S(1)}, u32[]{:S(2)}, u32[]{:S(2)}) collective-permute-start(bf16[256,1024]{1,0:T(8,128)(2,1)S(1)} %pad_maximum_fusion.refs_2_), channel_id=1, source_target_pairs={{0,64},{64,0},{128,192},{192,128},{1,65},{65,1},{129,193},{193,129... | collective-permute-start | bytes 1572872 | tf_op jit(solution)/shard_map/ppermute | solution.py:35
  55.3 26.9 %collective-permute-start.15 = (bf16[256,1024]{1,0:T(8,128)(2,1)S(1)}, bf16[256,1024]{1,0:T(8,128)(2,1)S(1)}, u32[]{:S(2)}, u32[]{:S(2)}) collective-permute-start(bf16[256,1024]{1,0:T(8,128)(2,1)S(1)} %pad_maximum_fusion.1.refs_3_), channel_id=1, source_target_pairs={{0,192},{64,128},{128,64},{192,0},{1,193},{65,129},{129,65},{193,1... | collective-permute-start | bytes 1572872 | tf_op jit(solution)/shard_map/ppermute | solution.py:35
  60.0 24.7 %collective-permute-start.12 = (bf16[256,2048]{1,0:T(8,128)(2,1)S(1)}, bf16[256,2048]{1,0:T(8,128)(2,1)S(1)}, u32[]{:S(2)}, u32[]{:S(2)}) collective-permute-start(bf16[256,2048]{1,0:T(8,128)(2,1)S(1)} %constant_dynamic-update-slice_fusion.12.refs_0_), channel_id=1, source_target_pairs={{0,2},{2,0},{4,6},{6,4},{1,3},{3,1},{5,7},{7,5},{8,10},{10,8},{12,... | collective-permute-start | bytes 3145736 | tf_op jit(solution)/shard_map/ppermute | solution.py:35
  61.4 23.3 %collective-permute-start.16 = (bf16[256,2048]{1,0:T(8,128)(2,1)S(1)}, bf16[256,2048]{1,0:T(8,128)(2,1)S(1)}, u32[]{:S(2)}, u32[]{:S(2)}) collective-permute-start(bf16[256,2048]{1,0:T(8,128)(2,1)S(1)} %constant_dynamic-update-slice_fusion.16.refs_1_), channel_id=1, source_target_pairs={{0,6},{2,4},{4,2},{6,0},{1,7},{3,5},{5,3},{7,1},{8,14},{10,12},{12... | collective-permute-start | bytes 3145736 | tf_op jit(solution)/shard_map/ppermute | solution.py:35
  89.7 22.4 %collective-permute-start.17 = (bf16[256,2048]{1,0:T(8,128)(2,1)S(1)}, bf16[256,2048]{1,0:T(8,128)(2,1)S(1)}, u32[]{:S(2)}, u32[]{:S(2)}) collective-permute-start(bf16[256,2048]{1,0:T(8,128)(2,1)S(1)} %out.8), channel_id=1, source_target_pairs={{0,2},{2,0},{4,6},{6,4},{1,3},{3,1},{5,7},{7,5},{8,10},{10,8},{12,... | collective-permute-start | bytes 3145736 | tf_op jit(solution)/shard_map/ppermute | solution.py:35
  93.6 25.5 %collective-permute-start.21 = (bf16[256,2048]{1,0:T(8,128)(2,1)S(1)}, bf16[256,2048]{1,0:T(8,128)(2,1)S(1)}, u32[]{:S(2)}, u32[]{:S(2)}) collective-permute-start(bf16[256,2048]{1,0:T(8,128)(2,1)S(1)} %out.9), channel_id=1, source_target_pairs={{0,6},{2,4},{4,2},{6,0},{1,7},{3,5},{5,3},{7,1},{8,14},{10,12},{12... | collective-permute-start | bytes 3145736 | tf_op jit(solution)/shard_map/ppermute | solution.py:35
  96.9 26.7 %collective-permute-start.19 = (bf16[256,1024]{1,0:T(8,128)(2,1)S(1)}, bf16[256,1024]{1,0:T(8,128)(2,1)S(1)}, u32[]{:S(2)}, u32[]{:S(2)}) collective-permute-start(bf16[256,1024]{1,0:T(8,128)(2,1)S(1)} %out.11), channel_id=1, source_target_pairs={{0,192},{64,128},{128,64},{192,0},{1,193},{65,129},{129,65},{193,1... | collective-permute-start | bytes 1572872 | tf_op jit(solution)/shard_map/ppermute | solution.py:35
  98.2 23.8 %collective-permute-start.20 = (bf16[256,1024]{1,0:T(8,128)(2,1)S(1)}, bf16[256,1024]{1,0:T(8,128)(2,1)S(1)}, u32[]{:S(2)}, u32[]{:S(2)}) collective-permute-start(bf16[256,1024]{1,0:T(8,128)(2,1)S(1)} %out.10), channel_id=1, source_target_pairs={{0,64},{64,0},{128,192},{192,128},{1,65},{65,1},{129,193},{193,129... | collective-permute-start | bytes 1572872 | tf_op jit(solution)/shard_map/ppermute | solution.py:35
  112.2 14.9 %collective-permute-start.18 = (bf16[128,2048]{1,0:T(8,128)(2,1)S(1)}, bf16[128,2048]{1,0:T(8,128)(2,1)S(1)}, u32[]{:S(2)}, u32[]{:S(2)}) collective-permute-start(bf16[128,2048]{1,0:T(8,128)(2,1)S(1)} %add_convert_fusion.1), channel_id=1, source_target_pairs={{0,6},{2,4},{4,2},{6,0},{1,7},{3,5},{5,3},{7,1},{8,14},{10,12},{12... | collective-permute-start | bytes 1572872 | tf_op jit(solution)/shard_map/ppermute | solution.py:35
  119.2 12.5 %collective-permute-start.23 = (bf16[128,2048]{1,0:T(8,128)(2,1)S(1)}, bf16[128,2048]{1,0:T(8,128)(2,1)S(1)}, u32[]{:S(2)}, u32[]{:S(2)}) collective-permute-start(bf16[128,2048]{1,0:T(8,128)(2,1)S(1)} %add_convert_fusion), channel_id=1, source_target_pairs={{0,2},{2,0},{4,6},{6,4},{1,3},{3,1},{5,7},{7,5},{8,10},{10,8},{12,... | collective-permute-start | bytes 1572872 | tf_op jit(solution)/shard_map/ppermute | solution.py:35
  122.1 11.7 %collective-permute-start.25 = (bf16[128,1024]{1,0:T(8,128)(2,1)S(1)}, bf16[128,1024]{1,0:T(8,128)(2,1)S(1)}, u32[]{:S(2)}, u32[]{:S(2)}) collective-permute-start(bf16[128,1024]{1,0:T(8,128)(2,1)S(1)} %add_convert_fusion.5), channel_id=1, source_target_pairs={{0,192},{64,128},{128,64},{192,0},{1,193},{65,129},{129,65},{193,1... | collective-permute-start | bytes 786440 | tf_op jit(solution)/shard_map/ppermute | solution.py:35
  123.6 10.3 %collective-permute-start.26 = (bf16[128,1024]{1,0:T(8,128)(2,1)S(1)}, bf16[128,1024]{1,0:T(8,128)(2,1)S(1)}, u32[]{:S(2)}, u32[]{:S(2)}) collective-permute-start(bf16[128,1024]{1,0:T(8,128)(2,1)S(1)} %add_convert_fusion.4), channel_id=1, source_target_pairs={{0,64},{64,0},{128,192},{192,128},{1,65},{65,1},{129,193},{193,129... | collective-permute-start | bytes 786440 | tf_op jit(solution)/shard_map/ppermute | solution.py:35
  127.2 17.3 %collective-permute-start.22 = (bf16[64,2048]{1,0:T(8,128)(2,1)S(1)}, bf16[64,2048]{1,0:T(8,128)(2,1)S(1)}, u32[]{:S(2)}, u32[]{:S(2)}) collective-permute-start(bf16[64,2048]{1,0:T(8,128)(2,1)S(1)} %add_convert_fusion.3), channel_id=1, source_target_pairs={{0,192},{64,128},{128,64},{192,0},{1,193},{65,129},{129,65},{193,1... | collective-permute-start | bytes 786440 | tf_op jit(solution)/shard_map/ppermute | solution.py:35
  131.8 14.9 %collective-permute-start.24 = (bf16[64,2048]{1,0:T(8,128)(2,1)S(1)}, bf16[64,2048]{1,0:T(8,128)(2,1)S(1)}, u32[]{:S(2)}, u32[]{:S(2)}) collective-permute-start(bf16[64,2048]{1,0:T(8,128)(2,1)S(1)} %add_convert_fusion.2), channel_id=1, source_target_pairs={{0,64},{64,0},{128,192},{192,128},{1,65},{65,1},{129,193},{193,129... | collective-permute-start | bytes 786440 | tf_op jit(solution)/shard_map/ppermute | solution.py:35
  134.0 14.9 %collective-permute-start.27 = (bf16[64,2048]{1,0:T(8,128)(2,1)S(1)}, bf16[64,2048]{1,0:T(8,128)(2,1)S(1)}, u32[]{:S(2)}, u32[]{:S(2)}) collective-permute-start(bf16[64,2048]{1,0:T(8,128)(2,1)S(1)} %pad_maximum_fusion.4), channel_id=1, source_target_pairs={{0,6},{2,4},{4,2},{6,0},{1,7},{3,5},{5,3},{7,1},{8,14},{10,12},{12... | collective-permute-start | bytes 786440 | tf_op jit(solution)/shard_map/ppermute | solution.py:35
  144.7 11.7 %collective-permute-start.28 = (bf16[32,2048]{1,0:T(8,128)(2,1)S(1)}, bf16[32,2048]{1,0:T(8,128)(2,1)S(1)}, u32[]{:S(2)}, u32[]{:S(2)}) collective-permute-start(bf16[32,2048]{1,0:T(8,128)(2,1)S(1)} %get-tuple-element.91), channel_id=1, source_target_pairs={{0,64},{64,0},{128,192},{192,128},{1,65},{65,1},{129,193},{193,129... | collective-permute-start | bytes 393224 | tf_op jit(solution)/shard_map/ppermute | solution.py:35
  (13 other events, 192.4 us)
